TPU v7x, 512 devices: a whole 4x8x8 slice. The times are simulated.
512 devices in a mesh: replica: 32 (over z_hi, y, core), fsdp: 16 (over x, z_lo).
Axes of the slice: x: 4, y: 8, z: 8 (z_hi: 2, z_lo: 4; z = z_hi * 4 + z_lo), core: 2. Of those that a mesh axis runs over, the one named last changes fastest.
Arguments:
- hidden: bfloat16 [32, 2, 1024, 8192], P('replica', None, 'fsdp'), may hold values from -6 to 6
- targets: bfloat16 [32, 2, 1024, 512], P('replica', None, 'fsdp'), may hold values from -16 to 16
- doc_ids: int32 [32, 2, 1024], P('replica', None, 'fsdp'), may hold values from 0 to 7, never falling along the last dimension, each value on 1 to 256 neighbouring positions
- weights: bfloat16 [32, 8192, 512], P('replica', 'fsdp'), may hold values from -5 to 5
- adam_m: bfloat16 [32, 8192, 512], P('replica', 'fsdp'), may hold values from -6.67572e-06 to 6.67572e-06
- adam_v: bfloat16 [32, 8192, 512], P('replica', 'fsdp'), may hold values from 9.05942e-14 to 9.094947e-12
- anchor: bfloat16 [8192, 128], P('fsdp'), may hold values from -5 to 5
- momentum: bfloat16 [8192, 128], P('fsdp'), may hold values from -5 to 5
- fragment: int32 [1], replicated, may hold values from 0 to 3
Outputs:
- new_weights: float32 [32, 8192, 512], P('replica', 'fsdp')
- losses: float32 [32, 2], P('replica')
Inputs may be any that keep to these rules, and one draw needn't show every extreme that they name: `doc_ids`: in each row (replica, step) the document numbers never fall, every number 0 to 7 occurs, each document has 1 to 256 tokens and one has exactly 256.
All inputs are finite; a program needn't handle non-finite values.
Results may differ from a plain program's by a relative error of at most 0.0003.
Values may be sent and summed in bfloat16 or wider, within the bound.
No kernel may reach another device: no remote copies, remote signals or barrier semaphores. Data moves between devices by JAX's collectives and lax.ppermute only.
A program may use at most 64 MiB of HBM per device.

v0:
```python
import jax
import jax.numpy as jnp
from jax import lax
from jax.sharding import PartitionSpec as P

DOCS = 8


NORM_EPS = 1e-05
ADAM_EPS = 1e-08
INNER_RATE = 0.1
DECAY_RATE = 0.1
BETA_FIRST = 0.9
BETA_SECOND = 0.95
OUTER_RATE = 0.7
NESTEROV = 0.9
MIXING = 0.5


def normalize(block):
    wide = block.astype(jnp.float32)
    power = jnp.mean(wide * wide, axis=-1, keepdims=True)
    return (wide * lax.rsqrt(power + NORM_EPS)).astype(jnp.bfloat16)


def outer_update(anchor_rows, moment_rows, mean_delta):
    new_moment = NESTEROV * moment_rows + mean_delta
    return anchor_rows - OUTER_RATE * (mean_delta + NESTEROV * new_moment)


def adam_update(master, first, second, gradient):
    first = BETA_FIRST * first + (1.0 - BETA_FIRST) * gradient
    second = BETA_SECOND * second + (1.0 - BETA_SECOND) * gradient * gradient
    master = master - INNER_RATE * (first / (jnp.sqrt(second) + ADAM_EPS) + DECAY_RATE * master)
    return (master, first, second)


def body(hidden, targets, doc_ids, weights, adam_m, adam_v, anchor, momentum, fragment):
    steps_total = hidden.shape[1]
    model_width = hidden.shape[3]
    value_width = weights.shape[2]
    shard_rows = weights.shape[1]
    frag_width = anchor.shape[1]
    scale = model_width ** (-0.5)
    zero = jnp.zeros((), jnp.int32)
    start = fragment[0] * frag_width
    local = lax.dynamic_slice(weights[0], (zero, start), (shard_rows, frag_width))
    delta = anchor.astype(jnp.float32) - local.astype(jnp.float32)
    replicas = lax.axis_size("replica")
    mean_delta = lax.psum(delta, "replica") / replicas
    global_fragment = outer_update(
        anchor.astype(jnp.float32), momentum.astype(jnp.float32), mean_delta
    )
    doc_range = jnp.arange(DOCS, dtype=jnp.int32)
    onehot = (doc_ids[0][..., None] == doc_range).astype(jnp.float32)
    counts = lax.psum(jnp.sum(onehot, axis=1), "fsdp")
    inverse = 1.0 / (DOCS * counts)
    normed_all = normalize(hidden[0])
    master = weights[0].astype(jnp.float32)
    first = adam_m[0].astype(jnp.float32)
    second = adam_v[0].astype(jnp.float32)
    partial_losses = []
    for step_index in range(steps_total):
        normed = normed_all[step_index]
        columns = lax.all_to_all(normed, "fsdp", split_axis=1, concat_axis=0, tiled=True)
        current = master.astype(jnp.bfloat16)
        weight_row = jnp.dot(
            onehot[step_index], inverse[step_index], precision=lax.Precision.HIGHEST
        )
        empty = jnp.zeros((shard_rows, value_width), jnp.float32)

        def project(first_row, count, columns=columns, current=current):
            return jnp.dot(columns, current, preferred_element_type=jnp.float32)

        values = (
            lax.psum_scatter(
                project(jnp.int32(0), normed.shape[0] * lax.axis_size("fsdp")),
                "fsdp",
                scatter_dimension=0,
                tiled=True,
            )
            * scale
        )
        error = values - targets[0, step_index].astype(jnp.float32)
        partial_losses.append(jnp.sum(weight_row * 0.5 * jnp.mean(error * error, axis=-1)))
        error_grad = (weight_row[:, None] * error / value_width).astype(jnp.bfloat16)

        def accumulate(carry, piece, first_row, columns=columns):
            return lax.dot_general(
                columns, piece, (((0,), (0,)), ((), ())), preferred_element_type=jnp.float32
            )

        gradient = (
            accumulate(empty, lax.all_gather(error_grad, "fsdp", axis=0, tiled=True), jnp.int32(0))
            * scale
        )
        master, first, second = adam_update(master, first, second, gradient)
    losses = lax.psum(jnp.stack(partial_losses), "fsdp")
    merged = (
        MIXING * lax.dynamic_slice(master, (zero, start), (shard_rows, frag_width))
        + (1.0 - MIXING) * global_fragment
    )
    master = lax.dynamic_update_slice(master, merged, (zero, start))
    return (master[None], losses[None])


def solution(mesh):
    placed = (
        P("replica", None, "fsdp", None),
        P("replica", None, "fsdp", None),
        P("replica", None, "fsdp"),
        P("replica", "fsdp", None),
        P("replica", "fsdp", None),
        P("replica", "fsdp", None),
        P("fsdp", None),
        P("fsdp", None),
        P(),
    )
    return jax.shard_map(
        body,
        mesh=mesh,
        in_specs=placed,
        out_specs=(P("replica", "fsdp", None), P("replica", None)),
        check_vma=False,
    )
```

profile of v0, /device:TPU:56, one launch (start us, length us, event | category | flops | bytes accessed | tf_op | source)
XLA Modules:
  0.0 677.5 jit_solution(8864248015249444035)
XLA Ops:
  8.1 2.2 fusion
  10.3 0.4 fusion.1
  11.3 0.6 copy.15
  11.9 37.4 %all_to_all.38 = bf16[64,16,512]{2,0,1:T(8,128)(2,1)S(1)} all-to-all(bf16[64,16,512]{2,0,1:T(8,128)(2,1)S(1)} %copy.15), channel_id=1, replica_groups=mesh['replica'=32,'fsdp'=16] {'fsdp'}, dimensions={1} | all-to-all | bytes 2097152 | tf_op jit(solution)/shard_map/all_to_all | solution.py:65
  49.3 2.1 fusion.4
  51.5 39.9 %psum.21 = f32[2,8]{1,0:T(2,128)S(1)} all-reduce(f32[2,8]{1,0:T(2,128)S(1)} %convert_reduce_fusion), channel_id=1, replica_groups=mesh['replica'=32,'fsdp'=16] {'fsdp'}, use_global_device_ids=true, to_apply=%region_2.0 | all-reduce | flops 16 | bytes 128 | tf_op jit(solution)/shard_map/psum | solution.py:56
  91.5 54.1 %reduce-scatter.3.cloned.1.call-done = f32[64,512]{1,0:T(8,128)} async-done(((f32[1024,512]{1,0:T(8,128)}), f32[64,512]{1,0:T(8,128)}) %reduce-scatter.3.cloned.1.call-update) | async-done | bytes 131088 | tf_op jit(solution)/shard_map/reduce_scatter | solution.py:76
  145.6 1.6 multiply_convert_fusion.1
  147.6 1.6 copy.16
  149.3 3.7 all-to-all-start.1
  153.0 78.4 %all-gather.3.cloned.1.call-done = bf16[1024,512]{1,0:T(8,128)(2,1)} async-done(((bf16[64,512]{1,0:T(8,128)(2,1)}), bf16[1024,512]{1,0:T(8,128)(2,1)}) %all-gather.3.cloned.1.call-update) | async-done | bytes 1048592 | tf_op jit(solution)/shard_map/all_gather | solution.py:94
  231.4 2.9 fusion.13
  234.3 4.1 fusion.6
  238.6 92.6 %reduce-scatter.5.cloned.1.call-done = f32[64,512]{1,0:T(8,128)} async-done(((f32[1024,512]{1,0:T(8,128)}), f32[64,512]{1,0:T(8,128)}) %reduce-scatter.5.cloned.1.call-update) | async-done | bytes 131088 | tf_op jit(solution)/shard_map/reduce_scatter | solution.py:76
  331.1 1.7 multiply_reduce_fusion.1
  333.6 0.8 convert_subtract_fusion.2
  334.3 0.6 multiply_reduce_fusion.2
  335.0 1.3 maximum_bitcast_fusion
  336.3 39.3 %psum.23 = f32[1,2]{1,0:T(1,128)} all-reduce(f32[1,2]{1,0:T(1,128)S(1)} %maximum_bitcast_fusion), channel_id=1, replica_groups=mesh['replica'=32,'fsdp'=16] {'fsdp'}, use_global_device_ids=true, to_apply=%region_10.0 | all-reduce | flops 2 | bytes 16 | tf_op jit(solution)/shard_map/psum | solution.py:98
  375.7 38.7 %all-gather.5.cloned.1.call-done = bf16[1024,512]{1,0:T(8,128)(2,1)} async-done(((bf16[64,512]{1,0:T(8,128)(2,1)}), bf16[1024,512]{1,0:T(8,128)(2,1)}) %all-gather.5.cloned.1.call-update) | async-done | bytes 1048592 | tf_op jit(solution)/shard_map/all_gather | solution.py:94
  414.4 3.8 multiply_subtract_fusion
  418.3 250.0 %all-reduce.2.cloned.1.call-done = f32[512,128]{1,0:T(8,128)} async-done(((f32[512,128]{1,0:T(8,128)}), f32[512,128]{1,0:T(8,128)}) %all-reduce.2.cloned.1.call-update) | async-done | bytes 262160 | tf_op jit(solution)/shard_map/psum | solution.py:50
  668.3 1.1 fusion.11
  669.4 1.0 copy-done.1
  (38 shorter events, 1.6 us)
Async XLA Ops:
  8.0 2.3 copy-start
  8.0 137.6 %reduce-scatter.3.cloned.1.call-start = ((), (), s32[]{:S(2)}) async-start(), calls=%async_computation.4 | async-start | bytes 2228224 | tf_op jit(solution)/shard_map/reduce_scatter | solution.py:76
  11.3 38.0 %copy-start.2 = (bf16[1,512,512]{2,1,0:T(8,128)(2,1)S(1)}, bf16[1,512,512]{2,1,0:T(8,128)(2,1)}, u32[]{:S(2)}) copy-start(bf16[1,512,512]{2,1,0:T(8,128)(2,1)} %param.12) | copy-start | bytes 1572868
  49.2 2.1 copy-start.7
  49.3 96.4 %copy-start.5 = (bf16[1,2,64,512]{3,2,1,0:T(8,128)(2,1)S(1)}, bf16[1,2,64,512]{3,2,1,0:T(8,128)(2,1)}, u32[]{:S(2)}) copy-start(bf16[1,2,64,512]{3,2,1,0:T(8,128)(2,1)} %param.10) | copy-start | bytes 393220
  51.3 180.0 %all-gather.3.cloned.1.call-start = ((), (), s32[]{:S(2)}) async-start(), calls=%async_computation.5 | async-start | bytes 1114112 | tf_op jit(solution)/shard_map/all_gather | solution.py:94
  149.3 85.0 %all-to-all-start.1 = ((bf16[64,16,512]{2,0,1:T(8,128)(2,1)}), bf16[64,16,512]{2,0,1:T(8,128)(2,1)S(1)}, u32[]{:S(2)}, u32[]{:S(2)}) async-start(bf16[64,16,512]{2,0,1:T(8,128)(2,1)} %copy.16), calls=%async_computation.2 | async-start | bytes 2097152 | tf_op jit(solution)/shard_map/all_to_all | solution.py:65
  152.9 81.4 %copy-start.8 = (bf16[1,512,512]{2,1,0:T(8,128)(2,1)S(1)}, bf16[1,512,512]{2,1,0:T(8,128)(2,1)}, u32[]{:S(2)}) copy-start(bf16[1,512,512]{2,1,0:T(8,128)(2,1)} %param.13) | copy-start | bytes 1572868
  152.9 178.2 %reduce-scatter.5.cloned.1.call-start = ((), (), s32[]{:S(2)}) async-start(), calls=%async_computation.6 | async-start | bytes 2228224 | tf_op jit(solution)/shard_map/reduce_scatter | solution.py:76
  238.4 92.8 %copy-start.3 = (f32[64,512]{1,0:T(8,128)S(1)}, f32[64,512]{1,0:T(8,128)}, u32[]{:S(2)}) copy-start(f32[64,512]{1,0:T(8,128)} %reduce-scatter.3.cloned.1.call-done) | copy-start | bytes 393220
  238.4 95.2 %copy-start.4 = (bf16[512,128]{1,0:T(8,128)(2,1)S(1)}, bf16[512,128]{1,0:T(8,128)(2,1)}, u32[]{:S(2)}) copy-start(bf16[512,128]{1,0:T(8,128)(2,1)} %param.15) | copy-start | bytes 393220
  238.4 176.0 %all-gather.5.cloned.1.call-start = ((), (), s32[]{:S(2)}) async-start(), calls=%async_computation.7 | async-start | bytes 1114112 | tf_op jit(solution)/shard_map/all_gather | solution.py:94
  332.9 335.4 %all-reduce.2.cloned.1.call-start = ((), (), s32[]{:S(2)}) async-start(), calls=%async_computation.8 | async-start | bytes 524288 | tf_op jit(solution)/shard_map/psum | solution.py:50
  418.2 250.1 %copy-start.6 = (bf16[512,128]{1,0:T(8,128)(2,1)S(1)}, bf16[512,128]{1,0:T(8,128)(2,1)}, u32[]{:S(2)}) copy-start(bf16[512,128]{1,0:T(8,128)(2,1)} %param.16) | copy-start | bytes 393220
  669.3 1.0 copy-start.1
Sparse Core Ops, SparseCore 0:
  51.5 94.1 reduce-scatter.2
  148.3 83.0 all-gather.2
  238.5 92.5 reduce-scatter.4
  333.1 81.2 all-gather.4
Sparse Core Ops, SparseCore 1:
  336.4 331.8 all-reduce.1
where the time goes:
time: 682 us; the launch traced here: 677 us
  waiting for transfers between devices  514 us (75%)
  blocking collectives  117 us (17%)
  between operations  16 us (2%)
  matrix products  13.1 us (2%)
  other arithmetic  9.91 us (1%)
    psum x1, waiting for transfers between devices, body(): mean_delta = lax.psum(delta, 'replica') / replicas  250 us
    reduce_scatter x2, waiting for transfers between devices, body(): lax.psum_scatter(project(jnp.int32(0), normed.shape[0] * lax.axis_size('f...  147 us
    all_gather x2, waiting for transfers between devices, body(): lax.all_gather(error_grad, 'fsdp', axis=0, tiled=True)  117 us
    psum x1, blocking collectives, body(): counts = lax.psum(jnp.sum(onehot, axis=1), 'fsdp')  39.9 us
    psum x1, blocking collectives, body(): losses = lax.psum(jnp.stack(partial_losses), 'fsdp')  39.3 us
    all_to_all x1, blocking collectives, body(): lax.all_to_all(normed, 'fsdp', split_axis=1, concat_axis=0, tiled=True)  37.4 us
  transfers between devices with their start and end apart: 6, of which 5 were waited for; matrix products, arithmetic and copies ran while one was open for 2% of the time, Pallas kernels for 0%

commit v1 on v0

v1 whole, which is shorter than its diff:
```python
import jax
import jax.numpy as jnp
from jax import lax
from jax.sharding import Mesh, PartitionSpec as P

DOCS = 8


NORM_EPS = 1e-05
ADAM_EPS = 1e-08
INNER_RATE = 0.1
DECAY_RATE = 0.1
BETA_FIRST = 0.9
BETA_SECOND = 0.95
OUTER_RATE = 0.7
NESTEROV = 0.9
MIXING = 0.5

REPLICA = ("zh", "y", "c")
FSDP = ("x", "zl")
EXTRA = 16


def normalize(block):
    wide = block.astype(jnp.float32)
    power = jnp.mean(wide * wide, axis=-1, keepdims=True)
    return (wide * lax.rsqrt(power + NORM_EPS)).astype(jnp.bfloat16)


def adam_update(master, first, second, gradient):
    first = BETA_FIRST * first + (1.0 - BETA_FIRST) * gradient
    second = BETA_SECOND * second + (1.0 - BETA_SECOND) * gradient * gradient
    master = master - INNER_RATE * (first / (jnp.sqrt(second) + ADAM_EPS) + DECAY_RATE * master)
    return (master, first, second)


def exchange(blocks, axes):
    return lax.all_to_all(blocks, axes, split_axis=0, concat_axis=0, tiled=False)


def split_up(value):
    high = value.astype(jnp.bfloat16)
    rest = value - high.astype(jnp.float32)
    middle = rest.astype(jnp.bfloat16)
    low = (rest - middle.astype(jnp.float32)).astype(jnp.bfloat16)
    return high, middle, low


def body(hidden, targets, doc_ids, weights, adam_m, adam_v, anchor, momentum, fragment):
    steps_total, rows, model_width = hidden.shape[1:]
    shard_rows, value_width = weights.shape[1:]
    frag_width = anchor.shape[1]
    nx, nz = lax.axis_size("x"), lax.axis_size("zl")
    shards = nx * nz
    scale = model_width ** (-0.5)
    zero = jnp.zeros((), jnp.int32)
    start = fragment[0] * frag_width
    replicas = lax.axis_size(REPLICA)

    doc_range = jnp.arange(DOCS, dtype=jnp.int32)
    onehot = (doc_ids[0][..., None] == doc_range).astype(jnp.float32)
    local_counts = jnp.sum(onehot, axis=1).reshape(1, 1, -1)
    count_rows = jnp.pad(
        local_counts.astype(jnp.bfloat16),
        ((0, 0), (0, EXTRA - 1), (0, value_width - steps_total * DOCS)),
    )

    columns = []
    for step_index in range(steps_total):
        normed = normalize(hidden[0, step_index])
        blocks = normed.reshape(rows, shards, shard_rows).transpose(1, 0, 2)
        columns.append(exchange(blocks, FSDP).reshape(shards * rows, shard_rows))

    local = lax.dynamic_slice(weights[0], (zero, start), (shard_rows, frag_width))
    pieces = exchange(local.reshape(replicas, shard_rows // replicas, frag_width), REPLICA)
    mean_piece = jnp.sum(pieces.astype(jnp.float32), axis=0) / replicas
    mean_weights = exchange(
        jnp.broadcast_to(mean_piece[None], (replicas,) + mean_piece.shape), REPLICA
    ).reshape(shard_rows, frag_width)
    anchor_rows = anchor.astype(jnp.float32)
    mean_delta = anchor_rows - mean_weights
    new_moment = NESTEROV * momentum.astype(jnp.float32) + mean_delta
    global_fragment = anchor_rows - OUTER_RATE * (mean_delta + NESTEROV * new_moment)

    master = weights[0].astype(jnp.float32)
    first = adam_m[0].astype(jnp.float32)
    second = adam_v[0].astype(jnp.float32)
    losses = []
    inverse = None
    for step_index in range(steps_total):
        current = master.astype(jnp.bfloat16)
        partial = jnp.dot(columns[step_index], current, preferred_element_type=jnp.float32)
        partial = partial.astype(jnp.bfloat16).reshape(nx, nz, rows, value_width)
        if step_index == 0:
            extra = jnp.broadcast_to(count_rows[None], (nx, nz, EXTRA, value_width))
            partial = jnp.concatenate([partial, extra], axis=2)
        block = partial.shape[2]
        partial = exchange(partial.reshape(nx, nz * block, value_width), "x")
        partial = jnp.sum(partial.astype(jnp.float32), axis=0).astype(jnp.bfloat16)
        partial = exchange(partial.reshape(nz, block, value_width), "zl")
        total = jnp.sum(partial.astype(jnp.float32), axis=0)
        if step_index == 0:
            counts = total[rows, : steps_total * DOCS].reshape(steps_total, DOCS)
            inverse = 1.0 / (DOCS * counts)
        values = total[:rows] * scale
        weight_row = jnp.sum(onehot[step_index] * inverse[step_index][None], axis=1)
        error = values - targets[0, step_index].astype(jnp.float32)
        loss = jnp.sum(weight_row * 0.5 * jnp.mean(error * error, axis=-1))
        error_grad = (weight_row[:, None] * error / value_width).astype(jnp.bfloat16)
        terms = jnp.stack(split_up(loss)).reshape(1, 3)
        loss_rows = jnp.pad(terms, ((0, EXTRA - 1), (0, value_width - 3)))
        sent = jnp.concatenate([error_grad, loss_rows], axis=0)
        got = exchange(jnp.broadcast_to(sent[None], (nz,) + sent.shape), "zl")
        got = exchange(jnp.broadcast_to(got[None], (nx,) + got.shape), "x")
        got = got.reshape(shards, rows + EXTRA, value_width)
        losses.append(jnp.sum(got[:, rows, :3].astype(jnp.float32)))
        everyone = got[:, :rows].reshape(shards * rows, value_width)
        gradient = (
            lax.dot_general(
                columns[step_index],
                everyone,
                (((0,), (0,)), ((), ())),
                preferred_element_type=jnp.float32,
            )
            * scale
        )
        master, first, second = adam_update(master, first, second, gradient)
    merged = (
        MIXING * lax.dynamic_slice(master, (zero, start), (shard_rows, frag_width))
        + (1.0 - MIXING) * global_fragment
    )
    master = lax.dynamic_update_slice(master, merged, (zero, start))
    return (master[None], jnp.stack(losses)[None])


def solution(mesh):
    fine = Mesh(mesh.devices.reshape(2, 8, 2, 4, 4), REPLICA + FSDP)
    placed = (
        P(REPLICA, None, FSDP, None),
        P(REPLICA, None, FSDP, None),
        P(REPLICA, None, FSDP),
        P(REPLICA, FSDP, None),
        P(REPLICA, FSDP, None),
        P(REPLICA, FSDP, None),
        P(FSDP, None),
        P(FSDP, None),
        P(),
    )
    return jax.shard_map(
        body,
        mesh=fine,
        in_specs=placed,
        out_specs=(P(REPLICA, FSDP, None), P(REPLICA, None)),
        check_vma=False,
    )
```

time: 682 us -> 262 us (0.38)
  waiting for transfers between devices: 514 us -> 110 us
  blocking collectives: 117 us -> 62.3 us
  starting transfers between devices: 3.86 us -> 47.2 us
  between operations: 16 us -> 4.2 us
    psum x1 -> x0, waiting for transfers between devices: 250 us -> none  [body(): mean_delta = lax.psum(delta, 'replica') / replicas]
    reduce_scatter x2 -> x0, waiting for transfers between devices: 147 us -> none  [body(): lax.psum_scatter(project(jnp.int32(0), normed.shape[0] * lax.axis_size('f...]
    all_gather x2 -> x0, waiting for transfers between devices: 117 us -> none  [body(): lax.all_gather(error_grad, 'fsdp', axis=0, tiled=True)]
    all_to_all x1 -> x8, waiting for transfers between devices: 0.01 us -> 110 us  [exchange(): lax.all_to_all(blocks, axes, split_axis=0, concat_axis=0, tiled=False)]
    psum x2 -> x0, blocking collectives: 79.2 us -> none  [the longest x1 39.9 us: body(): counts = lax.psum(jnp.sum(onehot, axis=1), 'fsdp')]
    all_to_all x1 -> x8, starting transfers between devices: 3.65 us -> 47.2 us  [exchange(): lax.all_to_all(blocks, axes, split_axis=0, concat_axis=0, tiled=False)]
    all_to_all x1 -> x4, blocking collectives: 37.4 us -> 62.3 us  [exchange(): lax.all_to_all(blocks, axes, split_axis=0, concat_axis=0, tiled=False)]
  transfers between devices with their start and end apart: 6 -> 8, of which waited for: 5 -> 8; matrix products, arithmetic and copies ran while one was open for 2% -> 6% of each run, Pallas kernels for 0% -> 0%
where the time goes in v1:
time: 262 us; the launch traced here: 257 us
  waiting for transfers between devices  110 us (42%)
  blocking collectives  62.3 us (24%)
  starting transfers between devices  47.2 us (18%)
  other arithmetic  14.5 us (6%)
  matrix products  11.2 us (4%)
  local copies, waits for them, and re-layouts  7.66 us (3%)
  between operations  4.2 us (2%)
    all_to_all x8, waiting for transfers between devices, exchange(): lax.all_to_all(blocks, axes, split_axis=0, concat_axis=0, tiled=False)  110 us
    all_to_all x4, blocking collectives, exchange(): lax.all_to_all(blocks, axes, split_axis=0, concat_axis=0, tiled=False)  62.3 us
    all_to_all x8, starting transfers between devices, exchange(): lax.all_to_all(blocks, axes, split_axis=0, concat_axis=0, tiled=False)  47.2 us
    dot_general x2, matrix products, body(): lax.dot_general(columns[step_index], everyone, (((0,), (0,)), ((), ())),...  5.7 us
    dot_general x2, matrix products, body(): jnp.dot(columns[step_index], current, preferred_element_type=jnp.float32)  5.49 us
  transfers between devices with their start and end apart: 8, of which 8 were waited for; matrix products, arithmetic and copies ran while one was open for 6% of the time, Pallas kernels for 0%

profile of v1, /device:TPU:56, one launch (start us, length us, event | category | flops | bytes accessed | tf_op | source)
XLA Modules:
  0.0 257.5 jit_solution(14401607997472042116)
XLA Ops:
  4.6 2.1 fusion.4
  6.7 9.8 %all-to-all-start = ((bf16[16,64,512]{2,1,0:T(8,128)(2,1)}), bf16[16,64,512]{2,1,0:T(8,128)(2,1)S(1)}, u32[]{:S(2)}, u32[]{:S(2)}) async-start(bf16[16,64,512]{2,1,0:T(8,128)(2,1)} %fusion.4), calls=%async_computation | async-start | bytes 2097152 | tf_op jit(solution)/shard_map/all_to_all | solution.py:38
  16.8 27.6 %all-to-all-done = bf16[16,64,512]{2,1,0:T(8,128)(2,1)S(1)} async-done(((bf16[16,64,512]{2,1,0:T(8,128)(2,1)}), bf16[16,64,512]{2,1,0:T(8,128)(2,1)S(1)}, u32[]{:S(2)}, u32[]{:S(2)}) %all-to-all-start) | async-done | bytes 1048608 | tf_op jit(solution)/shard_map/all_to_all | solution.py:38
  46.6 19.7 %all_to_all.60 = bf16[4,320,512]{2,1,0:T(8,128)(2,1)S(1)} all-to-all(bf16[4,320,512]{2,1,0:T(8,128)(2,1)S(1)} %bitcast.116), channel_id=1, replica_groups=mesh['zh'=2,'y'=8,'c'=2,'x'=4,'zl'=4] {'x'}, dimensions={0} | all-to-all | bytes 2621440 | tf_op jit(solution)/shard_map/all_to_all | solution.py:38
  67.3 3.5 %all-to-all-start.2 = ((bf16[4,80,512]{2,1,0:T(8,128)(2,1)}), bf16[4,80,512]{2,1,0:T(8,128)(2,1)S(1)}, u32[]{:S(2)}, u32[]{:S(2)}) async-start(bf16[4,80,512]{2,1,0:T(8,128)(2,1)} %bitcast.122), calls=%async_computation.2 | async-start | bytes 655360 | tf_op jit(solution)/shard_map/all_to_all | solution.py:38
  70.8 9.0 %all-to-all-done.2 = bf16[4,80,512]{2,1,0:T(8,128)(2,1)S(1)} async-done(((bf16[4,80,512]{2,1,0:T(8,128)(2,1)}), bf16[4,80,512]{2,1,0:T(8,128)(2,1)S(1)}, u32[]{:S(2)}, u32[]{:S(2)}) %all-to-all-start.2) | async-done | bytes 327712 | tf_op jit(solution)/shard_map/all_to_all | solution.py:38
  82.2 11.8 %all_to_all.61 = bf16[4,80,512]{2,1,0:T(8,128)(2,1)S(1)} all-to-all(bf16[4,80,512]{2,1,0:T(8,128)(2,1)S(1)} %broadcast_in_dim.22), channel_id=1, replica_groups=mesh['zh'=2,'y'=8,'c'=2,'x'=4,'zl'=4] {'zl'}, dimensions={0} | all-to-all | bytes 655360 | tf_op jit(solution)/shard_map/all_to_all | solution.py:38
  95.2 3.5 %all-to-all-start.4 = ((bf16[4,4,80,512]{3,2,1,0:T(8,128)(2,1)}), bf16[4,4,80,512]{3,2,1,0:T(8,128)(2,1)S(1)}, u32[]{:S(2)}, u32[]{:S(2)}) async-start(bf16[4,4,80,512]{3,2,1,0:T(8,128)(2,1)} %broadcast_in_dim.23), calls=%async_computation.4 | async-start | bytes 2621440 | tf_op jit(solution)/shard_map/all_to_all | solution.py:38
  100.0 2.1 fusion.5
  102.1 12.0 %all-to-all-done.4 = bf16[4,4,80,512]{3,2,1,0:T(8,128)(2,1)S(1)} async-done(((bf16[4,4,80,512]{3,2,1,0:T(8,128)(2,1)}), bf16[4,4,80,512]{3,2,1,0:T(8,128)(2,1)S(1)}, u32[]{:S(2)}, u32[]{:S(2)}) %all-to-all-start.4) | async-done | bytes 1310752 | tf_op jit(solution)/shard_map/all_to_all | solution.py:38
  114.0 5.4 %all-to-all-start.5 = ((bf16[16,64,512]{2,1,0:T(8,128)(2,1)}), bf16[16,64,512]{2,1,0:T(8,128)(2,1)S(1)}, u32[]{:S(2)}, u32[]{:S(2)}) async-start(bf16[16,64,512]{2,1,0:T(8,128)(2,1)} %fusion.5), calls=%async_computation.5 | async-start | bytes 2097152 | tf_op jit(solution)/shard_map/all_to_all | solution.py:38
  121.2 24.2 %all-to-all-done.5 = bf16[16,64,512]{2,1,0:T(8,128)(2,1)S(1)} async-done(((bf16[16,64,512]{2,1,0:T(8,128)(2,1)}), bf16[16,64,512]{2,1,0:T(8,128)(2,1)S(1)}, u32[]{:S(2)}, u32[]{:S(2)}) %all-to-all-start.5) | async-done | bytes 1048608 | tf_op jit(solution)/shard_map/all_to_all | solution.py:38
  145.4 3.4 %convolution_convert_fusion = bf16[1024,512]{1,0:T(8,128)(2,1)S(1)} fusion(bf16[1024,512]{1,0:T(8,128)(2,1)S(1)} %bitcast.123, f32[512,512]{1,0:T(8,128)} %convolution_bitcast_fusion.1, bf16[1,512,512]{2,1,0:T(8,128)(2,1)} %param.13, bf16[1,512,512]{2,1,0:T(8,128)(2,1)} %param.12, bf16[1,512,512]{2,1,0:T(8,128)(2,1)} %param.14), kind=kOutput, calls=%fused_computation.6 | convolution fusion | flops 542113792 | bytes 4718592 | tf_op jit(solution)/shard_map/dot_general | solution.py:92
  148.8 16.8 %all_to_all.62 = bf16[4,256,512]{2,1,0:T(8,128)(2,1)S(1)} all-to-all(bf16[4,256,512]{2,1,0:T(8,128)(2,1)S(1)} %bitcast.126), channel_id=1, replica_groups=mesh['zh'=2,'y'=8,'c'=2,'x'=4,'zl'=4] {'x'}, dimensions={0} | all-to-all | bytes 2097152 | tf_op jit(solution)/shard_map/all_to_all | solution.py:38
  166.5 3.4 %all-to-all-start.7 = ((bf16[4,64,512]{2,1,0:T(8,128)(2,1)}), bf16[4,64,512]{2,1,0:T(8,128)(2,1)S(1)}, u32[]{:S(2)}, u32[]{:S(2)}) async-start(bf16[4,64,512]{2,1,0:T(8,128)(2,1)} %bitcast.24), calls=%async_computation.7 | async-start | bytes 524288 | tf_op jit(solution)/shard_map/all_to_all | solution.py:38
  171.3 5.4 %all-to-all-done.7 = bf16[4,64,512]{2,1,0:T(8,128)(2,1)S(1)} async-done(((bf16[4,64,512]{2,1,0:T(8,128)(2,1)}), bf16[4,64,512]{2,1,0:T(8,128)(2,1)S(1)}, u32[]{:S(2)}, u32[]{:S(2)}) %all-to-all-start.7) | async-done | bytes 262176 | tf_op jit(solution)/shard_map/all_to_all | solution.py:38
  176.7 12.8 %all-to-all-start.10 = ((bf16[32,16,128]{2,1,0:T(8,128)(2,1)}), bf16[32,16,128]{2,1,0:T(8,128)(2,1)S(1)}, u32[]{:S(2)}, u32[]{:S(2)}) async-start(bf16[32,16,128]{2,1,0:T(8,128)(2,1)} %bitcast.34), calls=%async_computation.10 | async-start | bytes 262144 | tf_op jit(solution)/shard_map/all_to_all | solution.py:38
  191.6 8.9 %all-to-all-done.10 = bf16[32,16,128]{2,1,0:T(8,128)(2,1)S(1)} async-done(((bf16[32,16,128]{2,1,0:T(8,128)(2,1)}), bf16[32,16,128]{2,1,0:T(8,128)(2,1)S(1)}, u32[]{:S(2)}, u32[]{:S(2)}) %all-to-all-start.10) | async-done | bytes 131104 | tf_op jit(solution)/shard_map/all_to_all | solution.py:38
  200.6 14.0 %all_to_all.63 = bf16[4,80,512]{2,1,0:T(8,128)(2,1)S(1)} all-to-all(bf16[4,80,512]{2,1,0:T(8,128)(2,1)S(1)} %broadcast_in_dim.24), channel_id=1, replica_groups=mesh['zh'=2,'y'=8,'c'=2,'x'=4,'zl'=4] {'zl'}, dimensions={0} | all-to-all | bytes 655360 | tf_op jit(solution)/shard_map/all_to_all | solution.py:38
  215.8 3.5 %all-to-all-start.9 = ((bf16[4,4,80,512]{3,2,1,0:T(8,128)(2,1)}), bf16[4,4,80,512]{3,2,1,0:T(8,128)(2,1)S(1)}, u32[]{:S(2)}, u32[]{:S(2)}) async-start(bf16[4,4,80,512]{3,2,1,0:T(8,128)(2,1)} %broadcast_in_dim.25), calls=%async_computation.9 | async-start | bytes 2621440 | tf_op jit(solution)/shard_map/all_to_all | solution.py:38
  220.0 16.6 %all-to-all-done.9 = bf16[4,4,80,512]{3,2,1,0:T(8,128)(2,1)S(1)} async-done(((bf16[4,4,80,512]{3,2,1,0:T(8,128)(2,1)}), bf16[4,4,80,512]{3,2,1,0:T(8,128)(2,1)S(1)}, u32[]{:S(2)}, u32[]{:S(2)}) %all-to-all-start.9) | async-done | bytes 1310752 | tf_op jit(solution)/shard_map/all_to_all | solution.py:38
  237.3 5.2 %all-to-all-start.11 = ((f32[32,16,128]{2,1,0:T(8,128)}), f32[32,16,128]{2,1,0:T(8,128)S(1)}, u32[]{:S(2)}, u32[]{:S(2)}) async-start(f32[32,16,128]{2,1,0:T(8,128)} %broadcast_in_dim.27), calls=%async_computation.11 | async-start | bytes 524288 | tf_op jit(solution)/shard_map/all_to_all | solution.py:38
  242.5 4.0 %multiply_subtract_fusion = f32[512,512]{1,0:T(8,128)S(1)} fusion(bf16[16,64,512]{2,1,0:T(8,128)(2,1)} %copy-done.1, bf16[16,80,512]{2,1,0:T(8,128)(2,1)S(1)} %bitcast.120, f32[512,512]{1,0:T(8,128)} %convolution_bitcast_fusion.1, bf16[1,512,512]{2,1,0:T(8,128)(2,1)} %param.13, bf16[1,512,512]{2,1,0:T(8,128)(2,1)} %param.14, ...), kind=kOutput, calls=%fused_computation.21 | convolution fusion | flops 544997376 | bytes 5767168 | tf_op jit(solution)/shard_map/dot_general | solution.py:119
  249.9 6.7 %all-to-all-done.11 = f32[32,16,128]{2,1,0:T(8,128)S(1)} async-done(((f32[32,16,128]{2,1,0:T(8,128)}), f32[32,16,128]{2,1,0:T(8,128)S(1)}, u32[]{:S(2)}, u32[]{:S(2)}) %all-to-all-start.11) | async-done | bytes 262176 | tf_op jit(solution)/shard_map/all_to_all | solution.py:38
  (60 shorter events, 21.8 us)
Async XLA Ops:
  0.6 2.2 copy-start
  4.6 12.0 %copy-start.8 = (s32[1,2,64]{2,1,0:T(2,128)S(1)}, s32[1,2,64]{2,1,0:T(2,128)}, u32[]{:S(2)}) copy-start(s32[1,2,64]{2,1,0:T(2,128)} %param.11) | copy-start | bytes 1540
  6.7 37.6 %all-to-all-start = ((bf16[16,64,512]{2,1,0:T(8,128)(2,1)}), bf16[16,64,512]{2,1,0:T(8,128)(2,1)S(1)}, u32[]{:S(2)}, u32[]{:S(2)}) async-start(bf16[16,64,512]{2,1,0:T(8,128)(2,1)} %fusion.4), calls=%async_computation | async-start | bytes 2097152 | tf_op jit(solution)/shard_map/all_to_all | solution.py:38
  44.3 2.3 copy-start.2
  46.6 33.4 %copy-start.4 = (bf16[1,2,64,512]{3,2,1,0:T(8,128)(2,1)S(1)}, bf16[1,2,64,512]{3,2,1,0:T(8,128)(2,1)}, u32[]{:S(2)}) copy-start(bf16[1,2,64,512]{3,2,1,0:T(8,128)(2,1)} %param.10) | copy-start | bytes 393220
  67.3 12.5 %all-to-all-start.2 = ((bf16[4,80,512]{2,1,0:T(8,128)(2,1)}), bf16[4,80,512]{2,1,0:T(8,128)(2,1)S(1)}, u32[]{:S(2)}, u32[]{:S(2)}) async-start(bf16[4,80,512]{2,1,0:T(8,128)(2,1)} %bitcast.122), calls=%async_computation.2 | async-start | bytes 655360 | tf_op jit(solution)/shard_map/all_to_all | solution.py:38
  95.2 18.8 %all-to-all-start.4 = ((bf16[4,4,80,512]{3,2,1,0:T(8,128)(2,1)}), bf16[4,4,80,512]{3,2,1,0:T(8,128)(2,1)S(1)}, u32[]{:S(2)}, u32[]{:S(2)}) async-start(bf16[4,4,80,512]{3,2,1,0:T(8,128)(2,1)} %broadcast_in_dim.23), calls=%async_computation.4 | async-start | bytes 2621440 | tf_op jit(solution)/shard_map/all_to_all | solution.py:38
  100.0 19.5 %copy-start.3 = (bf16[16,64,512]{2,1,0:T(8,128)(2,1)S(1)}, bf16[16,64,512]{2,1,0:T(8,128)(2,1)}, u32[]{:S(2)}) copy-start(bf16[16,64,512]{2,1,0:T(8,128)(2,1)} %copy-done.2) | copy-start | bytes 3145732
  114.0 31.3 %all-to-all-start.5 = ((bf16[16,64,512]{2,1,0:T(8,128)(2,1)}), bf16[16,64,512]{2,1,0:T(8,128)(2,1)S(1)}, u32[]{:S(2)}, u32[]{:S(2)}) async-start(bf16[16,64,512]{2,1,0:T(8,128)(2,1)} %fusion.5), calls=%async_computation.5 | async-start | bytes 2097152 | tf_op jit(solution)/shard_map/all_to_all | solution.py:38
  145.4 3.4 %copy-start.1 = (bf16[16,64,512]{2,1,0:T(8,128)(2,1)}, bf16[16,64,512]{2,1,0:T(8,128)(2,1)S(1)}, u32[]{:S(2)}) copy-start(bf16[16,64,512]{2,1,0:T(8,128)(2,1)S(1)} %all-to-all-done.5) | copy-start | bytes 3145732
  148.8 21.8 %copy-start.7 = (bf16[1,512,512]{2,1,0:T(8,128)(2,1)S(1)}, bf16[1,512,512]{2,1,0:T(8,128)(2,1)}, u32[]{:S(2)}) copy-start(bf16[1,512,512]{2,1,0:T(8,128)(2,1)} %param.12) | copy-start | bytes 1572868
  166.5 10.2 %all-to-all-start.7 = ((bf16[4,64,512]{2,1,0:T(8,128)(2,1)}), bf16[4,64,512]{2,1,0:T(8,128)(2,1)S(1)}, u32[]{:S(2)}, u32[]{:S(2)}) async-start(bf16[4,64,512]{2,1,0:T(8,128)(2,1)} %bitcast.24), calls=%async_computation.7 | async-start | bytes 524288 | tf_op jit(solution)/shard_map/all_to_all | solution.py:38
  176.7 23.9 %all-to-all-start.10 = ((bf16[32,16,128]{2,1,0:T(8,128)(2,1)}), bf16[32,16,128]{2,1,0:T(8,128)(2,1)S(1)}, u32[]{:S(2)}, u32[]{:S(2)}) async-start(bf16[32,16,128]{2,1,0:T(8,128)(2,1)} %bitcast.34), calls=%async_computation.10 | async-start | bytes 262144 | tf_op jit(solution)/shard_map/all_to_all | solution.py:38
  215.8 20.8 %all-to-all-start.9 = ((bf16[4,4,80,512]{3,2,1,0:T(8,128)(2,1)}), bf16[4,4,80,512]{3,2,1,0:T(8,128)(2,1)S(1)}, u32[]{:S(2)}, u32[]{:S(2)}) async-start(bf16[4,4,80,512]{3,2,1,0:T(8,128)(2,1)} %broadcast_in_dim.25), calls=%async_computation.9 | async-start | bytes 2621440 | tf_op jit(solution)/shard_map/all_to_all | solution.py:38
  237.3 19.3 %all-to-all-start.11 = ((f32[32,16,128]{2,1,0:T(8,128)}), f32[32,16,128]{2,1,0:T(8,128)S(1)}, u32[]{:S(2)}, u32[]{:S(2)}) async-start(f32[32,16,128]{2,1,0:T(8,128)} %broadcast_in_dim.27), calls=%async_computation.11 | async-start | bytes 524288 | tf_op jit(solution)/shard_map/all_to_all | solution.py:38
  246.5 10.2 %copy-start.5 = (bf16[512,128]{1,0:T(8,128)(2,1)S(1)}, bf16[512,128]{1,0:T(8,128)(2,1)}, u32[]{:S(2)}) copy-start(bf16[512,128]{1,0:T(8,128)(2,1)} %param.15) | copy-start | bytes 393220
  246.5 10.2 %copy-start.6 = (bf16[512,128]{1,0:T(8,128)(2,1)S(1)}, bf16[512,128]{1,0:T(8,128)(2,1)}, u32[]{:S(2)}) copy-start(bf16[512,128]{1,0:T(8,128)(2,1)} %param.16) | copy-start | bytes 393220

commit v2 on v1

v2 whole, which is shorter than its diff:
```python
import functools

import jax
import jax.numpy as jnp
from jax import lax
from jax.experimental import pallas as pl
from jax.experimental.pallas import tpu as pltpu
from jax.sharding import Mesh, PartitionSpec as P

DOCS = 8


NORM_EPS = 1e-05
ADAM_EPS = 1e-08
INNER_RATE = 0.1
DECAY_RATE = 0.1
BETA_FIRST = 0.9
BETA_SECOND = 0.95
OUTER_RATE = 0.7
NESTEROV = 0.9
MIXING = 0.5

REPLICA = ("zh", "y", "c")
FSDP = ("x", "zf", "zn")
ORDER = ("x", "zn", "zf")
GROUP = ("x", "zn")
EXTRA = 16
CHUNK = 16
VMEM = 48 * 1024 * 1024

bf16, f32 = jnp.bfloat16, jnp.float32


def adam_update(master, first, second, gradient):
    first = BETA_FIRST * first + (1.0 - BETA_FIRST) * gradient
    second = BETA_SECOND * second + (1.0 - BETA_SECOND) * gradient * gradient
    master = master - INNER_RATE * (first / (jnp.sqrt(second) + ADAM_EPS) + DECAY_RATE * master)
    return (master, first, second)


def exchange(blocks, axes):
    return lax.all_to_all(blocks, axes, split_axis=0, concat_axis=0, tiled=False)


def swap(block, axis, bit=1):
    size = lax.axis_size(axis)
    return lax.ppermute(block, axis, [(i, i ^ bit) for i in range(size)])


def tie(*values):
    return lax.optimization_barrier(values)


def normalize_kernel(width, hidden_ref, out_ref):
    wide = hidden_ref[0, 0].astype(f32)
    power = jnp.mean(wide * wide, axis=-1, keepdims=True)
    normed = (wide * lax.rsqrt(power + NORM_EPS)).astype(bf16)
    for at in range(out_ref.shape[0]):
        x, zn, zf = at // 4, (at // 2) % 2, at % 2
        owner = x * 4 + zf * 2 + zn
        out_ref[at] = normed[:, owner * width : (owner + 1) * width]


def normalize(hidden, step, shards):
    rows, model_width = hidden.shape[2:]
    width = model_width // shards
    return pl.pallas_call(
        functools.partial(normalize_kernel, width),
        grid=(rows // CHUNK,),
        in_specs=[pl.BlockSpec((1, 1, CHUNK, model_width), lambda i: (0, step, i, 0))],
        out_specs=pl.BlockSpec((shards, CHUNK, width), lambda i: (0, i, 0)),
        out_shape=jax.ShapeDtypeStruct((shards, rows, width), bf16),
        compiler_params=pltpu.CompilerParams(vmem_limit_bytes=VMEM),
        cost_estimate=pl.CostEstimate(
            flops=4 * rows * model_width, bytes_accessed=4 * rows * model_width, transcendentals=rows
        ),
        name="normalize",
    )(hidden)


def error_kernel(scale, with_counts, own_ref, got_ref, target_ref, hot_ref, *rest):
    if with_counts:
        out_ref, inverse_ref = rest
    else:
        inverse_in_ref, out_ref = rest
    tokens, columns = target_ref.shape
    total = own_ref[:tokens] + got_ref[:tokens].astype(f32)
    if with_counts:
        counts = (own_ref[tokens:] + got_ref[tokens:].astype(f32))[:1, :128]
        inverse = jnp.where(counts > 0.0, 1.0 / (DOCS * jnp.maximum(counts, 1.0)), 0.0)
        inverse_ref[...] = jnp.broadcast_to(inverse, inverse_ref.shape)
    else:
        inverse = inverse_in_ref[:1]
    weight = jnp.sum(hot_ref[...] * inverse, axis=-1, keepdims=True)
    error = total * scale - target_ref[...].astype(f32)
    grad = (weight * error / columns).astype(bf16)
    each = jnp.sum(error * error, axis=-1, keepdims=True) / columns
    loss = jnp.sum(weight * 0.5 * each, axis=0, keepdims=True)
    high = loss.astype(bf16).astype(f32)
    middle = (loss - high).astype(bf16).astype(f32)
    low = loss - high - middle
    lane = lax.broadcasted_iota(jnp.int32, (EXTRA, columns), 1)
    row = jnp.where(lane == 0, high, jnp.where(lane == 1, middle, jnp.where(lane == 2, low, 0.0)))
    row = row.astype(bf16)
    for at in range(out_ref.shape[0]):
        out_ref[at, :tokens] = grad
        out_ref[at, tokens:] = row


def errors(own, got, target, hot, inverse, copies, scale):
    tokens, columns = target.shape
    sent = jax.ShapeDtypeStruct((copies, tokens + EXTRA, columns), bf16)
    kept = jax.ShapeDtypeStruct((8, 128), f32)
    with_counts = inverse is None
    return pl.pallas_call(
        functools.partial(error_kernel, scale, with_counts),
        out_shape=(sent, kept) if with_counts else sent,
        compiler_params=pltpu.CompilerParams(vmem_limit_bytes=VMEM),
        cost_estimate=pl.CostEstimate(
            flops=8 * tokens * columns, bytes_accessed=30 * tokens * columns, transcendentals=0
        ),
        name="errors",
    )(own, got, target, hot, *(() if with_counts else (inverse,)))


def body(hidden, targets, doc_ids, weights, adam_m, adam_v, anchor, momentum, fragment):
    steps_total, rows, model_width = hidden.shape[1:]
    shard_rows, value_width = weights.shape[1:]
    frag_width = anchor.shape[1]
    nx, nn, nf = (lax.axis_size(a) for a in ORDER)
    shards, groups = nx * nn * nf, nx * nn
    x_at, n_at, f_at = (lax.axis_index(a) for a in ORDER)
    scale = model_width ** (-0.5)
    zero = jnp.zeros((), jnp.int32)
    start = fragment[0] * frag_width
    replicas = lax.axis_size(REPLICA)
    tokens = nf * rows

    def pick(array, at, axis):
        return lax.dynamic_index_in_dim(array, at, axis, keepdims=False)

    blocks = normalize(hidden, 0, shards)
    blocks, hidden, weights, targets, doc_ids = tie(blocks, hidden, weights, targets, doc_ids)
    columns = exchange(blocks, ORDER).reshape(shards * rows, shard_rows)

    blocks = normalize(hidden, 1, shards).reshape(nx, nn, nf, rows, shard_rows)
    over_x = [pick(blocks, x_at, 0)]
    for bit in range(1, nx):
        over_x.append(swap(pick(blocks, x_at ^ bit, 0), "x", bit))
    over_x = jnp.stack(over_x)
    over_x = jnp.stack([pick(over_x, x_at ^ at, 0) for at in range(nx)])
    kept = pick(over_x, n_at, 1)
    given = swap(pick(over_x, n_at ^ 1, 1), "zn")
    near = jnp.stack(
        [jnp.where(n_at == 0, kept, given), jnp.where(n_at == 0, given, kept)], axis=1
    )
    far_kept = pick(near, f_at, 2)
    far_sent = pick(near, f_at ^ 1, 2)

    id_rows = jnp.pad(
        doc_ids[0].astype(bf16)[:, None, :],
        ((0, 0), (0, EXTRA - 1), (0, value_width - rows)),
    )
    own_rows = jnp.concatenate([targets[0], id_rows], axis=1)
    far_rows = swap(own_rows, "zf")
    pair = jnp.stack(
        [jnp.where(f_at == 0, own_rows, far_rows), jnp.where(f_at == 0, far_rows, own_rows)], axis=1
    )
    pair_targets = pair[:, :, :rows].reshape(steps_total, tokens, value_width)
    pair_ids = pair[:, :, rows, :rows].reshape(steps_total, tokens, 1).astype(jnp.int32)
    step_shift = DOCS * jnp.arange(steps_total, dtype=jnp.int32)[:, None, None]
    hot = (pair_ids + step_shift == jnp.arange(128, dtype=jnp.int32)).astype(f32)

    local = lax.dynamic_slice(weights[0], (zero, start), (shard_rows, frag_width))
    summed = local.astype(f32) + swap(local, "zh").astype(f32)
    summed = summed + swap(summed, "c")

    doc_range = jnp.arange(DOCS, dtype=jnp.int32)
    own_hot = (doc_ids[0][..., None] == doc_range).astype(f32)
    count_rows = jnp.pad(
        jnp.sum(own_hot, axis=1).reshape(1, 1, -1).astype(bf16),
        ((0, 0), (0, EXTRA - 1), (0, value_width - steps_total * DOCS)),
    )

    columns, far_kept, far_sent, pair_targets, hot, summed = tie(
        columns, far_kept, far_sent, pair_targets, hot, summed
    )
    summed = lax.psum(summed, "y")

    master = weights[0].astype(f32)
    first = adam_m[0].astype(f32)
    second = adam_v[0].astype(f32)
    losses = []
    inverse = None
    for step in range(steps_total):
        current = master.astype(bf16)
        partial = jnp.dot(columns, current, preferred_element_type=f32)
        partial = partial.astype(bf16).reshape(groups, tokens, value_width)
        if step == 0:
            extra = jnp.broadcast_to(count_rows, (groups, EXTRA, value_width))
            partial = jnp.concatenate([partial, extra], axis=1)
        partial = exchange(partial, GROUP)
        if step == 0:
            far_a = swap(far_sent[: nx // 2], "zf")
            partial, far_a = tie(partial, far_a)
        own = jnp.sum(partial.astype(f32), axis=0)
        got = swap(own.astype(bf16), "zf")
        sent = errors(own, got, pair_targets[step], hot[step], inverse, groups, scale)
        if step == 0:
            sent, inverse = sent
        if step == 0:
            sent, far_sent = tie(sent, far_sent)
        got = exchange(sent, GROUP)
        if step == 0:
            far_b = swap(far_sent[nx // 2 :], "zf")
            far_given = jnp.concatenate([far_a, far_b], axis=0)
            later = jnp.stack(
                [
                    jnp.where(f_at == 0, far_kept, far_given),
                    jnp.where(f_at == 0, far_given, far_kept),
                ],
                axis=2,
            ).reshape(shards * rows, shard_rows)
            got, later = tie(got, later)
        losses.append(jnp.sum(got[:, tokens, :3].astype(f32)))
        everyone = got[:, :tokens].reshape(shards * rows, value_width)
        gradient = (
            lax.dot_general(
                columns, everyone, (((0,), (0,)), ((), ())), preferred_element_type=f32
            )
            * scale
        )
        master, first, second = adam_update(master, first, second, gradient)
        columns = later

    anchor_rows = anchor.astype(f32)
    mean_delta = anchor_rows - summed / replicas
    new_moment = NESTEROV * momentum.astype(f32) + mean_delta
    global_fragment = anchor_rows - OUTER_RATE * (mean_delta + NESTEROV * new_moment)
    merged = (
        MIXING * lax.dynamic_slice(master, (zero, start), (shard_rows, frag_width))
        + (1.0 - MIXING) * global_fragment
    )
    master = lax.dynamic_update_slice(master, merged, (zero, start))
    return (master[None], jnp.stack(losses)[None])


def solution(mesh):
    fine = Mesh(mesh.devices.reshape(2, 8, 2, 4, 2, 2), REPLICA + FSDP)
    placed = (
        P(REPLICA, None, FSDP, None),
        P(REPLICA, None, FSDP, None),
        P(REPLICA, None, FSDP),
        P(REPLICA, FSDP, None),
        P(REPLICA, FSDP, None),
        P(REPLICA, FSDP, None),
        P(FSDP, None),
        P(FSDP, None),
        P(),
    )
    return jax.shard_map(
        body,
        mesh=fine,
        in_specs=placed,
        out_specs=(P(REPLICA, FSDP, None), P(REPLICA, None)),
        check_vma=False,
    )
```

time: 262 us -> 264 us (level)
  blocking collectives: 62.3 us -> 15.7 us
  waiting for transfers between devices: 110 us -> 137 us
  starting transfers between devices: 47.2 us -> 58.3 us
  between operations: 4.2 us -> 15.2 us
  Pallas kernels: 0 us -> 5.35 us
    all_to_all x8 -> x4, waiting for transfers between devices: 110 us -> 19.3 us  [exchange(): lax.all_to_all(blocks, axes, split_axis=0, concat_axis=0, tiled=False)]
    psum x0 -> x1, waiting for transfers between devices: none -> 61.2 us  [body(): summed = lax.psum(summed, 'y')]
    ppermute x0 -> x11, waiting for transfers between devices: none -> 56.1 us  [swap(): return lax.ppermute(block, axis, [(i, i ^ bit) for i in range(size)])]
    all_to_all x4 -> x1, blocking collectives: 62.3 us -> 15.7 us  [exchange(): lax.all_to_all(blocks, axes, split_axis=0, concat_axis=0, tiled=False)]
    ppermute x0 -> x11, starting transfers between devices: none -> 36.8 us  [swap(): return lax.ppermute(block, axis, [(i, i ^ bit) for i in range(size)])]
    all_to_all x8 -> x4, starting transfers between devices: 47.2 us -> 21.4 us  [exchange(): lax.all_to_all(blocks, axes, split_axis=0, concat_axis=0, tiled=False)]
    pallas_call x0 -> x4, Pallas kernels: none -> 5.35 us  [the longest x2 2.9 us: normalize(): pl.pallas_call(functools.partial(normalize_kernel, width), grid=(rows //...]
    transpose x2 -> x0, other arithmetic: 4.22 us -> none  [body(): blocks = normed.reshape(rows, shards, shard_rows).transpose(1, 0, 2)]
  transfers between devices with their start and end apart: 8 -> 16, of which waited for: 8 -> 11; matrix products, arithmetic and copies ran while one was open for 6% -> 7% of each run, Pallas kernels for 0% -> 0%
where the time goes in v2:
time: 264 us; the launch traced here: 262 us
  waiting for transfers between devices  137 us (52%)
  starting transfers between devices  58.3 us (22%)
  blocking collectives  15.7 us (6%)
  between operations  15.2 us (6%)
  other arithmetic  13.2 us (5%)
  matrix products  8.96 us (3%)
  local copies, waits for them, and re-layouts  7.93 us (3%)
  Pallas kernels  5.35 us (2%)
    psum x1, waiting for transfers between devices, body(): summed = lax.psum(summed, 'y')  61.2 us
    ppermute x11, waiting for transfers between devices, swap(): return lax.ppermute(block, axis, [(i, i ^ bit) for i in range(size)])  56.1 us
    ppermute x11, starting transfers between devices, swap(): return lax.ppermute(block, axis, [(i, i ^ bit) for i in range(size)])  36.8 us
    all_to_all x4, starting transfers between devices, exchange(): lax.all_to_all(blocks, axes, split_axis=0, concat_axis=0, tiled=False)  21.4 us
    all_to_all x4, waiting for transfers between devices, exchange(): lax.all_to_all(blocks, axes, split_axis=0, concat_axis=0, tiled=False)  19.3 us
    all_to_all x1, blocking collectives, exchange(): lax.all_to_all(blocks, axes, split_axis=0, concat_axis=0, tiled=False)  15.7 us
    unnamed x32, local copies, waits for them, and re-layouts  5.79 us
    dot_general x2, matrix products, body(): lax.dot_general(columns, everyone, (((0,), (0,)), ((), ())), preferred_el...  5.69 us
  transfers between devices with their start and end apart: 16, of which 11 were waited for; matrix products, arithmetic and copies ran while one was open for 7% of the time, Pallas kernels for 0%

profile of v2, /device:TPU:56, one launch (start us, length us, event | category | flops | bytes accessed | tf_op | source)
XLA Modules:
  0.0 262.0 jit_solution(14262809520834977597)
XLA Ops:
  10.8 10.0 %all-to-all-start = ((bf16[16,64,512]{2,1,0:T(8,128)(2,1)}), bf16[16,64,512]{2,1,0:T(8,128)(2,1)}, u32[]{:S(2)}, u32[]{:S(2)}) async-start(bf16[16,64,512]{2,1,0:T(8,128)(2,1)} %normalize.2), calls=%async_computation | async-start | bytes 2097152 | tf_op jit(solution)/shard_map/all_to_all | solution.py:42
  22.4 8.2 %collective-permute-start.5 = (bf16[512,128]{1,0:T(8,128)(2,1)S(1)}, bf16[512,128]{1,0:T(8,128)(2,1)S(1)}, u32[]{:S(2)}, u32[]{:S(2)}) collective-permute-start(bf16[512,128]{1,0:T(8,128)(2,1)S(1)} %dynamic-slice_bitcast_fusion.5), channel_id=1, source_target_pairs={{0,256},{256,0},{1,257},{257,1},{2,258},{258,2},{3,259},{259,3},{4... | collective-permute-start | bytes 393224 | tf_op jit(solution)/shard_map/ppermute | solution.py:47
  31.3 4.7 %collective-permute-start.4 = (bf16[2,80,512]{2,1,0:T(8,128)(2,1)}, bf16[2,80,512]{2,1,0:T(8,128)(2,1)}, u32[]{:S(2)}, u32[]{:S(2)}) collective-permute-start(bf16[2,80,512]{2,1,0:T(8,128)(2,1)} %fusion.14), channel_id=1, source_target_pairs={{0,2},{2,0},{1,3},{3,1},{4,6},{6,4},{5,7},{7,5},{8,10},{10,8},{9,1... | collective-permute-start | bytes 491528 | tf_op jit(solution)/shard_map/ppermute | solution.py:47
  37.1 4.6 %collective-permute-start.2 = (bf16[2,2,64,512]{3,2,1,0:T(8,128)(2,1)S(1)}, bf16[2,2,64,512]{3,2,1,0:T(8,128)(2,1)S(1)}, u32[]{:S(2)}, u32[]{:S(2)}) collective-permute-start(bf16[2,2,64,512]{3,2,1,0:T(8,128)(2,1)S(1)} %get-tuple-element.51), channel_id=1, source_target_pairs={{0,12},{4,8},{8,4},{12,0},{1,13},{5,9},{9,5},{13,1},{2,14},{6,10},... | collective-permute-start | bytes 786440 | tf_op jit(solution)/shard_map/ppermute | solution.py:47
  41.7 2.8 %collective-permute-start.1 = (bf16[2,2,64,512]{3,2,1,0:T(8,128)(2,1)S(1)}, bf16[2,2,64,512]{3,2,1,0:T(8,128)(2,1)S(1)}, u32[]{:S(2)}, u32[]{:S(2)}) collective-permute-start(bf16[2,2,64,512]{3,2,1,0:T(8,128)(2,1)S(1)} %get-tuple-element.52), channel_id=1, source_target_pairs={{0,8},{4,12},{8,0},{12,4},{1,9},{5,13},{9,1},{13,5},{2,10},{6,14},... | collective-permute-start | bytes 786440 | tf_op jit(solution)/shard_map/ppermute | solution.py:47
  44.5 2.5 collective-permute-start
  47.1 4.1 %collective-permute-done.5 = bf16[512,128]{1,0:T(8,128)(2,1)S(1)} collective-permute-done((bf16[512,128]{1,0:T(8,128)(2,1)S(1)}, bf16[512,128]{1,0:T(8,128)(2,1)S(1)}, u32[]{:S(2)}, u32[]{:S(2)}) %collective-permute-start.5) | collective-permute-done | bytes 131104 | tf_op jit(solution)/shard_map/ppermute | solution.py:47
  54.1 5.1 %collective-permute-done.4 = bf16[2,80,512]{2,1,0:T(8,128)(2,1)} collective-permute-done((bf16[2,80,512]{2,1,0:T(8,128)(2,1)}, bf16[2,80,512]{2,1,0:T(8,128)(2,1)}, u32[]{:S(2)}, u32[]{:S(2)}) %collective-permute-start.4) | collective-permute-done | bytes 163872 | tf_op jit(solution)/shard_map/ppermute | solution.py:47
  65.7 10.1 %collective-permute-done.3 = bf16[4,2,64,512]{3,2,1,0:T(8,128)(2,1)} collective-permute-done((bf16[4,2,64,512]{3,2,1,0:T(8,128)(2,1)S(1)}, bf16[4,2,64,512]{3,2,1,0:T(8,128)(2,1)}, u32[]{:S(2)}, u32[]{:S(2)}) %collective-permute-start.3) | collective-permute-done | bytes 524320 | tf_op jit(solution)/shard_map/ppermute | solution.py:47
  81.1 4.3 %all-to-all-start.1 = ((bf16[8,144,512]{2,1,0:T(8,128)(2,1)}), bf16[8,144,512]{2,1,0:T(8,128)(2,1)S(1)}, u32[]{:S(2)}, u32[]{:S(2)}) async-start(bf16[8,144,512]{2,1,0:T(8,128)(2,1)} %pad_maximum_fusion), calls=%async_computation.1 | async-start | bytes 2359296 | tf_op jit(solution)/shard_map/all_to_all | solution.py:42
  85.4 3.4 %collective-permute-start.7 = (bf16[2,2,64,512]{3,2,1,0:T(8,128)(2,1)S(1)}, bf16[2,2,64,512]{3,2,1,0:T(8,128)(2,1)}, u32[]{:S(2)}, u32[]{:S(2)}) collective-permute-start(bf16[2,2,64,512]{3,2,1,0:T(8,128)(2,1)S(1)} %slice.38), channel_id=1, source_target_pairs={{0,2},{2,0},{1,3},{3,1},{4,6},{6,4},{5,7},{7,5},{8,10},{10,8},{9,1... | collective-permute-start | bytes 786440 | tf_op jit(solution)/shard_map/ppermute | solution.py:47
  88.9 12.8 %collective-permute-done.7 = bf16[2,2,64,512]{3,2,1,0:T(8,128)(2,1)} collective-permute-done((bf16[2,2,64,512]{3,2,1,0:T(8,128)(2,1)S(1)}, bf16[2,2,64,512]{3,2,1,0:T(8,128)(2,1)}, u32[]{:S(2)}, u32[]{:S(2)}) %collective-permute-start.7) | collective-permute-done | bytes 262176 | tf_op jit(solution)/shard_map/ppermute | solution.py:47
  101.7 4.3 %all-to-all-done.1 = bf16[8,144,512]{2,1,0:T(8,128)(2,1)S(1)} async-done(((bf16[8,144,512]{2,1,0:T(8,128)(2,1)}), bf16[8,144,512]{2,1,0:T(8,128)(2,1)S(1)}, u32[]{:S(2)}, u32[]{:S(2)}) %all-to-all-start.1) | async-done | bytes 1179680 | tf_op jit(solution)/shard_map/all_to_all | solution.py:42
  108.2 6.6 %collective-permute-done.8.got_ref = bf16[144,512]{1,0:T(8,128)(2,1)S(1)} collective-permute-done((bf16[144,512]{1,0:T(8,128)(2,1)S(1)}, bf16[144,512]{1,0:T(8,128)(2,1)S(1)}, u32[]{:S(2)}, u32[]{:S(2)}) %collective-permute-start.8) | collective-permute-done | bytes 147488 | tf_op jit(solution)/shard_map/ppermute | solution.py:47
  116.0 3.6 %all-to-all-start.2 = ((bf16[8,144,512]{2,1,0:T(8,128)(2,1)}), bf16[8,144,512]{2,1,0:T(8,128)(2,1)S(1)}, u32[]{:S(2)}, u32[]{:S(2)}) async-start(bf16[8,144,512]{2,1,0:T(8,128)(2,1)} %get-tuple-element.32), calls=%async_computation.2 | async-start | bytes 2359296 | tf_op jit(solution)/shard_map/all_to_all | solution.py:42
  119.6 3.0 %collective-permute-start.9 = (bf16[2,2,64,512]{3,2,1,0:T(8,128)(2,1)S(1)}, bf16[2,2,64,512]{3,2,1,0:T(8,128)(2,1)S(1)}, u32[]{:S(2)}, u32[]{:S(2)}) collective-permute-start(bf16[2,2,64,512]{3,2,1,0:T(8,128)(2,1)S(1)} %slice.41), channel_id=1, source_target_pairs={{0,2},{2,0},{1,3},{3,1},{4,6},{6,4},{5,7},{7,5},{8,10},{10,8},{9,1... | collective-permute-start | bytes 786440 | tf_op jit(solution)/shard_map/ppermute | solution.py:47
  123.6 10.2 %collective-permute-done.9 = bf16[2,2,64,512]{3,2,1,0:T(8,128)(2,1)S(1)} collective-permute-done((bf16[2,2,64,512]{3,2,1,0:T(8,128)(2,1)S(1)}, bf16[2,2,64,512]{3,2,1,0:T(8,128)(2,1)S(1)}, u32[]{:S(2)}, u32[]{:S(2)}) %collective-permute-start.9) | collective-permute-done | bytes 262176 | tf_op jit(solution)/shard_map/ppermute | solution.py:47
  134.1 4.0 %all-to-all-done.2 = bf16[8,144,512]{2,1,0:T(8,128)(2,1)S(1)} async-done(((bf16[8,144,512]{2,1,0:T(8,128)(2,1)}), bf16[8,144,512]{2,1,0:T(8,128)(2,1)S(1)}, u32[]{:S(2)}, u32[]{:S(2)}) %all-to-all-start.2) | async-done | bytes 1179680 | tf_op jit(solution)/shard_map/all_to_all | solution.py:42
  141.6 15.7 %all_to_all.25 = bf16[8,128,512]{2,1,0:T(8,128)(2,1)S(1)} all-to-all(bf16[8,128,512]{2,1,0:T(8,128)(2,1)S(1)} %bitcast.120), channel_id=1, replica_groups=mesh['zh'=2,'y'=8,'c'=2,'x'=4,'zf'=2,'zn'=2] {'x','zn'}, dimensions={0} | all-to-all | bytes 2097152 | tf_op jit(solution)/shard_map/all_to_all | solution.py:42
  159.4 7.2 %collective-permute-done.10.got_ref = bf16[128,512]{1,0:T(8,128)(2,1)S(1)} collective-permute-done((bf16[128,512]{1,0:T(8,128)(2,1)S(1)}, bf16[128,512]{1,0:T(8,128)(2,1)S(1)}, u32[]{:S(2)}, u32[]{:S(2)}) %collective-permute-start.10) | collective-permute-done | bytes 131104 | tf_op jit(solution)/shard_map/ppermute | solution.py:47
  167.8 3.6 %all-to-all-start.4 = ((bf16[8,144,512]{2,1,0:T(8,128)(2,1)}), bf16[8,144,512]{2,1,0:T(8,128)(2,1)S(1)}, u32[]{:S(2)}, u32[]{:S(2)}) async-start(bf16[8,144,512]{2,1,0:T(8,128)(2,1)} %errors.3), calls=%async_computation.4 | async-start | bytes 2359296 | tf_op jit(solution)/shard_map/all_to_all | solution.py:42
  172.7 11.0 %all-to-all-done.4 = bf16[8,144,512]{2,1,0:T(8,128)(2,1)S(1)} async-done(((bf16[8,144,512]{2,1,0:T(8,128)(2,1)}), bf16[8,144,512]{2,1,0:T(8,128)(2,1)S(1)}, u32[]{:S(2)}, u32[]{:S(2)}) %all-to-all-start.4) | async-done | bytes 1179680 | tf_op jit(solution)/shard_map/all_to_all | solution.py:42
  185.0 3.7 %multiply_subtract_fusion = f32[512,512]{1,0:T(8,128)S(1)} fusion(f32[512,512]{1,0:T(8,128)S(1)} %copy-done.13, bf16[1,512,512]{2,1,0:T(8,128)(2,1)} %param.13, bf16[1,512,512]{2,1,0:T(8,128)(2,1)} %param.14, bf16[1,512,512]{2,1,0:T(8,128)(2,1)S(1)} %copy-done.4, bf16[1024,512]{1,0:T(8,128)(2,1)} %bitcast.116, bf16[1024,512]{1,0:T(8,128)(2,1)S(1)} %bitcast.118), kind=kOutput, calls=%fused_computation.18 | convolution fusion | flops 544997376 | bytes 5767168 | tf_op jit(solution)/shard_map/dot_general | solution.py:228
  192.1 61.2 %all-reduce.4.cloned.1.call-done = f32[512,128]{1,0:T(8,128)} async-done(((f32[512,128]{1,0:T(8,128)}), f32[512,128]{1,0:T(8,128)}) %all-reduce.4.cloned.1.call-update) | async-done | bytes 262160 | tf_op jit(solution)/shard_map/psum | solution.py:188
  (95 shorter events, 40.2 us)
Async XLA Ops:
  10.8 19.8 %copy-start.11 = (s32[1,2,64]{2,1,0:T(2,128)S(1)}, s32[1,2,64]{2,1,0:T(2,128)}, u32[]{:S(2)}) copy-start(s32[1,2,64]{2,1,0:T(2,128)} %param.11) | copy-start | bytes 1540
  10.8 19.9 %copy-start.3 = (bf16[1,2,64,512]{3,2,1,0:T(8,128)(2,1)S(1)}, bf16[1,2,64,512]{3,2,1,0:T(8,128)(2,1)}, u32[]{:S(2)}) copy-start(bf16[1,2,64,512]{3,2,1,0:T(8,128)(2,1)} %param.10) | copy-start | bytes 393220
  10.8 25.3 %copy-start.1 = (bf16[1,2,64,8192]{3,2,1,0:T(8,128)(2,1)S(1)}, bf16[1,2,64,8192]{3,2,1,0:T(8,128)(2,1)}, u32[]{:S(2)}) copy-start(bf16[1,2,64,8192]{3,2,1,0:T(8,128)(2,1)} %hidden_ref.2) | copy-start | bytes 6291460
  10.8 66.3 %all-to-all-start = ((bf16[16,64,512]{2,1,0:T(8,128)(2,1)}), bf16[16,64,512]{2,1,0:T(8,128)(2,1)}, u32[]{:S(2)}, u32[]{:S(2)}) async-start(bf16[16,64,512]{2,1,0:T(8,128)(2,1)} %normalize.2), calls=%async_computation | async-start | bytes 2097152 | tf_op jit(solution)/shard_map/all_to_all | solution.py:42
  22.4 28.9 %collective-permute-start.5 = (bf16[512,128]{1,0:T(8,128)(2,1)S(1)}, bf16[512,128]{1,0:T(8,128)(2,1)S(1)}, u32[]{:S(2)}, u32[]{:S(2)}) collective-permute-start(bf16[512,128]{1,0:T(8,128)(2,1)S(1)} %dynamic-slice_bitcast_fusion.5), channel_id=1, source_target_pairs={{0,256},{256,0},{1,257},{257,1},{2,258},{258,2},{3,259},{259,3},{4... | collective-permute-start | bytes 393224 | tf_op jit(solution)/shard_map/ppermute | solution.py:47
  30.6 5.4 %copy-start.7 = (bf16[2,1,64]{2,1,0:T(2,128)(2,1)}, bf16[2,1,64]{2,1,0:T(2,128)(2,1)S(1)}, u32[]{:S(2)}) copy-start(bf16[2,1,64]{2,1,0:T(2,128)(2,1)S(1)} %copy.60) | copy-start | bytes 772
  31.3 27.8 %collective-permute-start.4 = (bf16[2,80,512]{2,1,0:T(8,128)(2,1)}, bf16[2,80,512]{2,1,0:T(8,128)(2,1)}, u32[]{:S(2)}, u32[]{:S(2)}) collective-permute-start(bf16[2,80,512]{2,1,0:T(8,128)(2,1)} %fusion.14), channel_id=1, source_target_pairs={{0,2},{2,0},{1,3},{3,1},{4,6},{6,4},{5,7},{7,5},{8,10},{10,8},{9,1... | collective-permute-start | bytes 491528 | tf_op jit(solution)/shard_map/ppermute | solution.py:47
  37.0 22.2 %copy-start.8 = (bf16[2,1,64]{2,1,0:T(2,128)(2,1)S(1)}, bf16[2,1,64]{2,1,0:T(2,128)(2,1)}, u32[]{:S(2)}) copy-start(bf16[2,1,64]{2,1,0:T(2,128)(2,1)} %copy-done.7) | copy-start | bytes 772
  37.1 23.7 %collective-permute-start.2 = (bf16[2,2,64,512]{3,2,1,0:T(8,128)(2,1)S(1)}, bf16[2,2,64,512]{3,2,1,0:T(8,128)(2,1)S(1)}, u32[]{:S(2)}, u32[]{:S(2)}) collective-permute-start(bf16[2,2,64,512]{3,2,1,0:T(8,128)(2,1)S(1)} %get-tuple-element.51), channel_id=1, source_target_pairs={{0,12},{4,8},{8,4},{12,0},{1,13},{5,9},{9,5},{13,1},{2,14},{6,10},... | collective-permute-start | bytes 786440 | tf_op jit(solution)/shard_map/ppermute | solution.py:47
  41.7 19.1 %collective-permute-start.1 = (bf16[2,2,64,512]{3,2,1,0:T(8,128)(2,1)S(1)}, bf16[2,2,64,512]{3,2,1,0:T(8,128)(2,1)S(1)}, u32[]{:S(2)}, u32[]{:S(2)}) collective-permute-start(bf16[2,2,64,512]{3,2,1,0:T(8,128)(2,1)S(1)} %get-tuple-element.52), channel_id=1, source_target_pairs={{0,8},{4,12},{8,0},{12,4},{1,9},{5,13},{9,1},{13,5},{2,10},{6,14},... | collective-permute-start | bytes 786440 | tf_op jit(solution)/shard_map/ppermute | solution.py:47
  44.5 16.4 %collective-permute-start = (bf16[2,2,64,512]{3,2,1,0:T(8,128)(2,1)S(1)}, bf16[2,2,64,512]{3,2,1,0:T(8,128)(2,1)S(1)}, u32[]{:S(2)}, u32[]{:S(2)}) collective-permute-start(bf16[2,2,64,512]{3,2,1,0:T(8,128)(2,1)S(1)} %get-tuple-element.53), channel_id=1, source_target_pairs={{0,4},{4,0},{8,12},{12,8},{1,5},{5,1},{9,13},{13,9},{2,6},{6,2},{1... | collective-permute-start | bytes 786440 | tf_op jit(solution)/shard_map/ppermute | solution.py:47
  52.2 11.8 %collective-permute-start.6 = (f32[512,128]{1,0:T(8,128)S(1)}, f32[512,128]{1,0:T(8,128)}, u32[]{:S(2)}, u32[]{:S(2)}) collective-permute-start(f32[512,128]{1,0:T(8,128)S(1)} %convert_add_fusion), channel_id=1, source_target_pairs={{0,16},{16,0},{1,17},{17,1},{2,18},{18,2},{3,19},{19,3},{4,20},{20... | collective-permute-start | bytes 786440 | tf_op jit(solution)/shard_map/ppermute | solution.py:47
  61.3 14.5 %collective-permute-start.3 = (bf16[4,2,64,512]{3,2,1,0:T(8,128)(2,1)S(1)}, bf16[4,2,64,512]{3,2,1,0:T(8,128)(2,1)}, u32[]{:S(2)}, u32[]{:S(2)}) collective-permute-start(bf16[4,2,64,512]{3,2,1,0:T(8,128)(2,1)S(1)} %dynamic-slice_bitcast_fusion), channel_id=1, source_target_pairs={{0,1},{1,0},{2,3},{3,2},{4,5},{5,4},{6,7},{7,6},{8,9},{9,8},{10,11... | collective-permute-start | bytes 1572872 | tf_op jit(solution)/shard_map/ppermute | solution.py:47
  81.1 25.0 %all-to-all-start.1 = ((bf16[8,144,512]{2,1,0:T(8,128)(2,1)}), bf16[8,144,512]{2,1,0:T(8,128)(2,1)S(1)}, u32[]{:S(2)}, u32[]{:S(2)}) async-start(bf16[8,144,512]{2,1,0:T(8,128)(2,1)} %pad_maximum_fusion), calls=%async_computation.1 | async-start | bytes 2359296 | tf_op jit(solution)/shard_map/all_to_all | solution.py:42
  85.4 16.3 %collective-permute-start.7 = (bf16[2,2,64,512]{3,2,1,0:T(8,128)(2,1)S(1)}, bf16[2,2,64,512]{3,2,1,0:T(8,128)(2,1)}, u32[]{:S(2)}, u32[]{:S(2)}) collective-permute-start(bf16[2,2,64,512]{3,2,1,0:T(8,128)(2,1)S(1)} %slice.38), channel_id=1, source_target_pairs={{0,2},{2,0},{1,3},{3,1},{4,6},{6,4},{5,7},{7,5},{8,10},{10,8},{9,1... | collective-permute-start | bytes 786440 | tf_op jit(solution)/shard_map/ppermute | solution.py:47
  106.2 8.5 %collective-permute-start.8 = (bf16[144,512]{1,0:T(8,128)(2,1)S(1)}, bf16[144,512]{1,0:T(8,128)(2,1)S(1)}, u32[]{:S(2)}, u32[]{:S(2)}) collective-permute-start(bf16[144,512]{1,0:T(8,128)(2,1)S(1)} %convert_element_type.115), channel_id=1, source_target_pairs={{0,2},{2,0},{1,3},{3,1},{4,6},{6,4},{5,7},{7,5},{8,10},{10,8},{9,1... | collective-permute-start | bytes 442376 | tf_op jit(solution)/shard_map/ppermute | solution.py:47
  116.0 22.1 %all-to-all-start.2 = ((bf16[8,144,512]{2,1,0:T(8,128)(2,1)}), bf16[8,144,512]{2,1,0:T(8,128)(2,1)S(1)}, u32[]{:S(2)}, u32[]{:S(2)}) async-start(bf16[8,144,512]{2,1,0:T(8,128)(2,1)} %get-tuple-element.32), calls=%async_computation.2 | async-start | bytes 2359296 | tf_op jit(solution)/shard_map/all_to_all | solution.py:42
  119.6 14.2 %collective-permute-start.9 = (bf16[2,2,64,512]{3,2,1,0:T(8,128)(2,1)S(1)}, bf16[2,2,64,512]{3,2,1,0:T(8,128)(2,1)S(1)}, u32[]{:S(2)}, u32[]{:S(2)}) collective-permute-start(bf16[2,2,64,512]{3,2,1,0:T(8,128)(2,1)S(1)} %slice.41), channel_id=1, source_target_pairs={{0,2},{2,0},{1,3},{3,1},{4,6},{6,4},{5,7},{7,5},{8,10},{10,8},{9,1... | collective-permute-start | bytes 786440 | tf_op jit(solution)/shard_map/ppermute | solution.py:47
  134.1 6.2 %copy-start.2 = (bf16[4,2,2,64,512]{4,3,2,1,0:T(8,128)(2,1)}, bf16[4,2,2,64,512]{4,3,2,1,0:T(8,128)(2,1)S(1)}, u32[]{:S(2)}) copy-start(bf16[4,2,2,64,512]{4,3,2,1,0:T(8,128)(2,1)S(1)} %copy.58) | copy-start | bytes 3145732
  157.4 9.2 %collective-permute-start.10 = (bf16[128,512]{1,0:T(8,128)(2,1)S(1)}, bf16[128,512]{1,0:T(8,128)(2,1)S(1)}, u32[]{:S(2)}, u32[]{:S(2)}) collective-permute-start(bf16[128,512]{1,0:T(8,128)(2,1)S(1)} %convert_element_type.120), channel_id=1, source_target_pairs={{0,2},{2,0},{1,3},{3,1},{4,6},{6,4},{5,7},{7,5},{8,10},{10,8},{9,1... | collective-permute-start | bytes 393224 | tf_op jit(solution)/shard_map/ppermute | solution.py:47
  167.8 15.9 %all-to-all-start.4 = ((bf16[8,144,512]{2,1,0:T(8,128)(2,1)}), bf16[8,144,512]{2,1,0:T(8,128)(2,1)S(1)}, u32[]{:S(2)}, u32[]{:S(2)}) async-start(bf16[8,144,512]{2,1,0:T(8,128)(2,1)} %errors.3), calls=%async_computation.4 | async-start | bytes 2359296 | tf_op jit(solution)/shard_map/all_to_all | solution.py:42
  171.4 82.0 %all-reduce.4.cloned.1.call-start = ((), (), s32[]{:S(2)}) async-start(), calls=%async_computation.5 | async-start | bytes 524288 | tf_op jit(solution)/shard_map/psum | solution.py:188
  188.6 64.7 %copy-start.5 = (bf16[512,128]{1,0:T(8,128)(2,1)S(1)}, bf16[512,128]{1,0:T(8,128)(2,1)}, u32[]{:S(2)}) copy-start(bf16[512,128]{1,0:T(8,128)(2,1)} %param.15) | copy-start | bytes 393220
  188.6 64.7 %copy-start.6 = (bf16[512,128]{1,0:T(8,128)(2,1)S(1)}, bf16[512,128]{1,0:T(8,128)(2,1)}, u32[]{:S(2)}) copy-start(bf16[512,128]{1,0:T(8,128)(2,1)} %param.16) | copy-start | bytes 393220
  (6 other events, 9.4 us)
Sparse Core Ops, SparseCore 0:
  174.5 78.7 all-reduce.3

commit v3 on v2

v3 whole, which is shorter than its diff:
```python
import functools

import jax
import jax.numpy as jnp
from jax import lax
from jax.experimental import pallas as pl
from jax.experimental.pallas import tpu as pltpu
from jax.sharding import Mesh, PartitionSpec as P

DOCS = 8


NORM_EPS = 1e-05
ADAM_EPS = 1e-08
INNER_RATE = 0.1
DECAY_RATE = 0.1
BETA_FIRST = 0.9
BETA_SECOND = 0.95
OUTER_RATE = 0.7
NESTEROV = 0.9
MIXING = 0.5

REPLICA = ("zh", "y", "c")
FSDP = ("x", "zf", "zn")
ORDER = ("x", "zn", "zf")
GROUP = ("x", "zn")
EXTRA = 16
CHUNK = 16
VMEM = 48 * 1024 * 1024

bf16, f32 = jnp.bfloat16, jnp.float32


def adam_update(master, first, second, gradient):
    first = BETA_FIRST * first + (1.0 - BETA_FIRST) * gradient
    second = BETA_SECOND * second + (1.0 - BETA_SECOND) * gradient * gradient
    master = master - INNER_RATE * (first / (jnp.sqrt(second) + ADAM_EPS) + DECAY_RATE * master)
    return (master, first, second)


def exchange(blocks, axes):
    return lax.all_to_all(blocks, axes, split_axis=0, concat_axis=0, tiled=False)


def swap(block, axis, bit=1):
    size = lax.axis_size(axis)
    return lax.ppermute(block, axis, [(i, i ^ bit) for i in range(size)])


def tie(*values):
    return lax.optimization_barrier(values)


def normalize_kernel(width, hidden_ref, out_ref):
    wide = hidden_ref[0, 0].astype(f32)
    power = jnp.mean(wide * wide, axis=-1, keepdims=True)
    normed = (wide * lax.rsqrt(power + NORM_EPS)).astype(bf16)
    for at in range(out_ref.shape[0]):
        x, zn, zf = at // 4, (at // 2) % 2, at % 2
        owner = x * 4 + zf * 2 + zn
        out_ref[at, 0] = normed[:, owner * width : (owner + 1) * width]


def normalize(hidden, shards):
    _, steps, rows, model_width = hidden.shape
    width = model_width // shards
    return pl.pallas_call(
        functools.partial(normalize_kernel, width),
        grid=(steps, rows // CHUNK),
        in_specs=[pl.BlockSpec((1, 1, CHUNK, model_width), lambda s, i: (0, s, i, 0))],
        out_specs=pl.BlockSpec((shards, 1, CHUNK, width), lambda s, i: (0, s, i, 0)),
        out_shape=jax.ShapeDtypeStruct((shards, steps, rows, width), bf16),
        compiler_params=pltpu.CompilerParams(vmem_limit_bytes=VMEM),
        cost_estimate=pl.CostEstimate(
            flops=8 * rows * model_width, bytes_accessed=8 * rows * model_width, transcendentals=rows
        ),
        name="normalize",
    )(hidden)


def error_kernel(scale, own_ref, got_ref, target_ref, weight_ref, out_ref):
    tokens, columns = target_ref.shape
    weight = weight_ref[...]
    values = (own_ref[...] + got_ref[...].astype(f32)) * scale
    error = values - target_ref[...].astype(f32)
    grad = (weight * error / columns).astype(bf16)
    each = jnp.sum(error * error, axis=-1, keepdims=True) / columns
    loss = jnp.sum(weight * 0.5 * each, axis=0, keepdims=True)
    high = loss.astype(bf16).astype(f32)
    middle = (loss - high).astype(bf16).astype(f32)
    low = loss - high - middle
    lane = lax.broadcasted_iota(jnp.int32, (EXTRA, columns), 1)
    row = jnp.where(lane == 0, high, jnp.where(lane == 1, middle, jnp.where(lane == 2, low, 0.0)))
    row = row.astype(bf16)
    for at in range(out_ref.shape[0]):
        out_ref[at, :tokens] = grad
        out_ref[at, tokens:] = row


def errors(own, got, target, weight, copies, scale):
    tokens, columns = target.shape
    return pl.pallas_call(
        functools.partial(error_kernel, scale),
        out_shape=jax.ShapeDtypeStruct((copies, tokens + EXTRA, columns), bf16),
        compiler_params=pltpu.CompilerParams(vmem_limit_bytes=VMEM),
        cost_estimate=pl.CostEstimate(
            flops=8 * tokens * columns, bytes_accessed=30 * tokens * columns, transcendentals=0
        ),
        name="errors",
    )(own, got, target, weight)


def body(hidden, targets, doc_ids, weights, adam_m, adam_v, anchor, momentum, fragment):
    steps_total, rows, model_width = hidden.shape[1:]
    shard_rows, value_width = weights.shape[1:]
    frag_width = anchor.shape[1]
    nx, nn, nf = (lax.axis_size(a) for a in ORDER)
    shards, groups = nx * nn * nf, nx * nn
    f_at, c_at = lax.axis_index("zf"), lax.axis_index("c")
    scale = model_width ** (-0.5)
    zero = jnp.zeros((), jnp.int32)
    start = fragment[0] * frag_width
    replicas = lax.axis_size(REPLICA)
    tokens = nf * rows

    def pick(array, at, axis):
        return lax.dynamic_index_in_dim(array, at, axis, keepdims=False)

    blocks = normalize(hidden, shards)
    blocks, weights, targets, doc_ids = tie(blocks, weights, targets, doc_ids)
    columns = exchange(blocks, ORDER)

    id_rows = jnp.pad(
        doc_ids[0].astype(bf16)[:, None, :],
        ((0, 0), (0, EXTRA - 1), (0, value_width - rows)),
    )
    own_rows = jnp.concatenate([targets[0], id_rows], axis=1)
    far_rows = swap(own_rows, "zf")
    pair = jnp.stack(
        [jnp.where(f_at == 0, own_rows, far_rows), jnp.where(f_at == 0, far_rows, own_rows)], axis=1
    )
    pair_targets = pair[:, :, :rows].reshape(steps_total, tokens, value_width)
    pair_ids = pair[:, :, rows, :rows].reshape(steps_total, tokens, 1).astype(jnp.int32)
    doc_range = jnp.arange(DOCS, dtype=jnp.int32)
    counts = jnp.sum((doc_ids[0][..., None] == doc_range).astype(f32), axis=1)
    for axis, bit in (("x", 1), ("x", 2), ("zn", 1), ("zf", 1)):
        counts = counts + swap(counts, axis, bit)
    inverse = 1.0 / (DOCS * counts)
    hot = (pair_ids == doc_range).astype(f32)
    token_weight = jnp.sum(hot * inverse[:, None, :], axis=-1, keepdims=True)

    half = shard_rows // 2
    local = lax.dynamic_slice(weights[0], (zero, start), (shard_rows, frag_width))
    local = local.reshape(2, half, frag_width)
    summed = pick(local, c_at, 0).astype(f32) + swap(pick(local, c_at ^ 1, 0), "c").astype(f32)
    for bit in (1, 2, 4):
        summed = summed + swap(summed, "y", bit)

    columns, pair_targets, token_weight, summed = tie(columns, pair_targets, token_weight, summed)

    master = weights[0].astype(f32)
    first = adam_m[0].astype(f32)
    second = adam_v[0].astype(f32)
    losses = []
    for step in range(steps_total):
        current = master.astype(bf16)
        rows_now = columns[:, step].reshape(shards * rows, shard_rows)
        partial = jnp.dot(rows_now, current, preferred_element_type=f32)
        partial = partial.astype(bf16).reshape(groups, tokens, value_width)
        partial = exchange(partial, GROUP)
        if step == 0:
            summed = summed + swap(summed, "zh")
            partial, summed = tie(partial, summed)
        own = jnp.sum(partial.astype(f32), axis=0)
        got = swap(own.astype(bf16), "zf")
        sent = errors(own, got, pair_targets[step], token_weight[step], groups, scale)
        if step == 0:
            sent, summed = tie(sent, summed)
        got = exchange(sent, GROUP)
        if step == 0:
            other = swap(summed, "c")
            got, summed, other = tie(got, summed, other)
        losses.append(jnp.sum(got[:, tokens, :3].astype(f32)))
        everyone = got[:, :tokens].reshape(shards * rows, value_width)
        gradient = (
            lax.dot_general(
                rows_now, everyone, (((0,), (0,)), ((), ())), preferred_element_type=f32
            )
            * scale
        )
        master, first, second = adam_update(master, first, second, gradient)

    anchor_rows = anchor.astype(f32)
    summed = jnp.concatenate(
        [jnp.where(c_at == 0, summed, other), jnp.where(c_at == 0, other, summed)], axis=0
    )
    mean_delta = anchor_rows - summed / replicas
    new_moment = NESTEROV * momentum.astype(f32) + mean_delta
    global_fragment = anchor_rows - OUTER_RATE * (mean_delta + NESTEROV * new_moment)
    merged = (
        MIXING * lax.dynamic_slice(master, (zero, start), (shard_rows, frag_width))
        + (1.0 - MIXING) * global_fragment
    )
    master = lax.dynamic_update_slice(master, merged, (zero, start))
    return (master[None], jnp.stack(losses)[None])


def solution(mesh):
    fine = Mesh(mesh.devices.reshape(2, 8, 2, 4, 2, 2), REPLICA + FSDP)
    placed = (
        P(REPLICA, None, FSDP, None),
        P(REPLICA, None, FSDP, None),
        P(REPLICA, None, FSDP),
        P(REPLICA, FSDP, None),
        P(REPLICA, FSDP, None),
        P(REPLICA, FSDP, None),
        P(FSDP, None),
        P(FSDP, None),
        P(),
    )
    return jax.shard_map(
        body,
        mesh=fine,
        in_specs=placed,
        out_specs=(P(REPLICA, FSDP, None), P(REPLICA, None)),
        check_vma=False,
    )
```

time: 264 us -> 204 us (0.77)
  waiting for transfers between devices: 137 us -> 80.6 us
  starting transfers between devices: 58.3 us -> 79.6 us
  between operations: 15.2 us -> 1.82 us
  other arithmetic: 13.2 us -> 6.57 us
  matrix products: 8.96 us -> 5.92 us
    psum x1 -> x0, waiting for transfers between devices: 61.2 us -> none  [body(): summed = lax.psum(summed, 'y')]
    ppermute x11 -> x13, starting transfers between devices: 36.8 us -> 57.2 us  [swap(): return lax.ppermute(block, axis, [(i, i ^ bit) for i in range(size)])]
    ppermute x11 -> x13, waiting for transfers between devices: 56.1 us -> 60.3 us  [swap(): return lax.ppermute(block, axis, [(i, i ^ bit) for i in range(size)])]
    dot_general x4, matrix products: 8.96 us -> 5.92 us  [the longest x2 3.06 us: body(): partial = jnp.dot(rows_now, current, preferred_element_type=f32)]
    pallas_call x4 -> x3, Pallas kernels: 5.35 us -> 6.49 us  [the longest x1 3.9 us: normalize(): pl.pallas_call(functools.partial(normalize_kernel, width), grid=(steps, r...]
    unnamed x32 -> x40, local copies, waits for them, and re-layouts: 5.79 us -> 5.51 us
  transfers between devices with their start and end apart: 16 -> 17, of which waited for: 11 -> 12; matrix products, arithmetic and copies ran while one was open for 7% -> 3% of each run, Pallas kernels for 0% -> 0%
where the time goes in v3:
time: 204 us; the launch traced here: 203 us
  waiting for transfers between devices  80.6 us (40%)
  starting transfers between devices  79.6 us (39%)
  blocking collectives  14.5 us (7%)
  local copies, waits for them, and re-layouts  7.69 us (4%)
  other arithmetic  6.57 us (3%)
  Pallas kernels  6.49 us (3%)
  matrix products  5.92 us (3%)
    ppermute x13, waiting for transfers between devices, swap(): return lax.ppermute(block, axis, [(i, i ^ bit) for i in range(size)])  60.3 us
    ppermute x13, starting transfers between devices, swap(): return lax.ppermute(block, axis, [(i, i ^ bit) for i in range(size)])  57.2 us
    all_to_all x4, starting transfers between devices, exchange(): lax.all_to_all(blocks, axes, split_axis=0, concat_axis=0, tiled=False)  22.5 us
    all_to_all x4, waiting for transfers between devices, exchange(): lax.all_to_all(blocks, axes, split_axis=0, concat_axis=0, tiled=False)  20.3 us
    all_to_all x1, blocking collectives, exchange(): lax.all_to_all(blocks, axes, split_axis=0, concat_axis=0, tiled=False)  14.5 us
    unnamed x40, local copies, waits for them, and re-layouts  5.51 us
  transfers between devices with their start and end apart: 17, of which 12 were waited for; matrix products, arithmetic and copies ran while one was open for 3% of the time, Pallas kernels for 0%

profile of v3, /device:TPU:56, one launch (start us, length us, event | category | flops | bytes accessed | tf_op | source)
XLA Modules:
  0.0 203.3 jit_solution(3352684688782453028)
XLA Ops:
  2.2 3.9 %normalize.1 = bf16[16,2,64,512]{3,2,1,0:T(8,128)(2,1)} custom-call(bf16[1,2,64,8192]{3,2,1,0:T(8,128)(2,1)S(1)} %copy-done), custom_call_target="tpu_custom_call" | custom-call | flops 4194304 | bytes 4194304 | tf_op jit(solution)/shard_map/normalize/pallas_call | solution.py:67
  6.1 10.0 %all-to-all-start = ((bf16[16,2,64,512]{3,2,1,0:T(8,128)(2,1)}), bf16[16,2,64,512]{3,2,1,0:T(8,128)(2,1)S(1)}, u32[]{:S(2)}, u32[]{:S(2)}) async-start(bf16[16,2,64,512]{3,2,1,0:T(8,128)(2,1)} %normalize.1), calls=%async_computation | async-start | bytes 4194304 | tf_op jit(solution)/shard_map/all_to_all | solution.py:42
  16.2 3.8 %collective-permute-start.1 = (f32[2,8]{1,0:T(2,128)S(1)}, f32[2,8]{1,0:T(2,128)S(1)}, u32[]{:S(2)}, u32[]{:S(2)}) collective-permute-start(f32[2,8]{1,0:T(2,128)S(1)} %convert_reduce_fusion.2), channel_id=1, source_target_pairs={{0,4},{4,0},{8,12},{12,8},{1,5},{5,1},{9,13},{13,9},{2,6},{6,2},{1... | collective-permute-start | bytes 200 | tf_op jit(solution)/shard_map/ppermute | solution.py:47
  23.6 4.3 %collective-permute-start = (bf16[2,80,512]{2,1,0:T(8,128)(2,1)S(1)}, bf16[2,80,512]{2,1,0:T(8,128)(2,1)S(1)}, u32[]{:S(2)}, u32[]{:S(2)}) collective-permute-start(bf16[2,80,512]{2,1,0:T(8,128)(2,1)S(1)} %fusion.10), channel_id=1, source_target_pairs={{0,2},{2,0},{1,3},{3,1},{4,6},{6,4},{5,7},{7,5},{8,10},{10,8},{9,1... | collective-permute-start | bytes 491528 | tf_op jit(solution)/shard_map/ppermute | solution.py:47
  31.0 6.0 %collective-permute-start.2 = (f32[2,8]{1,0:T(2,128)S(1)}, f32[2,8]{1,0:T(2,128)S(1)}, u32[]{:S(2)}, u32[]{:S(2)}) collective-permute-start(f32[2,8]{1,0:T(2,128)S(1)} %add.75), channel_id=1, source_target_pairs={{0,8},{4,12},{8,0},{12,4},{1,9},{5,13},{9,1},{13,5},{2,10},{6,14},... | collective-permute-start | bytes 200 | tf_op jit(solution)/shard_map/ppermute | solution.py:47
  42.0 11.5 %collective-permute-done.3 = f32[2,8]{1,0:T(2,128)S(1)} collective-permute-done((f32[2,8]{1,0:T(2,128)S(1)}, f32[2,8]{1,0:T(2,128)S(1)}, u32[]{:S(2)}, u32[]{:S(2)}) %collective-permute-start.3) | collective-permute-done | bytes 96 | tf_op jit(solution)/shard_map/ppermute | solution.py:47
  53.6 6.4 %collective-permute-start.4 = (f32[2,8]{1,0:T(2,128)S(1)}, f32[2,8]{1,0:T(2,128)S(1)}, u32[]{:S(2)}, u32[]{:S(2)}) collective-permute-start(f32[2,8]{1,0:T(2,128)S(1)} %add.77), channel_id=1, source_target_pairs={{0,2},{2,0},{1,3},{3,1},{4,6},{6,4},{5,7},{7,5},{8,10},{10,8},{9,1... | collective-permute-start | bytes 200 | tf_op jit(solution)/shard_map/ppermute | solution.py:47
  63.3 8.0 %collective-permute-done.4 = f32[2,8]{1,0:T(2,128)S(1)} collective-permute-done((f32[2,8]{1,0:T(2,128)S(1)}, f32[2,8]{1,0:T(2,128)S(1)}, u32[]{:S(2)}, u32[]{:S(2)}) %collective-permute-start.4) | collective-permute-done | bytes 96 | tf_op jit(solution)/shard_map/ppermute | solution.py:47
  71.3 4.0 %collective-permute-start.7 = (f32[256,128]{1,0:T(8,128)S(1)}, f32[256,128]{1,0:T(8,128)S(1)}, u32[]{:S(2)}, u32[]{:S(2)}) collective-permute-start(f32[256,128]{1,0:T(8,128)S(1)} %add.83), channel_id=1, source_target_pairs={{0,64},{32,96},{64,0},{96,32},{128,192},{160,224},{192,128},{224,1... | collective-permute-start | bytes 393224 | tf_op jit(solution)/shard_map/ppermute | solution.py:47
  76.6 4.3 %collective-permute-done.7 = f32[256,128]{1,0:T(8,128)S(1)} collective-permute-done((f32[256,128]{1,0:T(8,128)S(1)}, f32[256,128]{1,0:T(8,128)S(1)}, u32[]{:S(2)}, u32[]{:S(2)}) %collective-permute-start.7) | collective-permute-done | bytes 131104 | tf_op jit(solution)/shard_map/ppermute | solution.py:47
  81.0 4.6 %collective-permute-start.8 = (f32[256,128]{1,0:T(8,128)S(1)}, f32[256,128]{1,0:T(8,128)S(1)}, u32[]{:S(2)}, u32[]{:S(2)}) collective-permute-start(f32[256,128]{1,0:T(8,128)S(1)} %add.84), channel_id=1, source_target_pairs={{0,128},{32,160},{64,192},{96,224},{128,0},{160,32},{192,64},{224,... | collective-permute-start | bytes 393224 | tf_op jit(solution)/shard_map/ppermute | solution.py:47
  85.8 6.9 %collective-permute-done.8 = f32[256,128]{1,0:T(8,128)S(1)} collective-permute-done((f32[256,128]{1,0:T(8,128)S(1)}, f32[256,128]{1,0:T(8,128)S(1)}, u32[]{:S(2)}, u32[]{:S(2)}) %collective-permute-start.8) | collective-permute-done | bytes 131104 | tf_op jit(solution)/shard_map/ppermute | solution.py:47
  95.6 4.2 %all-to-all-start.1 = ((bf16[8,128,512]{2,1,0:T(8,128)(2,1)}), bf16[8,128,512]{2,1,0:T(8,128)(2,1)S(1)}, u32[]{:S(2)}, u32[]{:S(2)}) async-start(bf16[8,128,512]{2,1,0:T(8,128)(2,1)} %bitcast.14), calls=%async_computation.1 | async-start | bytes 2097152 | tf_op jit(solution)/shard_map/all_to_all | solution.py:42
  99.9 8.2 %collective-permute-start.9 = (f32[256,128]{1,0:T(8,128)S(1)}, f32[256,128]{1,0:T(8,128)S(1)}, u32[]{:S(2)}, u32[]{:S(2)}) collective-permute-start(f32[256,128]{1,0:T(8,128)S(1)} %add.85), channel_id=1, source_target_pairs={{0,256},{256,0},{1,257},{257,1},{2,258},{258,2},{3,259},{259,3},{4... | collective-permute-start | bytes 393224 | tf_op jit(solution)/shard_map/ppermute | solution.py:47
  108.2 14.5 %collective-permute-done.9 = f32[256,128]{1,0:T(8,128)S(1)} collective-permute-done((f32[256,128]{1,0:T(8,128)S(1)}, f32[256,128]{1,0:T(8,128)S(1)}, u32[]{:S(2)}, u32[]{:S(2)}) %collective-permute-start.9) | collective-permute-done | bytes 131104 | tf_op jit(solution)/shard_map/ppermute | solution.py:47
  123.8 4.4 %collective-permute-start.10 = (bf16[128,512]{1,0:T(8,128)(2,1)S(1)}, bf16[128,512]{1,0:T(8,128)(2,1)S(1)}, u32[]{:S(2)}, u32[]{:S(2)}) collective-permute-start(bf16[128,512]{1,0:T(8,128)(2,1)S(1)} %convert_element_type.98), channel_id=1, source_target_pairs={{0,2},{2,0},{1,3},{3,1},{4,6},{6,4},{5,7},{7,5},{8,10},{10,8},{9,1... | collective-permute-start | bytes 393224 | tf_op jit(solution)/shard_map/ppermute | solution.py:47
  128.2 4.7 %collective-permute-done.10.got_ref = bf16[128,512]{1,0:T(8,128)(2,1)S(1)} collective-permute-done((bf16[128,512]{1,0:T(8,128)(2,1)S(1)}, bf16[128,512]{1,0:T(8,128)(2,1)S(1)}, u32[]{:S(2)}, u32[]{:S(2)}) %collective-permute-start.10) | collective-permute-done | bytes 131104 | tf_op jit(solution)/shard_map/ppermute | solution.py:47
  134.3 4.7 %all-to-all-start.2 = ((bf16[8,144,512]{2,1,0:T(8,128)(2,1)}), bf16[8,144,512]{2,1,0:T(8,128)(2,1)S(1)}, u32[]{:S(2)}, u32[]{:S(2)}) async-start(bf16[8,144,512]{2,1,0:T(8,128)(2,1)} %errors.2), calls=%async_computation.2 | async-start | bytes 2359296 | tf_op jit(solution)/shard_map/all_to_all | solution.py:42
  142.3 9.9 %all-to-all-done.2 = bf16[8,144,512]{2,1,0:T(8,128)(2,1)S(1)} async-done(((bf16[8,144,512]{2,1,0:T(8,128)(2,1)}), bf16[8,144,512]{2,1,0:T(8,128)(2,1)S(1)}, u32[]{:S(2)}, u32[]{:S(2)}) %all-to-all-start.2) | async-done | bytes 1179680 | tf_op jit(solution)/shard_map/all_to_all | solution.py:42
  155.1 14.5 %all_to_all.25 = bf16[8,128,512]{2,1,0:T(8,128)(2,1)S(1)} all-to-all(bf16[8,128,512]{2,1,0:T(8,128)(2,1)S(1)} %bitcast.82), channel_id=1, replica_groups=mesh['zh'=2,'y'=8,'c'=2,'x'=4,'zf'=2,'zn'=2] {'x','zn'}, dimensions={0} | all-to-all | bytes 2097152 | tf_op jit(solution)/shard_map/all_to_all | solution.py:42
  169.8 4.9 %collective-permute-start.12 = (bf16[128,512]{1,0:T(8,128)(2,1)S(1)}, bf16[128,512]{1,0:T(8,128)(2,1)S(1)}, u32[]{:S(2)}, u32[]{:S(2)}) collective-permute-start(bf16[128,512]{1,0:T(8,128)(2,1)S(1)} %convert_element_type.103), channel_id=1, source_target_pairs={{0,2},{2,0},{1,3},{3,1},{4,6},{6,4},{5,7},{7,5},{8,10},{10,8},{9,1... | collective-permute-start | bytes 393224 | tf_op jit(solution)/shard_map/ppermute | solution.py:47
  174.8 4.2 %collective-permute-done.12.got_ref = bf16[128,512]{1,0:T(8,128)(2,1)S(1)} collective-permute-done((bf16[128,512]{1,0:T(8,128)(2,1)S(1)}, bf16[128,512]{1,0:T(8,128)(2,1)S(1)}, u32[]{:S(2)}, u32[]{:S(2)}) %collective-permute-start.12) | collective-permute-done | bytes 131104 | tf_op jit(solution)/shard_map/ppermute | solution.py:47
  180.3 3.6 %all-to-all-start.4 = ((bf16[8,144,512]{2,1,0:T(8,128)(2,1)}), bf16[8,144,512]{2,1,0:T(8,128)(2,1)S(1)}, u32[]{:S(2)}, u32[]{:S(2)}) async-start(bf16[8,144,512]{2,1,0:T(8,128)(2,1)} %errors.3), calls=%async_computation.4 | async-start | bytes 2359296 | tf_op jit(solution)/shard_map/all_to_all | solution.py:42
  185.6 10.4 %all-to-all-done.4 = bf16[8,144,512]{2,1,0:T(8,128)(2,1)S(1)} async-done(((bf16[8,144,512]{2,1,0:T(8,128)(2,1)}), bf16[8,144,512]{2,1,0:T(8,128)(2,1)S(1)}, u32[]{:S(2)}, u32[]{:S(2)}) %all-to-all-start.4) | async-done | bytes 1179680 | tf_op jit(solution)/shard_map/all_to_all | solution.py:42
  (96 shorter events, 39.4 us)
Async XLA Ops:
  6.1 10.0 %copy-start.12 = (s32[1,2,64]{2,1,0:T(2,128)S(1)}, s32[1,2,64]{2,1,0:T(2,128)}, u32[]{:S(2)}) copy-start(s32[1,2,64]{2,1,0:T(2,128)} %param.11) | copy-start | bytes 1540
  6.1 17.5 %copy-start.6 = (bf16[1,2,64,512]{3,2,1,0:T(8,128)(2,1)S(1)}, bf16[1,2,64,512]{3,2,1,0:T(8,128)(2,1)}, u32[]{:S(2)}) copy-start(bf16[1,2,64,512]{3,2,1,0:T(8,128)(2,1)} %param.10) | copy-start | bytes 393220
  6.1 86.6 %all-to-all-start = ((bf16[16,2,64,512]{3,2,1,0:T(8,128)(2,1)}), bf16[16,2,64,512]{3,2,1,0:T(8,128)(2,1)S(1)}, u32[]{:S(2)}, u32[]{:S(2)}) async-start(bf16[16,2,64,512]{3,2,1,0:T(8,128)(2,1)} %normalize.1), calls=%async_computation | async-start | bytes 4194304 | tf_op jit(solution)/shard_map/all_to_all | solution.py:42
  16.2 14.8 %collective-permute-start.1 = (f32[2,8]{1,0:T(2,128)S(1)}, f32[2,8]{1,0:T(2,128)S(1)}, u32[]{:S(2)}, u32[]{:S(2)}) collective-permute-start(f32[2,8]{1,0:T(2,128)S(1)} %convert_reduce_fusion.2), channel_id=1, source_target_pairs={{0,4},{4,0},{8,12},{12,8},{1,5},{5,1},{9,13},{13,9},{2,6},{6,2},{1... | collective-permute-start | bytes 200 | tf_op jit(solution)/shard_map/ppermute | solution.py:47
  21.6 38.3 %collective-permute-start.5 = (bf16[256,128]{1,0:T(8,128)(2,1)S(1)}, bf16[256,128]{1,0:T(8,128)(2,1)S(1)}, u32[]{:S(2)}, u32[]{:S(2)}) collective-permute-start(bf16[256,128]{1,0:T(8,128)(2,1)S(1)} %dynamic-slice_bitcast_fusion), channel_id=1, source_target_pairs={{0,16},{16,0},{1,17},{17,1},{2,18},{18,2},{3,19},{19,3},{4,20},{20... | collective-permute-start | bytes 196616 | tf_op jit(solution)/shard_map/ppermute | solution.py:47
  23.6 51.8 %collective-permute-start = (bf16[2,80,512]{2,1,0:T(8,128)(2,1)S(1)}, bf16[2,80,512]{2,1,0:T(8,128)(2,1)S(1)}, u32[]{:S(2)}, u32[]{:S(2)}) collective-permute-start(bf16[2,80,512]{2,1,0:T(8,128)(2,1)S(1)} %fusion.10), channel_id=1, source_target_pairs={{0,2},{2,0},{1,3},{3,1},{4,6},{6,4},{5,7},{7,5},{8,10},{10,8},{9,1... | collective-permute-start | bytes 491528 | tf_op jit(solution)/shard_map/ppermute | solution.py:47
  31.0 7.6 %collective-permute-start.2 = (f32[2,8]{1,0:T(2,128)S(1)}, f32[2,8]{1,0:T(2,128)S(1)}, u32[]{:S(2)}, u32[]{:S(2)}) collective-permute-start(f32[2,8]{1,0:T(2,128)S(1)} %add.75), channel_id=1, source_target_pairs={{0,8},{4,12},{8,0},{12,4},{1,9},{5,13},{9,1},{13,5},{2,10},{6,14},... | collective-permute-start | bytes 200 | tf_op jit(solution)/shard_map/ppermute | solution.py:47
  38.6 14.9 %collective-permute-start.3 = (f32[2,8]{1,0:T(2,128)S(1)}, f32[2,8]{1,0:T(2,128)S(1)}, u32[]{:S(2)}, u32[]{:S(2)}) collective-permute-start(f32[2,8]{1,0:T(2,128)S(1)} %add.76), channel_id=1, source_target_pairs={{0,1},{1,0},{2,3},{3,2},{4,5},{5,4},{6,7},{7,6},{8,9},{9,8},{10,11... | collective-permute-start | bytes 200 | tf_op jit(solution)/shard_map/ppermute | solution.py:47
  53.6 17.7 %collective-permute-start.4 = (f32[2,8]{1,0:T(2,128)S(1)}, f32[2,8]{1,0:T(2,128)S(1)}, u32[]{:S(2)}, u32[]{:S(2)}) collective-permute-start(f32[2,8]{1,0:T(2,128)S(1)} %add.77), channel_id=1, source_target_pairs={{0,2},{2,0},{1,3},{3,1},{4,6},{6,4},{5,7},{7,5},{8,10},{10,8},{9,1... | collective-permute-start | bytes 200 | tf_op jit(solution)/shard_map/ppermute | solution.py:47
  60.0 11.3 %collective-permute-start.6 = (f32[256,128]{1,0:T(8,128)S(1)}, f32[256,128]{1,0:T(8,128)S(1)}, u32[]{:S(2)}, u32[]{:S(2)}) collective-permute-start(f32[256,128]{1,0:T(8,128)S(1)} %convert_add_fusion), channel_id=1, source_target_pairs={{0,32},{32,0},{64,96},{96,64},{128,160},{160,128},{192,224},{224,1... | collective-permute-start | bytes 393224 | tf_op jit(solution)/shard_map/ppermute | solution.py:47
  71.3 9.6 %collective-permute-start.7 = (f32[256,128]{1,0:T(8,128)S(1)}, f32[256,128]{1,0:T(8,128)S(1)}, u32[]{:S(2)}, u32[]{:S(2)}) collective-permute-start(f32[256,128]{1,0:T(8,128)S(1)} %add.83), channel_id=1, source_target_pairs={{0,64},{32,96},{64,0},{96,32},{128,192},{160,224},{192,128},{224,1... | collective-permute-start | bytes 393224 | tf_op jit(solution)/shard_map/ppermute | solution.py:47
  81.0 11.7 %collective-permute-start.8 = (f32[256,128]{1,0:T(8,128)S(1)}, f32[256,128]{1,0:T(8,128)S(1)}, u32[]{:S(2)}, u32[]{:S(2)}) collective-permute-start(f32[256,128]{1,0:T(8,128)S(1)} %add.84), channel_id=1, source_target_pairs={{0,128},{32,160},{64,192},{96,224},{128,0},{160,32},{192,64},{224,... | collective-permute-start | bytes 393224 | tf_op jit(solution)/shard_map/ppermute | solution.py:47
  92.7 15.5 %copy-start.5 = (f32[256,128]{1,0:T(8,128)}, f32[256,128]{1,0:T(8,128)S(1)}, u32[]{:S(2)}) copy-start(f32[256,128]{1,0:T(8,128)S(1)} %add.85) | copy-start | bytes 393220
  95.6 28.0 %all-to-all-start.1 = ((bf16[8,128,512]{2,1,0:T(8,128)(2,1)}), bf16[8,128,512]{2,1,0:T(8,128)(2,1)S(1)}, u32[]{:S(2)}, u32[]{:S(2)}) async-start(bf16[8,128,512]{2,1,0:T(8,128)(2,1)} %bitcast.14), calls=%async_computation.1 | async-start | bytes 2097152 | tf_op jit(solution)/shard_map/all_to_all | solution.py:42
  99.9 22.8 %collective-permute-start.9 = (f32[256,128]{1,0:T(8,128)S(1)}, f32[256,128]{1,0:T(8,128)S(1)}, u32[]{:S(2)}, u32[]{:S(2)}) collective-permute-start(f32[256,128]{1,0:T(8,128)S(1)} %add.85), channel_id=1, source_target_pairs={{0,256},{256,0},{1,257},{257,1},{2,258},{258,2},{3,259},{259,3},{4... | collective-permute-start | bytes 393224 | tf_op jit(solution)/shard_map/ppermute | solution.py:47
  123.6 29.5 %copy-start.4 = (f32[256,128]{1,0:T(8,128)}, f32[256,128]{1,0:T(8,128)S(1)}, u32[]{:S(2)}) copy-start(f32[256,128]{1,0:T(8,128)S(1)} %add.86) | copy-start | bytes 393220
  123.8 9.2 %collective-permute-start.10 = (bf16[128,512]{1,0:T(8,128)(2,1)S(1)}, bf16[128,512]{1,0:T(8,128)(2,1)S(1)}, u32[]{:S(2)}, u32[]{:S(2)}) collective-permute-start(bf16[128,512]{1,0:T(8,128)(2,1)S(1)} %convert_element_type.98), channel_id=1, source_target_pairs={{0,2},{2,0},{1,3},{3,1},{4,6},{6,4},{5,7},{7,5},{8,10},{10,8},{9,1... | collective-permute-start | bytes 393224 | tf_op jit(solution)/shard_map/ppermute | solution.py:47
  134.3 18.1 %copy-start.3 = (bf16[16,1,64,512]{3,2,1,0:T(8,128)(2,1)S(1)}, bf16[16,1,64,512]{3,2,1,0:T(8,128)(2,1)}, u32[]{:S(2)}) copy-start(bf16[16,1,64,512]{3,2,1,0:T(8,128)(2,1)} %copy-done.2) | copy-start | bytes 3145732
  134.3 18.0 %all-to-all-start.2 = ((bf16[8,144,512]{2,1,0:T(8,128)(2,1)}), bf16[8,144,512]{2,1,0:T(8,128)(2,1)S(1)}, u32[]{:S(2)}, u32[]{:S(2)}) async-start(bf16[8,144,512]{2,1,0:T(8,128)(2,1)} %errors.2), calls=%async_computation.2 | async-start | bytes 2359296 | tf_op jit(solution)/shard_map/all_to_all | solution.py:42
  139.0 3.4 %collective-permute-start.11 = (f32[256,128]{1,0:T(8,128)S(1)}, f32[256,128]{1,0:T(8,128)}, u32[]{:S(2)}, u32[]{:S(2)}) collective-permute-start(f32[256,128]{1,0:T(8,128)S(1)} %add.86), channel_id=1, source_target_pairs={{0,16},{16,0},{1,17},{17,1},{2,18},{18,2},{3,19},{19,3},{4,20},{20... | collective-permute-start | bytes 393224 | tf_op jit(solution)/shard_map/ppermute | solution.py:47
  169.8 9.3 %collective-permute-start.12 = (bf16[128,512]{1,0:T(8,128)(2,1)S(1)}, bf16[128,512]{1,0:T(8,128)(2,1)S(1)}, u32[]{:S(2)}, u32[]{:S(2)}) collective-permute-start(bf16[128,512]{1,0:T(8,128)(2,1)S(1)} %convert_element_type.103), channel_id=1, source_target_pairs={{0,2},{2,0},{1,3},{3,1},{4,6},{6,4},{5,7},{7,5},{8,10},{10,8},{9,1... | collective-permute-start | bytes 393224 | tf_op jit(solution)/shard_map/ppermute | solution.py:47
  180.3 15.7 %all-to-all-start.4 = ((bf16[8,144,512]{2,1,0:T(8,128)(2,1)}), bf16[8,144,512]{2,1,0:T(8,128)(2,1)S(1)}, u32[]{:S(2)}, u32[]{:S(2)}) async-start(bf16[8,144,512]{2,1,0:T(8,128)(2,1)} %errors.3), calls=%async_computation.4 | async-start | bytes 2359296 | tf_op jit(solution)/shard_map/all_to_all | solution.py:42
  184.6 11.6 %copy-start.11 = (bf16[1,512,512]{2,1,0:T(8,128)(2,1)S(1)}, bf16[1,512,512]{2,1,0:T(8,128)(2,1)}, u32[]{:S(2)}) copy-start(bf16[1,512,512]{2,1,0:T(8,128)(2,1)} %param.12) | copy-start | bytes 1572868
  184.6 11.6 %copy-start.14 = (bf16[1,512,512]{2,1,0:T(8,128)(2,1)S(1)}, bf16[1,512,512]{2,1,0:T(8,128)(2,1)}, u32[]{:S(2)}) copy-start(bf16[1,512,512]{2,1,0:T(8,128)(2,1)} %param.13) | copy-start | bytes 1572868
  (12 other events, 17.9 us)

commit v4 on v3

--- a/solution.py
+++ b/solution.py
@@ -25,8 +25,8 @@
 ORDER = ("x", "zn", "zf")
 GROUP = ("x", "zn")
 EXTRA = 16
-CHUNK = 16
-VMEM = 48 * 1024 * 1024
+CHUNK = 32
+VMEM = 16 * 1024 * 1024
 
 bf16, f32 = jnp.bfloat16, jnp.float32
 
@@ -51,14 +51,30 @@
     return lax.optimization_barrier(values)
 
 
-def normalize_kernel(width, hidden_ref, out_ref):
-    wide = hidden_ref[0, 0].astype(f32)
-    power = jnp.mean(wide * wide, axis=-1, keepdims=True)
-    normed = (wide * lax.rsqrt(power + NORM_EPS)).astype(bf16)
-    for at in range(out_ref.shape[0]):
-        x, zn, zf = at // 4, (at // 2) % 2, at % 2
-        owner = x * 4 + zf * 2 + zn
-        out_ref[at, 0] = normed[:, owner * width : (owner + 1) * width]
+def normalize_kernel(width, hidden_ref, out_ref, held, arrived):
+    steps, rows, _ = held.shape
+    parts = rows // CHUNK
+
+    def copy(at):
+        where = (at // parts, pl.ds(pl.multiple_of((at % parts) * CHUNK, CHUNK), CHUNK))
+        return pltpu.make_async_copy(hidden_ref.at[(0,) + where], held.at[where], arrived.at[at])
+
+    for at in range(steps * parts):
+        copy(at).start()
+
+    def chunk(at, carry):
+        copy(at).wait()
+        step, here = at // parts, pl.ds(pl.multiple_of((at % parts) * CHUNK, CHUNK), CHUNK)
+        wide = held[step, here].astype(f32)
+        power = jnp.mean(wide * wide, axis=-1, keepdims=True)
+        normed = (wide * lax.rsqrt(power + NORM_EPS)).astype(bf16)
+        for block in range(out_ref.shape[0]):
+            x, zn, zf = block // 4, (block // 2) % 2, block % 2
+            owner = x * 4 + zf * 2 + zn
+            out_ref[block, step, here] = normed[:, owner * width : (owner + 1) * width]
+        return carry
+
+    lax.fori_loop(0, steps * parts, chunk, 0)
 
 
 def normalize(hidden, shards):
@@ -66,10 +82,13 @@
     width = model_width // shards
     return pl.pallas_call(
         functools.partial(normalize_kernel, width),
-        grid=(steps, rows // CHUNK),
-        in_specs=[pl.BlockSpec((1, 1, CHUNK, model_width), lambda s, i: (0, s, i, 0))],
-        out_specs=pl.BlockSpec((shards, 1, CHUNK, width), lambda s, i: (0, s, i, 0)),
+        in_specs=[pl.BlockSpec(memory_space=pltpu.MemorySpace.HBM)],
+        out_specs=pl.BlockSpec(memory_space=pltpu.MemorySpace.VMEM),
         out_shape=jax.ShapeDtypeStruct((shards, steps, rows, width), bf16),
+        scratch_shapes=[
+            pltpu.VMEM((steps, rows, model_width), bf16),
+            pltpu.SemaphoreType.DMA((steps * rows // CHUNK,)),
+        ],
         compiler_params=pltpu.CompilerParams(vmem_limit_bytes=VMEM),
         cost_estimate=pl.CostEstimate(
             flops=8 * rows * model_width, bytes_accessed=8 * rows * model_width, transcendentals=rows
@@ -90,6 +109,7 @@
     middle = (loss - high).astype(bf16).astype(f32)
     low = loss - high - middle
     lane = lax.broadcasted_iota(jnp.int32, (EXTRA, columns), 1)
+    lane = lane + columns * lax.broadcasted_iota(jnp.int32, (EXTRA, columns), 0)
     row = jnp.where(lane == 0, high, jnp.where(lane == 1, middle, jnp.where(lane == 2, low, 0.0)))
     row = row.astype(bf16)
     for at in range(out_ref.shape[0]):
@@ -108,6 +128,60 @@
         ),
         name="errors",
     )(own, got, target, weight)
+
+
+def finish_kernel(
+    scale, got_ref, columns_ref, master_ref, first_ref, second_ref, outer_ref, start_ref, loss_ref,
+    out_ref, losses_ref, everyone, done, sent,
+):
+    groups = got_ref.shape[0]
+    features = columns_ref.shape[1]
+    tokens, width = everyone.shape[0] // groups, outer_ref.shape[1]
+    for at in range(groups):
+        everyone[at * tokens : (at + 1) * tokens] = got_ref[at, :tokens]
+    half = features // 2
+    here = pl.ds(pl.multiple_of(start_ref[0], 128), width)
+
+    def copy(at):
+        rows = pl.ds(at * half, half)
+        return pltpu.make_async_copy(done.at[rows], out_ref.at[0, rows], sent.at[at])
+
+    for at in range(2):
+        rows = slice(at * half, (at + 1) * half)
+        gradient = scale * lax.dot_general(
+            columns_ref[:, rows], everyone[...], (((0,), (0,)), ((), ())), preferred_element_type=f32
+        )
+        done[rows] = adam_update(master_ref[rows], first_ref[rows], second_ref[rows], gradient)[0]
+        done[rows, here] = MIXING * done[rows, here] + (1.0 - MIXING) * outer_ref[rows]
+        copy(at).start()
+    last = jnp.sum(got_ref[:, tokens:].astype(f32), axis=0)
+    last = jnp.sum(jnp.sum(last, axis=0, keepdims=True), axis=1, keepdims=True)
+    lane = lax.broadcasted_iota(jnp.int32, losses_ref.shape, 1)
+    losses_ref[...] = jnp.where(lane == 0, loss_ref[...], last)
+    for at in range(2):
+        copy(at).wait()
+
+
+def finish(got, columns, master, first, second, outer, start, loss, scale):
+    groups, rows, wide = got.shape
+    features = columns.shape[1]
+    vmem = pl.BlockSpec(memory_space=pltpu.MemorySpace.VMEM)
+    return pl.pallas_call(
+        functools.partial(finish_kernel, scale),
+        in_specs=[vmem] * 6 + [pl.BlockSpec(memory_space=pltpu.MemorySpace.SMEM), vmem],
+        out_specs=(pl.BlockSpec(memory_space=pltpu.MemorySpace.HBM), vmem),
+        out_shape=(
+            jax.ShapeDtypeStruct((1, features, wide), f32),
+            jax.ShapeDtypeStruct((1, 2), f32),
+        ),
+        scratch_shapes=[
+            pltpu.VMEM((groups * (rows - EXTRA), wide), bf16),
+            pltpu.VMEM((features, wide), f32),
+            pltpu.SemaphoreType.DMA((2,)),
+        ],
+        compiler_params=pltpu.CompilerParams(vmem_limit_bytes=VMEM),
+        name="finish",
+    )(got, columns, master, first, second, outer, start, loss)
 
 
 def body(hidden, targets, doc_ids, weights, adam_m, adam_v, anchor, momentum, fragment):
@@ -130,38 +204,42 @@
     blocks, weights, targets, doc_ids = tie(blocks, weights, targets, doc_ids)
     columns = exchange(blocks, ORDER)
 
-    id_rows = jnp.pad(
-        doc_ids[0].astype(bf16)[:, None, :],
-        ((0, 0), (0, EXTRA - 1), (0, value_width - rows)),
-    )
-    own_rows = jnp.concatenate([targets[0], id_rows], axis=1)
-    far_rows = swap(own_rows, "zf")
-    pair = jnp.stack(
-        [jnp.where(f_at == 0, own_rows, far_rows), jnp.where(f_at == 0, far_rows, own_rows)], axis=1
-    )
-    pair_targets = pair[:, :, :rows].reshape(steps_total, tokens, value_width)
-    pair_ids = pair[:, :, rows, :rows].reshape(steps_total, tokens, 1).astype(jnp.int32)
     doc_range = jnp.arange(DOCS, dtype=jnp.int32)
     counts = jnp.sum((doc_ids[0][..., None] == doc_range).astype(f32), axis=1)
-    for axis, bit in (("x", 1), ("x", 2), ("zn", 1), ("zf", 1)):
+    for axis, bit in (("x", 1), ("x", 2), ("zn", 1)):
         counts = counts + swap(counts, axis, bit)
+
+    def extra_row(values):
+        values = values.astype(bf16)
+        return jnp.pad(values, ((0, 0), (0, value_width - values.shape[1])))[:, None]
+
+    extra = [extra_row(doc_ids[0]), extra_row(counts)]
+    extra.append(jnp.zeros((steps_total, EXTRA - len(extra), value_width), bf16))
+    own_rows = jnp.concatenate([targets[0], *extra], axis=1)
+    far_rows = swap(own_rows, "zf")
+    pair = jnp.concatenate(
+        [jnp.where(f_at == 0, own_rows, far_rows), jnp.where(f_at == 0, far_rows, own_rows)], axis=1
+    )
+    cuts = [at * (rows + EXTRA) for at in range(nf)]
+    pair_targets = jnp.concatenate([pair[:, at : at + rows] for at in cuts], axis=1)
+    pair_ids = jnp.concatenate([pair[:, at + rows, :rows] for at in cuts], axis=1).astype(jnp.int32)
+    counts = counts + far_rows[:, rows + 1, :DOCS].astype(f32)
     inverse = 1.0 / (DOCS * counts)
-    hot = (pair_ids == doc_range).astype(f32)
+    hot = (pair_ids[..., None] == doc_range).astype(f32)
     token_weight = jnp.sum(hot * inverse[:, None, :], axis=-1, keepdims=True)
 
     half = shard_rows // 2
     local = lax.dynamic_slice(weights[0], (zero, start), (shard_rows, frag_width))
     local = local.reshape(2, half, frag_width)
     summed = pick(local, c_at, 0).astype(f32) + swap(pick(local, c_at ^ 1, 0), "c").astype(f32)
-    for bit in (1, 2, 4):
-        summed = summed + swap(summed, "y", bit)
+    summed = summed + swap(summed, "zh")
+    summed = summed + swap(summed, "y", 1)
 
     columns, pair_targets, token_weight, summed = tie(columns, pair_targets, token_weight, summed)
 
     master = weights[0].astype(f32)
     first = adam_m[0].astype(f32)
     second = adam_v[0].astype(f32)
-    losses = []
     for step in range(steps_total):
         current = master.astype(bf16)
         rows_now = columns[:, step].reshape(shards * rows, shard_rows)
@@ -169,8 +247,11 @@
         partial = partial.astype(bf16).reshape(groups, tokens, value_width)
         partial = exchange(partial, GROUP)
         if step == 0:
-            summed = summed + swap(summed, "zh")
+            summed = summed + swap(summed, "y", 2)
             partial, summed = tie(partial, summed)
+        else:
+            other = swap(summed, "c")
+            partial, summed, other = tie(partial, summed, other)
         own = jnp.sum(partial.astype(f32), axis=0)
         got = swap(own.astype(bf16), "zf")
         sent = errors(own, got, pair_targets[step], token_weight[step], groups, scale)
@@ -178,17 +259,17 @@
             sent, summed = tie(sent, summed)
         got = exchange(sent, GROUP)
         if step == 0:
-            other = swap(summed, "c")
-            got, summed, other = tie(got, summed, other)
-        losses.append(jnp.sum(got[:, tokens, :3].astype(f32)))
-        everyone = got[:, :tokens].reshape(shards * rows, value_width)
-        gradient = (
-            lax.dot_general(
-                rows_now, everyone, (((0,), (0,)), ((), ())), preferred_element_type=f32
+            summed = summed + swap(summed, "y", 4)
+            got, summed = tie(got, summed)
+            loss = jnp.sum(got[:, tokens:].astype(f32)).reshape(1, 1)
+            everyone = got[:, :tokens].reshape(shards * rows, value_width)
+            gradient = (
+                lax.dot_general(
+                    rows_now, everyone, (((0,), (0,)), ((), ())), preferred_element_type=f32
+                )
+                * scale
             )
-            * scale
-        )
-        master, first, second = adam_update(master, first, second, gradient)
+            master, first, second = adam_update(master, first, second, gradient)
 
     anchor_rows = anchor.astype(f32)
     summed = jnp.concatenate(
@@ -197,12 +278,12 @@
     mean_delta = anchor_rows - summed / replicas
     new_moment = NESTEROV * momentum.astype(f32) + mean_delta
     global_fragment = anchor_rows - OUTER_RATE * (mean_delta + NESTEROV * new_moment)
-    merged = (
-        MIXING * lax.dynamic_slice(master, (zero, start), (shard_rows, frag_width))
-        + (1.0 - MIXING) * global_fragment
-    )
-    master = lax.dynamic_update_slice(master, merged, (zero, start))
-    return (master[None], jnp.stack(losses)[None])
+    got, rows_now, master, first, second, global_fragment, loss = tie(
+        got, rows_now, master, first, second, global_fragment, loss
+    )
+    return finish(
+        got, rows_now, master, first, second, global_fragment, start.reshape(1), loss, scale
+    )
 
 
 def solution(mesh):

time: 204 us -> 190 us (0.931)
  blocking collectives: 14.5 us -> 0 us
  starting transfers between devices: 79.6 us -> 76 us
  matrix products: 5.92 us -> 9.06 us
    all_to_all x1 -> x0, blocking collectives: 14.5 us -> none  [exchange(): lax.all_to_all(blocks, axes, split_axis=0, concat_axis=0, tiled=False)]
    ppermute x13 -> x12, starting transfers between devices: 57.2 us -> 49.9 us  [swap(): return lax.ppermute(block, axis, [(i, i ^ bit) for i in range(size)])]
    all_to_all x4 -> x5, starting transfers between devices: 22.5 us -> 26.1 us  [exchange(): lax.all_to_all(blocks, axes, split_axis=0, concat_axis=0, tiled=False)]
    all_to_all x4 -> x5, waiting for transfers between devices: 20.3 us -> 23 us  [exchange(): lax.all_to_all(blocks, axes, split_axis=0, concat_axis=0, tiled=False)]
    ppermute x13 -> x12, waiting for transfers between devices: 60.3 us -> 58.2 us  [swap(): return lax.ppermute(block, axis, [(i, i ^ bit) for i in range(size)])]
    pallas_call x1 -> x2, Pallas kernels: 3.9 us -> 5.87 us  [the longest x1 3.37 us: finish(): pl.pallas_call(functools.partial(finish_kernel, scale), in_specs=[vmem] *...]
    dot_general x2 -> x1, matrix products: 2.86 us -> 4.45 us  [body(): lax.dot_general(rows_now, everyone, (((0,), (0,)), ((), ())), preferred_e...]
    unnamed x40 -> x15, local copies, waits for them, and re-layouts: 5.51 us -> 5.02 us
  transfers between devices with their start and end apart: 17 -> 17, of which waited for: 12 -> 14; matrix products, arithmetic and copies ran while one was open for 3% -> 2% of each run, Pallas kernels for 0% -> 0%
where the time goes in v4:
time: 190 us; the launch traced here: 189 us
  waiting for transfers between devices  81.2 us (43%)
  starting transfers between devices  76 us (40%)
  matrix products  9.06 us (5%)
  Pallas kernels  8.42 us (4%)
  local copies, waits for them, and re-layouts  7.58 us (4%)
  other arithmetic  4.94 us (3%)
    ppermute x12, waiting for transfers between devices, swap(): return lax.ppermute(block, axis, [(i, i ^ bit) for i in range(size)])  58.2 us
    ppermute x12, starting transfers between devices, swap(): return lax.ppermute(block, axis, [(i, i ^ bit) for i in range(size)])  49.9 us
    all_to_all x5, starting transfers between devices, exchange(): lax.all_to_all(blocks, axes, split_axis=0, concat_axis=0, tiled=False)  26.1 us
    all_to_all x5, waiting for transfers between devices, exchange(): lax.all_to_all(blocks, axes, split_axis=0, concat_axis=0, tiled=False)  23 us
    unnamed x15, local copies, waits for them, and re-layouts  5.02 us
    dot_general x2, matrix products, body(): partial = jnp.dot(rows_now, current, preferred_element_type=f32)  4.61 us
    dot_general x1, matrix products, body(): lax.dot_general(rows_now, everyone, (((0,), (0,)), ((), ())), preferred_e...  4.45 us
  transfers between devices with their start and end apart: 17, of which 14 were waited for; matrix products, arithmetic and copies ran while one was open for 2% of the time, Pallas kernels for 0%

profile of v4, /device:TPU:56, one launch (start us, length us, event | category | flops | bytes accessed | tf_op | source)
XLA Modules:
  0.0 188.9 jit_solution(288604320791680610)
XLA Ops:
  4.8 10.0 %all-to-all-start = ((bf16[16,2,64,512]{3,2,1,0:T(8,128)(2,1)}), bf16[16,2,64,512]{3,2,1,0:T(8,128)(2,1)S(1)}, u32[]{:S(2)}, u32[]{:S(2)}) async-start(bf16[16,2,64,512]{3,2,1,0:T(8,128)(2,1)} %normalize.1), calls=%async_computation | async-start | bytes 4194304 | tf_op jit(solution)/shard_map/all_to_all | solution.py:42
  14.8 3.8 %collective-permute-start = (f32[2,8]{1,0:T(2,128)S(1)}, f32[2,8]{1,0:T(2,128)S(1)}, u32[]{:S(2)}, u32[]{:S(2)}) collective-permute-start(f32[2,8]{1,0:T(2,128)S(1)} %convert_reduce_fusion.3), channel_id=1, source_target_pairs={{0,4},{4,0},{8,12},{12,8},{1,5},{5,1},{9,13},{13,9},{2,6},{6,2},{1... | collective-permute-start | bytes 200 | tf_op jit(solution)/shard_map/ppermute | solution.py:47
  22.2 7.4 %collective-permute-done = f32[2,8]{1,0:T(2,128)S(1)} collective-permute-done((f32[2,8]{1,0:T(2,128)S(1)}, f32[2,8]{1,0:T(2,128)S(1)}, u32[]{:S(2)}, u32[]{:S(2)}) %collective-permute-start) | collective-permute-done | bytes 96 | tf_op jit(solution)/shard_map/ppermute | solution.py:47
  29.7 6.0 %collective-permute-start.1 = (f32[2,8]{1,0:T(2,128)S(1)}, f32[2,8]{1,0:T(2,128)S(1)}, u32[]{:S(2)}, u32[]{:S(2)}) collective-permute-start(f32[2,8]{1,0:T(2,128)S(1)} %add.62), channel_id=1, source_target_pairs={{0,8},{4,12},{8,0},{12,4},{1,9},{5,13},{9,1},{13,5},{2,10},{6,14},... | collective-permute-start | bytes 200 | tf_op jit(solution)/shard_map/ppermute | solution.py:47
  37.2 3.4 %collective-permute-start.2 = (f32[2,8]{1,0:T(2,128)S(1)}, f32[2,8]{1,0:T(2,128)S(1)}, u32[]{:S(2)}, u32[]{:S(2)}) collective-permute-start(f32[2,8]{1,0:T(2,128)S(1)} %add.63), channel_id=1, source_target_pairs={{0,1},{1,0},{2,3},{3,2},{4,5},{5,4},{6,7},{7,6},{8,9},{9,8},{10,11... | collective-permute-start | bytes 200 | tf_op jit(solution)/shard_map/ppermute | solution.py:47
  40.8 7.9 %collective-permute-done.2 = f32[2,8]{1,0:T(2,128)S(1)} collective-permute-done((f32[2,8]{1,0:T(2,128)S(1)}, f32[2,8]{1,0:T(2,128)S(1)}, u32[]{:S(2)}, u32[]{:S(2)}) %collective-permute-start.2) | collective-permute-done | bytes 96 | tf_op jit(solution)/shard_map/ppermute | solution.py:47
  48.8 6.5 %collective-permute-start.3 = (bf16[2,80,512]{2,1,0:T(8,128)(2,1)S(1)}, bf16[2,80,512]{2,1,0:T(8,128)(2,1)S(1)}, u32[]{:S(2)}, u32[]{:S(2)}) collective-permute-start(bf16[2,80,512]{2,1,0:T(8,128)(2,1)S(1)} %maximum_maximum_fusion), channel_id=1, source_target_pairs={{0,2},{2,0},{1,3},{3,1},{4,6},{6,4},{5,7},{7,5},{8,10},{10,8},{9,1... | collective-permute-start | bytes 491528 | tf_op jit(solution)/shard_map/ppermute | solution.py:47
  55.4 8.2 %collective-permute-start.5 = (f32[256,128]{1,0:T(8,128)S(1)}, f32[256,128]{1,0:T(8,128)S(1)}, u32[]{:S(2)}, u32[]{:S(2)}) collective-permute-start(f32[256,128]{1,0:T(8,128)S(1)} %convert_add_fusion), channel_id=1, source_target_pairs={{0,256},{256,0},{1,257},{257,1},{2,258},{258,2},{3,259},{259,3},{4... | collective-permute-start | bytes 393224 | tf_op jit(solution)/shard_map/ppermute | solution.py:47
  63.6 11.8 %collective-permute-done.3 = bf16[2,80,512]{2,1,0:T(8,128)(2,1)S(1)} collective-permute-done((bf16[2,80,512]{2,1,0:T(8,128)(2,1)S(1)}, bf16[2,80,512]{2,1,0:T(8,128)(2,1)S(1)}, u32[]{:S(2)}, u32[]{:S(2)}) %collective-permute-start.3) | collective-permute-done | bytes 163872 | tf_op jit(solution)/shard_map/ppermute | solution.py:47
  79.2 3.5 %collective-permute-done.6 = f32[256,128]{1,0:T(8,128)S(1)} collective-permute-done((f32[256,128]{1,0:T(8,128)S(1)}, f32[256,128]{1,0:T(8,128)S(1)}, u32[]{:S(2)}, u32[]{:S(2)}) %collective-permute-start.6) | collective-permute-done | bytes 131104 | tf_op jit(solution)/shard_map/ppermute | solution.py:47
  86.8 4.3 %all-to-all-start.1 = ((bf16[8,128,512]{2,1,0:T(8,128)(2,1)}), bf16[8,128,512]{2,1,0:T(8,128)(2,1)S(1)}, u32[]{:S(2)}, u32[]{:S(2)}) async-start(bf16[8,128,512]{2,1,0:T(8,128)(2,1)} %bitcast.14), calls=%async_computation.1 | async-start | bytes 2097152 | tf_op jit(solution)/shard_map/all_to_all | solution.py:42
  91.1 4.0 %collective-permute-start.7 = (f32[256,128]{1,0:T(8,128)S(1)}, f32[256,128]{1,0:T(8,128)S(1)}, u32[]{:S(2)}, u32[]{:S(2)}) collective-permute-start(f32[256,128]{1,0:T(8,128)S(1)} %add.71), channel_id=1, source_target_pairs={{0,64},{32,96},{64,0},{96,32},{128,192},{160,224},{192,128},{224,1... | collective-permute-start | bytes 393224 | tf_op jit(solution)/shard_map/ppermute | solution.py:47
  95.2 5.0 %collective-permute-done.7 = f32[256,128]{1,0:T(8,128)S(1)} collective-permute-done((f32[256,128]{1,0:T(8,128)S(1)}, f32[256,128]{1,0:T(8,128)S(1)}, u32[]{:S(2)}, u32[]{:S(2)}) %collective-permute-start.7) | collective-permute-done | bytes 131104 | tf_op jit(solution)/shard_map/ppermute | solution.py:47
  100.2 4.3 %all-to-all-done.1 = bf16[8,128,512]{2,1,0:T(8,128)(2,1)S(1)} async-done(((bf16[8,128,512]{2,1,0:T(8,128)(2,1)}), bf16[8,128,512]{2,1,0:T(8,128)(2,1)S(1)}, u32[]{:S(2)}, u32[]{:S(2)}) %all-to-all-start.1) | async-done | bytes 1048608 | tf_op jit(solution)/shard_map/all_to_all | solution.py:42
  108.2 5.7 %collective-permute-done.8.got_ref = bf16[128,512]{1,0:T(8,128)(2,1)S(1)} collective-permute-done((bf16[128,512]{1,0:T(8,128)(2,1)S(1)}, bf16[128,512]{1,0:T(8,128)(2,1)S(1)}, u32[]{:S(2)}, u32[]{:S(2)}) %collective-permute-start.8) | collective-permute-done | bytes 131104 | tf_op jit(solution)/shard_map/ppermute | solution.py:47
  115.1 3.6 %all-to-all-start.2 = ((bf16[8,144,512]{2,1,0:T(8,128)(2,1)}), bf16[8,144,512]{2,1,0:T(8,128)(2,1)S(1)}, u32[]{:S(2)}, u32[]{:S(2)}) async-start(bf16[8,144,512]{2,1,0:T(8,128)(2,1)} %errors.2), calls=%async_computation.2 | async-start | bytes 2359296 | tf_op jit(solution)/shard_map/all_to_all | solution.py:42
  118.7 4.7 %collective-permute-start.9 = (f32[256,128]{1,0:T(8,128)S(1)}, f32[256,128]{1,0:T(8,128)S(1)}, u32[]{:S(2)}, u32[]{:S(2)}) collective-permute-start(f32[256,128]{1,0:T(8,128)S(1)} %add.72), channel_id=1, source_target_pairs={{0,128},{32,160},{64,192},{96,224},{128,0},{160,32},{192,64},{224,... | collective-permute-start | bytes 393224 | tf_op jit(solution)/shard_map/ppermute | solution.py:47
  123.4 7.4 %collective-permute-done.9 = f32[256,128]{1,0:T(8,128)S(1)} collective-permute-done((f32[256,128]{1,0:T(8,128)S(1)}, f32[256,128]{1,0:T(8,128)S(1)}, u32[]{:S(2)}, u32[]{:S(2)}) %collective-permute-start.9) | collective-permute-done | bytes 131104 | tf_op jit(solution)/shard_map/ppermute | solution.py:47
  132.8 4.4 %convert_subtract_fusion = (f32[512,512]{1,0:T(8,128)S(1)}, f32[512,512]{1,0:T(8,128)}, f32[512,512]{1,0:T(8,128)}) fusion(bf16[1,512,512]{2,1,0:T(8,128)(2,1)} %param.12, bf16[1,512,512]{2,1,0:T(8,128)(2,1)} %param.14, bf16[1,512,512]{2,1,0:T(8,128)(2,1)} %param.13, bf16[1024,512]{1,0:T(8,128)(2,1)} %bitcast.13, bf16[1024,512]{1,0:T(8,128)(2,1)S(1)} %bitcast.51), kind=kOutput, calls=%fused_computation.4 | convolution fusion | flops 541327360 | bytes 6815744 | tf_op jit(solution)/shard_map/dot_general | solution.py:267
  139.0 4.7 %all-to-all-start.3 = ((bf16[8,128,512]{2,1,0:T(8,128)(2,1)}), bf16[8,128,512]{2,1,0:T(8,128)(2,1)}, u32[]{:S(2)}, u32[]{:S(2)}) async-start(bf16[8,128,512]{2,1,0:T(8,128)(2,1)} %bitcast.50), calls=%async_computation.3 | async-start | bytes 2097152 | tf_op jit(solution)/shard_map/all_to_all | solution.py:42
  146.9 8.4 %all-to-all-done.3 = bf16[8,128,512]{2,1,0:T(8,128)(2,1)} async-done(((bf16[8,128,512]{2,1,0:T(8,128)(2,1)}), bf16[8,128,512]{2,1,0:T(8,128)(2,1)}, u32[]{:S(2)}, u32[]{:S(2)}) %all-to-all-start.3) | async-done | bytes 1048608 | tf_op jit(solution)/shard_map/all_to_all | solution.py:42
  159.5 6.5 %collective-permute-done.11.got_ref = bf16[128,512]{1,0:T(8,128)(2,1)S(1)} collective-permute-done((bf16[128,512]{1,0:T(8,128)(2,1)S(1)}, bf16[128,512]{1,0:T(8,128)(2,1)S(1)}, u32[]{:S(2)}, u32[]{:S(2)}) %collective-permute-start.11) | collective-permute-done | bytes 131104 | tf_op jit(solution)/shard_map/ppermute | solution.py:47
  167.3 3.6 %all-to-all-start.4 = ((bf16[8,144,512]{2,1,0:T(8,128)(2,1)}), bf16[8,144,512]{2,1,0:T(8,128)(2,1)S(1)}, u32[]{:S(2)}, u32[]{:S(2)}) async-start(bf16[8,144,512]{2,1,0:T(8,128)(2,1)} %errors.3), calls=%async_computation.4 | async-start | bytes 2359296 | tf_op jit(solution)/shard_map/all_to_all | solution.py:42
  173.6 9.4 %all-to-all-done.4.got_ref = bf16[8,144,512]{2,1,0:T(8,128)(2,1)S(1)} async-done(((bf16[8,144,512]{2,1,0:T(8,128)(2,1)}), bf16[8,144,512]{2,1,0:T(8,128)(2,1)S(1)}, u32[]{:S(2)}, u32[]{:S(2)}) %all-to-all-start.4) | async-done | bytes 1179680 | tf_op jit(solution)/shard_map/all_to_all | solution.py:42
  (74 shorter events, 42.4 us)
Async XLA Ops:
  0.6 1.6 copy-start
  4.7 10.0 %copy-start.6 = (s32[1,2,64]{2,1,0:T(2,128)S(1)}, s32[1,2,64]{2,1,0:T(2,128)}, u32[]{:S(2)}) copy-start(s32[1,2,64]{2,1,0:T(2,128)} %param.11) | copy-start | bytes 1540
  4.7 44.0 %copy-start.4 = (bf16[1,2,64,512]{3,2,1,0:T(8,128)(2,1)S(1)}, bf16[1,2,64,512]{3,2,1,0:T(8,128)(2,1)}, u32[]{:S(2)}) copy-start(bf16[1,2,64,512]{3,2,1,0:T(8,128)(2,1)} %param.10) | copy-start | bytes 393220
  4.8 77.9 %all-to-all-start = ((bf16[16,2,64,512]{3,2,1,0:T(8,128)(2,1)}), bf16[16,2,64,512]{3,2,1,0:T(8,128)(2,1)S(1)}, u32[]{:S(2)}, u32[]{:S(2)}) async-start(bf16[16,2,64,512]{3,2,1,0:T(8,128)(2,1)} %normalize.1), calls=%async_computation | async-start | bytes 4194304 | tf_op jit(solution)/shard_map/all_to_all | solution.py:42
  14.8 14.8 %collective-permute-start = (f32[2,8]{1,0:T(2,128)S(1)}, f32[2,8]{1,0:T(2,128)S(1)}, u32[]{:S(2)}, u32[]{:S(2)}) collective-permute-start(f32[2,8]{1,0:T(2,128)S(1)} %convert_reduce_fusion.3), channel_id=1, source_target_pairs={{0,4},{4,0},{8,12},{12,8},{1,5},{5,1},{9,13},{13,9},{2,6},{6,2},{1... | collective-permute-start | bytes 200 | tf_op jit(solution)/shard_map/ppermute | solution.py:47
  20.3 35.1 %collective-permute-start.4 = (bf16[256,128]{1,0:T(8,128)(2,1)S(1)}, bf16[256,128]{1,0:T(8,128)(2,1)S(1)}, u32[]{:S(2)}, u32[]{:S(2)}) collective-permute-start(bf16[256,128]{1,0:T(8,128)(2,1)S(1)} %dynamic-slice_bitcast_fusion), channel_id=1, source_target_pairs={{0,16},{16,0},{1,17},{17,1},{2,18},{18,2},{3,19},{19,3},{4,20},{20... | collective-permute-start | bytes 196616 | tf_op jit(solution)/shard_map/ppermute | solution.py:47
  29.7 7.6 %collective-permute-start.1 = (f32[2,8]{1,0:T(2,128)S(1)}, f32[2,8]{1,0:T(2,128)S(1)}, u32[]{:S(2)}, u32[]{:S(2)}) collective-permute-start(f32[2,8]{1,0:T(2,128)S(1)} %add.62), channel_id=1, source_target_pairs={{0,8},{4,12},{8,0},{12,4},{1,9},{5,13},{9,1},{13,5},{2,10},{6,14},... | collective-permute-start | bytes 200 | tf_op jit(solution)/shard_map/ppermute | solution.py:47
  37.2 11.5 %collective-permute-start.2 = (f32[2,8]{1,0:T(2,128)S(1)}, f32[2,8]{1,0:T(2,128)S(1)}, u32[]{:S(2)}, u32[]{:S(2)}) collective-permute-start(f32[2,8]{1,0:T(2,128)S(1)} %add.63), channel_id=1, source_target_pairs={{0,1},{1,0},{2,3},{3,2},{4,5},{5,4},{6,7},{7,6},{8,9},{9,8},{10,11... | collective-permute-start | bytes 200 | tf_op jit(solution)/shard_map/ppermute | solution.py:47
  48.8 26.6 %collective-permute-start.3 = (bf16[2,80,512]{2,1,0:T(8,128)(2,1)S(1)}, bf16[2,80,512]{2,1,0:T(8,128)(2,1)S(1)}, u32[]{:S(2)}, u32[]{:S(2)}) collective-permute-start(bf16[2,80,512]{2,1,0:T(8,128)(2,1)S(1)} %maximum_maximum_fusion), channel_id=1, source_target_pairs={{0,2},{2,0},{1,3},{3,1},{4,6},{6,4},{5,7},{7,5},{8,10},{10,8},{9,1... | collective-permute-start | bytes 491528 | tf_op jit(solution)/shard_map/ppermute | solution.py:47
  55.4 20.3 %collective-permute-start.5 = (f32[256,128]{1,0:T(8,128)S(1)}, f32[256,128]{1,0:T(8,128)S(1)}, u32[]{:S(2)}, u32[]{:S(2)}) collective-permute-start(f32[256,128]{1,0:T(8,128)S(1)} %convert_add_fusion), channel_id=1, source_target_pairs={{0,256},{256,0},{1,257},{257,1},{2,258},{258,2},{3,259},{259,3},{4... | collective-permute-start | bytes 393224 | tf_op jit(solution)/shard_map/ppermute | solution.py:47
  75.8 6.9 %collective-permute-start.6 = (f32[256,128]{1,0:T(8,128)S(1)}, f32[256,128]{1,0:T(8,128)S(1)}, u32[]{:S(2)}, u32[]{:S(2)}) collective-permute-start(f32[256,128]{1,0:T(8,128)S(1)} %add.70), channel_id=1, source_target_pairs={{0,32},{32,0},{64,96},{96,64},{128,160},{160,128},{192,224},{224,1... | collective-permute-start | bytes 393224 | tf_op jit(solution)/shard_map/ppermute | solution.py:47
  82.7 1.2 copy-start.5
  86.8 17.7 %all-to-all-start.1 = ((bf16[8,128,512]{2,1,0:T(8,128)(2,1)}), bf16[8,128,512]{2,1,0:T(8,128)(2,1)S(1)}, u32[]{:S(2)}, u32[]{:S(2)}) async-start(bf16[8,128,512]{2,1,0:T(8,128)(2,1)} %bitcast.14), calls=%async_computation.1 | async-start | bytes 2097152 | tf_op jit(solution)/shard_map/all_to_all | solution.py:42
  91.1 9.2 %collective-permute-start.7 = (f32[256,128]{1,0:T(8,128)S(1)}, f32[256,128]{1,0:T(8,128)S(1)}, u32[]{:S(2)}, u32[]{:S(2)}) collective-permute-start(f32[256,128]{1,0:T(8,128)S(1)} %add.71), channel_id=1, source_target_pairs={{0,64},{32,96},{64,0},{96,32},{128,192},{160,224},{192,128},{224,1... | collective-permute-start | bytes 393224 | tf_op jit(solution)/shard_map/ppermute | solution.py:47
  104.7 9.2 %collective-permute-start.8 = (bf16[128,512]{1,0:T(8,128)(2,1)S(1)}, bf16[128,512]{1,0:T(8,128)(2,1)S(1)}, u32[]{:S(2)}, u32[]{:S(2)}) collective-permute-start(bf16[128,512]{1,0:T(8,128)(2,1)S(1)} %convert_element_type.91), channel_id=1, source_target_pairs={{0,2},{2,0},{1,3},{3,1},{4,6},{6,4},{5,7},{7,5},{8,10},{10,8},{9,1... | collective-permute-start | bytes 393224 | tf_op jit(solution)/shard_map/ppermute | solution.py:47
  115.1 16.7 %all-to-all-start.2 = ((bf16[8,144,512]{2,1,0:T(8,128)(2,1)}), bf16[8,144,512]{2,1,0:T(8,128)(2,1)S(1)}, u32[]{:S(2)}, u32[]{:S(2)}) async-start(bf16[8,144,512]{2,1,0:T(8,128)(2,1)} %errors.2), calls=%async_computation.2 | async-start | bytes 2359296 | tf_op jit(solution)/shard_map/all_to_all | solution.py:42
  118.7 12.2 %collective-permute-start.9 = (f32[256,128]{1,0:T(8,128)S(1)}, f32[256,128]{1,0:T(8,128)S(1)}, u32[]{:S(2)}, u32[]{:S(2)}) collective-permute-start(f32[256,128]{1,0:T(8,128)S(1)} %add.72), channel_id=1, source_target_pairs={{0,128},{32,160},{64,192},{96,224},{128,0},{160,32},{192,64},{224,... | collective-permute-start | bytes 393224 | tf_op jit(solution)/shard_map/ppermute | solution.py:47
  131.8 1.0 copy-start.3
  139.0 16.4 %all-to-all-start.3 = ((bf16[8,128,512]{2,1,0:T(8,128)(2,1)}), bf16[8,128,512]{2,1,0:T(8,128)(2,1)}, u32[]{:S(2)}, u32[]{:S(2)}) async-start(bf16[8,128,512]{2,1,0:T(8,128)(2,1)} %bitcast.50), calls=%async_computation.3 | async-start | bytes 2097152 | tf_op jit(solution)/shard_map/all_to_all | solution.py:42
  143.7 3.2 %collective-permute-start.10 = (f32[256,128]{1,0:T(8,128)S(1)}, f32[256,128]{1,0:T(8,128)S(1)}, u32[]{:S(2)}, u32[]{:S(2)}) collective-permute-start(f32[256,128]{1,0:T(8,128)S(1)} %add.73), channel_id=1, source_target_pairs={{0,16},{16,0},{1,17},{17,1},{2,18},{18,2},{3,19},{19,3},{4,20},{20... | collective-permute-start | bytes 393224 | tf_op jit(solution)/shard_map/ppermute | solution.py:47
  156.8 9.3 %collective-permute-start.11 = (bf16[128,512]{1,0:T(8,128)(2,1)S(1)}, bf16[128,512]{1,0:T(8,128)(2,1)S(1)}, u32[]{:S(2)}, u32[]{:S(2)}) collective-permute-start(bf16[128,512]{1,0:T(8,128)(2,1)S(1)} %convert_element_type.96), channel_id=1, source_target_pairs={{0,2},{2,0},{1,3},{3,1},{4,6},{6,4},{5,7},{7,5},{8,10},{10,8},{9,1... | collective-permute-start | bytes 393224 | tf_op jit(solution)/shard_map/ppermute | solution.py:47
  167.3 15.7 %all-to-all-start.4 = ((bf16[8,144,512]{2,1,0:T(8,128)(2,1)}), bf16[8,144,512]{2,1,0:T(8,128)(2,1)S(1)}, u32[]{:S(2)}, u32[]{:S(2)}) async-start(bf16[8,144,512]{2,1,0:T(8,128)(2,1)} %errors.3), calls=%async_computation.4 | async-start | bytes 2359296 | tf_op jit(solution)/shard_map/all_to_all | solution.py:42
  183.0 1.2 copy-start.1
  184.3 1.2 copy-start.2

commit v5 on v4

--- a/solution.py
+++ b/solution.py
@@ -27,6 +27,7 @@
 EXTRA = 16
 CHUNK = 32
 VMEM = 16 * 1024 * 1024
+ALL_VMEM = 60 * 1024 * 1024
 
 bf16, f32 = jnp.bfloat16, jnp.float32
 
@@ -82,14 +83,14 @@
     width = model_width // shards
     return pl.pallas_call(
         functools.partial(normalize_kernel, width),
-        in_specs=[pl.BlockSpec(memory_space=pltpu.MemorySpace.HBM)],
+        in_specs=[pl.BlockSpec(memory_space=pl.ANY)],
         out_specs=pl.BlockSpec(memory_space=pltpu.MemorySpace.VMEM),
         out_shape=jax.ShapeDtypeStruct((shards, steps, rows, width), bf16),
         scratch_shapes=[
             pltpu.VMEM((steps, rows, model_width), bf16),
             pltpu.SemaphoreType.DMA((steps * rows // CHUNK,)),
         ],
-        compiler_params=pltpu.CompilerParams(vmem_limit_bytes=VMEM),
+        compiler_params=pltpu.CompilerParams(vmem_limit_bytes=ALL_VMEM),
         cost_estimate=pl.CostEstimate(
             flops=8 * rows * model_width, bytes_accessed=8 * rows * model_width, transcendentals=rows
         ),
@@ -130,58 +131,186 @@
     )(own, got, target, weight)
 
 
+def lay(into, blocks):
+    for at, block in enumerate(blocks):
+        rows = block.shape[0]
+        into[at * rows : (at + 1) * rows] = block[...]
+
+
+def step_rows(columns_ref, step):
+    return [columns_ref.at[at, step] for at in range(columns_ref.shape[0])]
+
+
+def token_rows(got_ref):
+    tokens = got_ref.shape[1] - EXTRA
+    return [got_ref.at[at, pl.ds(0, tokens)] for at in range(got_ref.shape[0])]
+
+
+def loss_of(got_ref):
+    tokens = got_ref.shape[1] - EXTRA
+    total = jnp.sum(got_ref[:, tokens:].astype(f32), axis=0)
+    return jnp.sum(jnp.sum(total, axis=0, keepdims=True), axis=1, keepdims=True)
+
+
+def gradient_of(columns, everyone, scale):
+    product = lax.dot_general(
+        columns, everyone, (((0,), (0,)), ((), ())), preferred_element_type=f32
+    )
+    return product * scale
+
+
+def project_rows(out_ref, lhs, current):
+    tokens = out_ref.shape[1]
+    for at in range(out_ref.shape[0]):
+        rows = lhs[at * tokens : (at + 1) * tokens]
+        out_ref[at] = jnp.dot(rows, current, preferred_element_type=f32).astype(bf16)
+
+
+def project_kernel(columns_ref, weights_ref, out_ref, lhs, weights, sems):
+    copy = pltpu.make_async_copy(weights_ref.at[0], weights, sems.at[0])
+    copy.start()
+    lay(lhs, step_rows(columns_ref, 0))
+    copy.wait()
+    project_rows(out_ref, lhs, weights[...])
+
+
+def update_kernel(
+    scale, got_ref, columns_ref, weights_ref, first_ref, second_ref,
+    out_ref, gradient_ref, loss_ref, everyone, lhs, states, current, sems,
+):
+    sources = (weights_ref, first_ref, second_ref)
+    copies = [
+        pltpu.make_async_copy(r.at[0], states.at[at], sems.at[at]) for at, r in enumerate(sources)
+    ]
+    for copy in copies:
+        copy.start()
+    lay(everyone, token_rows(got_ref))
+    lay(lhs, step_rows(columns_ref, 0))
+    features = current.shape[0]
+    half = features // 2
+    for at in range(2):
+        rows = slice(at * half, (at + 1) * half)
+        gradient = gradient_of(lhs[:, rows], everyone[...], scale)
+        gradient_ref[rows] = gradient
+        if at == 0:
+            for copy in copies:
+                copy.wait()
+        state = [states[k, rows].astype(f32) for k in range(3)]
+        current[rows] = adam_update(*state, gradient)[0].astype(bf16)
+    lay(lhs, step_rows(columns_ref, 1))
+    project_rows(out_ref, lhs, current[...])
+    loss_ref[...] = loss_of(got_ref)
+
+
 def finish_kernel(
-    scale, got_ref, columns_ref, master_ref, first_ref, second_ref, outer_ref, start_ref, loss_ref,
-    out_ref, losses_ref, everyone, done, sent,
+    scale, got_ref, columns_ref, weights_ref, first_ref, second_ref, before_ref, outer_ref, start_ref,
+    loss_ref, out_ref, losses_ref, everyone, lhs, states, before, done, sems, sent,
 ):
-    groups = got_ref.shape[0]
-    features = columns_ref.shape[1]
-    tokens, width = everyone.shape[0] // groups, outer_ref.shape[1]
-    for at in range(groups):
-        everyone[at * tokens : (at + 1) * tokens] = got_ref[at, :tokens]
+    sources = (weights_ref, first_ref, second_ref)
+    copies = [
+        pltpu.make_async_copy(r.at[0], states.at[at], sems.at[at]) for at, r in enumerate(sources)
+    ]
+    copies.append(pltpu.make_async_copy(before_ref, before, sems.at[3]))
+    for copy in copies:
+        copy.start()
+    lay(everyone, token_rows(got_ref))
+    lay(lhs, step_rows(columns_ref, 1))
+    features, width = done.shape[0], outer_ref.shape[1]
     half = features // 2
     here = pl.ds(pl.multiple_of(start_ref[0], 128), width)
 
-    def copy(at):
+    def give(at):
         rows = pl.ds(at * half, half)
         return pltpu.make_async_copy(done.at[rows], out_ref.at[0, rows], sent.at[at])
 
     for at in range(2):
         rows = slice(at * half, (at + 1) * half)
-        gradient = scale * lax.dot_general(
-            columns_ref[:, rows], everyone[...], (((0,), (0,)), ((), ())), preferred_element_type=f32
-        )
-        done[rows] = adam_update(master_ref[rows], first_ref[rows], second_ref[rows], gradient)[0]
+        gradient = gradient_of(lhs[:, rows], everyone[...], scale)
+        if at == 0:
+            for copy in copies:
+                copy.wait()
+        state = [states[k, rows].astype(f32) for k in range(3)]
+        state = adam_update(*state, before[rows])
+        done[rows] = adam_update(*state, gradient)[0]
         done[rows, here] = MIXING * done[rows, here] + (1.0 - MIXING) * outer_ref[rows]
-        copy(at).start()
-    last = jnp.sum(got_ref[:, tokens:].astype(f32), axis=0)
-    last = jnp.sum(jnp.sum(last, axis=0, keepdims=True), axis=1, keepdims=True)
+        give(at).start()
     lane = lax.broadcasted_iota(jnp.int32, losses_ref.shape, 1)
-    losses_ref[...] = jnp.where(lane == 0, loss_ref[...], last)
+    losses_ref[...] = jnp.where(lane == 0, loss_ref[...], loss_of(got_ref))
     for at in range(2):
-        copy(at).wait()
-
-
-def finish(got, columns, master, first, second, outer, start, loss, scale):
-    groups, rows, wide = got.shape
-    features = columns.shape[1]
-    vmem = pl.BlockSpec(memory_space=pltpu.MemorySpace.VMEM)
+        give(at).wait()
+
+
+IN_VMEM = pl.BlockSpec(memory_space=pltpu.MemorySpace.VMEM)
+ANYWHERE = pl.BlockSpec(memory_space=pl.ANY)
+
+
+def project(columns, weights, groups):
+    shards, _, rows, features = columns.shape
+    tokens, wide = shards * rows, weights.shape[2]
+    return pl.pallas_call(
+        project_kernel,
+        in_specs=[IN_VMEM, ANYWHERE],
+        out_specs=IN_VMEM,
+        out_shape=jax.ShapeDtypeStruct((groups, tokens // groups, wide), bf16),
+        scratch_shapes=[
+            pltpu.VMEM((tokens, features), bf16),
+            pltpu.VMEM((features, wide), bf16),
+            pltpu.SemaphoreType.DMA((1,)),
+        ],
+        compiler_params=pltpu.CompilerParams(vmem_limit_bytes=VMEM),
+        name="project",
+    )(columns, weights)
+
+
+def update(got, columns, weights, first, second, scale):
+    shards, _, rows, features = columns.shape
+    groups, tokens, wide = got.shape[0], shards * rows, weights.shape[2]
+    return pl.pallas_call(
+        functools.partial(update_kernel, scale),
+        in_specs=[IN_VMEM] * 2 + [ANYWHERE] * 3,
+        out_specs=(IN_VMEM, IN_VMEM, IN_VMEM),
+        out_shape=(
+            jax.ShapeDtypeStruct((groups, tokens // groups, wide), bf16),
+            jax.ShapeDtypeStruct((features, wide), f32),
+            jax.ShapeDtypeStruct((1, 1), f32),
+        ),
+        scratch_shapes=[
+            pltpu.VMEM((tokens, wide), bf16),
+            pltpu.VMEM((tokens, features), bf16),
+            pltpu.VMEM((3, features, wide), bf16),
+            pltpu.VMEM((features, wide), bf16),
+            pltpu.SemaphoreType.DMA((3,)),
+        ],
+        compiler_params=pltpu.CompilerParams(vmem_limit_bytes=VMEM),
+        name="update",
+    )(got, columns, weights, first, second)
+
+
+def finish(got, columns, weights, first, second, before, outer, start, loss, scale):
+    shards, _, rows, features = columns.shape
+    tokens, wide = shards * rows, weights.shape[2]
     return pl.pallas_call(
         functools.partial(finish_kernel, scale),
-        in_specs=[vmem] * 6 + [pl.BlockSpec(memory_space=pltpu.MemorySpace.SMEM), vmem],
-        out_specs=(pl.BlockSpec(memory_space=pltpu.MemorySpace.HBM), vmem),
+        in_specs=[IN_VMEM] * 2
+        + [ANYWHERE] * 4
+        + [IN_VMEM, pl.BlockSpec(memory_space=pltpu.MemorySpace.SMEM), IN_VMEM],
+        out_specs=(ANYWHERE, IN_VMEM),
         out_shape=(
             jax.ShapeDtypeStruct((1, features, wide), f32),
             jax.ShapeDtypeStruct((1, 2), f32),
         ),
         scratch_shapes=[
-            pltpu.VMEM((groups * (rows - EXTRA), wide), bf16),
+            pltpu.VMEM((tokens, wide), bf16),
+            pltpu.VMEM((tokens, features), bf16),
+            pltpu.VMEM((3, features, wide), bf16),
             pltpu.VMEM((features, wide), f32),
+            pltpu.VMEM((features, wide), f32),
+            pltpu.SemaphoreType.DMA((4,)),
             pltpu.SemaphoreType.DMA((2,)),
         ],
         compiler_params=pltpu.CompilerParams(vmem_limit_bytes=VMEM),
         name="finish",
-    )(got, columns, master, first, second, outer, start, loss)
+    )(got, columns, weights, first, second, before, outer, start, loss)
 
 
 def body(hidden, targets, doc_ids, weights, adam_m, adam_v, anchor, momentum, fragment):
@@ -216,6 +345,16 @@
     extra = [extra_row(doc_ids[0]), extra_row(counts)]
     extra.append(jnp.zeros((steps_total, EXTRA - len(extra), value_width), bf16))
     own_rows = jnp.concatenate([targets[0], *extra], axis=1)
+
+    half = shard_rows // 2
+    local = lax.dynamic_slice(weights[0], (zero, start), (shard_rows, frag_width))
+    local = local.reshape(2, half, frag_width)
+    summed = pick(local, c_at, 0).astype(f32) + swap(pick(local, c_at ^ 1, 0), "c").astype(f32)
+    summed = summed + swap(summed, "y", 1)
+    summed = summed + swap(summed, "y", 2)
+    columns, own_rows, counts, summed = tie(columns, own_rows, counts, summed)
+
+    partial = exchange(project(columns, weights, groups), GROUP)
     far_rows = swap(own_rows, "zf")
     pair = jnp.concatenate(
         [jnp.where(f_at == 0, own_rows, far_rows), jnp.where(f_at == 0, far_rows, own_rows)], axis=1
@@ -228,49 +367,26 @@
     hot = (pair_ids[..., None] == doc_range).astype(f32)
     token_weight = jnp.sum(hot * inverse[:, None, :], axis=-1, keepdims=True)
 
-    half = shard_rows // 2
-    local = lax.dynamic_slice(weights[0], (zero, start), (shard_rows, frag_width))
-    local = local.reshape(2, half, frag_width)
-    summed = pick(local, c_at, 0).astype(f32) + swap(pick(local, c_at ^ 1, 0), "c").astype(f32)
-    summed = summed + swap(summed, "zh")
-    summed = summed + swap(summed, "y", 1)
-
-    columns, pair_targets, token_weight, summed = tie(columns, pair_targets, token_weight, summed)
-
-    master = weights[0].astype(f32)
-    first = adam_m[0].astype(f32)
-    second = adam_v[0].astype(f32)
-    for step in range(steps_total):
-        current = master.astype(bf16)
-        rows_now = columns[:, step].reshape(shards * rows, shard_rows)
-        partial = jnp.dot(rows_now, current, preferred_element_type=f32)
-        partial = partial.astype(bf16).reshape(groups, tokens, value_width)
-        partial = exchange(partial, GROUP)
-        if step == 0:
-            summed = summed + swap(summed, "y", 2)
-            partial, summed = tie(partial, summed)
-        else:
-            other = swap(summed, "c")
-            partial, summed, other = tie(partial, summed, other)
+    partial, pair_targets, token_weight, summed = tie(partial, pair_targets, token_weight, summed)
+
+    def share_errors(partial, step):
         own = jnp.sum(partial.astype(f32), axis=0)
         got = swap(own.astype(bf16), "zf")
-        sent = errors(own, got, pair_targets[step], token_weight[step], groups, scale)
-        if step == 0:
-            sent, summed = tie(sent, summed)
-        got = exchange(sent, GROUP)
-        if step == 0:
-            summed = summed + swap(summed, "y", 4)
-            got, summed = tie(got, summed)
-            loss = jnp.sum(got[:, tokens:].astype(f32)).reshape(1, 1)
-            everyone = got[:, :tokens].reshape(shards * rows, value_width)
-            gradient = (
-                lax.dot_general(
-                    rows_now, everyone, (((0,), (0,)), ((), ())), preferred_element_type=f32
-                )
-                * scale
-            )
-            master, first, second = adam_update(master, first, second, gradient)
-
+        return errors(own, got, pair_targets[step], token_weight[step], groups, scale)
+
+    sent, summed = tie(share_errors(partial, 0), summed)
+    got = exchange(sent, GROUP)
+    summed = summed + swap(summed, "y", 4)
+    got, summed = tie(got, summed)
+    states = (weights, adam_m, adam_v)
+    partial, gradient, loss = update(got, columns, *states, scale)
+    partial, summed = tie(partial, summed)
+    partial = exchange(partial, GROUP)
+    summed = summed + swap(summed, "zh")
+    partial, summed = tie(partial, summed)
+    sent, summed = tie(share_errors(partial, 1), summed)
+    got = exchange(sent, GROUP)
+    other = swap(summed, "c")
     anchor_rows = anchor.astype(f32)
     summed = jnp.concatenate(
         [jnp.where(c_at == 0, summed, other), jnp.where(c_at == 0, other, summed)], axis=0
@@ -278,11 +394,9 @@
     mean_delta = anchor_rows - summed / replicas
     new_moment = NESTEROV * momentum.astype(f32) + mean_delta
     global_fragment = anchor_rows - OUTER_RATE * (mean_delta + NESTEROV * new_moment)
-    got, rows_now, master, first, second, global_fragment, loss = tie(
-        got, rows_now, master, first, second, global_fragment, loss
-    )
+    got, global_fragment = tie(got, global_fragment)
     return finish(
-        got, rows_now, master, first, second, global_fragment, start.reshape(1), loss, scale
+        got, columns, *states, gradient, global_fragment, start.reshape(1), loss, scale
     )
 
 

time: 190 us -> 192 us (1.011)
  matrix products: 9.06 us -> 0 us
  Pallas kernels: 8.42 us -> 16.4 us
  local copies, waits for them, and re-layouts: 7.58 us -> 13.2 us
  waiting for transfers between devices: 81.2 us -> 77.7 us
  starting transfers between devices: 76 us -> 73.4 us
  other arithmetic: 4.94 us -> 7.21 us
    dot_general x3 -> x0, matrix products: 9.06 us -> none  [the longest x2 4.61 us: body(): partial = jnp.dot(rows_now, current, preferred_element_type=f32)]
    pallas_call x1 -> x3, Pallas kernels: 3.37 us -> 11.6 us  [the longest x1 6.44 us: finish(): pl.pallas_call(functools.partial(finish_kernel, scale), in_specs=[IN_VMEM...]
    all_to_all x5, waiting for transfers between devices: 23 us -> 16.3 us  [exchange(): lax.all_to_all(blocks, axes, split_axis=0, concat_axis=0, tiled=False)]
    unnamed x15 -> x37, local copies, waits for them, and re-layouts: 5.02 us -> 11.5 us
    ppermute x12, starting transfers between devices: 49.9 us -> 43.8 us  [swap(): return lax.ppermute(block, axis, [(i, i ^ bit) for i in range(size)])]
    all_to_all x5, starting transfers between devices: 26.1 us -> 29.6 us  [exchange(): lax.all_to_all(blocks, axes, split_axis=0, concat_axis=0, tiled=False)]
    ppermute x12, waiting for transfers between devices: 58.2 us -> 61.4 us  [swap(): return lax.ppermute(block, axis, [(i, i ^ bit) for i in range(size)])]
  transfers between devices with their start and end apart: 17 -> 17, of which waited for: 14 -> 14; matrix products, arithmetic and copies ran while one was open for 2% -> 3% of each run, Pallas kernels for 0% -> 0%
where the time goes in v5:
time: 192 us; the launch traced here: 190 us
  waiting for transfers between devices  77.7 us (40%)
  starting transfers between devices  73.4 us (38%)
  Pallas kernels  16.4 us (9%)
  local copies, waits for them, and re-layouts  13.2 us (7%)
  other arithmetic  7.21 us (4%)
    ppermute x12, waiting for transfers between devices, swap(): return lax.ppermute(block, axis, [(i, i ^ bit) for i in range(size)])  61.4 us
    ppermute x12, starting transfers between devices, swap(): return lax.ppermute(block, axis, [(i, i ^ bit) for i in range(size)])  43.8 us
    all_to_all x5, starting transfers between devices, exchange(): lax.all_to_all(blocks, axes, split_axis=0, concat_axis=0, tiled=False)  29.6 us
    all_to_all x5, waiting for transfers between devices, exchange(): lax.all_to_all(blocks, axes, split_axis=0, concat_axis=0, tiled=False)  16.3 us
    unnamed x37, local copies, waits for them, and re-layouts  11.5 us
    pallas_call x1, Pallas kernels, finish(): pl.pallas_call(functools.partial(finish_kernel, scale), in_specs=[IN_VMEM...  6.44 us
    pallas_call x1, Pallas kernels, update(): pl.pallas_call(functools.partial(update_kernel, scale), in_specs=[IN_VMEM...  4.32 us
  transfers between devices with their start and end apart: 17, of which 14 were waited for; matrix products, arithmetic and copies ran while one was open for 3% of the time, Pallas kernels for 0%

profile of v5, /device:TPU:56, one launch (start us, length us, event | category | flops | bytes accessed | tf_op | source)
XLA Modules:
  0.0 189.6 jit_solution(3383360411443679079)
XLA Ops:
  4.1 10.0 %all-to-all-start = ((bf16[16,2,64,512]{3,2,1,0:T(8,128)(2,1)}), bf16[16,2,64,512]{3,2,1,0:T(8,128)(2,1)S(1)}, u32[]{:S(2)}, u32[]{:S(2)}) async-start(bf16[16,2,64,512]{3,2,1,0:T(8,128)(2,1)} %normalize.1), calls=%async_computation | async-start | bytes 4194304 | tf_op jit(solution)/shard_map/all_to_all | solution.py:43
  14.2 3.8 %collective-permute-start = (f32[2,8]{1,0:T(2,128)S(1)}, f32[2,8]{1,0:T(2,128)S(1)}, u32[]{:S(2)}, u32[]{:S(2)}) collective-permute-start(f32[2,8]{1,0:T(2,128)S(1)} %convert_reduce_fusion.2), channel_id=1, source_target_pairs={{0,4},{4,0},{8,12},{12,8},{1,5},{5,1},{9,13},{13,9},{2,6},{6,2},{1... | collective-permute-start | bytes 200 | tf_op jit(solution)/shard_map/ppermute | solution.py:48
  20.8 8.2 %collective-permute-done = f32[2,8]{1,0:T(2,128)S(1)} collective-permute-done((f32[2,8]{1,0:T(2,128)S(1)}, f32[2,8]{1,0:T(2,128)S(1)}, u32[]{:S(2)}, u32[]{:S(2)}) %collective-permute-start) | collective-permute-done | bytes 96 | tf_op jit(solution)/shard_map/ppermute | solution.py:48
  29.0 6.0 %collective-permute-start.1 = (f32[2,8]{1,0:T(2,128)S(1)}, f32[2,8]{1,0:T(2,128)S(1)}, u32[]{:S(2)}, u32[]{:S(2)}) collective-permute-start(f32[2,8]{1,0:T(2,128)S(1)} %add.47), channel_id=1, source_target_pairs={{0,8},{4,12},{8,0},{12,4},{1,9},{5,13},{9,1},{13,5},{2,10},{6,14},... | collective-permute-start | bytes 200 | tf_op jit(solution)/shard_map/ppermute | solution.py:48
  36.6 3.4 %collective-permute-start.2 = (f32[2,8]{1,0:T(2,128)S(1)}, f32[2,8]{1,0:T(2,128)S(1)}, u32[]{:S(2)}, u32[]{:S(2)}) collective-permute-start(f32[2,8]{1,0:T(2,128)S(1)} %add.48), channel_id=1, source_target_pairs={{0,1},{1,0},{2,3},{3,2},{4,5},{5,4},{6,7},{7,6},{8,9},{9,8},{10,11... | collective-permute-start | bytes 200 | tf_op jit(solution)/shard_map/ppermute | solution.py:48
  43.3 4.7 %collective-permute-done.2 = f32[2,8]{1,0:T(2,128)S(1)} collective-permute-done((f32[2,8]{1,0:T(2,128)S(1)}, f32[2,8]{1,0:T(2,128)S(1)}, u32[]{:S(2)}, u32[]{:S(2)}) %collective-permute-start.2) | collective-permute-done | bytes 96 | tf_op jit(solution)/shard_map/ppermute | solution.py:48
  48.1 4.0 %collective-permute-start.5 = (f32[256,128]{1,0:T(8,128)S(1)}, f32[256,128]{1,0:T(8,128)S(1)}, u32[]{:S(2)}, u32[]{:S(2)}) collective-permute-start(f32[256,128]{1,0:T(8,128)S(1)} %add.54), channel_id=1, source_target_pairs={{0,64},{32,96},{64,0},{96,32},{128,192},{160,224},{192,128},{224,1... | collective-permute-start | bytes 393224 | tf_op jit(solution)/shard_map/ppermute | solution.py:48
  52.3 5.8 %collective-permute-done.5 = f32[256,128]{1,0:T(8,128)S(1)} collective-permute-done((f32[256,128]{1,0:T(8,128)S(1)}, f32[256,128]{1,0:T(8,128)S(1)}, u32[]{:S(2)}, u32[]{:S(2)}) %collective-permute-start.5) | collective-permute-done | bytes 131104 | tf_op jit(solution)/shard_map/ppermute | solution.py:48
  58.7 3.4 %all-to-all-done.columns_ref = bf16[16,2,64,512]{3,2,1,0:T(8,128)(2,1)S(1)} async-done(((bf16[16,2,64,512]{3,2,1,0:T(8,128)(2,1)}), bf16[16,2,64,512]{3,2,1,0:T(8,128)(2,1)S(1)}, u32[]{:S(2)}, u32[]{:S(2)}) %all-to-all-start) | async-done | bytes 2097184 | tf_op jit(solution)/shard_map/all_to_all | solution.py:43
  64.0 4.3 %all-to-all-start.1 = ((bf16[8,128,512]{2,1,0:T(8,128)(2,1)}), bf16[8,128,512]{2,1,0:T(8,128)(2,1)}, u32[]{:S(2)}, u32[]{:S(2)}) async-start(bf16[8,128,512]{2,1,0:T(8,128)(2,1)} %copy-done.3), calls=%async_computation.1 | async-start | bytes 2097152 | tf_op jit(solution)/shard_map/all_to_all | solution.py:43
  70.9 11.0 %collective-permute-done.6 = bf16[2,80,512]{2,1,0:T(8,128)(2,1)S(1)} collective-permute-done((bf16[2,80,512]{2,1,0:T(8,128)(2,1)S(1)}, bf16[2,80,512]{2,1,0:T(8,128)(2,1)S(1)}, u32[]{:S(2)}, u32[]{:S(2)}) %collective-permute-start.6) | collective-permute-done | bytes 163872 | tf_op jit(solution)/shard_map/ppermute | solution.py:48
  82.2 4.1 %all-to-all-done.1 = bf16[8,128,512]{2,1,0:T(8,128)(2,1)} async-done(((bf16[8,128,512]{2,1,0:T(8,128)(2,1)}), bf16[8,128,512]{2,1,0:T(8,128)(2,1)}, u32[]{:S(2)}, u32[]{:S(2)}) %all-to-all-start.1) | async-done | bytes 1048608 | tf_op jit(solution)/shard_map/all_to_all | solution.py:43
  90.4 5.1 %collective-permute-done.7.got_ref = bf16[128,512]{1,0:T(8,128)(2,1)S(1)} collective-permute-done((bf16[128,512]{1,0:T(8,128)(2,1)S(1)}, bf16[128,512]{1,0:T(8,128)(2,1)S(1)}, u32[]{:S(2)}, u32[]{:S(2)}) %collective-permute-start.7) | collective-permute-done | bytes 131104 | tf_op jit(solution)/shard_map/ppermute | solution.py:48
  99.1 4.2 %all-to-all-start.2 = ((bf16[8,144,512]{2,1,0:T(8,128)(2,1)}), bf16[8,144,512]{2,1,0:T(8,128)(2,1)}, u32[]{:S(2)}, u32[]{:S(2)}) async-start(bf16[8,144,512]{2,1,0:T(8,128)(2,1)} %copy-done.2), calls=%async_computation.2 | async-start | bytes 2359296 | tf_op jit(solution)/shard_map/all_to_all | solution.py:43
  103.4 4.7 %collective-permute-start.8 = (f32[256,128]{1,0:T(8,128)}, f32[256,128]{1,0:T(8,128)S(1)}, u32[]{:S(2)}, u32[]{:S(2)}) collective-permute-start(f32[256,128]{1,0:T(8,128)} %add.55), channel_id=1, source_target_pairs={{0,128},{32,160},{64,192},{96,224},{128,0},{160,32},{192,64},{224,... | collective-permute-start | bytes 393224 | tf_op jit(solution)/shard_map/ppermute | solution.py:48
  108.1 7.7 %collective-permute-done.8 = f32[256,128]{1,0:T(8,128)S(1)} collective-permute-done((f32[256,128]{1,0:T(8,128)}, f32[256,128]{1,0:T(8,128)S(1)}, u32[]{:S(2)}, u32[]{:S(2)}) %collective-permute-start.8) | collective-permute-done | bytes 131104 | tf_op jit(solution)/shard_map/ppermute | solution.py:48
  118.4 4.3 %update.1 = (bf16[8,128,512]{2,1,0:T(8,128)(2,1)S(1)}, f32[512,512]{1,0:T(8,128)S(1)}, f32[1,1]{1,0:T(1,128)}) custom-call(bf16[8,144,512]{2,1,0:T(8,128)(2,1)} %all-to-all-done.2.got_ref, bf16[16,2,64,512]{3,2,1,0:T(8,128)(2,1)S(1)} %all-to-all-done.columns_ref, bf16[1,512,512]{2,1,0:T(8,128)(2,1)S(1)} %copy-done, bf16[1,512,512]{2,1,0:T(8,128)(2,1)S(1)} %copy-done.4, ...), custom_call_target="tpu_custom_call" | custom-call | tf_op jit(solution)/shard_map/update/pallas_call | solution.py:268
  124.7 4.9 %all-to-all-start.3 = ((bf16[8,128,512]{2,1,0:T(8,128)(2,1)}), bf16[8,128,512]{2,1,0:T(8,128)(2,1)}, u32[]{:S(2)}, u32[]{:S(2)}) async-start(bf16[8,128,512]{2,1,0:T(8,128)(2,1)} %copy-done.9), calls=%async_computation.3 | async-start | bytes 2097152 | tf_op jit(solution)/shard_map/all_to_all | solution.py:43
  129.6 8.2 %collective-permute-start.9 = (f32[256,128]{1,0:T(8,128)S(1)}, f32[256,128]{1,0:T(8,128)S(1)}, u32[]{:S(2)}, u32[]{:S(2)}) collective-permute-start(f32[256,128]{1,0:T(8,128)S(1)} %add.57), channel_id=1, source_target_pairs={{0,256},{256,0},{1,257},{257,1},{2,258},{258,2},{3,259},{259,3},{4... | collective-permute-start | bytes 393224 | tf_op jit(solution)/shard_map/ppermute | solution.py:48
  137.8 10.7 %collective-permute-done.9 = f32[256,128]{1,0:T(8,128)S(1)} collective-permute-done((f32[256,128]{1,0:T(8,128)S(1)}, f32[256,128]{1,0:T(8,128)S(1)}, u32[]{:S(2)}, u32[]{:S(2)}) %collective-permute-start.9) | collective-permute-done | bytes 131104 | tf_op jit(solution)/shard_map/ppermute | solution.py:48
  153.9 5.4 %collective-permute-done.10.got_ref = bf16[128,512]{1,0:T(8,128)(2,1)} collective-permute-done((bf16[128,512]{1,0:T(8,128)(2,1)}, bf16[128,512]{1,0:T(8,128)(2,1)}, u32[]{:S(2)}, u32[]{:S(2)}) %collective-permute-start.10) | collective-permute-done | bytes 131104 | tf_op jit(solution)/shard_map/ppermute | solution.py:48
  162.3 6.2 %all-to-all-start.4 = ((bf16[8,144,512]{2,1,0:T(8,128)(2,1)}), bf16[8,144,512]{2,1,0:T(8,128)(2,1)}, u32[]{:S(2)}, u32[]{:S(2)}) async-start(bf16[8,144,512]{2,1,0:T(8,128)(2,1)} %copy-done.1), calls=%async_computation.4 | async-start | bytes 2359296 | tf_op jit(solution)/shard_map/all_to_all | solution.py:43
  172.8 8.1 %all-to-all-done.4.got_ref = bf16[8,144,512]{2,1,0:T(8,128)(2,1)} async-done(((bf16[8,144,512]{2,1,0:T(8,128)(2,1)}), bf16[8,144,512]{2,1,0:T(8,128)(2,1)}, u32[]{:S(2)}, u32[]{:S(2)}) %all-to-all-start.4) | async-done | bytes 1179680 | tf_op jit(solution)/shard_map/all_to_all | solution.py:43
  183.1 6.4 %finish.1 = (f32[1,512,512]{2,1,0:T(8,128)}, f32[1,2]{1,0:T(1,128)}) custom-call(bf16[8,144,512]{2,1,0:T(8,128)(2,1)} %all-to-all-done.4.got_ref, bf16[16,2,64,512]{3,2,1,0:T(8,128)(2,1)S(1)} %all-to-all-done.columns_ref, bf16[1,512,512]{2,1,0:T(8,128)(2,1)S(1)} %copy-done, bf16[1,512,512]{2,1,0:T(8,128)(2,1)S(1)} %copy-done.4, ...), custom_call_target="tpu_custom_call" | custom-call | tf_op jit(solution)/shard_map/finish/pallas_call | solution.py:292
  (92 shorter events, 43.1 us)
Async XLA Ops:
  4.0 10.0 %copy-start.17 = (s32[1,2,64]{2,1,0:T(2,128)S(1)}, s32[1,2,64]{2,1,0:T(2,128)}, u32[]{:S(2)}) copy-start(s32[1,2,64]{2,1,0:T(2,128)} %param.11) | copy-start | bytes 1540
  4.1 14.6 %copy-start = (bf16[1,512,512]{2,1,0:T(8,128)(2,1)S(1)}, bf16[1,512,512]{2,1,0:T(8,128)(2,1)}, u32[]{:S(2)}) copy-start(bf16[1,512,512]{2,1,0:T(8,128)(2,1)} %weights_ref.2) | copy-start | bytes 1572868
  4.1 48.1 %copy-start.15 = (bf16[1,2,64,512]{3,2,1,0:T(8,128)(2,1)S(1)}, bf16[1,2,64,512]{3,2,1,0:T(8,128)(2,1)}, u32[]{:S(2)}) copy-start(bf16[1,2,64,512]{3,2,1,0:T(8,128)(2,1)} %param.10) | copy-start | bytes 393220
  4.1 58.1 %all-to-all-start = ((bf16[16,2,64,512]{3,2,1,0:T(8,128)(2,1)}), bf16[16,2,64,512]{3,2,1,0:T(8,128)(2,1)S(1)}, u32[]{:S(2)}, u32[]{:S(2)}) async-start(bf16[16,2,64,512]{3,2,1,0:T(8,128)(2,1)} %normalize.1), calls=%async_computation | async-start | bytes 4194304 | tf_op jit(solution)/shard_map/all_to_all | solution.py:43
  14.2 14.8 %collective-permute-start = (f32[2,8]{1,0:T(2,128)S(1)}, f32[2,8]{1,0:T(2,128)S(1)}, u32[]{:S(2)}, u32[]{:S(2)}) collective-permute-start(f32[2,8]{1,0:T(2,128)S(1)} %convert_reduce_fusion.2), channel_id=1, source_target_pairs={{0,4},{4,0},{8,12},{12,8},{1,5},{5,1},{9,13},{13,9},{2,6},{6,2},{1... | collective-permute-start | bytes 200 | tf_op jit(solution)/shard_map/ppermute | solution.py:48
  18.7 21.3 %collective-permute-start.3 = (bf16[256,128]{1,0:T(8,128)(2,1)S(1)}, bf16[256,128]{1,0:T(8,128)(2,1)S(1)}, u32[]{:S(2)}, u32[]{:S(2)}) collective-permute-start(bf16[256,128]{1,0:T(8,128)(2,1)S(1)} %dynamic-slice_bitcast_fusion), channel_id=1, source_target_pairs={{0,16},{16,0},{1,17},{17,1},{2,18},{18,2},{3,19},{19,3},{4,20},{20... | collective-permute-start | bytes 196616 | tf_op jit(solution)/shard_map/ppermute | solution.py:48
  29.0 7.6 %collective-permute-start.1 = (f32[2,8]{1,0:T(2,128)S(1)}, f32[2,8]{1,0:T(2,128)S(1)}, u32[]{:S(2)}, u32[]{:S(2)}) collective-permute-start(f32[2,8]{1,0:T(2,128)S(1)} %add.47), channel_id=1, source_target_pairs={{0,8},{4,12},{8,0},{12,4},{1,9},{5,13},{9,1},{13,5},{2,10},{6,14},... | collective-permute-start | bytes 200 | tf_op jit(solution)/shard_map/ppermute | solution.py:48
  36.6 11.5 %collective-permute-start.2 = (f32[2,8]{1,0:T(2,128)S(1)}, f32[2,8]{1,0:T(2,128)S(1)}, u32[]{:S(2)}, u32[]{:S(2)}) collective-permute-start(f32[2,8]{1,0:T(2,128)S(1)} %add.48), channel_id=1, source_target_pairs={{0,1},{1,0},{2,3},{3,2},{4,5},{5,4},{6,7},{7,6},{8,9},{9,8},{10,11... | collective-permute-start | bytes 200 | tf_op jit(solution)/shard_map/ppermute | solution.py:48
  40.1 8.0 %collective-permute-start.4 = (f32[256,128]{1,0:T(8,128)S(1)}, f32[256,128]{1,0:T(8,128)S(1)}, u32[]{:S(2)}, u32[]{:S(2)}) collective-permute-start(f32[256,128]{1,0:T(8,128)S(1)} %convert_add_fusion), channel_id=1, source_target_pairs={{0,32},{32,0},{64,96},{96,64},{128,160},{160,128},{192,224},{224,1... | collective-permute-start | bytes 393224 | tf_op jit(solution)/shard_map/ppermute | solution.py:48
  48.1 10.0 %collective-permute-start.5 = (f32[256,128]{1,0:T(8,128)S(1)}, f32[256,128]{1,0:T(8,128)S(1)}, u32[]{:S(2)}, u32[]{:S(2)}) collective-permute-start(f32[256,128]{1,0:T(8,128)S(1)} %add.54), channel_id=1, source_target_pairs={{0,64},{32,96},{64,0},{96,32},{128,192},{160,224},{192,128},{224,1... | collective-permute-start | bytes 393224 | tf_op jit(solution)/shard_map/ppermute | solution.py:48
  64.0 22.3 %all-to-all-start.1 = ((bf16[8,128,512]{2,1,0:T(8,128)(2,1)}), bf16[8,128,512]{2,1,0:T(8,128)(2,1)}, u32[]{:S(2)}, u32[]{:S(2)}) async-start(bf16[8,128,512]{2,1,0:T(8,128)(2,1)} %copy-done.3), calls=%async_computation.1 | async-start | bytes 2097152 | tf_op jit(solution)/shard_map/all_to_all | solution.py:43
  68.2 13.7 %collective-permute-start.6 = (bf16[2,80,512]{2,1,0:T(8,128)(2,1)S(1)}, bf16[2,80,512]{2,1,0:T(8,128)(2,1)S(1)}, u32[]{:S(2)}, u32[]{:S(2)}) collective-permute-start(bf16[2,80,512]{2,1,0:T(8,128)(2,1)S(1)} %maximum_maximum_fusion), channel_id=1, source_target_pairs={{0,2},{2,0},{1,3},{3,1},{4,6},{6,4},{5,7},{7,5},{8,10},{10,8},{9,1... | collective-permute-start | bytes 491528 | tf_op jit(solution)/shard_map/ppermute | solution.py:48
  87.7 7.8 %collective-permute-start.7 = (bf16[128,512]{1,0:T(8,128)(2,1)S(1)}, bf16[128,512]{1,0:T(8,128)(2,1)S(1)}, u32[]{:S(2)}, u32[]{:S(2)}) collective-permute-start(bf16[128,512]{1,0:T(8,128)(2,1)S(1)} %convert_element_type.64), channel_id=1, source_target_pairs={{0,2},{2,0},{1,3},{3,1},{4,6},{6,4},{5,7},{7,5},{8,10},{10,8},{9,1... | collective-permute-start | bytes 393224 | tf_op jit(solution)/shard_map/ppermute | solution.py:48
  97.9 19.5 %copy-start.4 = (bf16[1,512,512]{2,1,0:T(8,128)(2,1)S(1)}, bf16[1,512,512]{2,1,0:T(8,128)(2,1)}, u32[]{:S(2)}) copy-start(bf16[1,512,512]{2,1,0:T(8,128)(2,1)} %first_ref.3) | copy-start | bytes 1572868
  99.1 18.2 %all-to-all-start.2 = ((bf16[8,144,512]{2,1,0:T(8,128)(2,1)}), bf16[8,144,512]{2,1,0:T(8,128)(2,1)}, u32[]{:S(2)}, u32[]{:S(2)}) async-start(bf16[8,144,512]{2,1,0:T(8,128)(2,1)} %copy-done.2), calls=%async_computation.2 | async-start | bytes 2359296 | tf_op jit(solution)/shard_map/all_to_all | solution.py:43
  103.4 12.4 %collective-permute-start.8 = (f32[256,128]{1,0:T(8,128)}, f32[256,128]{1,0:T(8,128)S(1)}, u32[]{:S(2)}, u32[]{:S(2)}) collective-permute-start(f32[256,128]{1,0:T(8,128)} %add.55), channel_id=1, source_target_pairs={{0,128},{32,160},{64,192},{96,224},{128,0},{160,32},{192,64},{224,... | collective-permute-start | bytes 393224 | tf_op jit(solution)/shard_map/ppermute | solution.py:48
  124.7 24.5 %all-to-all-start.3 = ((bf16[8,128,512]{2,1,0:T(8,128)(2,1)}), bf16[8,128,512]{2,1,0:T(8,128)(2,1)}, u32[]{:S(2)}, u32[]{:S(2)}) async-start(bf16[8,128,512]{2,1,0:T(8,128)(2,1)} %copy-done.9), calls=%async_computation.3 | async-start | bytes 2097152 | tf_op jit(solution)/shard_map/all_to_all | solution.py:43
  129.6 18.9 %collective-permute-start.9 = (f32[256,128]{1,0:T(8,128)S(1)}, f32[256,128]{1,0:T(8,128)S(1)}, u32[]{:S(2)}, u32[]{:S(2)}) collective-permute-start(f32[256,128]{1,0:T(8,128)S(1)} %add.57), channel_id=1, source_target_pairs={{0,256},{256,0},{1,257},{257,1},{2,258},{258,2},{3,259},{259,3},{4... | collective-permute-start | bytes 393224 | tf_op jit(solution)/shard_map/ppermute | solution.py:48
  151.2 8.1 %collective-permute-start.10 = (bf16[128,512]{1,0:T(8,128)(2,1)}, bf16[128,512]{1,0:T(8,128)(2,1)}, u32[]{:S(2)}, u32[]{:S(2)}) collective-permute-start(bf16[128,512]{1,0:T(8,128)(2,1)} %convert_element_type.66), channel_id=1, source_target_pairs={{0,2},{2,0},{1,3},{3,1},{4,6},{6,4},{5,7},{7,5},{8,10},{10,8},{9,1... | collective-permute-start | bytes 393224 | tf_op jit(solution)/shard_map/ppermute | solution.py:48
  162.3 6.2 %copy-start.14 = (f32[256,128]{1,0:T(8,128)S(1)}, f32[256,128]{1,0:T(8,128)}, u32[]{:S(2)}) copy-start(f32[256,128]{1,0:T(8,128)} %add.58) | copy-start | bytes 393220
  162.3 9.5 %copy-start.16 = (bf16[512,128]{1,0:T(8,128)(2,1)S(1)}, bf16[512,128]{1,0:T(8,128)(2,1)}, u32[]{:S(2)}) copy-start(bf16[512,128]{1,0:T(8,128)(2,1)} %param.15) | copy-start | bytes 393220
  162.3 18.5 %all-to-all-start.4 = ((bf16[8,144,512]{2,1,0:T(8,128)(2,1)}), bf16[8,144,512]{2,1,0:T(8,128)(2,1)}, u32[]{:S(2)}, u32[]{:S(2)}) async-start(bf16[8,144,512]{2,1,0:T(8,128)(2,1)} %copy-done.1), calls=%async_computation.4 | async-start | bytes 2359296 | tf_op jit(solution)/shard_map/all_to_all | solution.py:43
  168.5 3.2 %collective-permute-start.11 = (f32[256,128]{1,0:T(8,128)S(1)}, f32[256,128]{1,0:T(8,128)S(1)}, u32[]{:S(2)}, u32[]{:S(2)}) collective-permute-start(f32[256,128]{1,0:T(8,128)S(1)} %copy-done.14), channel_id=1, source_target_pairs={{0,16},{16,0},{1,17},{17,1},{2,18},{18,2},{3,19},{19,3},{4,20},{20... | collective-permute-start | bytes 393224 | tf_op jit(solution)/shard_map/ppermute | solution.py:48
  181.9 1.2 copy-start.8
  (11 other events, 10.3 us)

commit v6 on v3

v6 whole, which is shorter than its diff:
```python
import functools

import jax
import jax.numpy as jnp
from jax import lax
from jax.experimental import pallas as pl
from jax.experimental.pallas import tpu as pltpu
from jax.sharding import Mesh, PartitionSpec as P

DOCS = 8


NORM_EPS = 1e-05
ADAM_EPS = 1e-08
INNER_RATE = 0.1
DECAY_RATE = 0.1
BETA_FIRST = 0.9
BETA_SECOND = 0.95
OUTER_RATE = 0.7
NESTEROV = 0.9
MIXING = 0.5

REPLICA = ("zh", "y", "c")
FSDP = ("x", "zf", "zn")
ORDER = ("x", "zn", "zf")
GROUP = ("x", "zn")
EXTRA = 16
CHUNK = 32
VMEM = 60 * 1024 * 1024

bf16, f32 = jnp.bfloat16, jnp.float32


def moments(first, second, gradient):
    first = BETA_FIRST * first + (1.0 - BETA_FIRST) * gradient
    second = BETA_SECOND * second + (1.0 - BETA_SECOND) * gradient * gradient
    return (first, second)


def adam_update(master, first, second, gradient):
    first, second = moments(first, second, gradient)
    master = master - INNER_RATE * (first / (jnp.sqrt(second) + ADAM_EPS) + DECAY_RATE * master)
    return (master, first, second)


def exchange(blocks, axes):
    return lax.all_to_all(blocks, axes, split_axis=0, concat_axis=0, tiled=False)


def swap(block, axis, bit=1):
    size = lax.axis_size(axis)
    return lax.ppermute(block, axis, [(i, i ^ bit) for i in range(size)])


def tie(*values):
    return lax.optimization_barrier(values)


ANYWHERE = pl.BlockSpec(memory_space=pl.ANY)
IN_VMEM = pl.BlockSpec(memory_space=pltpu.MemorySpace.VMEM)
IN_SMEM = pl.BlockSpec(memory_space=pltpu.MemorySpace.SMEM)


def call(kernel, name, in_specs, out_specs, out_shape, scratch):
    return pl.pallas_call(
        kernel,
        in_specs=in_specs,
        out_specs=out_specs,
        out_shape=out_shape,
        scratch_shapes=scratch,
        compiler_params=pltpu.CompilerParams(vmem_limit_bytes=VMEM),
        name=name,
    )


def copies_of(pairs, sems, first=0):
    copies = [
        pltpu.make_async_copy(source, target, sems.at[first + at])
        for at, (source, target) in enumerate(pairs)
    ]
    for copy in copies:
        copy.start()
    return copies


def wait_all(copies):
    for copy in copies:
        copy.wait()


def normalize_kernel(width, hidden_ref, out_ref, held, normed, arrived, sent):
    steps, rows, _ = held.shape
    parts = rows // CHUNK

    def place(at):
        return at // parts, pl.ds(pl.multiple_of((at % parts) * CHUNK, CHUNK), CHUNK)

    def take(at):
        step, here = place(at)
        return pltpu.make_async_copy(hidden_ref.at[0, step, here], held.at[step, here], arrived.at[at])

    def give(at):
        step, here = place(at)
        return pltpu.make_async_copy(
            normed.at[:, step, here], out_ref.at[:, step, here], sent.at[at]
        )

    for at in range(steps * parts):
        take(at).start()

    def chunk(at, carry):
        take(at).wait()
        step, here = place(at)
        wide = held[step, here].astype(f32)
        power = jnp.mean(wide * wide, axis=-1, keepdims=True)
        narrow = (wide * lax.rsqrt(power + NORM_EPS)).astype(bf16)
        for block in range(out_ref.shape[0]):
            x, zn, zf = block // 4, (block // 2) % 2, block % 2
            owner = x * 4 + zf * 2 + zn
            normed[block, step, here] = narrow[:, owner * width : (owner + 1) * width]
        give(at).start()
        return carry

    lax.fori_loop(0, steps * parts, chunk, 0)
    for at in range(steps * parts):
        give(at).wait()


def normalize(hidden, shards):
    _, steps, rows, model_width = hidden.shape
    width = model_width // shards
    parts = steps * rows // CHUNK
    return call(
        functools.partial(normalize_kernel, width),
        "normalize",
        [ANYWHERE],
        ANYWHERE,
        jax.ShapeDtypeStruct((shards, steps, rows, width), bf16),
        [
            pltpu.VMEM((steps, rows, model_width), bf16),
            pltpu.VMEM((shards, steps, rows, width), bf16),
            pltpu.SemaphoreType.DMA((parts,)),
            pltpu.SemaphoreType.DMA((parts,)),
        ],
    )(hidden)


def combine_kernel(got_ref, total_ref, narrow_ref, held, sems):
    copies = copies_of([(got_ref.at[at], held.at[at]) for at in range(held.shape[0])], sems)
    total = None
    for at, copy in enumerate(copies):
        copy.wait()
        term = held[at].astype(f32)
        total = term if total is None else total + term
    total_ref[...] = total
    narrow_ref[...] = total.astype(bf16)


def combine(got):
    return call(
        combine_kernel,
        "combine",
        [ANYWHERE],
        (IN_VMEM, IN_VMEM),
        (jax.ShapeDtypeStruct(got.shape[1:], f32), jax.ShapeDtypeStruct(got.shape[1:], bf16)),
        [pltpu.VMEM(got.shape, bf16), pltpu.SemaphoreType.DMA((got.shape[0],))],
    )(got)


def error_kernel(
    scale, own_ref, got_ref, target_ref, weight_ref, out_ref, own, got, target, weight, made, sems, sent
):
    tokens, columns = target.shape
    wait_all(
        copies_of([(own_ref, own), (got_ref, got), (target_ref, target), (weight_ref, weight)], sems)
    )
    each_weight = weight[:, :1]
    values = (own[...] + got[...].astype(f32)) * scale
    error = values - target[...].astype(f32)
    made[:tokens] = (each_weight * error / columns).astype(bf16)
    each = jnp.sum(error * error, axis=-1, keepdims=True) / columns
    loss = jnp.sum(each_weight * 0.5 * each, axis=0, keepdims=True)
    high = loss.astype(bf16).astype(f32)
    middle = (loss - high).astype(bf16).astype(f32)
    low = loss - high - middle
    lane = lax.broadcasted_iota(jnp.int32, (EXTRA, columns), 1)
    lane = lane + columns * lax.broadcasted_iota(jnp.int32, (EXTRA, columns), 0)
    row = jnp.where(lane == 0, high, jnp.where(lane == 1, middle, jnp.where(lane == 2, low, 0.0)))
    made[tokens:] = row.astype(bf16)
    wait_all(copies_of([(made, out_ref.at[at]) for at in range(out_ref.shape[0])], sent))


def errors(own, got, target, weight, groups, scale):
    tokens, columns = target.shape
    return call(
        functools.partial(error_kernel, scale),
        "errors",
        [ANYWHERE] * 4,
        ANYWHERE,
        jax.ShapeDtypeStruct((groups, tokens + EXTRA, columns), bf16),
        [
            pltpu.VMEM((tokens, columns), f32),
            pltpu.VMEM((tokens, columns), bf16),
            pltpu.VMEM((tokens, columns), bf16),
            pltpu.VMEM(weight.shape, f32),
            pltpu.VMEM((tokens + EXTRA, columns), bf16),
            pltpu.SemaphoreType.DMA((4,)),
            pltpu.SemaphoreType.DMA((groups,)),
        ],
    )(own, got, target, weight)


def step_rows(columns_ref, step, into):
    rows = columns_ref.shape[2]
    return [
        (columns_ref.at[at, step], into.at[pl.ds(at * rows, rows)])
        for at in range(columns_ref.shape[0])
    ]


def token_rows(got_ref, into, extra):
    groups, tokens = got_ref.shape[0], got_ref.shape[1] - EXTRA
    pairs = [
        (got_ref.at[at, pl.ds(0, tokens)], into.at[pl.ds(at * tokens, tokens)])
        for at in range(groups)
    ]
    return pairs + [(got_ref.at[at, pl.ds(tokens, EXTRA)], extra.at[at]) for at in range(groups)]


def loss_of(extra):
    total = jnp.sum(extra[...].astype(f32), axis=0)
    return jnp.sum(jnp.sum(total, axis=0, keepdims=True), axis=1, keepdims=True)


def gradient_of(columns, everyone, scale):
    product = lax.dot_general(
        columns, everyone, (((0,), (0,)), ((), ())), preferred_element_type=f32
    )
    return product * scale


def project_rows(arriving, lhs, current, made, out_ref, sent):
    groups, tokens, _ = made.shape
    leaving, share = [], len(arriving) * 2 // groups
    for at in range(0, groups, 2):
        wait_all(arriving[at // 2 * share : (at // 2 + 1) * share])
        rows = lhs[at * tokens : (at + 2) * tokens]
        product = jnp.dot(rows, current, preferred_element_type=f32).astype(bf16)
        made[at : at + 2] = product.reshape(2, tokens, product.shape[1])
        leaving += copies_of([(made.at[pl.ds(at, 2)], out_ref.at[pl.ds(at, 2)])], sent, at // 2)
    return leaving


def project_kernel(columns_ref, weights_ref, out_ref, lhs, weights, made, sems, sent):
    (state,) = copies_of([(weights_ref.at[0], weights)], sems)
    arriving = copies_of(step_rows(columns_ref, 0, lhs), sems, 1)
    state.wait()
    wait_all(project_rows(arriving, lhs, weights[...], made, out_ref, sent))


def project(columns, weights, groups):
    shards, _, rows, features = columns.shape
    tokens, wide = shards * rows, weights.shape[2]
    return call(
        project_kernel,
        "project",
        [ANYWHERE] * 2,
        ANYWHERE,
        jax.ShapeDtypeStruct((groups, tokens // groups, wide), bf16),
        [
            pltpu.VMEM((tokens, features), bf16),
            pltpu.VMEM((features, wide), bf16),
            pltpu.VMEM((groups, tokens // groups, wide), bf16),
            pltpu.SemaphoreType.DMA((1 + shards,)),
            pltpu.SemaphoreType.DMA((groups // 2,)),
        ],
    )(columns, weights)


def update_kernel(
    scale, got_ref, columns_ref, weights_ref, first_ref, second_ref,
    out_ref, gradient_ref, master_ref, loss_ref,
    everyone, extra, lhs, later, states, gradient, master, current, made, sems, kept, sent,
):
    pairs = token_rows(got_ref, everyone, extra) + step_rows(columns_ref, 0, lhs)
    now = copies_of(pairs, sems)
    sources = (weights_ref, first_ref, second_ref)
    loads = copies_of([(r.at[0], states.at[at]) for at, r in enumerate(sources)], sems, len(now))
    arriving = copies_of(step_rows(columns_ref, 1, later), sems, len(now) + len(loads))
    wait_all(now)
    leaving = []
    half = current.shape[0] // 2
    for at in range(2):
        rows = slice(at * half, (at + 1) * half)
        here = pl.ds(at * half, half)
        slope = gradient_of(lhs[:, rows], everyone[...], scale)
        gradient[rows] = slope
        if at == 0:
            wait_all(loads)
        after = adam_update(*(states[k, rows].astype(f32) for k in range(3)), slope)[0]
        master[rows] = after
        current[rows] = after.astype(bf16)
        pairs = [(gradient.at[here], gradient_ref.at[here]), (master.at[here], master_ref.at[here])]
        leaving += copies_of(pairs, kept, 2 * at)
    leaving += project_rows(arriving, later, current[...], made, out_ref, sent)
    loss_ref[...] = loss_of(extra)
    wait_all(leaving)


def update(got, columns, weights, first, second, scale):
    shards, _, rows, features = columns.shape
    groups, tokens, wide = got.shape[0], shards * rows, weights.shape[2]
    state = jax.ShapeDtypeStruct((features, wide), f32)
    return call(
        functools.partial(update_kernel, scale),
        "update",
        [ANYWHERE] * 5,
        (ANYWHERE, ANYWHERE, ANYWHERE, IN_VMEM),
        (
            jax.ShapeDtypeStruct((groups, tokens // groups, wide), bf16),
            state,
            state,
            jax.ShapeDtypeStruct((1, 1), f32),
        ),
        [
            pltpu.VMEM((tokens, wide), bf16),
            pltpu.VMEM((groups, EXTRA, wide), bf16),
            pltpu.VMEM((tokens, features), bf16),
            pltpu.VMEM((tokens, features), bf16),
            pltpu.VMEM((3, features, wide), bf16),
            pltpu.VMEM((features, wide), f32),
            pltpu.VMEM((features, wide), f32),
            pltpu.VMEM((features, wide), bf16),
            pltpu.VMEM((groups, tokens // groups, wide), bf16),
            pltpu.SemaphoreType.DMA((2 * groups + 2 * shards + 3,)),
            pltpu.SemaphoreType.DMA((4,)),
            pltpu.SemaphoreType.DMA((groups // 2,)),
        ],
    )(got, columns, weights, first, second)


def finish_kernel(
    scale, got_ref, columns_ref, first_ref, second_ref, before_ref, master_ref, outer_ref, start_ref,
    loss_ref, out_ref, losses_ref,
    everyone, extra, lhs, states, before, master, outer, done, sems, sent,
):
    pairs = token_rows(got_ref, everyone, extra) + step_rows(columns_ref, 1, lhs)
    now = copies_of(pairs, sems)
    pairs = [(first_ref.at[0], states.at[0]), (second_ref.at[0], states.at[1])]
    pairs += [(before_ref, before), (master_ref, master), (outer_ref, outer)]
    loads = copies_of(pairs, sems, len(now))
    wait_all(now)
    features, width = done.shape[0], outer.shape[1]
    half = features // 2
    start = pl.ds(pl.multiple_of(start_ref[0], 128), width)
    leaving = []
    for at in range(2):
        rows = slice(at * half, (at + 1) * half)
        here = pl.ds(at * half, half)
        slope = gradient_of(lhs[:, rows], everyone[...], scale)
        if at == 0:
            wait_all(loads)
        first, second = moments(*(states[k, rows].astype(f32) for k in range(2)), before[rows])
        done[rows] = adam_update(master[rows], first, second, slope)[0]
        done[rows, start] = MIXING * done[rows, start] + (1.0 - MIXING) * outer[rows]
        leaving += copies_of([(done.at[here], out_ref.at[0, here])], sent, at)
    lane = lax.broadcasted_iota(jnp.int32, losses_ref.shape, 1)
    losses_ref[...] = jnp.where(lane == 0, loss_ref[...], loss_of(extra))
    wait_all(leaving)


def finish(got, columns, first, second, before, master, outer, start, loss, scale):
    shards, _, rows, features = columns.shape
    groups, tokens, wide = got.shape[0], shards * rows, first.shape[2]
    return call(
        functools.partial(finish_kernel, scale),
        "finish",
        [ANYWHERE] * 7 + [IN_SMEM, IN_VMEM],
        (ANYWHERE, IN_VMEM),
        (
            jax.ShapeDtypeStruct((1, features, wide), f32),
            jax.ShapeDtypeStruct((1, 2), f32),
        ),
        [
            pltpu.VMEM((tokens, wide), bf16),
            pltpu.VMEM((groups, EXTRA, wide), bf16),
            pltpu.VMEM((tokens, features), bf16),
            pltpu.VMEM((2, features, wide), bf16),
            pltpu.VMEM((features, wide), f32),
            pltpu.VMEM((features, wide), f32),
            pltpu.VMEM(outer.shape, f32),
            pltpu.VMEM((features, wide), f32),
            pltpu.SemaphoreType.DMA((2 * groups + shards + 5,)),
            pltpu.SemaphoreType.DMA((2,)),
        ],
    )(got, columns, first, second, before, master, outer, start, loss)


def body(hidden, targets, doc_ids, weights, adam_m, adam_v, anchor, momentum, fragment):
    steps_total, rows, model_width = hidden.shape[1:]
    shard_rows, value_width = weights.shape[1:]
    frag_width = anchor.shape[1]
    nx, nn, nf = (lax.axis_size(a) for a in ORDER)
    shards, groups = nx * nn * nf, nx * nn
    f_at, c_at = lax.axis_index("zf"), lax.axis_index("c")
    scale = model_width ** (-0.5)
    zero = jnp.zeros((), jnp.int32)
    start = fragment[0] * frag_width
    replicas = lax.axis_size(REPLICA)
    tokens = nf * rows

    def pick(array, at, axis):
        return lax.dynamic_index_in_dim(array, at, axis, keepdims=False)

    blocks = normalize(hidden, shards)
    blocks, weights, targets, doc_ids = tie(blocks, weights, targets, doc_ids)
    columns = exchange(blocks, ORDER)

    doc_range = jnp.arange(DOCS, dtype=jnp.int32)
    counts = jnp.sum((doc_ids[0][..., None] == doc_range).astype(f32), axis=1)
    for axis, bit in (("x", 1), ("x", 2), ("zn", 1)):
        counts = counts + swap(counts, axis, bit)

    def extra_row(values):
        values = values.astype(bf16)
        return jnp.pad(values, ((0, 0), (0, value_width - values.shape[1])))[:, None]

    every_count = jnp.broadcast_to(counts.reshape(1, -1), (steps_total, counts.size))
    extra = [extra_row(doc_ids[0]), extra_row(every_count)]
    extra.append(jnp.zeros((steps_total, EXTRA - len(extra), value_width), bf16))
    own_rows = jnp.concatenate([targets[0], *extra], axis=1)

    half = shard_rows // 2
    local = lax.dynamic_slice(weights[0], (zero, start), (shard_rows, frag_width))
    local = local.reshape(2, half, frag_width)
    summed = pick(local, c_at, 0).astype(f32) + swap(pick(local, c_at ^ 1, 0), "c").astype(f32)
    summed = summed + swap(summed, "zh")
    columns, own_rows, counts, summed = tie(columns, own_rows, counts, summed)

    def of_pair(own, far):
        first, last = jnp.where(f_at == 0, own, far), jnp.where(f_at == 0, far, own)
        return jnp.concatenate([first[:rows], last[:rows]]), (first[rows], last[rows])

    def weights_of(ids, inverse):
        hot = (jnp.concatenate([i[:rows] for i in ids])[:, None].astype(jnp.int32) == doc_range)
        weight = jnp.sum(hot.astype(f32) * inverse[None, :], axis=-1, keepdims=True)
        return jnp.broadcast_to(weight, (tokens, 128))

    partial = exchange(project(columns, weights, groups), GROUP)
    far_rows = swap(own_rows[0], "zf")
    summed = summed + swap(summed, "y", 1)
    far_counts = far_rows[rows + 1, : steps_total * DOCS].astype(f32)
    inverse = 1.0 / (DOCS * (counts + far_counts.reshape(counts.shape)))
    target, ids = of_pair(own_rows[0], far_rows)
    weight = weights_of(ids, inverse[0])
    partial, target, weight, summed, inverse = tie(partial, target, weight, summed, inverse)

    def share_errors(partial, target, weight):
        own, narrow = combine(partial)
        return errors(own, swap(narrow, "zf"), target, weight, groups, scale)

    sent, summed, own_rows, inverse = tie(
        share_errors(partial, target, weight), summed, own_rows, inverse
    )
    got = exchange(sent, GROUP)
    target, ids = of_pair(own_rows[1], swap(own_rows[1], "zf"))
    weight = weights_of(ids, inverse[1])
    summed = summed + swap(summed, "y", 2)
    got, summed, target, weight = tie(got, summed, target, weight)
    partial, gradient, master, loss = update(got, columns, weights, adam_m, adam_v, scale)
    partial, summed = tie(partial, summed)
    partial = exchange(partial, GROUP)
    summed = summed + swap(summed, "y", 4)
    partial, summed = tie(partial, summed)
    sent, summed = tie(share_errors(partial, target, weight), summed)
    got = exchange(sent, GROUP)
    other = swap(summed, "c")
    anchor_rows = anchor.astype(f32)
    summed = jnp.concatenate(
        [jnp.where(c_at == 0, summed, other), jnp.where(c_at == 0, other, summed)], axis=0
    )
    mean_delta = anchor_rows - summed / replicas
    new_moment = NESTEROV * momentum.astype(f32) + mean_delta
    global_fragment = anchor_rows - OUTER_RATE * (mean_delta + NESTEROV * new_moment)
    got, global_fragment = tie(got, global_fragment)
    return finish(
        got, columns, adam_m, adam_v, gradient, master, global_fragment, start.reshape(1), loss, scale
    )


def solution(mesh):
    fine = Mesh(mesh.devices.reshape(2, 8, 2, 4, 2, 2), REPLICA + FSDP)
    placed = (
        P(REPLICA, None, FSDP, None),
        P(REPLICA, None, FSDP, None),
        P(REPLICA, None, FSDP),
        P(REPLICA, FSDP, None),
        P(REPLICA, FSDP, None),
        P(REPLICA, FSDP, None),
        P(FSDP, None),
        P(FSDP, None),
        P(),
    )
    return jax.shard_map(
        body,
        mesh=fine,
        in_specs=placed,
        out_specs=(P(REPLICA, FSDP, None), P(REPLICA, None)),
        check_vma=False,
    )
```

time: 204 us -> 191 us (0.936)
  Pallas kernels: 6.49 us -> 28.6 us
  blocking collectives: 14.5 us -> 0 us
  starting transfers between devices: 79.6 us -> 73.3 us
  matrix products: 5.92 us -> 0 us
  waiting for transfers between devices: 80.6 us -> 75.4 us
  other arithmetic: 6.57 us -> 2.82 us
    pallas_call x3 -> x8, Pallas kernels: 6.49 us -> 28.6 us  [the longest x1 6.77 us: finish(): call(functools.partial(finish_kernel, scale), 'finish', [ANYWHERE] * 7 +...]
    all_to_all x1 -> x0, blocking collectives: 14.5 us -> none  [exchange(): lax.all_to_all(blocks, axes, split_axis=0, concat_axis=0, tiled=False)]
    ppermute x13, starting transfers between devices: 57.2 us -> 47.1 us  [swap(): return lax.ppermute(block, axis, [(i, i ^ bit) for i in range(size)])]
    ppermute x13, waiting for transfers between devices: 60.3 us -> 52.1 us  [swap(): return lax.ppermute(block, axis, [(i, i ^ bit) for i in range(size)])]
    dot_general x4 -> x0, matrix products: 5.92 us -> none  [the longest x2 3.06 us: body(): partial = jnp.dot(rows_now, current, preferred_element_type=f32)]
    all_to_all x4 -> x5, starting transfers between devices: 22.5 us -> 26.1 us  [exchange(): lax.all_to_all(blocks, axes, split_axis=0, concat_axis=0, tiled=False)]
    all_to_all x4 -> x5, waiting for transfers between devices: 20.3 us -> 23.2 us  [exchange(): lax.all_to_all(blocks, axes, split_axis=0, concat_axis=0, tiled=False)]
    unnamed x40 -> x22, local copies, waits for them, and re-layouts: 5.51 us -> 5.09 us
  transfers between devices with their start and end apart: 17 -> 18, of which waited for: 12 -> 15; matrix products, arithmetic and copies ran while one was open for 3% -> 2% of each run, Pallas kernels for 0% -> 0%
where the time goes in v6:
time: 191 us; the launch traced here: 190 us
  waiting for transfers between devices  75.4 us (39%)
  starting transfers between devices  73.3 us (38%)
  Pallas kernels  28.6 us (15%)
  local copies, waits for them, and re-layouts  8 us (4%)
  other arithmetic  2.82 us (1%)
    ppermute x13, waiting for transfers between devices, swap(): return lax.ppermute(block, axis, [(i, i ^ bit) for i in range(size)])  52.1 us
    ppermute x13, starting transfers between devices, swap(): return lax.ppermute(block, axis, [(i, i ^ bit) for i in range(size)])  47.1 us
    all_to_all x5, starting transfers between devices, exchange(): lax.all_to_all(blocks, axes, split_axis=0, concat_axis=0, tiled=False)  26.1 us
    all_to_all x5, waiting for transfers between devices, exchange(): lax.all_to_all(blocks, axes, split_axis=0, concat_axis=0, tiled=False)  23.2 us
    pallas_call x1, Pallas kernels, finish(): call(functools.partial(finish_kernel, scale), 'finish', [ANYWHERE] * 7 +...  6.77 us
    pallas_call x1, Pallas kernels, update(): call(functools.partial(update_kernel, scale), 'update', [ANYWHERE] * 5, (...  6.66 us
    unnamed x22, local copies, waits for them, and re-layouts  5.09 us
    pallas_call x2, Pallas kernels, errors(): call(functools.partial(error_kernel, scale), 'errors', [ANYWHERE] * 4, AN...  4.84 us
  transfers between devices with their start and end apart: 18, of which 15 were waited for; matrix products, arithmetic and copies ran while one was open for 2% of the time, Pallas kernels for 0%

profile of v6, /device:TPU:56, one launch (start us, length us, event | category | flops | bytes accessed | tf_op | source)
XLA Modules:
  0.0 189.8 jit_solution(7412686895825446292)
XLA Ops:
  3.6 10.0 %all-to-all-start = ((bf16[16,2,64,512]{3,2,1,0:T(8,128)(2,1)}), bf16[16,2,64,512]{3,2,1,0:T(8,128)(2,1)S(1)}, u32[]{:S(2)}, u32[]{:S(2)}) async-start(bf16[16,2,64,512]{3,2,1,0:T(8,128)(2,1)} %normalize.1), calls=%async_computation | async-start | bytes 4194304 | tf_op jit(solution)/shard_map/all_to_all | solution.py:47
  13.7 3.8 %collective-permute-start = (f32[2,8]{1,0:T(2,128)S(1)}, f32[2,8]{1,0:T(2,128)S(1)}, u32[]{:S(2)}, u32[]{:S(2)}) collective-permute-start(f32[2,8]{1,0:T(2,128)S(1)} %convert_reduce_fusion), channel_id=1, source_target_pairs={{0,4},{4,0},{8,12},{12,8},{1,5},{5,1},{9,13},{13,9},{2,6},{6,2},{1... | collective-permute-start | bytes 200 | tf_op jit(solution)/shard_map/ppermute | solution.py:52
  21.1 7.4 %collective-permute-done = f32[2,8]{1,0:T(2,128)S(1)} collective-permute-done((f32[2,8]{1,0:T(2,128)S(1)}, f32[2,8]{1,0:T(2,128)S(1)}, u32[]{:S(2)}, u32[]{:S(2)}) %collective-permute-start) | collective-permute-done | bytes 96 | tf_op jit(solution)/shard_map/ppermute | solution.py:52
  28.5 6.0 %collective-permute-start.1 = (f32[2,8]{1,0:T(2,128)S(1)}, f32[2,8]{1,0:T(2,128)S(1)}, u32[]{:S(2)}, u32[]{:S(2)}) collective-permute-start(f32[2,8]{1,0:T(2,128)S(1)} %add.47), channel_id=1, source_target_pairs={{0,8},{4,12},{8,0},{12,4},{1,9},{5,13},{9,1},{13,5},{2,10},{6,14},... | collective-permute-start | bytes 200 | tf_op jit(solution)/shard_map/ppermute | solution.py:52
  36.1 3.4 %collective-permute-start.2 = (f32[2,8]{1,0:T(2,128)S(1)}, f32[2,8]{1,0:T(2,128)S(1)}, u32[]{:S(2)}, u32[]{:S(2)}) collective-permute-start(f32[2,8]{1,0:T(2,128)S(1)} %add.48), channel_id=1, source_target_pairs={{0,1},{1,0},{2,3},{3,2},{4,5},{5,4},{6,7},{7,6},{8,9},{9,8},{10,11... | collective-permute-start | bytes 200 | tf_op jit(solution)/shard_map/ppermute | solution.py:52
  39.6 7.9 %collective-permute-done.2 = f32[2,8]{1,0:T(2,128)S(1)} collective-permute-done((f32[2,8]{1,0:T(2,128)S(1)}, f32[2,8]{1,0:T(2,128)S(1)}, u32[]{:S(2)}, u32[]{:S(2)}) %collective-permute-start.2) | collective-permute-done | bytes 96 | tf_op jit(solution)/shard_map/ppermute | solution.py:52
  47.7 8.2 %collective-permute-start.4 = (f32[256,128]{1,0:T(8,128)S(1)}, f32[256,128]{1,0:T(8,128)S(1)}, u32[]{:S(2)}, u32[]{:S(2)}) collective-permute-start(f32[256,128]{1,0:T(8,128)S(1)} %convert_add_fusion), channel_id=1, source_target_pairs={{0,256},{256,0},{1,257},{257,1},{2,258},{258,2},{3,259},{259,3},{4... | collective-permute-start | bytes 393224 | tf_op jit(solution)/shard_map/ppermute | solution.py:52
  58.9 8.3 %all-to-all-done.columns_ref = bf16[16,2,64,512]{3,2,1,0:T(8,128)(2,1)S(1)} async-done(((bf16[16,2,64,512]{3,2,1,0:T(8,128)(2,1)}), bf16[16,2,64,512]{3,2,1,0:T(8,128)(2,1)S(1)}, u32[]{:S(2)}, u32[]{:S(2)}) %all-to-all-start) | async-done | bytes 2097184 | tf_op jit(solution)/shard_map/all_to_all | solution.py:47
  71.8 4.3 %all-to-all-start.1 = ((bf16[8,128,512]{2,1,0:T(8,128)(2,1)}), bf16[8,128,512]{2,1,0:T(8,128)(2,1)S(1)}, u32[]{:S(2)}, u32[]{:S(2)}) async-start(bf16[8,128,512]{2,1,0:T(8,128)(2,1)} %project.1), calls=%async_computation.1 | async-start | bytes 2097152 | tf_op jit(solution)/shard_map/all_to_all | solution.py:47
  81.9 5.9 %collective-permute-done.5 = bf16[80,512]{1,0:T(8,128)(2,1)S(1)} collective-permute-done((bf16[80,512]{1,0:T(8,128)(2,1)S(1)}, bf16[80,512]{1,0:T(8,128)(2,1)S(1)}, u32[]{:S(2)}, u32[]{:S(2)}) %collective-permute-start.5) | collective-permute-done | bytes 81952 | tf_op jit(solution)/shard_map/ppermute | solution.py:52
  88.8 3.3 %all-to-all-done.1.got_ref = bf16[8,128,512]{2,1,0:T(8,128)(2,1)S(1)} async-done(((bf16[8,128,512]{2,1,0:T(8,128)(2,1)}), bf16[8,128,512]{2,1,0:T(8,128)(2,1)S(1)}, u32[]{:S(2)}, u32[]{:S(2)}) %all-to-all-start.1) | async-done | bytes 1048608 | tf_op jit(solution)/shard_map/all_to_all | solution.py:47
  97.2 6.5 %collective-permute-done.7.got_ref = bf16[128,512]{1,0:T(8,128)(2,1)S(1)} collective-permute-done((bf16[128,512]{1,0:T(8,128)(2,1)}, bf16[128,512]{1,0:T(8,128)(2,1)S(1)}, u32[]{:S(2)}, u32[]{:S(2)}) %collective-permute-start.7) | collective-permute-done | bytes 131104 | tf_op jit(solution)/shard_map/ppermute | solution.py:52
  106.8 3.6 %all-to-all-start.2 = ((bf16[8,144,512]{2,1,0:T(8,128)(2,1)}), bf16[8,144,512]{2,1,0:T(8,128)(2,1)S(1)}, u32[]{:S(2)}, u32[]{:S(2)}) async-start(bf16[8,144,512]{2,1,0:T(8,128)(2,1)} %errors.2), calls=%async_computation.2 | async-start | bytes 2359296 | tf_op jit(solution)/shard_map/all_to_all | solution.py:47
  112.9 4.0 %collective-permute-start.8 = (f32[256,128]{1,0:T(8,128)S(1)}, f32[256,128]{1,0:T(8,128)S(1)}, u32[]{:S(2)}, u32[]{:S(2)}) collective-permute-start(f32[256,128]{1,0:T(8,128)S(1)} %add.56), channel_id=1, source_target_pairs={{0,64},{32,96},{64,0},{96,32},{128,192},{160,224},{192,128},{224,1... | collective-permute-start | bytes 393224 | tf_op jit(solution)/shard_map/ppermute | solution.py:52
  116.9 4.6 %collective-permute-done.9 = bf16[80,512]{1,0:T(8,128)(2,1)S(1)} collective-permute-done((bf16[80,512]{1,0:T(8,128)(2,1)S(1)}, bf16[80,512]{1,0:T(8,128)(2,1)S(1)}, u32[]{:S(2)}, u32[]{:S(2)}) %collective-permute-start.9) | collective-permute-done | bytes 81952 | tf_op jit(solution)/shard_map/ppermute | solution.py:52
  122.4 3.3 %all-to-all-done.2.got_ref = bf16[8,144,512]{2,1,0:T(8,128)(2,1)S(1)} async-done(((bf16[8,144,512]{2,1,0:T(8,128)(2,1)}), bf16[8,144,512]{2,1,0:T(8,128)(2,1)S(1)}, u32[]{:S(2)}, u32[]{:S(2)}) %all-to-all-start.2) | async-done | bytes 1179680 | tf_op jit(solution)/shard_map/all_to_all | solution.py:47
  126.8 6.7 %update.1 = (bf16[8,128,512]{2,1,0:T(8,128)(2,1)}, f32[512,512]{1,0:T(8,128)}, f32[512,512]{1,0:T(8,128)}, f32[1,1]{1,0:T(1,128)}) custom-call(bf16[8,144,512]{2,1,0:T(8,128)(2,1)} %copy-done.1, bf16[16,2,64,512]{3,2,1,0:T(8,128)(2,1)} %copy-done, bf16[1,512,512]{2,1,0:T(8,128)(2,1)} %weights_ref.1, bf16[1,512,512]{2,1,0:T(8,128)(2,1)} %first_ref.3, ...), custom_call_target="tpu_custom_call" | custom-call | tf_op jit(solution)/shard_map/update/pallas_call | solution.py:314
  133.5 3.6 %all-to-all-start.3 = ((bf16[8,128,512]{2,1,0:T(8,128)(2,1)}), bf16[8,128,512]{2,1,0:T(8,128)(2,1)S(1)}, u32[]{:S(2)}, u32[]{:S(2)}) async-start(bf16[8,128,512]{2,1,0:T(8,128)(2,1)} %get-tuple-element.61), calls=%async_computation.3 | async-start | bytes 2097152 | tf_op jit(solution)/shard_map/all_to_all | solution.py:47
  137.1 4.7 %collective-permute-start.10 = (f32[256,128]{1,0:T(8,128)S(1)}, f32[256,128]{1,0:T(8,128)S(1)}, u32[]{:S(2)}, u32[]{:S(2)}) collective-permute-start(f32[256,128]{1,0:T(8,128)S(1)} %add.57), channel_id=1, source_target_pairs={{0,128},{32,160},{64,192},{96,224},{128,0},{160,32},{192,64},{224,... | collective-permute-start | bytes 393224 | tf_op jit(solution)/shard_map/ppermute | solution.py:52
  141.8 7.5 %collective-permute-done.10 = f32[256,128]{1,0:T(8,128)S(1)} collective-permute-done((f32[256,128]{1,0:T(8,128)S(1)}, f32[256,128]{1,0:T(8,128)S(1)}, u32[]{:S(2)}, u32[]{:S(2)}) %collective-permute-start.10) | collective-permute-done | bytes 131104 | tf_op jit(solution)/shard_map/ppermute | solution.py:52
  155.3 6.6 %collective-permute-done.11.got_ref = bf16[128,512]{1,0:T(8,128)(2,1)S(1)} collective-permute-done((bf16[128,512]{1,0:T(8,128)(2,1)}, bf16[128,512]{1,0:T(8,128)(2,1)S(1)}, u32[]{:S(2)}, u32[]{:S(2)}) %collective-permute-start.11) | collective-permute-done | bytes 131104 | tf_op jit(solution)/shard_map/ppermute | solution.py:52
  165.0 4.8 %all-to-all-start.4 = ((bf16[8,144,512]{2,1,0:T(8,128)(2,1)}), bf16[8,144,512]{2,1,0:T(8,128)(2,1)S(1)}, u32[]{:S(2)}, u32[]{:S(2)}) async-start(bf16[8,144,512]{2,1,0:T(8,128)(2,1)} %errors.3), calls=%async_computation.4 | async-start | bytes 2359296 | tf_op jit(solution)/shard_map/all_to_all | solution.py:47
  173.8 8.2 %all-to-all-done.4.got_ref = bf16[8,144,512]{2,1,0:T(8,128)(2,1)S(1)} async-done(((bf16[8,144,512]{2,1,0:T(8,128)(2,1)}), bf16[8,144,512]{2,1,0:T(8,128)(2,1)S(1)}, u32[]{:S(2)}, u32[]{:S(2)}) %all-to-all-start.4) | async-done | bytes 1179680 | tf_op jit(solution)/shard_map/all_to_all | solution.py:47
  183.0 6.8 %finish.1 = (f32[1,512,512]{2,1,0:T(8,128)}, f32[1,2]{1,0:T(1,128)}) custom-call(bf16[8,144,512]{2,1,0:T(8,128)(2,1)} %copy-done.2, bf16[16,2,64,512]{3,2,1,0:T(8,128)(2,1)} %copy-done, bf16[1,512,512]{2,1,0:T(8,128)(2,1)} %first_ref.3, bf16[1,512,512]{2,1,0:T(8,128)(2,1)} %second_ref.3, f32[512,512]{1,0:T(8,128)} %get-tuple-element.72.before_ref, ...), custom_call_target="tpu_custom_call" | custom-call | tf_op jit(solution)/shard_map/finish/pallas_call | solution.py:375
  (88 shorter events, 48.8 us)
Async XLA Ops:
  3.6 10.0 %copy-start.10 = (s32[1,2,64]{2,1,0:T(2,128)S(1)}, s32[1,2,64]{2,1,0:T(2,128)}, u32[]{:S(2)}) copy-start(s32[1,2,64]{2,1,0:T(2,128)} %param.11) | copy-start | bytes 1540
  3.6 52.3 %copy-start.7 = (bf16[1,2,64,512]{3,2,1,0:T(8,128)(2,1)S(1)}, bf16[1,2,64,512]{3,2,1,0:T(8,128)(2,1)}, u32[]{:S(2)}) copy-start(bf16[1,2,64,512]{3,2,1,0:T(8,128)(2,1)} %param.10) | copy-start | bytes 393220
  3.6 63.7 %all-to-all-start = ((bf16[16,2,64,512]{3,2,1,0:T(8,128)(2,1)}), bf16[16,2,64,512]{3,2,1,0:T(8,128)(2,1)S(1)}, u32[]{:S(2)}, u32[]{:S(2)}) async-start(bf16[16,2,64,512]{3,2,1,0:T(8,128)(2,1)} %normalize.1), calls=%async_computation | async-start | bytes 4194304 | tf_op jit(solution)/shard_map/all_to_all | solution.py:47
  13.7 14.8 %collective-permute-start = (f32[2,8]{1,0:T(2,128)S(1)}, f32[2,8]{1,0:T(2,128)S(1)}, u32[]{:S(2)}, u32[]{:S(2)}) collective-permute-start(f32[2,8]{1,0:T(2,128)S(1)} %convert_reduce_fusion), channel_id=1, source_target_pairs={{0,4},{4,0},{8,12},{12,8},{1,5},{5,1},{9,13},{13,9},{2,6},{6,2},{1... | collective-permute-start | bytes 200 | tf_op jit(solution)/shard_map/ppermute | solution.py:52
  19.1 28.5 %collective-permute-start.3 = (bf16[256,128]{1,0:T(8,128)(2,1)S(1)}, bf16[256,128]{1,0:T(8,128)(2,1)S(1)}, u32[]{:S(2)}, u32[]{:S(2)}) collective-permute-start(bf16[256,128]{1,0:T(8,128)(2,1)S(1)} %dynamic-slice_bitcast_fusion), channel_id=1, source_target_pairs={{0,16},{16,0},{1,17},{17,1},{2,18},{18,2},{3,19},{19,3},{4,20},{20... | collective-permute-start | bytes 196616 | tf_op jit(solution)/shard_map/ppermute | solution.py:52
  28.5 7.6 %collective-permute-start.1 = (f32[2,8]{1,0:T(2,128)S(1)}, f32[2,8]{1,0:T(2,128)S(1)}, u32[]{:S(2)}, u32[]{:S(2)}) collective-permute-start(f32[2,8]{1,0:T(2,128)S(1)} %add.47), channel_id=1, source_target_pairs={{0,8},{4,12},{8,0},{12,4},{1,9},{5,13},{9,1},{13,5},{2,10},{6,14},... | collective-permute-start | bytes 200 | tf_op jit(solution)/shard_map/ppermute | solution.py:52
  36.1 11.5 %collective-permute-start.2 = (f32[2,8]{1,0:T(2,128)S(1)}, f32[2,8]{1,0:T(2,128)S(1)}, u32[]{:S(2)}, u32[]{:S(2)}) collective-permute-start(f32[2,8]{1,0:T(2,128)S(1)} %add.48), channel_id=1, source_target_pairs={{0,1},{1,0},{2,3},{3,2},{4,5},{5,4},{6,7},{7,6},{8,9},{9,8},{10,11... | collective-permute-start | bytes 200 | tf_op jit(solution)/shard_map/ppermute | solution.py:52
  47.7 11.3 %collective-permute-start.4 = (f32[256,128]{1,0:T(8,128)S(1)}, f32[256,128]{1,0:T(8,128)S(1)}, u32[]{:S(2)}, u32[]{:S(2)}) collective-permute-start(f32[256,128]{1,0:T(8,128)S(1)} %convert_add_fusion), channel_id=1, source_target_pairs={{0,256},{256,0},{1,257},{257,1},{2,258},{258,2},{3,259},{259,3},{4... | collective-permute-start | bytes 393224 | tf_op jit(solution)/shard_map/ppermute | solution.py:52
  67.3 1.4 copy-start
  71.8 20.3 %all-to-all-start.1 = ((bf16[8,128,512]{2,1,0:T(8,128)(2,1)}), bf16[8,128,512]{2,1,0:T(8,128)(2,1)S(1)}, u32[]{:S(2)}, u32[]{:S(2)}) async-start(bf16[8,128,512]{2,1,0:T(8,128)(2,1)} %project.1), calls=%async_computation.1 | async-start | bytes 2097152 | tf_op jit(solution)/shard_map/all_to_all | solution.py:47
  76.1 11.7 %collective-permute-start.5 = (bf16[80,512]{1,0:T(8,128)(2,1)S(1)}, bf16[80,512]{1,0:T(8,128)(2,1)S(1)}, u32[]{:S(2)}, u32[]{:S(2)}) collective-permute-start(bf16[80,512]{1,0:T(8,128)(2,1)S(1)} %slice_bitcast_fusion.1), channel_id=1, source_target_pairs={{0,2},{2,0},{1,3},{3,1},{4,6},{6,4},{5,7},{7,5},{8,10},{10,8},{9,1... | collective-permute-start | bytes 245768 | tf_op jit(solution)/shard_map/ppermute | solution.py:52
  78.6 10.2 %collective-permute-start.6 = (f32[256,128]{1,0:T(8,128)S(1)}, f32[256,128]{1,0:T(8,128)S(1)}, u32[]{:S(2)}, u32[]{:S(2)}) collective-permute-start(f32[256,128]{1,0:T(8,128)S(1)} %add.54), channel_id=1, source_target_pairs={{0,32},{32,0},{64,96},{96,64},{128,160},{160,128},{192,224},{224,1... | collective-permute-start | bytes 393224 | tf_op jit(solution)/shard_map/ppermute | solution.py:52
  95.2 8.5 %collective-permute-start.7 = (bf16[128,512]{1,0:T(8,128)(2,1)}, bf16[128,512]{1,0:T(8,128)(2,1)S(1)}, u32[]{:S(2)}, u32[]{:S(2)}) collective-permute-start(bf16[128,512]{1,0:T(8,128)(2,1)} %get-tuple-element.49), channel_id=1, source_target_pairs={{0,2},{2,0},{1,3},{3,1},{4,6},{6,4},{5,7},{7,5},{8,10},{10,8},{9,1... | collective-permute-start | bytes 393224 | tf_op jit(solution)/shard_map/ppermute | solution.py:52
  106.8 19.0 %all-to-all-start.2 = ((bf16[8,144,512]{2,1,0:T(8,128)(2,1)}), bf16[8,144,512]{2,1,0:T(8,128)(2,1)S(1)}, u32[]{:S(2)}, u32[]{:S(2)}) async-start(bf16[8,144,512]{2,1,0:T(8,128)(2,1)} %errors.2), calls=%async_computation.2 | async-start | bytes 2359296 | tf_op jit(solution)/shard_map/all_to_all | solution.py:47
  110.4 11.1 %collective-permute-start.9 = (bf16[80,512]{1,0:T(8,128)(2,1)S(1)}, bf16[80,512]{1,0:T(8,128)(2,1)S(1)}, u32[]{:S(2)}, u32[]{:S(2)}) collective-permute-start(bf16[80,512]{1,0:T(8,128)(2,1)S(1)} %slice_bitcast_fusion), channel_id=1, source_target_pairs={{0,2},{2,0},{1,3},{3,1},{4,6},{6,4},{5,7},{7,5},{8,10},{10,8},{9,1... | collective-permute-start | bytes 245768 | tf_op jit(solution)/shard_map/ppermute | solution.py:52
  112.9 9.6 %collective-permute-start.8 = (f32[256,128]{1,0:T(8,128)S(1)}, f32[256,128]{1,0:T(8,128)S(1)}, u32[]{:S(2)}, u32[]{:S(2)}) collective-permute-start(f32[256,128]{1,0:T(8,128)S(1)} %add.56), channel_id=1, source_target_pairs={{0,64},{32,96},{64,0},{96,32},{128,192},{160,224},{192,128},{224,1... | collective-permute-start | bytes 393224 | tf_op jit(solution)/shard_map/ppermute | solution.py:52
  125.8 1.1 copy-start.1
  133.5 15.9 %all-to-all-start.3 = ((bf16[8,128,512]{2,1,0:T(8,128)(2,1)}), bf16[8,128,512]{2,1,0:T(8,128)(2,1)S(1)}, u32[]{:S(2)}, u32[]{:S(2)}) async-start(bf16[8,128,512]{2,1,0:T(8,128)(2,1)} %get-tuple-element.61), calls=%async_computation.3 | async-start | bytes 2097152 | tf_op jit(solution)/shard_map/all_to_all | solution.py:47
  137.1 12.2 %collective-permute-start.10 = (f32[256,128]{1,0:T(8,128)S(1)}, f32[256,128]{1,0:T(8,128)S(1)}, u32[]{:S(2)}, u32[]{:S(2)}) collective-permute-start(f32[256,128]{1,0:T(8,128)S(1)} %add.57), channel_id=1, source_target_pairs={{0,128},{32,160},{64,192},{96,224},{128,0},{160,32},{192,64},{224,... | collective-permute-start | bytes 393224 | tf_op jit(solution)/shard_map/ppermute | solution.py:52
  152.5 9.4 %collective-permute-start.11 = (bf16[128,512]{1,0:T(8,128)(2,1)}, bf16[128,512]{1,0:T(8,128)(2,1)S(1)}, u32[]{:S(2)}, u32[]{:S(2)}) collective-permute-start(bf16[128,512]{1,0:T(8,128)(2,1)} %get-tuple-element.65), channel_id=1, source_target_pairs={{0,2},{2,0},{1,3},{3,1},{4,6},{6,4},{5,7},{7,5},{8,10},{10,8},{9,1... | collective-permute-start | bytes 393224 | tf_op jit(solution)/shard_map/ppermute | solution.py:52
  164.9 8.0 %copy-start.8 = (bf16[512,128]{1,0:T(8,128)(2,1)S(1)}, bf16[512,128]{1,0:T(8,128)(2,1)}, u32[]{:S(2)}) copy-start(bf16[512,128]{1,0:T(8,128)(2,1)} %param.15) | copy-start | bytes 393220
  165.0 8.0 %copy-start.9 = (bf16[512,128]{1,0:T(8,128)(2,1)S(1)}, bf16[512,128]{1,0:T(8,128)(2,1)}, u32[]{:S(2)}) copy-start(bf16[512,128]{1,0:T(8,128)(2,1)} %param.16) | copy-start | bytes 393220
  165.0 17.0 %all-to-all-start.4 = ((bf16[8,144,512]{2,1,0:T(8,128)(2,1)}), bf16[8,144,512]{2,1,0:T(8,128)(2,1)S(1)}, u32[]{:S(2)}, u32[]{:S(2)}) async-start(bf16[8,144,512]{2,1,0:T(8,128)(2,1)} %errors.3), calls=%async_computation.4 | async-start | bytes 2359296 | tf_op jit(solution)/shard_map/all_to_all | solution.py:47
  169.7 3.2 %collective-permute-start.12 = (f32[256,128]{1,0:T(8,128)S(1)}, f32[256,128]{1,0:T(8,128)S(1)}, u32[]{:S(2)}, u32[]{:S(2)}) collective-permute-start(f32[256,128]{1,0:T(8,128)S(1)} %add.58), channel_id=1, source_target_pairs={{0,16},{16,0},{1,17},{17,1},{2,18},{18,2},{3,19},{19,3},{4,20},{20... | collective-permute-start | bytes 393224 | tf_op jit(solution)/shard_map/ppermute | solution.py:52
  (5 other events, 4.3 us)

commit v7 on v3

--- a/solution.py
+++ b/solution.py
@@ -25,8 +25,9 @@
 ORDER = ("x", "zn", "zf")
 GROUP = ("x", "zn")
 EXTRA = 16
-CHUNK = 16
+CHUNK = 32
 VMEM = 48 * 1024 * 1024
+ALL_VMEM = 60 * 1024 * 1024
 
 bf16, f32 = jnp.bfloat16, jnp.float32
 
@@ -51,38 +52,68 @@
     return lax.optimization_barrier(values)
 
 
-def normalize_kernel(width, hidden_ref, out_ref):
-    wide = hidden_ref[0, 0].astype(f32)
-    power = jnp.mean(wide * wide, axis=-1, keepdims=True)
-    normed = (wide * lax.rsqrt(power + NORM_EPS)).astype(bf16)
-    for at in range(out_ref.shape[0]):
-        x, zn, zf = at // 4, (at // 2) % 2, at % 2
-        owner = x * 4 + zf * 2 + zn
-        out_ref[at, 0] = normed[:, owner * width : (owner + 1) * width]
+def normalize_kernel(width, hidden_ref, out_ref, held, normed, arrived, sent):
+    steps, rows, _ = held.shape
+    parts = rows // CHUNK
+
+    def place(at):
+        return at // parts, pl.ds(pl.multiple_of((at % parts) * CHUNK, CHUNK), CHUNK)
+
+    def take(at):
+        step, here = place(at)
+        return pltpu.make_async_copy(hidden_ref.at[0, step, here], held.at[step, here], arrived.at[at])
+
+    def give(at):
+        step, here = place(at)
+        return pltpu.make_async_copy(
+            normed.at[:, step, here], out_ref.at[:, step, here], sent.at[at]
+        )
+
+    for at in range(steps * parts):
+        take(at).start()
+
+    def chunk(at, carry):
+        take(at).wait()
+        step, here = place(at)
+        wide = held[step, here].astype(f32)
+        power = jnp.mean(wide * wide, axis=-1, keepdims=True)
+        narrow = (wide * lax.rsqrt(power + NORM_EPS)).astype(bf16)
+        for block in range(out_ref.shape[0]):
+            x, zn, zf = block // 4, (block // 2) % 2, block % 2
+            owner = x * 4 + zf * 2 + zn
+            normed[block, step, here] = narrow[:, owner * width : (owner + 1) * width]
+        give(at).start()
+        return carry
+
+    lax.fori_loop(0, steps * parts, chunk, 0)
+    for at in range(steps * parts):
+        give(at).wait()
 
 
 def normalize(hidden, shards):
     _, steps, rows, model_width = hidden.shape
     width = model_width // shards
+    parts = steps * rows // CHUNK
     return pl.pallas_call(
         functools.partial(normalize_kernel, width),
-        grid=(steps, rows // CHUNK),
-        in_specs=[pl.BlockSpec((1, 1, CHUNK, model_width), lambda s, i: (0, s, i, 0))],
-        out_specs=pl.BlockSpec((shards, 1, CHUNK, width), lambda s, i: (0, s, i, 0)),
+        in_specs=[pl.BlockSpec(memory_space=pl.ANY)],
+        out_specs=pl.BlockSpec(memory_space=pl.ANY),
         out_shape=jax.ShapeDtypeStruct((shards, steps, rows, width), bf16),
-        compiler_params=pltpu.CompilerParams(vmem_limit_bytes=VMEM),
-        cost_estimate=pl.CostEstimate(
-            flops=8 * rows * model_width, bytes_accessed=8 * rows * model_width, transcendentals=rows
-        ),
+        scratch_shapes=[
+            pltpu.VMEM((steps, rows, model_width), bf16),
+            pltpu.VMEM((shards, steps, rows, width), bf16),
+            pltpu.SemaphoreType.DMA((parts,)),
+            pltpu.SemaphoreType.DMA((parts,)),
+        ],
+        compiler_params=pltpu.CompilerParams(vmem_limit_bytes=ALL_VMEM),
         name="normalize",
     )(hidden)
 
 
-def error_kernel(scale, own_ref, got_ref, target_ref, weight_ref, out_ref):
-    tokens, columns = target_ref.shape
+def error_kernel(scale, own_ref, got_ref, weight_ref, out_ref):
+    tokens, columns = own_ref.shape
     weight = weight_ref[...]
-    values = (own_ref[...] + got_ref[...].astype(f32)) * scale
-    error = values - target_ref[...].astype(f32)
+    error = (own_ref[...] + got_ref[...].astype(f32)) * scale
     grad = (weight * error / columns).astype(bf16)
     each = jnp.sum(error * error, axis=-1, keepdims=True) / columns
     loss = jnp.sum(weight * 0.5 * each, axis=0, keepdims=True)
@@ -90,6 +121,7 @@
     middle = (loss - high).astype(bf16).astype(f32)
     low = loss - high - middle
     lane = lax.broadcasted_iota(jnp.int32, (EXTRA, columns), 1)
+    lane = lane + columns * lax.broadcasted_iota(jnp.int32, (EXTRA, columns), 0)
     row = jnp.where(lane == 0, high, jnp.where(lane == 1, middle, jnp.where(lane == 2, low, 0.0)))
     row = row.astype(bf16)
     for at in range(out_ref.shape[0]):
@@ -97,8 +129,8 @@
         out_ref[at, tokens:] = row
 
 
-def errors(own, got, target, weight, copies, scale):
-    tokens, columns = target.shape
+def errors(own, got, weight, copies, scale):
+    tokens, columns = own.shape
     return pl.pallas_call(
         functools.partial(error_kernel, scale),
         out_shape=jax.ShapeDtypeStruct((copies, tokens + EXTRA, columns), bf16),
@@ -107,7 +139,7 @@
             flops=8 * tokens * columns, bytes_accessed=30 * tokens * columns, transcendentals=0
         ),
         name="errors",
-    )(own, got, target, weight)
+    )(own, got, weight)
 
 
 def body(hidden, targets, doc_ids, weights, adam_m, adam_v, anchor, momentum, fragment):
@@ -130,57 +162,55 @@
     blocks, weights, targets, doc_ids = tie(blocks, weights, targets, doc_ids)
     columns = exchange(blocks, ORDER)
 
-    id_rows = jnp.pad(
-        doc_ids[0].astype(bf16)[:, None, :],
-        ((0, 0), (0, EXTRA - 1), (0, value_width - rows)),
-    )
-    own_rows = jnp.concatenate([targets[0], id_rows], axis=1)
-    far_rows = swap(own_rows, "zf")
-    pair = jnp.stack(
-        [jnp.where(f_at == 0, own_rows, far_rows), jnp.where(f_at == 0, far_rows, own_rows)], axis=1
-    )
-    pair_targets = pair[:, :, :rows].reshape(steps_total, tokens, value_width)
-    pair_ids = pair[:, :, rows, :rows].reshape(steps_total, tokens, 1).astype(jnp.int32)
     doc_range = jnp.arange(DOCS, dtype=jnp.int32)
     counts = jnp.sum((doc_ids[0][..., None] == doc_range).astype(f32), axis=1)
-    for axis, bit in (("x", 1), ("x", 2), ("zn", 1), ("zf", 1)):
+    for axis, bit in (("x", 1), ("x", 2), ("zn", 1)):
         counts = counts + swap(counts, axis, bit)
-    inverse = 1.0 / (DOCS * counts)
-    hot = (pair_ids == doc_range).astype(f32)
+    own_row = jnp.concatenate([doc_ids[0].astype(f32), counts], axis=1)
+    own_row = jnp.pad(own_row, ((0, 0), (0, 128 - own_row.shape[1])))
+    far_row = swap(own_row, "zf")
+    pair = [jnp.where(f_at == 0, own_row, far_row), jnp.where(f_at == 0, far_row, own_row)]
+    pair_ids = jnp.concatenate([row[:, :rows] for row in pair], axis=1).astype(jnp.int32)
+    inverse = 1.0 / (DOCS * (counts + far_row[:, rows : rows + DOCS]))
+    hot = (pair_ids[..., None] == doc_range).astype(f32)
     token_weight = jnp.sum(hot * inverse[:, None, :], axis=-1, keepdims=True)
+
+    goal = targets[0].astype(f32) / scale
+    goal = jnp.concatenate([jnp.where(f_at == at, goal, 0.0) for at in range(nf)], axis=1)
 
     half = shard_rows // 2
     local = lax.dynamic_slice(weights[0], (zero, start), (shard_rows, frag_width))
     local = local.reshape(2, half, frag_width)
     summed = pick(local, c_at, 0).astype(f32) + swap(pick(local, c_at ^ 1, 0), "c").astype(f32)
-    for bit in (1, 2, 4):
-        summed = summed + swap(summed, "y", bit)
-
-    columns, pair_targets, token_weight, summed = tie(columns, pair_targets, token_weight, summed)
+    summed = summed + swap(summed, "y", 1)
+
+    columns, goal, token_weight, summed = tie(columns, goal, token_weight, summed)
 
     master = weights[0].astype(f32)
     first = adam_m[0].astype(f32)
     second = adam_v[0].astype(f32)
-    losses = []
+    loss_rows = []
     for step in range(steps_total):
         current = master.astype(bf16)
         rows_now = columns[:, step].reshape(shards * rows, shard_rows)
         partial = jnp.dot(rows_now, current, preferred_element_type=f32)
         partial = partial.astype(bf16).reshape(groups, tokens, value_width)
+        partial, summed = tie(partial, summed)
         partial = exchange(partial, GROUP)
-        if step == 0:
-            summed = summed + swap(summed, "zh")
-            partial, summed = tie(partial, summed)
-        own = jnp.sum(partial.astype(f32), axis=0)
+        summed = summed + (swap(summed, "y", 2) if step == 0 else swap(summed, "zh"))
+        partial, summed = tie(partial, summed)
+        own = jnp.sum(partial.astype(f32), axis=0) - goal[step]
         got = swap(own.astype(bf16), "zf")
-        sent = errors(own, got, pair_targets[step], token_weight[step], groups, scale)
-        if step == 0:
-            sent, summed = tie(sent, summed)
+        sent = errors(own, got, token_weight[step], groups, scale)
+        sent, summed = tie(sent, summed)
         got = exchange(sent, GROUP)
         if step == 0:
+            summed = summed + swap(summed, "y", 4)
+            got, summed = tie(got, summed)
+        else:
             other = swap(summed, "c")
             got, summed, other = tie(got, summed, other)
-        losses.append(jnp.sum(got[:, tokens, :3].astype(f32)))
+        loss_rows.append(got[:, tokens, :128])
         everyone = got[:, :tokens].reshape(shards * rows, value_width)
         gradient = (
             lax.dot_general(
@@ -202,7 +232,8 @@
         + (1.0 - MIXING) * global_fragment
     )
     master = lax.dynamic_update_slice(master, merged, (zero, start))
-    return (master[None], jnp.stack(losses)[None])
+    losses = jnp.sum(jnp.stack(loss_rows).astype(f32), axis=(1, 2))
+    return (master[None], losses[None])
 
 
 def solution(mesh):

time: 204 us -> 180 us (0.88)
  blocking collectives: 14.5 us -> 0 us
  other arithmetic: 6.57 us -> 1.7 us
  waiting for transfers between devices: 80.6 us -> 78.1 us
  matrix products: 5.92 us -> 8.09 us
    all_to_all x1 -> x0, blocking collectives: 14.5 us -> none  [exchange(): lax.all_to_all(blocks, axes, split_axis=0, concat_axis=0, tiled=False)]
    ppermute x13 -> x12, starting transfers between devices: 57.2 us -> 49.5 us  [swap(): return lax.ppermute(block, axis, [(i, i ^ bit) for i in range(size)])]
    all_to_all x4 -> x5, waiting for transfers between devices: 20.3 us -> 13.9 us  [exchange(): lax.all_to_all(blocks, axes, split_axis=0, concat_axis=0, tiled=False)]
    all_to_all x4 -> x5, starting transfers between devices: 22.5 us -> 28.9 us  [exchange(): lax.all_to_all(blocks, axes, split_axis=0, concat_axis=0, tiled=False)]
    ppermute x13 -> x12, waiting for transfers between devices: 60.3 us -> 64.2 us  [swap(): return lax.ppermute(block, axis, [(i, i ^ bit) for i in range(size)])]
    unnamed x40 -> x36, local copies, waits for them, and re-layouts: 5.51 us -> 4.28 us
  transfers between devices with their start and end apart: 17 -> 17, of which waited for: 12 -> 14; matrix products, arithmetic and copies ran while one was open for 3% -> 0% of each run, Pallas kernels for 0% -> 0%
where the time goes in v7:
time: 180 us; the launch traced here: 179 us
  starting transfers between devices  78.3 us (44%)
  waiting for transfers between devices  78.1 us (43%)
  matrix products  8.09 us (4%)
  local copies, waits for them, and re-layouts  5.9 us (3%)
  Pallas kernels  5.43 us (3%)
    ppermute x12, waiting for transfers between devices, swap(): return lax.ppermute(block, axis, [(i, i ^ bit) for i in range(size)])  64.2 us
    ppermute x12, starting transfers between devices, swap(): return lax.ppermute(block, axis, [(i, i ^ bit) for i in range(size)])  49.5 us
    all_to_all x5, starting transfers between devices, exchange(): lax.all_to_all(blocks, axes, split_axis=0, concat_axis=0, tiled=False)  28.9 us
    all_to_all x5, waiting for transfers between devices, exchange(): lax.all_to_all(blocks, axes, split_axis=0, concat_axis=0, tiled=False)  13.9 us
    unnamed x36, local copies, waits for them, and re-layouts  4.28 us
    dot_general x2, matrix products, body(): lax.dot_general(rows_now, everyone, (((0,), (0,)), ((), ())), preferred_e...  4.08 us
    dot_general x2, matrix products, body(): partial = jnp.dot(rows_now, current, preferred_element_type=f32)  4.01 us
  transfers between devices with their start and end apart: 17, of which 14 were waited for; matrix products, arithmetic and copies ran while one was open for 0% of the time, Pallas kernels for 0%

profile of v7, /device:TPU:56, one launch (start us, length us, event | category | flops | bytes accessed | tf_op | source)
XLA Modules:
  0.0 179.3 jit_solution(17402411379285618777)
XLA Ops:
  3.6 10.0 %all-to-all-start = ((bf16[16,2,64,512]{3,2,1,0:T(8,128)(2,1)}), bf16[16,2,64,512]{3,2,1,0:T(8,128)(2,1)S(1)}, u32[]{:S(2)}, u32[]{:S(2)}) async-start(bf16[16,2,64,512]{3,2,1,0:T(8,128)(2,1)} %normalize.1), calls=%async_computation | async-start | bytes 4194304 | tf_op jit(solution)/shard_map/all_to_all | solution.py:43
  13.7 3.8 %collective-permute-start = (f32[2,8]{1,0:T(2,128)S(1)}, f32[2,8]{1,0:T(2,128)S(1)}, u32[]{:S(2)}, u32[]{:S(2)}) collective-permute-start(f32[2,8]{1,0:T(2,128)S(1)} %convert_reduce_fusion.3), channel_id=1, source_target_pairs={{0,4},{4,0},{8,12},{12,8},{1,5},{5,1},{9,13},{13,9},{2,6},{6,2},{1... | collective-permute-start | bytes 200 | tf_op jit(solution)/shard_map/ppermute | solution.py:48
  20.2 8.3 %collective-permute-done = f32[2,8]{1,0:T(2,128)S(1)} collective-permute-done((f32[2,8]{1,0:T(2,128)S(1)}, f32[2,8]{1,0:T(2,128)S(1)}, u32[]{:S(2)}, u32[]{:S(2)}) %collective-permute-start) | collective-permute-done | bytes 96 | tf_op jit(solution)/shard_map/ppermute | solution.py:48
  28.5 6.0 %collective-permute-start.1 = (f32[2,8]{1,0:T(2,128)S(1)}, f32[2,8]{1,0:T(2,128)S(1)}, u32[]{:S(2)}, u32[]{:S(2)}) collective-permute-start(f32[2,8]{1,0:T(2,128)S(1)} %add.75), channel_id=1, source_target_pairs={{0,8},{4,12},{8,0},{12,4},{1,9},{5,13},{9,1},{13,5},{2,10},{6,14},... | collective-permute-start | bytes 200 | tf_op jit(solution)/shard_map/ppermute | solution.py:48
  36.1 3.4 %collective-permute-start.2 = (f32[2,8]{1,0:T(2,128)S(1)}, f32[2,8]{1,0:T(2,128)S(1)}, u32[]{:S(2)}, u32[]{:S(2)}) collective-permute-start(f32[2,8]{1,0:T(2,128)S(1)} %add.76), channel_id=1, source_target_pairs={{0,1},{1,0},{2,3},{3,2},{4,5},{5,4},{6,7},{7,6},{8,9},{9,8},{10,11... | collective-permute-start | bytes 200 | tf_op jit(solution)/shard_map/ppermute | solution.py:48
  39.6 8.0 %collective-permute-done.2 = f32[2,8]{1,0:T(2,128)S(1)} collective-permute-done((f32[2,8]{1,0:T(2,128)S(1)}, f32[2,8]{1,0:T(2,128)S(1)}, u32[]{:S(2)}, u32[]{:S(2)}) %collective-permute-start.2) | collective-permute-done | bytes 96 | tf_op jit(solution)/shard_map/ppermute | solution.py:48
  47.6 6.5 %collective-permute-start.3 = (f32[2,128]{1,0:T(2,128)S(1)}, f32[2,128]{1,0:T(2,128)S(1)}, u32[]{:S(2)}, u32[]{:S(2)}) collective-permute-start(f32[2,128]{1,0:T(2,128)S(1)} %select_maximum_fusion), channel_id=1, source_target_pairs={{0,2},{2,0},{1,3},{3,1},{4,6},{6,4},{5,7},{7,5},{8,10},{10,8},{9,1... | collective-permute-start | bytes 3080 | tf_op jit(solution)/shard_map/ppermute | solution.py:48
  54.2 7.5 %collective-permute-done.3 = f32[2,128]{1,0:T(2,128)S(1)} collective-permute-done((f32[2,128]{1,0:T(2,128)S(1)}, f32[2,128]{1,0:T(2,128)S(1)}, u32[]{:S(2)}, u32[]{:S(2)}) %collective-permute-start.3) | collective-permute-done | bytes 1056 | tf_op jit(solution)/shard_map/ppermute | solution.py:48
  65.3 3.4 %collective-permute-done.5 = f32[256,128]{1,0:T(8,128)S(1)} collective-permute-done((f32[256,128]{1,0:T(8,128)S(1)}, f32[256,128]{1,0:T(8,128)S(1)}, u32[]{:S(2)}, u32[]{:S(2)}) %collective-permute-start.5) | collective-permute-done | bytes 131104 | tf_op jit(solution)/shard_map/ppermute | solution.py:48
  72.6 4.2 %all-to-all-start.1 = ((bf16[8,128,512]{2,1,0:T(8,128)(2,1)}), bf16[8,128,512]{2,1,0:T(8,128)(2,1)S(1)}, u32[]{:S(2)}, u32[]{:S(2)}) async-start(bf16[8,128,512]{2,1,0:T(8,128)(2,1)} %bitcast.11), calls=%async_computation.1 | async-start | bytes 2097152 | tf_op jit(solution)/shard_map/all_to_all | solution.py:43
  76.8 4.0 %collective-permute-start.6 = (f32[256,128]{1,0:T(8,128)S(1)}, f32[256,128]{1,0:T(8,128)S(1)}, u32[]{:S(2)}, u32[]{:S(2)}) collective-permute-start(f32[256,128]{1,0:T(8,128)S(1)} %add.83), channel_id=1, source_target_pairs={{0,64},{32,96},{64,0},{96,32},{128,192},{160,224},{192,128},{224,1... | collective-permute-start | bytes 393224 | tf_op jit(solution)/shard_map/ppermute | solution.py:48
  80.9 5.1 %collective-permute-done.6 = f32[256,128]{1,0:T(8,128)S(1)} collective-permute-done((f32[256,128]{1,0:T(8,128)S(1)}, f32[256,128]{1,0:T(8,128)S(1)}, u32[]{:S(2)}, u32[]{:S(2)}) %collective-permute-start.6) | collective-permute-done | bytes 131104 | tf_op jit(solution)/shard_map/ppermute | solution.py:48
  86.0 4.0 %all-to-all-done.1 = bf16[8,128,512]{2,1,0:T(8,128)(2,1)S(1)} async-done(((bf16[8,128,512]{2,1,0:T(8,128)(2,1)}), bf16[8,128,512]{2,1,0:T(8,128)(2,1)S(1)}, u32[]{:S(2)}, u32[]{:S(2)}) %all-to-all-start.1) | async-done | bytes 1048608 | tf_op jit(solution)/shard_map/all_to_all | solution.py:43
  90.2 3.7 %collective-permute-start.7 = (bf16[128,512]{1,0:T(8,128)(2,1)S(1)}, bf16[128,512]{1,0:T(8,128)(2,1)S(1)}, u32[]{:S(2)}, u32[]{:S(2)}) collective-permute-start(bf16[128,512]{1,0:T(8,128)(2,1)S(1)} %get-tuple-element.54), channel_id=1, source_target_pairs={{0,2},{2,0},{1,3},{3,1},{4,6},{6,4},{5,7},{7,5},{8,10},{10,8},{9,1... | collective-permute-start | bytes 393224 | tf_op jit(solution)/shard_map/ppermute | solution.py:48
  94.0 5.3 %collective-permute-done.7.got_ref = bf16[128,512]{1,0:T(8,128)(2,1)S(1)} collective-permute-done((bf16[128,512]{1,0:T(8,128)(2,1)S(1)}, bf16[128,512]{1,0:T(8,128)(2,1)S(1)}, u32[]{:S(2)}, u32[]{:S(2)}) %collective-permute-start.7) | collective-permute-done | bytes 131104 | tf_op jit(solution)/shard_map/ppermute | solution.py:48
  100.6 3.7 %all-to-all-start.2 = ((bf16[8,144,512]{2,1,0:T(8,128)(2,1)}), bf16[8,144,512]{2,1,0:T(8,128)(2,1)S(1)}, u32[]{:S(2)}, u32[]{:S(2)}) async-start(bf16[8,144,512]{2,1,0:T(8,128)(2,1)} %errors.2), calls=%async_computation.2 | async-start | bytes 2359296 | tf_op jit(solution)/shard_map/all_to_all | solution.py:43
  104.3 4.7 %collective-permute-start.8 = (f32[256,128]{1,0:T(8,128)S(1)}, f32[256,128]{1,0:T(8,128)S(1)}, u32[]{:S(2)}, u32[]{:S(2)}) collective-permute-start(f32[256,128]{1,0:T(8,128)S(1)} %add.84), channel_id=1, source_target_pairs={{0,128},{32,160},{64,192},{96,224},{128,0},{160,32},{192,64},{224,... | collective-permute-start | bytes 393224 | tf_op jit(solution)/shard_map/ppermute | solution.py:48
  109.0 7.5 %collective-permute-done.8 = f32[256,128]{1,0:T(8,128)S(1)} collective-permute-done((f32[256,128]{1,0:T(8,128)S(1)}, f32[256,128]{1,0:T(8,128)S(1)}, u32[]{:S(2)}, u32[]{:S(2)}) %collective-permute-start.8) | collective-permute-done | bytes 131104 | tf_op jit(solution)/shard_map/ppermute | solution.py:48
  121.5 4.7 %all-to-all-start.3 = ((bf16[8,128,512]{2,1,0:T(8,128)(2,1)}), bf16[8,128,512]{2,1,0:T(8,128)(2,1)S(1)}, u32[]{:S(2)}, u32[]{:S(2)}) async-start(bf16[8,128,512]{2,1,0:T(8,128)(2,1)} %bitcast.80), calls=%async_computation.3 | async-start | bytes 2097152 | tf_op jit(solution)/shard_map/all_to_all | solution.py:43
  126.2 8.2 %collective-permute-start.9 = (f32[256,128]{1,0:T(8,128)S(1)}, f32[256,128]{1,0:T(8,128)S(1)}, u32[]{:S(2)}, u32[]{:S(2)}) collective-permute-start(f32[256,128]{1,0:T(8,128)S(1)} %add.85), channel_id=1, source_target_pairs={{0,256},{256,0},{1,257},{257,1},{2,258},{258,2},{3,259},{259,3},{4... | collective-permute-start | bytes 393224 | tf_op jit(solution)/shard_map/ppermute | solution.py:48
  134.4 10.5 %collective-permute-done.9 = f32[256,128]{1,0:T(8,128)S(1)} collective-permute-done((f32[256,128]{1,0:T(8,128)S(1)}, f32[256,128]{1,0:T(8,128)S(1)}, u32[]{:S(2)}, u32[]{:S(2)}) %collective-permute-start.9) | collective-permute-done | bytes 131104 | tf_op jit(solution)/shard_map/ppermute | solution.py:48
  147.2 5.8 %collective-permute-done.10.got_ref = bf16[128,512]{1,0:T(8,128)(2,1)S(1)} collective-permute-done((bf16[128,512]{1,0:T(8,128)(2,1)S(1)}, bf16[128,512]{1,0:T(8,128)(2,1)S(1)}, u32[]{:S(2)}, u32[]{:S(2)}) %collective-permute-start.10) | collective-permute-done | bytes 131104 | tf_op jit(solution)/shard_map/ppermute | solution.py:48
  154.2 6.2 %all-to-all-start.4 = ((bf16[8,144,512]{2,1,0:T(8,128)(2,1)}), bf16[8,144,512]{2,1,0:T(8,128)(2,1)S(1)}, u32[]{:S(2)}, u32[]{:S(2)}) async-start(bf16[8,144,512]{2,1,0:T(8,128)(2,1)} %errors.3), calls=%async_computation.4 | async-start | bytes 2359296 | tf_op jit(solution)/shard_map/all_to_all | solution.py:43
  163.7 9.0 %all-to-all-done.4 = bf16[8,144,512]{2,1,0:T(8,128)(2,1)S(1)} async-done(((bf16[8,144,512]{2,1,0:T(8,128)(2,1)}), bf16[8,144,512]{2,1,0:T(8,128)(2,1)S(1)}, u32[]{:S(2)}, u32[]{:S(2)}) %all-to-all-start.4) | async-done | bytes 1179680 | tf_op jit(solution)/shard_map/all_to_all | solution.py:43
  (87 shorter events, 33.8 us)
Async XLA Ops:
  3.6 10.0 %copy-start.10 = (s32[1,2,64]{2,1,0:T(2,128)S(1)}, s32[1,2,64]{2,1,0:T(2,128)}, u32[]{:S(2)}) copy-start(s32[1,2,64]{2,1,0:T(2,128)} %param.11) | copy-start | bytes 1540
  3.6 14.6 %copy-start.7 = (bf16[1,512,512]{2,1,0:T(8,128)(2,1)S(1)}, bf16[1,512,512]{2,1,0:T(8,128)(2,1)}, u32[]{:S(2)}) copy-start(bf16[1,512,512]{2,1,0:T(8,128)(2,1)} %param.12) | copy-start | bytes 1572868
  3.6 30.9 %copy-start.4 = (bf16[1,2,64,512]{3,2,1,0:T(8,128)(2,1)S(1)}, bf16[1,2,64,512]{3,2,1,0:T(8,128)(2,1)}, u32[]{:S(2)}) copy-start(bf16[1,2,64,512]{3,2,1,0:T(8,128)(2,1)} %param.10) | copy-start | bytes 393220
  3.6 65.1 %all-to-all-start = ((bf16[16,2,64,512]{3,2,1,0:T(8,128)(2,1)}), bf16[16,2,64,512]{3,2,1,0:T(8,128)(2,1)S(1)}, u32[]{:S(2)}, u32[]{:S(2)}) async-start(bf16[16,2,64,512]{3,2,1,0:T(8,128)(2,1)} %normalize.1), calls=%async_computation | async-start | bytes 4194304 | tf_op jit(solution)/shard_map/all_to_all | solution.py:43
  13.7 14.8 %collective-permute-start = (f32[2,8]{1,0:T(2,128)S(1)}, f32[2,8]{1,0:T(2,128)S(1)}, u32[]{:S(2)}, u32[]{:S(2)}) collective-permute-start(f32[2,8]{1,0:T(2,128)S(1)} %convert_reduce_fusion.3), channel_id=1, source_target_pairs={{0,4},{4,0},{8,12},{12,8},{1,5},{5,1},{9,13},{13,9},{2,6},{6,2},{1... | collective-permute-start | bytes 200 | tf_op jit(solution)/shard_map/ppermute | solution.py:48
  18.2 43.6 %collective-permute-start.4 = (bf16[256,128]{1,0:T(8,128)(2,1)S(1)}, bf16[256,128]{1,0:T(8,128)(2,1)S(1)}, u32[]{:S(2)}, u32[]{:S(2)}) collective-permute-start(bf16[256,128]{1,0:T(8,128)(2,1)S(1)} %dynamic-slice_bitcast_fusion), channel_id=1, source_target_pairs={{0,16},{16,0},{1,17},{17,1},{2,18},{18,2},{3,19},{19,3},{4,20},{20... | collective-permute-start | bytes 196616 | tf_op jit(solution)/shard_map/ppermute | solution.py:48
  28.5 7.6 %collective-permute-start.1 = (f32[2,8]{1,0:T(2,128)S(1)}, f32[2,8]{1,0:T(2,128)S(1)}, u32[]{:S(2)}, u32[]{:S(2)}) collective-permute-start(f32[2,8]{1,0:T(2,128)S(1)} %add.75), channel_id=1, source_target_pairs={{0,8},{4,12},{8,0},{12,4},{1,9},{5,13},{9,1},{13,5},{2,10},{6,14},... | collective-permute-start | bytes 200 | tf_op jit(solution)/shard_map/ppermute | solution.py:48
  36.1 11.5 %collective-permute-start.2 = (f32[2,8]{1,0:T(2,128)S(1)}, f32[2,8]{1,0:T(2,128)S(1)}, u32[]{:S(2)}, u32[]{:S(2)}) collective-permute-start(f32[2,8]{1,0:T(2,128)S(1)} %add.76), channel_id=1, source_target_pairs={{0,1},{1,0},{2,3},{3,2},{4,5},{5,4},{6,7},{7,6},{8,9},{9,8},{10,11... | collective-permute-start | bytes 200 | tf_op jit(solution)/shard_map/ppermute | solution.py:48
  47.6 14.1 %collective-permute-start.3 = (f32[2,128]{1,0:T(2,128)S(1)}, f32[2,128]{1,0:T(2,128)S(1)}, u32[]{:S(2)}, u32[]{:S(2)}) collective-permute-start(f32[2,128]{1,0:T(2,128)S(1)} %select_maximum_fusion), channel_id=1, source_target_pairs={{0,2},{2,0},{1,3},{3,1},{4,6},{6,4},{5,7},{7,5},{8,10},{10,8},{9,1... | collective-permute-start | bytes 3080 | tf_op jit(solution)/shard_map/ppermute | solution.py:48
  61.9 6.9 %collective-permute-start.5 = (f32[256,128]{1,0:T(8,128)S(1)}, f32[256,128]{1,0:T(8,128)S(1)}, u32[]{:S(2)}, u32[]{:S(2)}) collective-permute-start(f32[256,128]{1,0:T(8,128)S(1)} %convert_add_fusion), channel_id=1, source_target_pairs={{0,32},{32,0},{64,96},{96,64},{128,160},{160,128},{192,224},{224,1... | collective-permute-start | bytes 393224 | tf_op jit(solution)/shard_map/ppermute | solution.py:48
  72.6 17.4 %all-to-all-start.1 = ((bf16[8,128,512]{2,1,0:T(8,128)(2,1)}), bf16[8,128,512]{2,1,0:T(8,128)(2,1)S(1)}, u32[]{:S(2)}, u32[]{:S(2)}) async-start(bf16[8,128,512]{2,1,0:T(8,128)(2,1)} %bitcast.11), calls=%async_computation.1 | async-start | bytes 2097152 | tf_op jit(solution)/shard_map/all_to_all | solution.py:43
  76.8 9.2 %collective-permute-start.6 = (f32[256,128]{1,0:T(8,128)S(1)}, f32[256,128]{1,0:T(8,128)S(1)}, u32[]{:S(2)}, u32[]{:S(2)}) collective-permute-start(f32[256,128]{1,0:T(8,128)S(1)} %add.83), channel_id=1, source_target_pairs={{0,64},{32,96},{64,0},{96,32},{128,192},{160,224},{192,128},{224,1... | collective-permute-start | bytes 393224 | tf_op jit(solution)/shard_map/ppermute | solution.py:48
  90.2 9.2 %collective-permute-start.7 = (bf16[128,512]{1,0:T(8,128)(2,1)S(1)}, bf16[128,512]{1,0:T(8,128)(2,1)S(1)}, u32[]{:S(2)}, u32[]{:S(2)}) collective-permute-start(bf16[128,512]{1,0:T(8,128)(2,1)S(1)} %get-tuple-element.54), channel_id=1, source_target_pairs={{0,2},{2,0},{1,3},{3,1},{4,6},{6,4},{5,7},{7,5},{8,10},{10,8},{9,1... | collective-permute-start | bytes 393224 | tf_op jit(solution)/shard_map/ppermute | solution.py:48
  100.6 16.9 %copy-start.3 = (bf16[16,1,64,512]{3,2,1,0:T(8,128)(2,1)S(1)}, bf16[16,1,64,512]{3,2,1,0:T(8,128)(2,1)}, u32[]{:S(2)}) copy-start(bf16[16,1,64,512]{3,2,1,0:T(8,128)(2,1)} %copy-done.2) | copy-start | bytes 3145732
  100.6 16.8 %all-to-all-start.2 = ((bf16[8,144,512]{2,1,0:T(8,128)(2,1)}), bf16[8,144,512]{2,1,0:T(8,128)(2,1)S(1)}, u32[]{:S(2)}, u32[]{:S(2)}) async-start(bf16[8,144,512]{2,1,0:T(8,128)(2,1)} %errors.2), calls=%async_computation.2 | async-start | bytes 2359296 | tf_op jit(solution)/shard_map/all_to_all | solution.py:43
  104.3 12.2 %collective-permute-start.8 = (f32[256,128]{1,0:T(8,128)S(1)}, f32[256,128]{1,0:T(8,128)S(1)}, u32[]{:S(2)}, u32[]{:S(2)}) collective-permute-start(f32[256,128]{1,0:T(8,128)S(1)} %add.84), channel_id=1, source_target_pairs={{0,128},{32,160},{64,192},{96,224},{128,0},{160,32},{192,64},{224,... | collective-permute-start | bytes 393224 | tf_op jit(solution)/shard_map/ppermute | solution.py:48
  121.5 23.5 %all-to-all-start.3 = ((bf16[8,128,512]{2,1,0:T(8,128)(2,1)}), bf16[8,128,512]{2,1,0:T(8,128)(2,1)S(1)}, u32[]{:S(2)}, u32[]{:S(2)}) async-start(bf16[8,128,512]{2,1,0:T(8,128)(2,1)} %bitcast.80), calls=%async_computation.3 | async-start | bytes 2097152 | tf_op jit(solution)/shard_map/all_to_all | solution.py:43
  126.2 18.7 %collective-permute-start.9 = (f32[256,128]{1,0:T(8,128)S(1)}, f32[256,128]{1,0:T(8,128)S(1)}, u32[]{:S(2)}, u32[]{:S(2)}) collective-permute-start(f32[256,128]{1,0:T(8,128)S(1)} %add.85), channel_id=1, source_target_pairs={{0,256},{256,0},{1,257},{257,1},{2,258},{258,2},{3,259},{259,3},{4... | collective-permute-start | bytes 393224 | tf_op jit(solution)/shard_map/ppermute | solution.py:48
  145.2 7.8 %collective-permute-start.10 = (bf16[128,512]{1,0:T(8,128)(2,1)S(1)}, bf16[128,512]{1,0:T(8,128)(2,1)S(1)}, u32[]{:S(2)}, u32[]{:S(2)}) collective-permute-start(bf16[128,512]{1,0:T(8,128)(2,1)S(1)} %get-tuple-element.52), channel_id=1, source_target_pairs={{0,2},{2,0},{1,3},{3,1},{4,6},{6,4},{5,7},{7,5},{8,10},{10,8},{9,1... | collective-permute-start | bytes 393224 | tf_op jit(solution)/shard_map/ppermute | solution.py:48
  154.2 18.6 %copy-start.9 = (bf16[1,512,512]{2,1,0:T(8,128)(2,1)S(1)}, bf16[1,512,512]{2,1,0:T(8,128)(2,1)}, u32[]{:S(2)}) copy-start(bf16[1,512,512]{2,1,0:T(8,128)(2,1)} %param.12) | copy-start | bytes 1572868
  154.2 18.5 %all-to-all-start.4 = ((bf16[8,144,512]{2,1,0:T(8,128)(2,1)}), bf16[8,144,512]{2,1,0:T(8,128)(2,1)S(1)}, u32[]{:S(2)}, u32[]{:S(2)}) async-start(bf16[8,144,512]{2,1,0:T(8,128)(2,1)} %errors.3), calls=%async_computation.4 | async-start | bytes 2359296 | tf_op jit(solution)/shard_map/all_to_all | solution.py:43
  160.5 3.2 %collective-permute-start.11 = (f32[256,128]{1,0:T(8,128)S(1)}, f32[256,128]{1,0:T(8,128)S(1)}, u32[]{:S(2)}, u32[]{:S(2)}) collective-permute-start(f32[256,128]{1,0:T(8,128)S(1)} %add.90), channel_id=1, source_target_pairs={{0,16},{16,0},{1,17},{17,1},{2,18},{18,2},{3,19},{19,3},{4,20},{20... | collective-permute-start | bytes 393224 | tf_op jit(solution)/shard_map/ppermute | solution.py:48
  162.4 10.4 %copy-start.12 = (bf16[1,512,512]{2,1,0:T(8,128)(2,1)S(1)}, bf16[1,512,512]{2,1,0:T(8,128)(2,1)}, u32[]{:S(2)}) copy-start(bf16[1,512,512]{2,1,0:T(8,128)(2,1)} %param.13) | copy-start | bytes 1572868
  162.4 10.4 %copy-start.14 = (bf16[1,512,512]{2,1,0:T(8,128)(2,1)S(1)}, bf16[1,512,512]{2,1,0:T(8,128)(2,1)}, u32[]{:S(2)}) copy-start(bf16[1,512,512]{2,1,0:T(8,128)(2,1)} %param.14) | copy-start | bytes 1572868
  (10 other events, 14.0 us)

commit v8 on v7

--- a/solution.py
+++ b/solution.py
@@ -26,7 +26,7 @@
 GROUP = ("x", "zn")
 EXTRA = 16
 CHUNK = 32
-VMEM = 48 * 1024 * 1024
+VMEM = 8 * 1024 * 1024
 ALL_VMEM = 60 * 1024 * 1024
 
 bf16, f32 = jnp.bfloat16, jnp.float32
@@ -110,10 +110,19 @@
     )(hidden)
 
 
-def error_kernel(scale, own_ref, got_ref, weight_ref, out_ref):
-    tokens, columns = own_ref.shape
-    weight = weight_ref[...]
-    error = (own_ref[...] + got_ref[...].astype(f32)) * scale
+def error_kernel(scale, counted, own_ref, got_ref, hot_ref, *rest):
+    tokens, columns = hot_ref.shape[0], own_ref.shape[1]
+    total = own_ref[...] + got_ref[...].astype(f32)
+    if counted:
+        out_ref, inverse_ref = rest
+        counts = total[tokens : tokens + 1, :128]
+        inverse = jnp.where(counts > 0.0, 1.0 / (DOCS * jnp.maximum(counts, 1.0)), 0.0)
+        inverse_ref[...] = jnp.broadcast_to(inverse, inverse_ref.shape)
+    else:
+        inverse_in_ref, out_ref = rest
+        inverse = inverse_in_ref[:1]
+    weight = jnp.sum(hot_ref[...] * inverse, axis=-1, keepdims=True)
+    error = total[:tokens] * scale
     grad = (weight * error / columns).astype(bf16)
     each = jnp.sum(error * error, axis=-1, keepdims=True) / columns
     loss = jnp.sum(weight * 0.5 * each, axis=0, keepdims=True)
@@ -129,17 +138,62 @@
         out_ref[at, tokens:] = row
 
 
-def errors(own, got, weight, copies, scale):
-    tokens, columns = own.shape
+def errors(own, got, hot, inverse, copies, scale):
+    tokens, columns = hot.shape[0], own.shape[1]
+    sent = jax.ShapeDtypeStruct((copies, tokens + EXTRA, columns), bf16)
+    kept = jax.ShapeDtypeStruct((8, 128), f32)
+    counted = inverse is None
     return pl.pallas_call(
-        functools.partial(error_kernel, scale),
-        out_shape=jax.ShapeDtypeStruct((copies, tokens + EXTRA, columns), bf16),
+        functools.partial(error_kernel, scale, counted),
+        out_shape=(sent, kept) if counted else sent,
         compiler_params=pltpu.CompilerParams(vmem_limit_bytes=VMEM),
         cost_estimate=pl.CostEstimate(
             flops=8 * tokens * columns, bytes_accessed=30 * tokens * columns, transcendentals=0
         ),
         name="errors",
-    )(own, got, weight)
+    )(own, got, hot, *(() if counted else (inverse,)))
+
+
+def project_kernel(columns_ref, weights_ref, counts_ref, out_ref, first_ref, later_ref, made, sent):
+    shards, _, rows, _ = columns_ref.shape
+    groups, tokens, _ = made.shape
+    tokens = tokens - EXTRA
+    share = tokens // rows
+
+    def give(at):
+        return pltpu.make_async_copy(made.at[pl.ds(at, 2)], out_ref.at[pl.ds(at, 2)], sent.at[at // 2])
+
+    for at in range(0, groups, 2):
+        for shard in range(at * share, (at + 2) * share):
+            first_ref[shard * rows : (shard + 1) * rows] = columns_ref[shard, 0]
+        product = jnp.dot(
+            first_ref[at * tokens : (at + 2) * tokens], weights_ref[0], preferred_element_type=f32
+        ).astype(bf16)
+        for group in range(2):
+            made[at + group, :tokens] = product[group * tokens : (group + 1) * tokens]
+            made[at + group, tokens:] = counts_ref[...]
+        give(at).start()
+    for shard in range(shards):
+        later_ref[shard * rows : (shard + 1) * rows] = columns_ref[shard, 1]
+    for at in range(0, groups, 2):
+        give(at).wait()
+
+
+def project(columns, weights, count_rows, groups):
+    shards, _, rows, features = columns.shape
+    tokens, wide = shards * rows, weights.shape[2]
+    block = jax.ShapeDtypeStruct((groups, tokens // groups + EXTRA, wide), bf16)
+    plain = jax.ShapeDtypeStruct((tokens, features), bf16)
+    vmem = pl.BlockSpec(memory_space=pltpu.MemorySpace.VMEM)
+    return pl.pallas_call(
+        project_kernel,
+        in_specs=[vmem, vmem, vmem],
+        out_specs=(pl.BlockSpec(memory_space=pl.ANY), vmem, vmem),
+        out_shape=(block, plain, plain),
+        scratch_shapes=[pltpu.VMEM(block.shape, bf16), pltpu.SemaphoreType.DMA((groups // 2,))],
+        compiler_params=pltpu.CompilerParams(vmem_limit_bytes=VMEM),
+        name="project",
+    )(columns, weights, count_rows)
 
 
 def body(hidden, targets, doc_ids, weights, adam_m, adam_v, anchor, momentum, fragment):
@@ -164,52 +218,57 @@
 
     doc_range = jnp.arange(DOCS, dtype=jnp.int32)
     counts = jnp.sum((doc_ids[0][..., None] == doc_range).astype(f32), axis=1)
-    for axis, bit in (("x", 1), ("x", 2), ("zn", 1)):
-        counts = counts + swap(counts, axis, bit)
-    own_row = jnp.concatenate([doc_ids[0].astype(f32), counts], axis=1)
-    own_row = jnp.pad(own_row, ((0, 0), (0, 128 - own_row.shape[1])))
-    far_row = swap(own_row, "zf")
-    pair = [jnp.where(f_at == 0, own_row, far_row), jnp.where(f_at == 0, far_row, own_row)]
-    pair_ids = jnp.concatenate([row[:, :rows] for row in pair], axis=1).astype(jnp.int32)
-    inverse = 1.0 / (DOCS * (counts + far_row[:, rows : rows + DOCS]))
-    hot = (pair_ids[..., None] == doc_range).astype(f32)
-    token_weight = jnp.sum(hot * inverse[:, None, :], axis=-1, keepdims=True)
+    count_rows = jnp.pad(
+        counts.reshape(1, -1).astype(bf16),
+        ((0, EXTRA - 1), (0, value_width - steps_total * DOCS)),
+    )
+    far_ids = swap(doc_ids[0], "zf")
+    pair_ids = jnp.concatenate(
+        [jnp.where(f_at == 0, doc_ids[0], far_ids), jnp.where(f_at == 0, far_ids, doc_ids[0])],
+        axis=1,
+    )
+    step_shift = DOCS * jnp.arange(steps_total, dtype=jnp.int32)[:, None, None]
+    hot = (pair_ids[..., None] + step_shift == jnp.arange(128, dtype=jnp.int32)).astype(f32)
+    hot = [hot[step] for step in range(steps_total)]
 
     goal = targets[0].astype(f32) / scale
     goal = jnp.concatenate([jnp.where(f_at == at, goal, 0.0) for at in range(nf)], axis=1)
+    goal = [jnp.pad(goal[0], ((0, EXTRA), (0, 0))), goal[1]]
 
     half = shard_rows // 2
     local = lax.dynamic_slice(weights[0], (zero, start), (shard_rows, frag_width))
     local = local.reshape(2, half, frag_width)
     summed = pick(local, c_at, 0).astype(f32) + swap(pick(local, c_at ^ 1, 0), "c").astype(f32)
-    summed = summed + swap(summed, "y", 1)
-
-    columns, goal, token_weight, summed = tie(columns, goal, token_weight, summed)
+    for bit in (1, 2, 4):
+        summed = summed + swap(summed, "y", bit)
+
+    columns, goal, hot, count_rows, summed = tie(columns, goal, hot, count_rows, summed)
+    partial, *step_rows = project(columns, weights, count_rows, groups)
 
     master = weights[0].astype(f32)
     first = adam_m[0].astype(f32)
     second = adam_v[0].astype(f32)
-    loss_rows = []
+    loss_rows, inverse = [], None
     for step in range(steps_total):
-        current = master.astype(bf16)
-        rows_now = columns[:, step].reshape(shards * rows, shard_rows)
-        partial = jnp.dot(rows_now, current, preferred_element_type=f32)
-        partial = partial.astype(bf16).reshape(groups, tokens, value_width)
-        partial, summed = tie(partial, summed)
+        rows_now = step_rows[step]
+        if step == 1:
+            partial = jnp.dot(rows_now, master.astype(bf16), preferred_element_type=f32)
+            partial = partial.astype(bf16).reshape(groups, tokens, value_width)
+            partial, summed = tie(partial, summed)
         partial = exchange(partial, GROUP)
-        summed = summed + (swap(summed, "y", 2) if step == 0 else swap(summed, "zh"))
-        partial, summed = tie(partial, summed)
+        if step == 1:
+            other = swap(summed, "c")
+            partial, summed, other = tie(partial, summed, other)
         own = jnp.sum(partial.astype(f32), axis=0) - goal[step]
         got = swap(own.astype(bf16), "zf")
-        sent = errors(own, got, token_weight[step], groups, scale)
-        sent, summed = tie(sent, summed)
+        sent = errors(own, got, hot[step], inverse, groups, scale)
+        if step == 0:
+            sent, inverse = sent
+            sent, summed = tie(sent, summed)
         got = exchange(sent, GROUP)
         if step == 0:
-            summed = summed + swap(summed, "y", 4)
+            summed = summed + swap(summed, "zh")
             got, summed = tie(got, summed)
-        else:
-            other = swap(summed, "c")
-            got, summed, other = tie(got, summed, other)
         loss_rows.append(got[:, tokens, :128])
         everyone = got[:, :tokens].reshape(shards * rows, value_width)
         gradient = (

time: 180 us -> 202 us (1.12)
  waiting for transfers between devices: 78.1 us -> 100 us
  starting transfers between devices: 78.3 us -> 57.8 us
  blocking collectives: 0 us -> 16.9 us
    all_to_all x0 -> x1, blocking collectives: none -> 16.9 us  [exchange(): lax.all_to_all(blocks, axes, split_axis=0, concat_axis=0, tiled=False)]
    ppermute x12 -> x9, waiting for transfers between devices: 64.2 us -> 80.3 us  [swap(): return lax.ppermute(block, axis, [(i, i ^ bit) for i in range(size)])]
    ppermute x12 -> x9, starting transfers between devices: 49.5 us -> 34.1 us  [swap(): return lax.ppermute(block, axis, [(i, i ^ bit) for i in range(size)])]
    all_to_all x5 -> x4, waiting for transfers between devices: 13.9 us -> 19.8 us  [exchange(): lax.all_to_all(blocks, axes, split_axis=0, concat_axis=0, tiled=False)]
    all_to_all x5 -> x4, starting transfers between devices: 28.9 us -> 23.7 us  [exchange(): lax.all_to_all(blocks, axes, split_axis=0, concat_axis=0, tiled=False)]
    unnamed x36 -> x35, local copies, waits for them, and re-layouts: 4.28 us -> 5.37 us
  transfers between devices with their start and end apart: 17 -> 13, of which waited for: 14 -> 10; matrix products, arithmetic and copies ran while one was open for 0% -> 1% of each run, Pallas kernels for 0% -> 0%
where the time goes in v8:
time: 202 us; the launch traced here: 201 us
  waiting for transfers between devices  100 us (50%)
  starting transfers between devices  57.8 us (29%)
  blocking collectives  16.9 us (8%)
  local copies, waits for them, and re-layouts  7.67 us (4%)
  Pallas kernels  6.83 us (3%)
  matrix products  6.57 us (3%)
  other arithmetic  3.7 us (2%)
    ppermute x9, waiting for transfers between devices, swap(): return lax.ppermute(block, axis, [(i, i ^ bit) for i in range(size)])  80.3 us
    ppermute x9, starting transfers between devices, swap(): return lax.ppermute(block, axis, [(i, i ^ bit) for i in range(size)])  34.1 us
    all_to_all x4, starting transfers between devices, exchange(): lax.all_to_all(blocks, axes, split_axis=0, concat_axis=0, tiled=False)  23.7 us
    all_to_all x4, waiting for transfers between devices, exchange(): lax.all_to_all(blocks, axes, split_axis=0, concat_axis=0, tiled=False)  19.8 us
    all_to_all x1, blocking collectives, exchange(): lax.all_to_all(blocks, axes, split_axis=0, concat_axis=0, tiled=False)  16.9 us
    unnamed x35, local copies, waits for them, and re-layouts  5.37 us
    dot_general x2, matrix products, body(): lax.dot_general(rows_now, everyone, (((0,), (0,)), ((), ())), preferred_e...  4.23 us
  transfers between devices with their start and end apart: 13, of which 10 were waited for; matrix products, arithmetic and copies ran while one was open for 1% of the time, Pallas kernels for 0%

profile of v8, /device:TPU:56, one launch (start us, length us, event | category | flops | bytes accessed | tf_op | source)
XLA Modules:
  0.0 201.4 jit_solution(17363670901723450263)
XLA Ops:
  0.6 2.9 %normalize.1 = bf16[16,2,64,512]{3,2,1,0:T(8,128)(2,1)} custom-call(bf16[1,2,64,8192]{3,2,1,0:T(8,128)(2,1)} %hidden_ref.1), custom_call_target="tpu_custom_call" | custom-call | tf_op jit(solution)/shard_map/normalize/pallas_call | solution.py:97
  3.6 10.0 %all-to-all-start = ((bf16[16,2,64,512]{3,2,1,0:T(8,128)(2,1)}), bf16[16,2,64,512]{3,2,1,0:T(8,128)(2,1)S(1)}, u32[]{:S(2)}, u32[]{:S(2)}) async-start(bf16[16,2,64,512]{3,2,1,0:T(8,128)(2,1)} %normalize.1), calls=%async_computation | async-start | bytes 4194304 | tf_op jit(solution)/shard_map/all_to_all | solution.py:43
  13.6 4.7 %collective-permute-start = (s32[2,64]{1,0:T(2,128)S(1)}, s32[2,64]{1,0:T(2,128)S(1)}, u32[]{:S(2)}, u32[]{:S(2)}) collective-permute-start(s32[2,64]{1,0:T(2,128)S(1)} %bitcast.80), channel_id=1, source_target_pairs={{0,2},{2,0},{1,3},{3,1},{4,6},{6,4},{5,7},{7,5},{8,10},{10,8},{9,1... | collective-permute-start | bytes 1544 | tf_op jit(solution)/shard_map/ppermute | solution.py:48
  21.9 39.8 %collective-permute-done = s32[2,64]{1,0:T(2,128)S(1)} collective-permute-done((s32[2,64]{1,0:T(2,128)S(1)}, s32[2,64]{1,0:T(2,128)S(1)}, u32[]{:S(2)}, u32[]{:S(2)}) %collective-permute-start) | collective-permute-done | bytes 544 | tf_op jit(solution)/shard_map/ppermute | solution.py:48
  62.6 3.3 %collective-permute-start.2 = (f32[256,128]{1,0:T(8,128)S(1)}, f32[256,128]{1,0:T(8,128)S(1)}, u32[]{:S(2)}, u32[]{:S(2)}) collective-permute-start(f32[256,128]{1,0:T(8,128)S(1)} %convert_add_fusion), channel_id=1, source_target_pairs={{0,32},{32,0},{64,96},{96,64},{128,160},{160,128},{192,224},{224,1... | collective-permute-start | bytes 393224 | tf_op jit(solution)/shard_map/ppermute | solution.py:48
  66.0 3.5 %collective-permute-done.2 = f32[256,128]{1,0:T(8,128)S(1)} collective-permute-done((f32[256,128]{1,0:T(8,128)S(1)}, f32[256,128]{1,0:T(8,128)S(1)}, u32[]{:S(2)}, u32[]{:S(2)}) %collective-permute-start.2) | collective-permute-done | bytes 131104 | tf_op jit(solution)/shard_map/ppermute | solution.py:48
  69.5 4.0 %collective-permute-start.3 = (f32[256,128]{1,0:T(8,128)S(1)}, f32[256,128]{1,0:T(8,128)S(1)}, u32[]{:S(2)}, u32[]{:S(2)}) collective-permute-start(f32[256,128]{1,0:T(8,128)S(1)} %add.84), channel_id=1, source_target_pairs={{0,64},{32,96},{64,0},{96,32},{128,192},{160,224},{192,128},{224,1... | collective-permute-start | bytes 393224 | tf_op jit(solution)/shard_map/ppermute | solution.py:48
  73.7 5.0 %collective-permute-done.3 = f32[256,128]{1,0:T(8,128)S(1)} collective-permute-done((f32[256,128]{1,0:T(8,128)S(1)}, f32[256,128]{1,0:T(8,128)S(1)}, u32[]{:S(2)}, u32[]{:S(2)}) %collective-permute-start.3) | collective-permute-done | bytes 131104 | tf_op jit(solution)/shard_map/ppermute | solution.py:48
  78.7 4.6 %collective-permute-start.4 = (f32[256,128]{1,0:T(8,128)S(1)}, f32[256,128]{1,0:T(8,128)S(1)}, u32[]{:S(2)}, u32[]{:S(2)}) collective-permute-start(f32[256,128]{1,0:T(8,128)S(1)} %add.85), channel_id=1, source_target_pairs={{0,128},{32,160},{64,192},{96,224},{128,0},{160,32},{192,64},{224,... | collective-permute-start | bytes 393224 | tf_op jit(solution)/shard_map/ppermute | solution.py:48
  83.3 6.9 %collective-permute-done.4 = f32[256,128]{1,0:T(8,128)S(1)} collective-permute-done((f32[256,128]{1,0:T(8,128)S(1)}, f32[256,128]{1,0:T(8,128)S(1)}, u32[]{:S(2)}, u32[]{:S(2)}) %collective-permute-start.4) | collective-permute-done | bytes 131104 | tf_op jit(solution)/shard_map/ppermute | solution.py:48
  93.7 16.9 %all_to_all.25 = bf16[8,144,512]{2,1,0:T(8,128)(2,1)S(1)} all-to-all(bf16[8,144,512]{2,1,0:T(8,128)(2,1)S(1)} %get-tuple-element.34), channel_id=1, replica_groups=mesh['zh'=2,'y'=8,'c'=2,'x'=4,'zf'=2,'zn'=2] {'x','zn'}, dimensions={0} | all-to-all | bytes 2359296 | tf_op jit(solution)/shard_map/all_to_all | solution.py:43
  110.9 3.5 %collective-permute-start.5 = (bf16[144,512]{1,0:T(8,128)(2,1)S(1)}, bf16[144,512]{1,0:T(8,128)(2,1)S(1)}, u32[]{:S(2)}, u32[]{:S(2)}) collective-permute-start(bf16[144,512]{1,0:T(8,128)(2,1)S(1)} %get-tuple-element.54), channel_id=1, source_target_pairs={{0,2},{2,0},{1,3},{3,1},{4,6},{6,4},{5,7},{7,5},{8,10},{10,8},{9,1... | collective-permute-start | bytes 442376 | tf_op jit(solution)/shard_map/ppermute | solution.py:48
  114.4 6.0 %collective-permute-done.5.got_ref = bf16[144,512]{1,0:T(8,128)(2,1)S(1)} collective-permute-done((bf16[144,512]{1,0:T(8,128)(2,1)S(1)}, bf16[144,512]{1,0:T(8,128)(2,1)S(1)}, u32[]{:S(2)}, u32[]{:S(2)}) %collective-permute-start.5) | collective-permute-done | bytes 147488 | tf_op jit(solution)/shard_map/ppermute | solution.py:48
  121.6 4.2 %all-to-all-start.2 = ((bf16[8,144,512]{2,1,0:T(8,128)(2,1)}), bf16[8,144,512]{2,1,0:T(8,128)(2,1)}, u32[]{:S(2)}, u32[]{:S(2)}) async-start(bf16[8,144,512]{2,1,0:T(8,128)(2,1)} %get-tuple-element.39), calls=%async_computation.2 | async-start | bytes 2359296 | tf_op jit(solution)/shard_map/all_to_all | solution.py:43
  125.9 8.2 %collective-permute-start.6 = (f32[256,128]{1,0:T(8,128)S(1)}, f32[256,128]{1,0:T(8,128)S(1)}, u32[]{:S(2)}, u32[]{:S(2)}) collective-permute-start(f32[256,128]{1,0:T(8,128)S(1)} %add.86), channel_id=1, source_target_pairs={{0,256},{256,0},{1,257},{257,1},{2,258},{258,2},{3,259},{259,3},{4... | collective-permute-start | bytes 393224 | tf_op jit(solution)/shard_map/ppermute | solution.py:48
  134.1 10.4 %collective-permute-done.6 = f32[256,128]{1,0:T(8,128)S(1)} collective-permute-done((f32[256,128]{1,0:T(8,128)S(1)}, f32[256,128]{1,0:T(8,128)S(1)}, u32[]{:S(2)}, u32[]{:S(2)}) %collective-permute-start.6) | collective-permute-done | bytes 131104 | tf_op jit(solution)/shard_map/ppermute | solution.py:48
  145.9 2.1 %fusion.13 = f32[512,512]{1,0:T(8,128)S(1)} fusion(bf16[1024,512]{1,0:T(8,128)(2,1)} %copy-done.3, bf16[1024,512]{1,0:T(8,128)(2,1)S(1)} %bitcast.75), kind=kOutput, calls=%fused_computation.47 | convolution fusion | flops 536870912 | bytes 3145728 | tf_op jit(solution)/shard_map/dot_general | solution.py:275
  148.0 2.3 %convolution_convert_fusion = bf16[1024,512]{1,0:T(8,128)(2,1)} fusion(bf16[1024,512]{1,0:T(8,128)(2,1)S(1)} %copy-done.2, f32[512,512]{1,0:T(8,128)S(1)} %fusion.13, bf16[1,512,512]{2,1,0:T(8,128)(2,1)S(1)} %copy-done.10, bf16[1,512,512]{2,1,0:T(8,128)(2,1)S(1)} %copy-done, bf16[1,512,512]{2,1,0:T(8,128)(2,1)S(1)} %copy-done.12), kind=kOutput, calls=%fused_computation.2 | convolution fusion | flops 542113792 | bytes 4718592 | tf_op jit(solution)/shard_map/dot_general | solution.py:255
  150.4 5.9 %all-to-all-start.3 = ((bf16[8,128,512]{2,1,0:T(8,128)(2,1)}), bf16[8,128,512]{2,1,0:T(8,128)(2,1)}, u32[]{:S(2)}, u32[]{:S(2)}) async-start(bf16[8,128,512]{2,1,0:T(8,128)(2,1)} %bitcast.73), calls=%async_computation.3 | async-start | bytes 2097152 | tf_op jit(solution)/shard_map/all_to_all | solution.py:43
  159.6 8.4 %all-to-all-done.3 = bf16[8,128,512]{2,1,0:T(8,128)(2,1)} async-done(((bf16[8,128,512]{2,1,0:T(8,128)(2,1)}), bf16[8,128,512]{2,1,0:T(8,128)(2,1)}, u32[]{:S(2)}, u32[]{:S(2)}) %all-to-all-start.3) | async-done | bytes 1048608 | tf_op jit(solution)/shard_map/all_to_all | solution.py:43
  171.3 7.3 %collective-permute-done.8.got_ref = bf16[128,512]{1,0:T(8,128)(2,1)S(1)} collective-permute-done((bf16[128,512]{1,0:T(8,128)(2,1)S(1)}, bf16[128,512]{1,0:T(8,128)(2,1)S(1)}, u32[]{:S(2)}, u32[]{:S(2)}) %collective-permute-start.8) | collective-permute-done | bytes 131104 | tf_op jit(solution)/shard_map/ppermute | solution.py:48
  179.9 3.6 %all-to-all-start.4 = ((bf16[8,144,512]{2,1,0:T(8,128)(2,1)}), bf16[8,144,512]{2,1,0:T(8,128)(2,1)S(1)}, u32[]{:S(2)}, u32[]{:S(2)}) async-start(bf16[8,144,512]{2,1,0:T(8,128)(2,1)} %errors.3), calls=%async_computation.4 | async-start | bytes 2359296 | tf_op jit(solution)/shard_map/all_to_all | solution.py:43
  184.2 11.4 %all-to-all-done.4 = bf16[8,144,512]{2,1,0:T(8,128)(2,1)S(1)} async-done(((bf16[8,144,512]{2,1,0:T(8,128)(2,1)}), bf16[8,144,512]{2,1,0:T(8,128)(2,1)S(1)}, u32[]{:S(2)}, u32[]{:S(2)}) %all-to-all-start.4) | async-done | bytes 1179680 | tf_op jit(solution)/shard_map/all_to_all | solution.py:43
  197.2 2.1 %multiply_subtract_fusion = f32[512,512]{1,0:T(8,128)S(1)} fusion(f32[512,512]{1,0:T(8,128)S(1)} %copy-done.15, bf16[1,512,512]{2,1,0:T(8,128)(2,1)S(1)} %copy-done.11, bf16[1,512,512]{2,1,0:T(8,128)(2,1)S(1)} %copy-done.13, bf16[1,512,512]{2,1,0:T(8,128)(2,1)S(1)} %copy-done, bf16[1024,512]{1,0:T(8,128)(2,1)S(1)} %copy-done.2, ...), kind=kOutput, calls=%fused_computation.9 | convolution fusion | flops 544997376 | bytes 5767168 | tf_op jit(solution)/shard_map/dot_general | solution.py:275
  (74 shorter events, 22.3 us)
Async XLA Ops:
  3.6 10.0 %copy-start.9 = (s32[1,2,64]{2,1,0:T(2,128)S(1)}, s32[1,2,64]{2,1,0:T(2,128)}, u32[]{:S(2)}) copy-start(s32[1,2,64]{2,1,0:T(2,128)} %param.11) | copy-start | bytes 1540
  3.6 15.4 %copy-start = (bf16[1,512,512]{2,1,0:T(8,128)(2,1)S(1)}, bf16[1,512,512]{2,1,0:T(8,128)(2,1)}, u32[]{:S(2)}) copy-start(bf16[1,512,512]{2,1,0:T(8,128)(2,1)} %weights_ref) | copy-start | bytes 1572868
  3.6 18.1 %copy-start.6 = (bf16[1,2,64,512]{3,2,1,0:T(8,128)(2,1)S(1)}, bf16[1,2,64,512]{3,2,1,0:T(8,128)(2,1)}, u32[]{:S(2)}) copy-start(bf16[1,2,64,512]{3,2,1,0:T(8,128)(2,1)} %param.10) | copy-start | bytes 393220
  3.6 86.7 %all-to-all-start = ((bf16[16,2,64,512]{3,2,1,0:T(8,128)(2,1)}), bf16[16,2,64,512]{3,2,1,0:T(8,128)(2,1)S(1)}, u32[]{:S(2)}, u32[]{:S(2)}) async-start(bf16[16,2,64,512]{3,2,1,0:T(8,128)(2,1)} %normalize.1), calls=%async_computation | async-start | bytes 4194304 | tf_op jit(solution)/shard_map/all_to_all | solution.py:43
  13.6 48.2 %collective-permute-start = (s32[2,64]{1,0:T(2,128)S(1)}, s32[2,64]{1,0:T(2,128)S(1)}, u32[]{:S(2)}, u32[]{:S(2)}) collective-permute-start(s32[2,64]{1,0:T(2,128)S(1)} %bitcast.80), channel_id=1, source_target_pairs={{0,2},{2,0},{1,3},{3,1},{4,6},{6,4},{5,7},{7,5},{8,10},{10,8},{9,1... | collective-permute-start | bytes 1544 | tf_op jit(solution)/shard_map/ppermute | solution.py:48
  19.7 42.1 %collective-permute-start.1 = (bf16[256,128]{1,0:T(8,128)(2,1)S(1)}, bf16[256,128]{1,0:T(8,128)(2,1)}, u32[]{:S(2)}, u32[]{:S(2)}) collective-permute-start(bf16[256,128]{1,0:T(8,128)(2,1)S(1)} %dynamic-slice_bitcast_fusion), channel_id=1, source_target_pairs={{0,16},{16,0},{1,17},{17,1},{2,18},{18,2},{3,19},{19,3},{4,20},{20... | collective-permute-start | bytes 196616 | tf_op jit(solution)/shard_map/ppermute | solution.py:48
  62.6 6.9 %collective-permute-start.2 = (f32[256,128]{1,0:T(8,128)S(1)}, f32[256,128]{1,0:T(8,128)S(1)}, u32[]{:S(2)}, u32[]{:S(2)}) collective-permute-start(f32[256,128]{1,0:T(8,128)S(1)} %convert_add_fusion), channel_id=1, source_target_pairs={{0,32},{32,0},{64,96},{96,64},{128,160},{160,128},{192,224},{224,1... | collective-permute-start | bytes 393224 | tf_op jit(solution)/shard_map/ppermute | solution.py:48
  69.5 9.2 %collective-permute-start.3 = (f32[256,128]{1,0:T(8,128)S(1)}, f32[256,128]{1,0:T(8,128)S(1)}, u32[]{:S(2)}, u32[]{:S(2)}) collective-permute-start(f32[256,128]{1,0:T(8,128)S(1)} %add.84), channel_id=1, source_target_pairs={{0,64},{32,96},{64,0},{96,32},{128,192},{160,224},{192,128},{224,1... | collective-permute-start | bytes 393224 | tf_op jit(solution)/shard_map/ppermute | solution.py:48
  78.7 11.5 %collective-permute-start.4 = (f32[256,128]{1,0:T(8,128)S(1)}, f32[256,128]{1,0:T(8,128)S(1)}, u32[]{:S(2)}, u32[]{:S(2)}) collective-permute-start(f32[256,128]{1,0:T(8,128)S(1)} %add.85), channel_id=1, source_target_pairs={{0,128},{32,160},{64,192},{96,224},{128,0},{160,32},{192,64},{224,... | collective-permute-start | bytes 393224 | tf_op jit(solution)/shard_map/ppermute | solution.py:48
  110.9 9.5 %collective-permute-start.5 = (bf16[144,512]{1,0:T(8,128)(2,1)S(1)}, bf16[144,512]{1,0:T(8,128)(2,1)S(1)}, u32[]{:S(2)}, u32[]{:S(2)}) collective-permute-start(bf16[144,512]{1,0:T(8,128)(2,1)S(1)} %get-tuple-element.54), channel_id=1, source_target_pairs={{0,2},{2,0},{1,3},{3,1},{4,6},{6,4},{5,7},{7,5},{8,10},{10,8},{9,1... | collective-permute-start | bytes 442376 | tf_op jit(solution)/shard_map/ppermute | solution.py:48
  121.6 22.9 %all-to-all-start.2 = ((bf16[8,144,512]{2,1,0:T(8,128)(2,1)}), bf16[8,144,512]{2,1,0:T(8,128)(2,1)}, u32[]{:S(2)}, u32[]{:S(2)}) async-start(bf16[8,144,512]{2,1,0:T(8,128)(2,1)} %get-tuple-element.39), calls=%async_computation.2 | async-start | bytes 2359296 | tf_op jit(solution)/shard_map/all_to_all | solution.py:43
  125.9 18.6 %collective-permute-start.6 = (f32[256,128]{1,0:T(8,128)S(1)}, f32[256,128]{1,0:T(8,128)S(1)}, u32[]{:S(2)}, u32[]{:S(2)}) collective-permute-start(f32[256,128]{1,0:T(8,128)S(1)} %add.86), channel_id=1, source_target_pairs={{0,256},{256,0},{1,257},{257,1},{2,258},{258,2},{3,259},{259,3},{4... | collective-permute-start | bytes 393224 | tf_op jit(solution)/shard_map/ppermute | solution.py:48
  145.9 2.2 %copy-start.2 = (bf16[1024,512]{1,0:T(8,128)(2,1)S(1)}, bf16[1024,512]{1,0:T(8,128)(2,1)}, u32[]{:S(2)}) copy-start(bf16[1024,512]{1,0:T(8,128)(2,1)} %copy-done.1) | copy-start | bytes 3145732
  145.9 2.2 %copy-start.10 = (bf16[1,512,512]{2,1,0:T(8,128)(2,1)S(1)}, bf16[1,512,512]{2,1,0:T(8,128)(2,1)}, u32[]{:S(2)}) copy-start(bf16[1,512,512]{2,1,0:T(8,128)(2,1)} %param.13) | copy-start | bytes 1572868
  145.9 2.2 %copy-start.12 = (bf16[1,512,512]{2,1,0:T(8,128)(2,1)S(1)}, bf16[1,512,512]{2,1,0:T(8,128)(2,1)}, u32[]{:S(2)}) copy-start(bf16[1,512,512]{2,1,0:T(8,128)(2,1)} %param.14) | copy-start | bytes 1572868
  148.0 2.4 %copy-start.14 = (f32[512,512]{1,0:T(8,128)}, f32[512,512]{1,0:T(8,128)S(1)}, u32[]{:S(2)}) copy-start(f32[512,512]{1,0:T(8,128)S(1)} %fusion.13) | copy-start | bytes 3145732
  150.4 17.6 %all-to-all-start.3 = ((bf16[8,128,512]{2,1,0:T(8,128)(2,1)}), bf16[8,128,512]{2,1,0:T(8,128)(2,1)}, u32[]{:S(2)}, u32[]{:S(2)}) async-start(bf16[8,128,512]{2,1,0:T(8,128)(2,1)} %bitcast.73), calls=%async_computation.3 | async-start | bytes 2097152 | tf_op jit(solution)/shard_map/all_to_all | solution.py:43
  156.3 3.2 %collective-permute-start.7 = (f32[256,128]{1,0:T(8,128)S(1)}, f32[256,128]{1,0:T(8,128)S(1)}, u32[]{:S(2)}, u32[]{:S(2)}) collective-permute-start(f32[256,128]{1,0:T(8,128)S(1)} %add.87), channel_id=1, source_target_pairs={{0,16},{16,0},{1,17},{17,1},{2,18},{18,2},{3,19},{19,3},{4,20},{20... | collective-permute-start | bytes 393224 | tf_op jit(solution)/shard_map/ppermute | solution.py:48
  169.4 9.3 %collective-permute-start.8 = (bf16[128,512]{1,0:T(8,128)(2,1)S(1)}, bf16[128,512]{1,0:T(8,128)(2,1)S(1)}, u32[]{:S(2)}, u32[]{:S(2)}) collective-permute-start(bf16[128,512]{1,0:T(8,128)(2,1)S(1)} %get-tuple-element.52), channel_id=1, source_target_pairs={{0,2},{2,0},{1,3},{3,1},{4,6},{6,4},{5,7},{7,5},{8,10},{10,8},{9,1... | collective-permute-start | bytes 393224 | tf_op jit(solution)/shard_map/ppermute | solution.py:48
  179.9 15.7 %all-to-all-start.4 = ((bf16[8,144,512]{2,1,0:T(8,128)(2,1)}), bf16[8,144,512]{2,1,0:T(8,128)(2,1)S(1)}, u32[]{:S(2)}, u32[]{:S(2)}) async-start(bf16[8,144,512]{2,1,0:T(8,128)(2,1)} %errors.3), calls=%async_computation.4 | async-start | bytes 2359296 | tf_op jit(solution)/shard_map/all_to_all | solution.py:43
  195.6 1.0 copy-start.11
  195.6 1.2 copy-start.13
  195.6 1.5 copy-start.15
  200.4 1.0 copy-start.4
  (5 other events, 4.5 us)

commit v9 on v8

--- a/solution.py
+++ b/solution.py
@@ -26,7 +26,7 @@
 GROUP = ("x", "zn")
 EXTRA = 16
 CHUNK = 32
-VMEM = 8 * 1024 * 1024
+VMEM = 48 * 1024 * 1024
 ALL_VMEM = 60 * 1024 * 1024
 
 bf16, f32 = jnp.bfloat16, jnp.float32
@@ -110,18 +110,26 @@
     )(hidden)
 
 
-def error_kernel(scale, counted, own_ref, got_ref, hot_ref, *rest):
-    tokens, columns = hot_ref.shape[0], own_ref.shape[1]
+def error_kernel(scale, counted, own_ref, got_ref, *rest):
+    tokens, columns = 128, own_ref.shape[1]
     total = own_ref[...] + got_ref[...].astype(f32)
     if counted:
-        out_ref, inverse_ref = rest
+        out_ref, later_ref = rest
         counts = total[tokens : tokens + 1, :128]
         inverse = jnp.where(counts > 0.0, 1.0 / (DOCS * jnp.maximum(counts, 1.0)), 0.0)
-        inverse_ref[...] = jnp.broadcast_to(inverse, inverse_ref.shape)
+        lane = lax.broadcasted_iota(jnp.int32, (tokens, 128), 1)
+        here = lane == lax.broadcasted_iota(jnp.int32, (tokens, 128), 0)
+        weights = []
+        for step in range(2):
+            ids = jnp.where(here, total[tokens + 1 + step : tokens + 2 + step, :128], 0.0)
+            ids = jnp.sum(ids, axis=-1, keepdims=True).astype(jnp.int32) + DOCS * step
+            hot = jnp.where(lane == ids, inverse, 0.0)
+            weights.append(jnp.sum(hot, axis=-1, keepdims=True))
+        weight = weights[0]
+        later_ref[...] = jnp.broadcast_to(weights[1], later_ref.shape)
     else:
-        inverse_in_ref, out_ref = rest
-        inverse = inverse_in_ref[:1]
-    weight = jnp.sum(hot_ref[...] * inverse, axis=-1, keepdims=True)
+        weight_ref, out_ref = rest
+        weight = weight_ref[:, :1]
     error = total[:tokens] * scale
     grad = (weight * error / columns).astype(bf16)
     each = jnp.sum(error * error, axis=-1, keepdims=True) / columns
@@ -138,11 +146,11 @@
         out_ref[at, tokens:] = row
 
 
-def errors(own, got, hot, inverse, copies, scale):
-    tokens, columns = hot.shape[0], own.shape[1]
+def errors(own, got, weight, tokens, copies, scale):
+    columns = own.shape[1]
     sent = jax.ShapeDtypeStruct((copies, tokens + EXTRA, columns), bf16)
-    kept = jax.ShapeDtypeStruct((8, 128), f32)
-    counted = inverse is None
+    kept = jax.ShapeDtypeStruct((tokens, 128), f32)
+    counted = weight is None
     return pl.pallas_call(
         functools.partial(error_kernel, scale, counted),
         out_shape=(sent, kept) if counted else sent,
@@ -151,7 +159,7 @@
             flops=8 * tokens * columns, bytes_accessed=30 * tokens * columns, transcendentals=0
         ),
         name="errors",
-    )(own, got, hot, *(() if counted else (inverse,)))
+    )(own, got, *(() if counted else (weight,)))
 
 
 def project_kernel(columns_ref, weights_ref, counts_ref, out_ref, first_ref, later_ref, made, sent):
@@ -222,18 +230,12 @@
         counts.reshape(1, -1).astype(bf16),
         ((0, EXTRA - 1), (0, value_width - steps_total * DOCS)),
     )
-    far_ids = swap(doc_ids[0], "zf")
-    pair_ids = jnp.concatenate(
-        [jnp.where(f_at == 0, doc_ids[0], far_ids), jnp.where(f_at == 0, far_ids, doc_ids[0])],
-        axis=1,
-    )
-    step_shift = DOCS * jnp.arange(steps_total, dtype=jnp.int32)[:, None, None]
-    hot = (pair_ids[..., None] + step_shift == jnp.arange(128, dtype=jnp.int32)).astype(f32)
-    hot = [hot[step] for step in range(steps_total)]
-
     goal = targets[0].astype(f32) / scale
     goal = jnp.concatenate([jnp.where(f_at == at, goal, 0.0) for at in range(nf)], axis=1)
-    goal = [jnp.pad(goal[0], ((0, EXTRA), (0, 0))), goal[1]]
+    ids = doc_ids[0].astype(f32)
+    ids = jnp.concatenate([jnp.where(f_at == at, ids, 0.0) for at in range(nf)], axis=1)
+    ids = jnp.pad(ids, ((1, EXTRA - 1 - steps_total), (0, value_width - tokens)))
+    goal = [jnp.concatenate([goal[0], -ids], axis=0), goal[1]]
 
     half = shard_rows // 2
     local = lax.dynamic_slice(weights[0], (zero, start), (shard_rows, frag_width))
@@ -242,13 +244,13 @@
     for bit in (1, 2, 4):
         summed = summed + swap(summed, "y", bit)
 
-    columns, goal, hot, count_rows, summed = tie(columns, goal, hot, count_rows, summed)
+    columns, goal, count_rows, summed = tie(columns, goal, count_rows, summed)
     partial, *step_rows = project(columns, weights, count_rows, groups)
 
     master = weights[0].astype(f32)
     first = adam_m[0].astype(f32)
     second = adam_v[0].astype(f32)
-    loss_rows, inverse = [], None
+    loss_rows, weight = [], None
     for step in range(steps_total):
         rows_now = step_rows[step]
         if step == 1:
@@ -261,9 +263,9 @@
             partial, summed, other = tie(partial, summed, other)
         own = jnp.sum(partial.astype(f32), axis=0) - goal[step]
         got = swap(own.astype(bf16), "zf")
-        sent = errors(own, got, hot[step], inverse, groups, scale)
+        sent = errors(own, got, weight, tokens, groups, scale)
         if step == 0:
-            sent, inverse = sent
+            sent, weight = sent
             sent, summed = tie(sent, summed)
         got = exchange(sent, GROUP)
         if step == 0:

time: 202 us -> 176 us (0.87)
  waiting for transfers between devices: 100 us -> 77.9 us
  starting transfers between devices: 57.8 us -> 52.4 us
  blocking collectives: 16.9 us -> 19.8 us
    ppermute x9 -> x8, waiting for transfers between devices: 80.3 us -> 47 us  [swap(): return lax.ppermute(block, axis, [(i, i ^ bit) for i in range(size)])]
    all_to_all x4, waiting for transfers between devices: 19.8 us -> 30.9 us  [exchange(): lax.all_to_all(blocks, axes, split_axis=0, concat_axis=0, tiled=False)]
    ppermute x9 -> x8, starting transfers between devices: 34.1 us -> 28.6 us  [swap(): return lax.ppermute(block, axis, [(i, i ^ bit) for i in range(size)])]
    all_to_all x1, blocking collectives: 16.9 us -> 19.8 us  [exchange(): lax.all_to_all(blocks, axes, split_axis=0, concat_axis=0, tiled=False)]
  transfers between devices with their start and end apart: 13 -> 12, of which waited for: 10 -> 11; matrix products, arithmetic and copies ran while one was open for 1% -> 3% of each run, Pallas kernels for 0% -> 0%
where the time goes in v9:
time: 176 us; the launch traced here: 175 us
  waiting for transfers between devices  77.9 us (44%)
  starting transfers between devices  52.4 us (30%)
  blocking collectives  19.8 us (11%)
  Pallas kernels  7.03 us (4%)
  local copies, waits for them, and re-layouts  5.81 us (3%)
  matrix products  5.17 us (3%)
  other arithmetic  4.89 us (3%)
    ppermute x8, waiting for transfers between devices, swap(): return lax.ppermute(block, axis, [(i, i ^ bit) for i in range(size)])  47 us
    all_to_all x4, waiting for transfers between devices, exchange(): lax.all_to_all(blocks, axes, split_axis=0, concat_axis=0, tiled=False)  30.9 us
    ppermute x8, starting transfers between devices, swap(): return lax.ppermute(block, axis, [(i, i ^ bit) for i in range(size)])  28.6 us
    all_to_all x4, starting transfers between devices, exchange(): lax.all_to_all(blocks, axes, split_axis=0, concat_axis=0, tiled=False)  23.8 us
    all_to_all x1, blocking collectives, exchange(): lax.all_to_all(blocks, axes, split_axis=0, concat_axis=0, tiled=False)  19.8 us
    unnamed x35, local copies, waits for them, and re-layouts  3.53 us
  transfers between devices with their start and end apart: 12, of which 11 were waited for; matrix products, arithmetic and copies ran while one was open for 3% of the time, Pallas kernels for 0%

profile of v9, /device:TPU:56, one launch (start us, length us, event | category | flops | bytes accessed | tf_op | source)
XLA Modules:
  0.0 174.6 jit_solution(6379320919188244837)
XLA Ops:
  0.6 3.0 %normalize.1 = bf16[16,2,64,512]{3,2,1,0:T(8,128)(2,1)} custom-call(bf16[1,2,64,8192]{3,2,1,0:T(8,128)(2,1)} %hidden_ref.1), custom_call_target="tpu_custom_call" | custom-call | tf_op jit(solution)/shard_map/normalize/pallas_call | solution.py:97
  3.6 10.0 %all-to-all-start = ((bf16[16,2,64,512]{3,2,1,0:T(8,128)(2,1)}), bf16[16,2,64,512]{3,2,1,0:T(8,128)(2,1)S(1)}, u32[]{:S(2)}, u32[]{:S(2)}) async-start(bf16[16,2,64,512]{3,2,1,0:T(8,128)(2,1)} %normalize.1), calls=%async_computation | async-start | bytes 4194304 | tf_op jit(solution)/shard_map/all_to_all | solution.py:43
  14.3 1.9 %collective-permute-start = (bf16[256,128]{1,0:T(8,128)(2,1)S(1)}, bf16[256,128]{1,0:T(8,128)(2,1)}, u32[]{:S(2)}, u32[]{:S(2)}) collective-permute-start(bf16[256,128]{1,0:T(8,128)(2,1)S(1)} %dynamic-slice_bitcast_fusion), channel_id=1, source_target_pairs={{0,16},{16,0},{1,17},{17,1},{2,18},{18,2},{3,19},{19,3},{4,20},{20... | collective-permute-start | bytes 196616 | tf_op jit(solution)/shard_map/ppermute | solution.py:48
  18.5 3.3 %collective-permute-start.1 = (f32[256,128]{1,0:T(8,128)S(1)}, f32[256,128]{1,0:T(8,128)S(1)}, u32[]{:S(2)}, u32[]{:S(2)}) collective-permute-start(f32[256,128]{1,0:T(8,128)S(1)} %convert_add_fusion), channel_id=1, source_target_pairs={{0,32},{32,0},{64,96},{96,64},{128,160},{160,128},{192,224},{224,1... | collective-permute-start | bytes 393224 | tf_op jit(solution)/shard_map/ppermute | solution.py:48
  21.8 4.2 %collective-permute-done.1 = f32[256,128]{1,0:T(8,128)S(1)} collective-permute-done((f32[256,128]{1,0:T(8,128)S(1)}, f32[256,128]{1,0:T(8,128)S(1)}, u32[]{:S(2)}, u32[]{:S(2)}) %collective-permute-start.1) | collective-permute-done | bytes 131104 | tf_op jit(solution)/shard_map/ppermute | solution.py:48
  26.0 4.0 %collective-permute-start.2 = (f32[256,128]{1,0:T(8,128)S(1)}, f32[256,128]{1,0:T(8,128)S(1)}, u32[]{:S(2)}, u32[]{:S(2)}) collective-permute-start(f32[256,128]{1,0:T(8,128)S(1)} %add.69), channel_id=1, source_target_pairs={{0,64},{32,96},{64,0},{96,32},{128,192},{160,224},{192,128},{224,1... | collective-permute-start | bytes 393224 | tf_op jit(solution)/shard_map/ppermute | solution.py:48
  30.8 5.5 %collective-permute-done.2 = f32[256,128]{1,0:T(8,128)S(1)} collective-permute-done((f32[256,128]{1,0:T(8,128)S(1)}, f32[256,128]{1,0:T(8,128)S(1)}, u32[]{:S(2)}, u32[]{:S(2)}) %collective-permute-start.2) | collective-permute-done | bytes 131104 | tf_op jit(solution)/shard_map/ppermute | solution.py:48
  36.3 4.6 %collective-permute-start.3 = (f32[256,128]{1,0:T(8,128)S(1)}, f32[256,128]{1,0:T(8,128)}, u32[]{:S(2)}, u32[]{:S(2)}) collective-permute-start(f32[256,128]{1,0:T(8,128)S(1)} %add.70), channel_id=1, source_target_pairs={{0,128},{32,160},{64,192},{96,224},{128,0},{160,32},{192,64},{224,... | collective-permute-start | bytes 393224 | tf_op jit(solution)/shard_map/ppermute | solution.py:48
  42.1 7.5 %collective-permute-done.3 = f32[256,128]{1,0:T(8,128)} collective-permute-done((f32[256,128]{1,0:T(8,128)S(1)}, f32[256,128]{1,0:T(8,128)}, u32[]{:S(2)}, u32[]{:S(2)}) %collective-permute-start.3) | collective-permute-done | bytes 131104 | tf_op jit(solution)/shard_map/ppermute | solution.py:48
  50.5 11.2 %all-to-all-done.columns_ref = bf16[16,2,64,512]{3,2,1,0:T(8,128)(2,1)S(1)} async-done(((bf16[16,2,64,512]{3,2,1,0:T(8,128)(2,1)}), bf16[16,2,64,512]{3,2,1,0:T(8,128)(2,1)S(1)}, u32[]{:S(2)}, u32[]{:S(2)}) %all-to-all-start) | async-done | bytes 2097184 | tf_op jit(solution)/shard_map/all_to_all | solution.py:43
  63.3 19.8 %all_to_all.25 = bf16[8,144,512]{2,1,0:T(8,128)(2,1)S(1)} all-to-all(bf16[8,144,512]{2,1,0:T(8,128)(2,1)S(1)} %get-tuple-element.32), channel_id=1, replica_groups=mesh['zh'=2,'y'=8,'c'=2,'x'=4,'zf'=2,'zn'=2] {'x','zn'}, dimensions={0} | all-to-all | bytes 2359296 | tf_op jit(solution)/shard_map/all_to_all | solution.py:43
  83.3 2.6 %collective-permute-start.4 = (bf16[144,512]{1,0:T(8,128)(2,1)S(1)}, bf16[144,512]{1,0:T(8,128)(2,1)S(1)}, u32[]{:S(2)}, u32[]{:S(2)}) collective-permute-start(bf16[144,512]{1,0:T(8,128)(2,1)S(1)} %get-tuple-element.50), channel_id=1, source_target_pairs={{0,2},{2,0},{1,3},{3,1},{4,6},{6,4},{5,7},{7,5},{8,10},{10,8},{9,1... | collective-permute-start | bytes 442376 | tf_op jit(solution)/shard_map/ppermute | solution.py:48
  85.8 6.9 %collective-permute-done.4.got_ref = bf16[144,512]{1,0:T(8,128)(2,1)S(1)} collective-permute-done((bf16[144,512]{1,0:T(8,128)(2,1)S(1)}, bf16[144,512]{1,0:T(8,128)(2,1)S(1)}, u32[]{:S(2)}, u32[]{:S(2)}) %collective-permute-start.4) | collective-permute-done | bytes 147488 | tf_op jit(solution)/shard_map/ppermute | solution.py:48
  94.1 4.3 %all-to-all-start.2 = ((bf16[8,144,512]{2,1,0:T(8,128)(2,1)}), bf16[8,144,512]{2,1,0:T(8,128)(2,1)}, u32[]{:S(2)}, u32[]{:S(2)}) async-start(bf16[8,144,512]{2,1,0:T(8,128)(2,1)} %get-tuple-element.36), calls=%async_computation.2 | async-start | bytes 2359296 | tf_op jit(solution)/shard_map/all_to_all | solution.py:43
  98.3 8.4 %collective-permute-start.5 = (f32[256,128]{1,0:T(8,128)S(1)}, f32[256,128]{1,0:T(8,128)S(1)}, u32[]{:S(2)}, u32[]{:S(2)}) collective-permute-start(f32[256,128]{1,0:T(8,128)S(1)} %add.71), channel_id=1, source_target_pairs={{0,256},{256,0},{1,257},{257,1},{2,258},{258,2},{3,259},{259,3},{4... | collective-permute-start | bytes 393224 | tf_op jit(solution)/shard_map/ppermute | solution.py:48
  106.7 13.0 %collective-permute-done.5 = f32[256,128]{1,0:T(8,128)S(1)} collective-permute-done((f32[256,128]{1,0:T(8,128)S(1)}, f32[256,128]{1,0:T(8,128)S(1)}, u32[]{:S(2)}, u32[]{:S(2)}) %collective-permute-start.5) | collective-permute-done | bytes 131104 | tf_op jit(solution)/shard_map/ppermute | solution.py:48
  122.6 2.3 %convolution_convert_fusion = bf16[1024,512]{1,0:T(8,128)(2,1)} fusion(bf16[1024,512]{1,0:T(8,128)(2,1)S(1)} %copy-done.2, f32[512,512]{1,0:T(8,128)S(1)} %fusion.14, bf16[1,512,512]{2,1,0:T(8,128)(2,1)S(1)} %copy-done.10, bf16[1,512,512]{2,1,0:T(8,128)(2,1)S(1)} %copy-done, bf16[1,512,512]{2,1,0:T(8,128)(2,1)S(1)} %copy-done.12), kind=kOutput, calls=%fused_computation.2 | convolution fusion | flops 542113792 | bytes 4718592 | tf_op jit(solution)/shard_map/dot_general | solution.py:257
  124.9 6.0 %all-to-all-start.3 = ((bf16[8,128,512]{2,1,0:T(8,128)(2,1)}), bf16[8,128,512]{2,1,0:T(8,128)(2,1)S(1)}, u32[]{:S(2)}, u32[]{:S(2)}) async-start(bf16[8,128,512]{2,1,0:T(8,128)(2,1)} %bitcast.69), calls=%async_computation.3 | async-start | bytes 2097152 | tf_op jit(solution)/shard_map/all_to_all | solution.py:43
  134.1 8.3 %all-to-all-done.3 = bf16[8,128,512]{2,1,0:T(8,128)(2,1)S(1)} async-done(((bf16[8,128,512]{2,1,0:T(8,128)(2,1)}), bf16[8,128,512]{2,1,0:T(8,128)(2,1)S(1)}, u32[]{:S(2)}, u32[]{:S(2)}) %all-to-all-start.3) | async-done | bytes 1048608 | tf_op jit(solution)/shard_map/all_to_all | solution.py:43
  142.6 1.9 %collective-permute-start.7 = (bf16[128,512]{1,0:T(8,128)(2,1)S(1)}, bf16[128,512]{1,0:T(8,128)(2,1)S(1)}, u32[]{:S(2)}, u32[]{:S(2)}) collective-permute-start(bf16[128,512]{1,0:T(8,128)(2,1)S(1)} %get-tuple-element.48), channel_id=1, source_target_pairs={{0,2},{2,0},{1,3},{3,1},{4,6},{6,4},{5,7},{7,5},{8,10},{10,8},{9,1... | collective-permute-start | bytes 393224 | tf_op jit(solution)/shard_map/ppermute | solution.py:48
  144.5 7.3 %collective-permute-done.7.got_ref = bf16[128,512]{1,0:T(8,128)(2,1)S(1)} collective-permute-done((bf16[128,512]{1,0:T(8,128)(2,1)S(1)}, bf16[128,512]{1,0:T(8,128)(2,1)S(1)}, u32[]{:S(2)}, u32[]{:S(2)}) %collective-permute-start.7) | collective-permute-done | bytes 131104 | tf_op jit(solution)/shard_map/ppermute | solution.py:48
  153.1 3.6 %all-to-all-start.4 = ((bf16[8,144,512]{2,1,0:T(8,128)(2,1)}), bf16[8,144,512]{2,1,0:T(8,128)(2,1)S(1)}, u32[]{:S(2)}, u32[]{:S(2)}) async-start(bf16[8,144,512]{2,1,0:T(8,128)(2,1)} %errors.3), calls=%async_computation.4 | async-start | bytes 2359296 | tf_op jit(solution)/shard_map/all_to_all | solution.py:43
  157.4 11.4 %all-to-all-done.4 = bf16[8,144,512]{2,1,0:T(8,128)(2,1)S(1)} async-done(((bf16[8,144,512]{2,1,0:T(8,128)(2,1)}), bf16[8,144,512]{2,1,0:T(8,128)(2,1)S(1)}, u32[]{:S(2)}, u32[]{:S(2)}) %all-to-all-start.4) | async-done | bytes 1179680 | tf_op jit(solution)/shard_map/all_to_all | solution.py:43
  170.4 2.1 %multiply_subtract_fusion = f32[512,512]{1,0:T(8,128)S(1)} fusion(f32[512,512]{1,0:T(8,128)S(1)} %copy-done.15, bf16[1,512,512]{2,1,0:T(8,128)(2,1)S(1)} %copy-done.11, bf16[1,512,512]{2,1,0:T(8,128)(2,1)S(1)} %copy-done.13, bf16[1,512,512]{2,1,0:T(8,128)(2,1)S(1)} %copy-done, bf16[1024,512]{1,0:T(8,128)(2,1)S(1)} %copy-done.2, ...), kind=kOutput, calls=%fused_computation.9 | convolution fusion | flops 544997376 | bytes 5767168 | tf_op jit(solution)/shard_map/dot_general | solution.py:277
  (69 shorter events, 20.0 us)
Async XLA Ops:
  3.6 10.7 %copy-start = (bf16[1,512,512]{2,1,0:T(8,128)(2,1)S(1)}, bf16[1,512,512]{2,1,0:T(8,128)(2,1)}, u32[]{:S(2)}) copy-start(bf16[1,512,512]{2,1,0:T(8,128)(2,1)} %weights_ref) | copy-start | bytes 1572868
  3.6 12.7 %copy-start.6 = (bf16[1,2,64,512]{3,2,1,0:T(8,128)(2,1)S(1)}, bf16[1,2,64,512]{3,2,1,0:T(8,128)(2,1)}, u32[]{:S(2)}) copy-start(bf16[1,2,64,512]{3,2,1,0:T(8,128)(2,1)} %param.10) | copy-start | bytes 393220
  3.6 58.1 %all-to-all-start = ((bf16[16,2,64,512]{3,2,1,0:T(8,128)(2,1)}), bf16[16,2,64,512]{3,2,1,0:T(8,128)(2,1)S(1)}, u32[]{:S(2)}, u32[]{:S(2)}) async-start(bf16[16,2,64,512]{3,2,1,0:T(8,128)(2,1)} %normalize.1), calls=%async_computation | async-start | bytes 4194304 | tf_op jit(solution)/shard_map/all_to_all | solution.py:43
  13.6 8.1 %copy-start.9 = (s32[1,2,64]{2,1,0:T(2,128)S(1)}, s32[1,2,64]{2,1,0:T(2,128)}, u32[]{:S(2)}) copy-start(s32[1,2,64]{2,1,0:T(2,128)} %param.11) | copy-start | bytes 1540
  14.3 3.3 %collective-permute-start = (bf16[256,128]{1,0:T(8,128)(2,1)S(1)}, bf16[256,128]{1,0:T(8,128)(2,1)}, u32[]{:S(2)}, u32[]{:S(2)}) collective-permute-start(bf16[256,128]{1,0:T(8,128)(2,1)S(1)} %dynamic-slice_bitcast_fusion), channel_id=1, source_target_pairs={{0,16},{16,0},{1,17},{17,1},{2,18},{18,2},{3,19},{19,3},{4,20},{20... | collective-permute-start | bytes 196616 | tf_op jit(solution)/shard_map/ppermute | solution.py:48
  18.5 7.5 %collective-permute-start.1 = (f32[256,128]{1,0:T(8,128)S(1)}, f32[256,128]{1,0:T(8,128)S(1)}, u32[]{:S(2)}, u32[]{:S(2)}) collective-permute-start(f32[256,128]{1,0:T(8,128)S(1)} %convert_add_fusion), channel_id=1, source_target_pairs={{0,32},{32,0},{64,96},{96,64},{128,160},{160,128},{192,224},{224,1... | collective-permute-start | bytes 393224 | tf_op jit(solution)/shard_map/ppermute | solution.py:48
  26.0 10.3 %collective-permute-start.2 = (f32[256,128]{1,0:T(8,128)S(1)}, f32[256,128]{1,0:T(8,128)S(1)}, u32[]{:S(2)}, u32[]{:S(2)}) collective-permute-start(f32[256,128]{1,0:T(8,128)S(1)} %add.69), channel_id=1, source_target_pairs={{0,64},{32,96},{64,0},{96,32},{128,192},{160,224},{192,128},{224,1... | collective-permute-start | bytes 393224 | tf_op jit(solution)/shard_map/ppermute | solution.py:48
  36.3 13.3 %collective-permute-start.3 = (f32[256,128]{1,0:T(8,128)S(1)}, f32[256,128]{1,0:T(8,128)}, u32[]{:S(2)}, u32[]{:S(2)}) collective-permute-start(f32[256,128]{1,0:T(8,128)S(1)} %add.70), channel_id=1, source_target_pairs={{0,128},{32,160},{64,192},{96,224},{128,0},{160,32},{192,64},{224,... | collective-permute-start | bytes 393224 | tf_op jit(solution)/shard_map/ppermute | solution.py:48
  63.2 19.8 %copy-start.1 = (bf16[1024,512]{1,0:T(8,128)(2,1)}, bf16[1024,512]{1,0:T(8,128)(2,1)S(1)}, u32[]{:S(2)}) copy-start(bf16[1024,512]{1,0:T(8,128)(2,1)S(1)} %get-tuple-element.39) | copy-start | bytes 3145732
  63.3 19.8 %copy-start.3 = (bf16[1024,512]{1,0:T(8,128)(2,1)}, bf16[1024,512]{1,0:T(8,128)(2,1)S(1)}, u32[]{:S(2)}) copy-start(bf16[1024,512]{1,0:T(8,128)(2,1)S(1)} %get-tuple-element.31) | copy-start | bytes 3145732
  83.3 9.5 %collective-permute-start.4 = (bf16[144,512]{1,0:T(8,128)(2,1)S(1)}, bf16[144,512]{1,0:T(8,128)(2,1)S(1)}, u32[]{:S(2)}, u32[]{:S(2)}) collective-permute-start(bf16[144,512]{1,0:T(8,128)(2,1)S(1)} %get-tuple-element.50), channel_id=1, source_target_pairs={{0,2},{2,0},{1,3},{3,1},{4,6},{6,4},{5,7},{7,5},{8,10},{10,8},{9,1... | collective-permute-start | bytes 442376 | tf_op jit(solution)/shard_map/ppermute | solution.py:48
  94.1 25.7 %all-to-all-start.2 = ((bf16[8,144,512]{2,1,0:T(8,128)(2,1)}), bf16[8,144,512]{2,1,0:T(8,128)(2,1)}, u32[]{:S(2)}, u32[]{:S(2)}) async-start(bf16[8,144,512]{2,1,0:T(8,128)(2,1)} %get-tuple-element.36), calls=%async_computation.2 | async-start | bytes 2359296 | tf_op jit(solution)/shard_map/all_to_all | solution.py:43
  98.3 22.7 %copy-start.4 = (bf16[1024,512]{1,0:T(8,128)(2,1)S(1)}, bf16[1024,512]{1,0:T(8,128)(2,1)}, u32[]{:S(2)}) copy-start(bf16[1024,512]{1,0:T(8,128)(2,1)} %copy-done.3) | copy-start | bytes 3145732
  98.3 21.4 %collective-permute-start.5 = (f32[256,128]{1,0:T(8,128)S(1)}, f32[256,128]{1,0:T(8,128)S(1)}, u32[]{:S(2)}, u32[]{:S(2)}) collective-permute-start(f32[256,128]{1,0:T(8,128)S(1)} %add.71), channel_id=1, source_target_pairs={{0,256},{256,0},{1,257},{257,1},{2,258},{258,2},{3,259},{259,3},{4... | collective-permute-start | bytes 393224 | tf_op jit(solution)/shard_map/ppermute | solution.py:48
  121.1 1.2 copy-start.2
  121.1 1.3 copy-start.10
  121.1 1.5 copy-start.12
  121.8 3.1 %copy-start.14 = (f32[512,512]{1,0:T(8,128)}, f32[512,512]{1,0:T(8,128)S(1)}, u32[]{:S(2)}) copy-start(f32[512,512]{1,0:T(8,128)S(1)} %fusion.14) | copy-start | bytes 3145732
  124.9 17.5 %all-to-all-start.3 = ((bf16[8,128,512]{2,1,0:T(8,128)(2,1)}), bf16[8,128,512]{2,1,0:T(8,128)(2,1)S(1)}, u32[]{:S(2)}, u32[]{:S(2)}) async-start(bf16[8,128,512]{2,1,0:T(8,128)(2,1)} %bitcast.69), calls=%async_computation.3 | async-start | bytes 2097152 | tf_op jit(solution)/shard_map/all_to_all | solution.py:43
  130.9 3.2 %collective-permute-start.6 = (f32[256,128]{1,0:T(8,128)S(1)}, f32[256,128]{1,0:T(8,128)S(1)}, u32[]{:S(2)}, u32[]{:S(2)}) collective-permute-start(f32[256,128]{1,0:T(8,128)S(1)} %add.72), channel_id=1, source_target_pairs={{0,16},{16,0},{1,17},{17,1},{2,18},{18,2},{3,19},{19,3},{4,20},{20... | collective-permute-start | bytes 393224 | tf_op jit(solution)/shard_map/ppermute | solution.py:48
  142.6 9.2 %collective-permute-start.7 = (bf16[128,512]{1,0:T(8,128)(2,1)S(1)}, bf16[128,512]{1,0:T(8,128)(2,1)S(1)}, u32[]{:S(2)}, u32[]{:S(2)}) collective-permute-start(bf16[128,512]{1,0:T(8,128)(2,1)S(1)} %get-tuple-element.48), channel_id=1, source_target_pairs={{0,2},{2,0},{1,3},{3,1},{4,6},{6,4},{5,7},{7,5},{8,10},{10,8},{9,1... | collective-permute-start | bytes 393224 | tf_op jit(solution)/shard_map/ppermute | solution.py:48
  153.1 15.7 %all-to-all-start.4 = ((bf16[8,144,512]{2,1,0:T(8,128)(2,1)}), bf16[8,144,512]{2,1,0:T(8,128)(2,1)S(1)}, u32[]{:S(2)}, u32[]{:S(2)}) async-start(bf16[8,144,512]{2,1,0:T(8,128)(2,1)} %errors.3), calls=%async_computation.4 | async-start | bytes 2359296 | tf_op jit(solution)/shard_map/all_to_all | solution.py:43
  168.9 1.2 copy-start.13
  168.9 1.5 copy-start.15
  (4 other events, 3.9 us)

commit v10 on v9

--- a/solution.py
+++ b/solution.py
@@ -241,8 +241,8 @@
     local = lax.dynamic_slice(weights[0], (zero, start), (shard_rows, frag_width))
     local = local.reshape(2, half, frag_width)
     summed = pick(local, c_at, 0).astype(f32) + swap(pick(local, c_at ^ 1, 0), "c").astype(f32)
-    for bit in (1, 2, 4):
-        summed = summed + swap(summed, "y", bit)
+    for axis, bit in (("y", 1), ("y", 2), ("zh", 1)):
+        summed = summed + swap(summed, axis, bit)
 
     columns, goal, count_rows, summed = tie(columns, goal, count_rows, summed)
     partial, *step_rows = project(columns, weights, count_rows, groups)
@@ -269,7 +269,7 @@
             sent, summed = tie(sent, summed)
         got = exchange(sent, GROUP)
         if step == 0:
-            summed = summed + swap(summed, "zh")
+            summed = summed + swap(summed, "y", 4)
             got, summed = tie(got, summed)
         loss_rows.append(got[:, tokens, :128])
         everyone = got[:, :tokens].reshape(shards * rows, value_width)

time: 176 us -> 172 us (0.977)
  waiting for transfers between devices: 77.9 us -> 75.4 us
    all_to_all x4, waiting for transfers between devices: 30.9 us -> 27.2 us  [exchange(): lax.all_to_all(blocks, axes, split_axis=0, concat_axis=0, tiled=False)]
  transfers between devices with their start and end apart: 12 -> 12, of which waited for: 11 -> 12; matrix products, arithmetic and copies ran while one was open for 3% -> 3% of each run, Pallas kernels for 0% -> 0%
where the time goes in v10:
time: 172 us; the launch traced here: 171 us
  waiting for transfers between devices  75.4 us (44%)
  starting transfers between devices  51 us (30%)
  blocking collectives  19.8 us (12%)
  Pallas kernels  7.03 us (4%)
  local copies, waits for them, and re-layouts  5.81 us (3%)
  matrix products  5.16 us (3%)
  other arithmetic  4.89 us (3%)
    ppermute x8, waiting for transfers between devices, swap(): return lax.ppermute(block, axis, [(i, i ^ bit) for i in range(size)])  48.3 us
    ppermute x8, starting transfers between devices, swap(): return lax.ppermute(block, axis, [(i, i ^ bit) for i in range(size)])  28.7 us
    all_to_all x4, waiting for transfers between devices, exchange(): lax.all_to_all(blocks, axes, split_axis=0, concat_axis=0, tiled=False)  27.2 us
    all_to_all x4, starting transfers between devices, exchange(): lax.all_to_all(blocks, axes, split_axis=0, concat_axis=0, tiled=False)  22.3 us
    all_to_all x1, blocking collectives, exchange(): lax.all_to_all(blocks, axes, split_axis=0, concat_axis=0, tiled=False)  19.8 us
    unnamed x35, local copies, waits for them, and re-layouts  3.53 us
  transfers between devices with their start and end apart: 12, of which 12 were waited for; matrix products, arithmetic and copies ran while one was open for 3% of the time, Pallas kernels for 0%

profile of v10, /device:TPU:56, one launch (start us, length us, event | category | flops | bytes accessed | tf_op | source)
XLA Modules:
  0.0 170.8 jit_solution(6414260059002914913)
XLA Ops:
  0.6 3.0 %normalize.1 = bf16[16,2,64,512]{3,2,1,0:T(8,128)(2,1)} custom-call(bf16[1,2,64,8192]{3,2,1,0:T(8,128)(2,1)} %hidden_ref.1), custom_call_target="tpu_custom_call" | custom-call | tf_op jit(solution)/shard_map/normalize/pallas_call | solution.py:97
  3.6 10.0 %all-to-all-start = ((bf16[16,2,64,512]{3,2,1,0:T(8,128)(2,1)}), bf16[16,2,64,512]{3,2,1,0:T(8,128)(2,1)S(1)}, u32[]{:S(2)}, u32[]{:S(2)}) async-start(bf16[16,2,64,512]{3,2,1,0:T(8,128)(2,1)} %normalize.1), calls=%async_computation | async-start | bytes 4194304 | tf_op jit(solution)/shard_map/all_to_all | solution.py:43
  14.3 1.9 %collective-permute-start = (bf16[256,128]{1,0:T(8,128)(2,1)S(1)}, bf16[256,128]{1,0:T(8,128)(2,1)}, u32[]{:S(2)}, u32[]{:S(2)}) collective-permute-start(bf16[256,128]{1,0:T(8,128)(2,1)S(1)} %dynamic-slice_bitcast_fusion), channel_id=1, source_target_pairs={{0,16},{16,0},{1,17},{17,1},{2,18},{18,2},{3,19},{19,3},{4,20},{20... | collective-permute-start | bytes 196616 | tf_op jit(solution)/shard_map/ppermute | solution.py:48
  18.5 3.3 %collective-permute-start.1 = (f32[256,128]{1,0:T(8,128)S(1)}, f32[256,128]{1,0:T(8,128)S(1)}, u32[]{:S(2)}, u32[]{:S(2)}) collective-permute-start(f32[256,128]{1,0:T(8,128)S(1)} %convert_add_fusion), channel_id=1, source_target_pairs={{0,32},{32,0},{64,96},{96,64},{128,160},{160,128},{192,224},{224,1... | collective-permute-start | bytes 393224 | tf_op jit(solution)/shard_map/ppermute | solution.py:48
  21.8 4.2 %collective-permute-done.1 = f32[256,128]{1,0:T(8,128)S(1)} collective-permute-done((f32[256,128]{1,0:T(8,128)S(1)}, f32[256,128]{1,0:T(8,128)S(1)}, u32[]{:S(2)}, u32[]{:S(2)}) %collective-permute-start.1) | collective-permute-done | bytes 131104 | tf_op jit(solution)/shard_map/ppermute | solution.py:48
  26.0 4.0 %collective-permute-start.2 = (f32[256,128]{1,0:T(8,128)S(1)}, f32[256,128]{1,0:T(8,128)S(1)}, u32[]{:S(2)}, u32[]{:S(2)}) collective-permute-start(f32[256,128]{1,0:T(8,128)S(1)} %add.69), channel_id=1, source_target_pairs={{0,64},{32,96},{64,0},{96,32},{128,192},{160,224},{192,128},{224,1... | collective-permute-start | bytes 393224 | tf_op jit(solution)/shard_map/ppermute | solution.py:48
  30.8 5.5 %collective-permute-done.2 = f32[256,128]{1,0:T(8,128)S(1)} collective-permute-done((f32[256,128]{1,0:T(8,128)S(1)}, f32[256,128]{1,0:T(8,128)S(1)}, u32[]{:S(2)}, u32[]{:S(2)}) %collective-permute-start.2) | collective-permute-done | bytes 131104 | tf_op jit(solution)/shard_map/ppermute | solution.py:48
  36.3 8.2 %collective-permute-start.3 = (f32[256,128]{1,0:T(8,128)S(1)}, f32[256,128]{1,0:T(8,128)}, u32[]{:S(2)}, u32[]{:S(2)}) collective-permute-start(f32[256,128]{1,0:T(8,128)S(1)} %add.70), channel_id=1, source_target_pairs={{0,256},{256,0},{1,257},{257,1},{2,258},{258,2},{3,259},{259,3},{4... | collective-permute-start | bytes 393224 | tf_op jit(solution)/shard_map/ppermute | solution.py:48
  45.7 14.4 %collective-permute-done.3 = f32[256,128]{1,0:T(8,128)} collective-permute-done((f32[256,128]{1,0:T(8,128)S(1)}, f32[256,128]{1,0:T(8,128)}, u32[]{:S(2)}, u32[]{:S(2)}) %collective-permute-start.3) | collective-permute-done | bytes 131104 | tf_op jit(solution)/shard_map/ppermute | solution.py:48
  61.0 6.3 %all-to-all-done.columns_ref = bf16[16,2,64,512]{3,2,1,0:T(8,128)(2,1)S(1)} async-done(((bf16[16,2,64,512]{3,2,1,0:T(8,128)(2,1)}), bf16[16,2,64,512]{3,2,1,0:T(8,128)(2,1)S(1)}, u32[]{:S(2)}, u32[]{:S(2)}) %all-to-all-start) | async-done | bytes 2097184 | tf_op jit(solution)/shard_map/all_to_all | solution.py:43
  68.9 19.8 %all_to_all.25 = bf16[8,144,512]{2,1,0:T(8,128)(2,1)S(1)} all-to-all(bf16[8,144,512]{2,1,0:T(8,128)(2,1)S(1)} %get-tuple-element.32), channel_id=1, replica_groups=mesh['zh'=2,'y'=8,'c'=2,'x'=4,'zf'=2,'zn'=2] {'x','zn'}, dimensions={0} | all-to-all | bytes 2359296 | tf_op jit(solution)/shard_map/all_to_all | solution.py:43
  88.9 2.6 %collective-permute-start.4 = (bf16[144,512]{1,0:T(8,128)(2,1)S(1)}, bf16[144,512]{1,0:T(8,128)(2,1)S(1)}, u32[]{:S(2)}, u32[]{:S(2)}) collective-permute-start(bf16[144,512]{1,0:T(8,128)(2,1)S(1)} %get-tuple-element.50), channel_id=1, source_target_pairs={{0,2},{2,0},{1,3},{3,1},{4,6},{6,4},{5,7},{7,5},{8,10},{10,8},{9,1... | collective-permute-start | bytes 442376 | tf_op jit(solution)/shard_map/ppermute | solution.py:48
  91.5 6.9 %collective-permute-done.4.got_ref = bf16[144,512]{1,0:T(8,128)(2,1)S(1)} collective-permute-done((bf16[144,512]{1,0:T(8,128)(2,1)S(1)}, bf16[144,512]{1,0:T(8,128)(2,1)S(1)}, u32[]{:S(2)}, u32[]{:S(2)}) %collective-permute-start.4) | collective-permute-done | bytes 147488 | tf_op jit(solution)/shard_map/ppermute | solution.py:48
  99.7 4.3 %all-to-all-start.2 = ((bf16[8,144,512]{2,1,0:T(8,128)(2,1)}), bf16[8,144,512]{2,1,0:T(8,128)(2,1)}, u32[]{:S(2)}, u32[]{:S(2)}) async-start(bf16[8,144,512]{2,1,0:T(8,128)(2,1)} %get-tuple-element.36), calls=%async_computation.2 | async-start | bytes 2359296 | tf_op jit(solution)/shard_map/all_to_all | solution.py:43
  104.0 4.8 %collective-permute-start.5 = (f32[256,128]{1,0:T(8,128)S(1)}, f32[256,128]{1,0:T(8,128)S(1)}, u32[]{:S(2)}, u32[]{:S(2)}) collective-permute-start(f32[256,128]{1,0:T(8,128)S(1)} %add.71), channel_id=1, source_target_pairs={{0,128},{32,160},{64,192},{96,224},{128,0},{160,32},{192,64},{224,... | collective-permute-start | bytes 393224 | tf_op jit(solution)/shard_map/ppermute | solution.py:48
  108.8 7.5 %collective-permute-done.5 = f32[256,128]{1,0:T(8,128)S(1)} collective-permute-done((f32[256,128]{1,0:T(8,128)S(1)}, f32[256,128]{1,0:T(8,128)S(1)}, u32[]{:S(2)}, u32[]{:S(2)}) %collective-permute-start.5) | collective-permute-done | bytes 131104 | tf_op jit(solution)/shard_map/ppermute | solution.py:48
  120.2 2.3 %convolution_convert_fusion = bf16[1024,512]{1,0:T(8,128)(2,1)} fusion(bf16[1024,512]{1,0:T(8,128)(2,1)S(1)} %copy-done.2, f32[512,512]{1,0:T(8,128)S(1)} %fusion.14, bf16[1,512,512]{2,1,0:T(8,128)(2,1)S(1)} %copy-done.10, bf16[1,512,512]{2,1,0:T(8,128)(2,1)S(1)} %copy-done, bf16[1,512,512]{2,1,0:T(8,128)(2,1)S(1)} %copy-done.12), kind=kOutput, calls=%fused_computation.2 | convolution fusion | flops 542113792 | bytes 4718592 | tf_op jit(solution)/shard_map/dot_general | solution.py:257
  122.5 4.5 %all-to-all-start.3 = ((bf16[8,128,512]{2,1,0:T(8,128)(2,1)}), bf16[8,128,512]{2,1,0:T(8,128)(2,1)S(1)}, u32[]{:S(2)}, u32[]{:S(2)}) async-start(bf16[8,128,512]{2,1,0:T(8,128)(2,1)} %bitcast.69), calls=%async_computation.3 | async-start | bytes 2097152 | tf_op jit(solution)/shard_map/all_to_all | solution.py:43
  130.3 8.3 %all-to-all-done.3 = bf16[8,128,512]{2,1,0:T(8,128)(2,1)S(1)} async-done(((bf16[8,128,512]{2,1,0:T(8,128)(2,1)}), bf16[8,128,512]{2,1,0:T(8,128)(2,1)S(1)}, u32[]{:S(2)}, u32[]{:S(2)}) %all-to-all-start.3) | async-done | bytes 1048608 | tf_op jit(solution)/shard_map/all_to_all | solution.py:43
  138.8 1.9 %collective-permute-start.7 = (bf16[128,512]{1,0:T(8,128)(2,1)S(1)}, bf16[128,512]{1,0:T(8,128)(2,1)S(1)}, u32[]{:S(2)}, u32[]{:S(2)}) collective-permute-start(bf16[128,512]{1,0:T(8,128)(2,1)S(1)} %get-tuple-element.48), channel_id=1, source_target_pairs={{0,2},{2,0},{1,3},{3,1},{4,6},{6,4},{5,7},{7,5},{8,10},{10,8},{9,1... | collective-permute-start | bytes 393224 | tf_op jit(solution)/shard_map/ppermute | solution.py:48
  140.7 7.3 %collective-permute-done.7.got_ref = bf16[128,512]{1,0:T(8,128)(2,1)S(1)} collective-permute-done((bf16[128,512]{1,0:T(8,128)(2,1)S(1)}, bf16[128,512]{1,0:T(8,128)(2,1)S(1)}, u32[]{:S(2)}, u32[]{:S(2)}) %collective-permute-start.7) | collective-permute-done | bytes 131104 | tf_op jit(solution)/shard_map/ppermute | solution.py:48
  149.3 3.6 %all-to-all-start.4 = ((bf16[8,144,512]{2,1,0:T(8,128)(2,1)}), bf16[8,144,512]{2,1,0:T(8,128)(2,1)S(1)}, u32[]{:S(2)}, u32[]{:S(2)}) async-start(bf16[8,144,512]{2,1,0:T(8,128)(2,1)} %errors.3), calls=%async_computation.4 | async-start | bytes 2359296 | tf_op jit(solution)/shard_map/all_to_all | solution.py:43
  153.6 11.4 %all-to-all-done.4 = bf16[8,144,512]{2,1,0:T(8,128)(2,1)S(1)} async-done(((bf16[8,144,512]{2,1,0:T(8,128)(2,1)}), bf16[8,144,512]{2,1,0:T(8,128)(2,1)S(1)}, u32[]{:S(2)}, u32[]{:S(2)}) %all-to-all-start.4) | async-done | bytes 1179680 | tf_op jit(solution)/shard_map/all_to_all | solution.py:43
  166.6 2.1 %multiply_subtract_fusion = f32[512,512]{1,0:T(8,128)S(1)} fusion(f32[512,512]{1,0:T(8,128)S(1)} %copy-done.15, bf16[1,512,512]{2,1,0:T(8,128)(2,1)S(1)} %copy-done.11, bf16[1,512,512]{2,1,0:T(8,128)(2,1)S(1)} %copy-done.13, bf16[1,512,512]{2,1,0:T(8,128)(2,1)S(1)} %copy-done, bf16[1024,512]{1,0:T(8,128)(2,1)S(1)} %copy-done.2, ...), kind=kOutput, calls=%fused_computation.9 | convolution fusion | flops 544997376 | bytes 5767168 | tf_op jit(solution)/shard_map/dot_general | solution.py:277
  (69 shorter events, 21.1 us)
Async XLA Ops:
  3.6 10.7 %copy-start = (bf16[1,512,512]{2,1,0:T(8,128)(2,1)S(1)}, bf16[1,512,512]{2,1,0:T(8,128)(2,1)}, u32[]{:S(2)}) copy-start(bf16[1,512,512]{2,1,0:T(8,128)(2,1)} %weights_ref) | copy-start | bytes 1572868
  3.6 12.7 %copy-start.6 = (bf16[1,2,64,512]{3,2,1,0:T(8,128)(2,1)S(1)}, bf16[1,2,64,512]{3,2,1,0:T(8,128)(2,1)}, u32[]{:S(2)}) copy-start(bf16[1,2,64,512]{3,2,1,0:T(8,128)(2,1)} %param.10) | copy-start | bytes 393220
  3.6 63.7 %all-to-all-start = ((bf16[16,2,64,512]{3,2,1,0:T(8,128)(2,1)}), bf16[16,2,64,512]{3,2,1,0:T(8,128)(2,1)S(1)}, u32[]{:S(2)}, u32[]{:S(2)}) async-start(bf16[16,2,64,512]{3,2,1,0:T(8,128)(2,1)} %normalize.1), calls=%async_computation | async-start | bytes 4194304 | tf_op jit(solution)/shard_map/all_to_all | solution.py:43
  13.6 8.1 %copy-start.9 = (s32[1,2,64]{2,1,0:T(2,128)S(1)}, s32[1,2,64]{2,1,0:T(2,128)}, u32[]{:S(2)}) copy-start(s32[1,2,64]{2,1,0:T(2,128)} %param.11) | copy-start | bytes 1540
  14.3 3.3 %collective-permute-start = (bf16[256,128]{1,0:T(8,128)(2,1)S(1)}, bf16[256,128]{1,0:T(8,128)(2,1)}, u32[]{:S(2)}, u32[]{:S(2)}) collective-permute-start(bf16[256,128]{1,0:T(8,128)(2,1)S(1)} %dynamic-slice_bitcast_fusion), channel_id=1, source_target_pairs={{0,16},{16,0},{1,17},{17,1},{2,18},{18,2},{3,19},{19,3},{4,20},{20... | collective-permute-start | bytes 196616 | tf_op jit(solution)/shard_map/ppermute | solution.py:48
  18.5 7.5 %collective-permute-start.1 = (f32[256,128]{1,0:T(8,128)S(1)}, f32[256,128]{1,0:T(8,128)S(1)}, u32[]{:S(2)}, u32[]{:S(2)}) collective-permute-start(f32[256,128]{1,0:T(8,128)S(1)} %convert_add_fusion), channel_id=1, source_target_pairs={{0,32},{32,0},{64,96},{96,64},{128,160},{160,128},{192,224},{224,1... | collective-permute-start | bytes 393224 | tf_op jit(solution)/shard_map/ppermute | solution.py:48
  26.0 10.3 %collective-permute-start.2 = (f32[256,128]{1,0:T(8,128)S(1)}, f32[256,128]{1,0:T(8,128)S(1)}, u32[]{:S(2)}, u32[]{:S(2)}) collective-permute-start(f32[256,128]{1,0:T(8,128)S(1)} %add.69), channel_id=1, source_target_pairs={{0,64},{32,96},{64,0},{96,32},{128,192},{160,224},{192,128},{224,1... | collective-permute-start | bytes 393224 | tf_op jit(solution)/shard_map/ppermute | solution.py:48
  36.3 23.7 %collective-permute-start.3 = (f32[256,128]{1,0:T(8,128)S(1)}, f32[256,128]{1,0:T(8,128)}, u32[]{:S(2)}, u32[]{:S(2)}) collective-permute-start(f32[256,128]{1,0:T(8,128)S(1)} %add.70), channel_id=1, source_target_pairs={{0,256},{256,0},{1,257},{257,1},{2,258},{258,2},{3,259},{259,3},{4... | collective-permute-start | bytes 393224 | tf_op jit(solution)/shard_map/ppermute | solution.py:48
  68.9 19.8 %copy-start.1 = (bf16[1024,512]{1,0:T(8,128)(2,1)}, bf16[1024,512]{1,0:T(8,128)(2,1)S(1)}, u32[]{:S(2)}) copy-start(bf16[1024,512]{1,0:T(8,128)(2,1)S(1)} %get-tuple-element.39) | copy-start | bytes 3145732
  68.9 19.8 %copy-start.3 = (bf16[1024,512]{1,0:T(8,128)(2,1)}, bf16[1024,512]{1,0:T(8,128)(2,1)S(1)}, u32[]{:S(2)}) copy-start(bf16[1024,512]{1,0:T(8,128)(2,1)S(1)} %get-tuple-element.31) | copy-start | bytes 3145732
  88.9 9.5 %collective-permute-start.4 = (bf16[144,512]{1,0:T(8,128)(2,1)S(1)}, bf16[144,512]{1,0:T(8,128)(2,1)S(1)}, u32[]{:S(2)}, u32[]{:S(2)}) collective-permute-start(bf16[144,512]{1,0:T(8,128)(2,1)S(1)} %get-tuple-element.50), channel_id=1, source_target_pairs={{0,2},{2,0},{1,3},{3,1},{4,6},{6,4},{5,7},{7,5},{8,10},{10,8},{9,1... | collective-permute-start | bytes 442376 | tf_op jit(solution)/shard_map/ppermute | solution.py:48
  99.7 17.7 %all-to-all-start.2 = ((bf16[8,144,512]{2,1,0:T(8,128)(2,1)}), bf16[8,144,512]{2,1,0:T(8,128)(2,1)}, u32[]{:S(2)}, u32[]{:S(2)}) async-start(bf16[8,144,512]{2,1,0:T(8,128)(2,1)} %get-tuple-element.36), calls=%async_computation.2 | async-start | bytes 2359296 | tf_op jit(solution)/shard_map/all_to_all | solution.py:43
  103.9 14.8 %copy-start.4 = (bf16[1024,512]{1,0:T(8,128)(2,1)S(1)}, bf16[1024,512]{1,0:T(8,128)(2,1)}, u32[]{:S(2)}) copy-start(bf16[1024,512]{1,0:T(8,128)(2,1)} %copy-done.3) | copy-start | bytes 3145732
  104.0 12.3 %collective-permute-start.5 = (f32[256,128]{1,0:T(8,128)S(1)}, f32[256,128]{1,0:T(8,128)S(1)}, u32[]{:S(2)}, u32[]{:S(2)}) collective-permute-start(f32[256,128]{1,0:T(8,128)S(1)} %add.71), channel_id=1, source_target_pairs={{0,128},{32,160},{64,192},{96,224},{128,0},{160,32},{192,64},{224,... | collective-permute-start | bytes 393224 | tf_op jit(solution)/shard_map/ppermute | solution.py:48
  118.7 1.2 copy-start.2
  118.7 1.3 copy-start.10
  118.7 1.5 copy-start.12
  119.5 3.1 %copy-start.14 = (f32[512,512]{1,0:T(8,128)}, f32[512,512]{1,0:T(8,128)S(1)}, u32[]{:S(2)}) copy-start(f32[512,512]{1,0:T(8,128)S(1)} %fusion.14) | copy-start | bytes 3145732
  122.5 16.1 %all-to-all-start.3 = ((bf16[8,128,512]{2,1,0:T(8,128)(2,1)}), bf16[8,128,512]{2,1,0:T(8,128)(2,1)S(1)}, u32[]{:S(2)}, u32[]{:S(2)}) async-start(bf16[8,128,512]{2,1,0:T(8,128)(2,1)} %bitcast.69), calls=%async_computation.3 | async-start | bytes 2097152 | tf_op jit(solution)/shard_map/all_to_all | solution.py:43
  127.0 3.2 %collective-permute-start.6 = (f32[256,128]{1,0:T(8,128)S(1)}, f32[256,128]{1,0:T(8,128)S(1)}, u32[]{:S(2)}, u32[]{:S(2)}) collective-permute-start(f32[256,128]{1,0:T(8,128)S(1)} %add.72), channel_id=1, source_target_pairs={{0,16},{16,0},{1,17},{17,1},{2,18},{18,2},{3,19},{19,3},{4,20},{20... | collective-permute-start | bytes 393224 | tf_op jit(solution)/shard_map/ppermute | solution.py:48
  138.8 9.2 %collective-permute-start.7 = (bf16[128,512]{1,0:T(8,128)(2,1)S(1)}, bf16[128,512]{1,0:T(8,128)(2,1)S(1)}, u32[]{:S(2)}, u32[]{:S(2)}) collective-permute-start(bf16[128,512]{1,0:T(8,128)(2,1)S(1)} %get-tuple-element.48), channel_id=1, source_target_pairs={{0,2},{2,0},{1,3},{3,1},{4,6},{6,4},{5,7},{7,5},{8,10},{10,8},{9,1... | collective-permute-start | bytes 393224 | tf_op jit(solution)/shard_map/ppermute | solution.py:48
  149.3 15.7 %all-to-all-start.4 = ((bf16[8,144,512]{2,1,0:T(8,128)(2,1)}), bf16[8,144,512]{2,1,0:T(8,128)(2,1)S(1)}, u32[]{:S(2)}, u32[]{:S(2)}) async-start(bf16[8,144,512]{2,1,0:T(8,128)(2,1)} %errors.3), calls=%async_computation.4 | async-start | bytes 2359296 | tf_op jit(solution)/shard_map/all_to_all | solution.py:43
  165.0 1.2 copy-start.13
  165.0 1.5 copy-start.15
  (4 other events, 3.9 us)

commit v11 on v10

--- a/solution.py
+++ b/solution.py
@@ -241,8 +241,14 @@
     local = lax.dynamic_slice(weights[0], (zero, start), (shard_rows, frag_width))
     local = local.reshape(2, half, frag_width)
     summed = pick(local, c_at, 0).astype(f32) + swap(pick(local, c_at ^ 1, 0), "c").astype(f32)
-    for axis, bit in (("y", 1), ("y", 2), ("zh", 1)):
+    y_at = lax.rem(lax.axis_index("y"), 2)
+    summed = summed.reshape(2, half // 2, frag_width)
+    summed = pick(summed, y_at, 0) + swap(pick(summed, y_at ^ 1, 0), "y")
+    for axis, bit in (("y", 2), ("zh", 1)):
         summed = summed + swap(summed, axis, bit)
+
+    def whole(mine, other, at):
+        return jnp.concatenate([jnp.where(at == 0, mine, other), jnp.where(at == 0, other, mine)])
 
     columns, goal, count_rows, summed = tie(columns, goal, count_rows, summed)
     partial, *step_rows = project(columns, weights, count_rows, groups)
@@ -250,6 +256,7 @@
     master = weights[0].astype(f32)
     first = adam_m[0].astype(f32)
     second = adam_v[0].astype(f32)
+    anchor_rows = anchor.astype(f32)
     loss_rows, weight = [], None
     for step in range(steps_total):
         rows_now = step_rows[step]
@@ -259,18 +266,24 @@
             partial, summed = tie(partial, summed)
         partial = exchange(partial, GROUP)
         if step == 1:
-            other = swap(summed, "c")
-            partial, summed, other = tie(partial, summed, other)
+            summed = whole(summed, swap(summed, "y"), y_at)
+            partial, summed = tie(partial, summed)
         own = jnp.sum(partial.astype(f32), axis=0) - goal[step]
         got = swap(own.astype(bf16), "zf")
         sent = errors(own, got, weight, tokens, groups, scale)
         if step == 0:
             sent, weight = sent
-            sent, summed = tie(sent, summed)
+        sent, summed = tie(sent, summed)
         got = exchange(sent, GROUP)
         if step == 0:
             summed = summed + swap(summed, "y", 4)
             got, summed = tie(got, summed)
+        else:
+            summed = whole(summed, swap(summed, "c"), c_at)
+            mean_delta = anchor_rows - summed / replicas
+            new_moment = NESTEROV * momentum.astype(f32) + mean_delta
+            global_fragment = anchor_rows - OUTER_RATE * (mean_delta + NESTEROV * new_moment)
+            got, global_fragment = tie(got, global_fragment)
         loss_rows.append(got[:, tokens, :128])
         everyone = got[:, :tokens].reshape(shards * rows, value_width)
         gradient = (
@@ -281,13 +294,6 @@
         )
         master, first, second = adam_update(master, first, second, gradient)
 
-    anchor_rows = anchor.astype(f32)
-    summed = jnp.concatenate(
-        [jnp.where(c_at == 0, summed, other), jnp.where(c_at == 0, other, summed)], axis=0
-    )
-    mean_delta = anchor_rows - summed / replicas
-    new_moment = NESTEROV * momentum.astype(f32) + mean_delta
-    global_fragment = anchor_rows - OUTER_RATE * (mean_delta + NESTEROV * new_moment)
     merged = (
         MIXING * lax.dynamic_slice(master, (zero, start), (shard_rows, frag_width))
         + (1.0 - MIXING) * global_fragment

time: 172 us -> 168 us (0.977)
  waiting for transfers between devices: 75.4 us -> 71.8 us
  other arithmetic: 4.89 us -> 2.37 us
  starting transfers between devices: 51 us -> 53.5 us
    ppermute x8 -> x9, starting transfers between devices: 28.7 us -> 32 us  [swap(): return lax.ppermute(block, axis, [(i, i ^ bit) for i in range(size)])]
    all_to_all x4, waiting for transfers between devices: 27.2 us -> 24.4 us  [exchange(): lax.all_to_all(blocks, axes, split_axis=0, concat_axis=0, tiled=False)]
    ppermute x8 -> x9, waiting for transfers between devices: 48.3 us -> 47.4 us  [swap(): return lax.ppermute(block, axis, [(i, i ^ bit) for i in range(size)])]
    unnamed x35 -> x34, local copies, waits for them, and re-layouts: 3.53 us -> 3.28 us
  transfers between devices with their start and end apart: 12 -> 13, of which waited for: 12 -> 13; matrix products, arithmetic and copies ran while one was open for 3% -> 1% of each run, Pallas kernels for 0% -> 0%
where the time goes in v11:
time: 168 us; the launch traced here: 167 us
  waiting for transfers between devices  71.8 us (43%)
  starting transfers between devices  53.5 us (32%)
  blocking collectives  19.8 us (12%)
  Pallas kernels  7.01 us (4%)
  local copies, waits for them, and re-layouts  5.57 us (3%)
  matrix products  5.19 us (3%)
  other arithmetic  2.37 us (1%)
  between operations  1.74 us (1%)
    ppermute x9, waiting for transfers between devices, swap(): return lax.ppermute(block, axis, [(i, i ^ bit) for i in range(size)])  47.4 us
    ppermute x9, starting transfers between devices, swap(): return lax.ppermute(block, axis, [(i, i ^ bit) for i in range(size)])  32 us
    all_to_all x4, waiting for transfers between devices, exchange(): lax.all_to_all(blocks, axes, split_axis=0, concat_axis=0, tiled=False)  24.4 us
    all_to_all x4, starting transfers between devices, exchange(): lax.all_to_all(blocks, axes, split_axis=0, concat_axis=0, tiled=False)  21.5 us
    all_to_all x1, blocking collectives, exchange(): lax.all_to_all(blocks, axes, split_axis=0, concat_axis=0, tiled=False)  19.8 us
  transfers between devices with their start and end apart: 13, of which 13 were waited for; matrix products, arithmetic and copies ran while one was open for 1% of the time, Pallas kernels for 0%

profile of v11, /device:TPU:56, one launch (start us, length us, event | category | flops | bytes accessed | tf_op | source)
XLA Modules:
  0.0 166.9 jit_solution(14100277985030810055)
XLA Ops:
  0.6 2.9 %normalize.1 = bf16[16,2,64,512]{3,2,1,0:T(8,128)(2,1)} custom-call(bf16[1,2,64,8192]{3,2,1,0:T(8,128)(2,1)} %hidden_ref.1), custom_call_target="tpu_custom_call" | custom-call | tf_op jit(solution)/shard_map/normalize/pallas_call | solution.py:97
  3.6 10.0 %all-to-all-start = ((bf16[16,2,64,512]{3,2,1,0:T(8,128)(2,1)}), bf16[16,2,64,512]{3,2,1,0:T(8,128)(2,1)S(1)}, u32[]{:S(2)}, u32[]{:S(2)}) async-start(bf16[16,2,64,512]{3,2,1,0:T(8,128)(2,1)} %normalize.1), calls=%async_computation | async-start | bytes 4194304 | tf_op jit(solution)/shard_map/all_to_all | solution.py:43
  18.5 3.3 %collective-permute-start.1 = (f32[128,128]{1,0:T(8,128)S(1)}, f32[128,128]{1,0:T(8,128)S(1)}, u32[]{:S(2)}, u32[]{:S(2)}) collective-permute-start(f32[128,128]{1,0:T(8,128)S(1)} %dynamic-slice_bitcast_fusion), channel_id=1, source_target_pairs={{0,32},{32,0},{64,96},{96,64},{128,160},{160,128},{192,224},{224,1... | collective-permute-start | bytes 196616 | tf_op jit(solution)/shard_map/ppermute | solution.py:48
  21.8 2.9 %collective-permute-done.1 = f32[128,128]{1,0:T(8,128)S(1)} collective-permute-done((f32[128,128]{1,0:T(8,128)S(1)}, f32[128,128]{1,0:T(8,128)S(1)}, u32[]{:S(2)}, u32[]{:S(2)}) %collective-permute-start.1) | collective-permute-done | bytes 65568 | tf_op jit(solution)/shard_map/ppermute | solution.py:48
  24.6 4.0 %collective-permute-start.2 = (f32[128,128]{1,0:T(8,128)S(1)}, f32[128,128]{1,0:T(8,128)S(1)}, u32[]{:S(2)}, u32[]{:S(2)}) collective-permute-start(f32[128,128]{1,0:T(8,128)S(1)} %bitcast_add_fusion.2), channel_id=1, source_target_pairs={{0,64},{32,96},{64,0},{96,32},{128,192},{160,224},{192,128},{224,1... | collective-permute-start | bytes 196616 | tf_op jit(solution)/shard_map/ppermute | solution.py:48
  28.8 2.9 %collective-permute-done.2 = f32[128,128]{1,0:T(8,128)S(1)} collective-permute-done((f32[128,128]{1,0:T(8,128)S(1)}, f32[128,128]{1,0:T(8,128)S(1)}, u32[]{:S(2)}, u32[]{:S(2)}) %collective-permute-start.2) | collective-permute-done | bytes 65568 | tf_op jit(solution)/shard_map/ppermute | solution.py:48
  31.7 8.2 %collective-permute-start.3 = (f32[128,128]{1,0:T(8,128)S(1)}, f32[128,128]{1,0:T(8,128)S(1)}, u32[]{:S(2)}, u32[]{:S(2)}) collective-permute-start(f32[128,128]{1,0:T(8,128)S(1)} %add.79), channel_id=1, source_target_pairs={{0,256},{256,0},{1,257},{257,1},{2,258},{258,2},{3,259},{259,3},{4... | collective-permute-start | bytes 196616 | tf_op jit(solution)/shard_map/ppermute | solution.py:48
  40.0 17.1 %collective-permute-done.3 = f32[128,128]{1,0:T(8,128)S(1)} collective-permute-done((f32[128,128]{1,0:T(8,128)S(1)}, f32[128,128]{1,0:T(8,128)S(1)}, u32[]{:S(2)}, u32[]{:S(2)}) %collective-permute-start.3) | collective-permute-done | bytes 65568 | tf_op jit(solution)/shard_map/ppermute | solution.py:48
  57.1 7.4 %all-to-all-done.columns_ref = bf16[16,2,64,512]{3,2,1,0:T(8,128)(2,1)S(1)} async-done(((bf16[16,2,64,512]{3,2,1,0:T(8,128)(2,1)}), bf16[16,2,64,512]{3,2,1,0:T(8,128)(2,1)S(1)}, u32[]{:S(2)}, u32[]{:S(2)}) %all-to-all-start) | async-done | bytes 2097184 | tf_op jit(solution)/shard_map/all_to_all | solution.py:43
  66.1 19.8 %all_to_all.25 = bf16[8,144,512]{2,1,0:T(8,128)(2,1)S(1)} all-to-all(bf16[8,144,512]{2,1,0:T(8,128)(2,1)S(1)} %get-tuple-element.35), channel_id=1, replica_groups=mesh['zh'=2,'y'=8,'c'=2,'x'=4,'zf'=2,'zn'=2] {'x','zn'}, dimensions={0} | all-to-all | bytes 2359296 | tf_op jit(solution)/shard_map/all_to_all | solution.py:43
  86.1 2.6 %collective-permute-start.4 = (bf16[144,512]{1,0:T(8,128)(2,1)S(1)}, bf16[144,512]{1,0:T(8,128)(2,1)S(1)}, u32[]{:S(2)}, u32[]{:S(2)}) collective-permute-start(bf16[144,512]{1,0:T(8,128)(2,1)S(1)} %get-tuple-element.56), channel_id=1, source_target_pairs={{0,2},{2,0},{1,3},{3,1},{4,6},{6,4},{5,7},{7,5},{8,10},{10,8},{9,1... | collective-permute-start | bytes 442376 | tf_op jit(solution)/shard_map/ppermute | solution.py:48
  88.6 6.9 %collective-permute-done.4.got_ref = bf16[144,512]{1,0:T(8,128)(2,1)S(1)} collective-permute-done((bf16[144,512]{1,0:T(8,128)(2,1)S(1)}, bf16[144,512]{1,0:T(8,128)(2,1)S(1)}, u32[]{:S(2)}, u32[]{:S(2)}) %collective-permute-start.4) | collective-permute-done | bytes 147488 | tf_op jit(solution)/shard_map/ppermute | solution.py:48
  96.8 4.3 %all-to-all-start.2 = ((bf16[8,144,512]{2,1,0:T(8,128)(2,1)}), bf16[8,144,512]{2,1,0:T(8,128)(2,1)}, u32[]{:S(2)}, u32[]{:S(2)}) async-start(bf16[8,144,512]{2,1,0:T(8,128)(2,1)} %get-tuple-element.39), calls=%async_computation.2 | async-start | bytes 2359296 | tf_op jit(solution)/shard_map/all_to_all | solution.py:43
  101.1 4.8 %collective-permute-start.5 = (f32[128,128]{1,0:T(8,128)S(1)}, f32[128,128]{1,0:T(8,128)S(1)}, u32[]{:S(2)}, u32[]{:S(2)}) collective-permute-start(f32[128,128]{1,0:T(8,128)S(1)} %add.80), channel_id=1, source_target_pairs={{0,128},{32,160},{64,192},{96,224},{128,0},{160,32},{192,64},{224,... | collective-permute-start | bytes 196616 | tf_op jit(solution)/shard_map/ppermute | solution.py:48
  106.0 6.0 %collective-permute-done.5 = f32[128,128]{1,0:T(8,128)S(1)} collective-permute-done((f32[128,128]{1,0:T(8,128)S(1)}, f32[128,128]{1,0:T(8,128)S(1)}, u32[]{:S(2)}, u32[]{:S(2)}) %collective-permute-start.5) | collective-permute-done | bytes 65568 | tf_op jit(solution)/shard_map/ppermute | solution.py:48
  112.0 2.5 %all-to-all-done.2 = bf16[8,144,512]{2,1,0:T(8,128)(2,1)} async-done(((bf16[8,144,512]{2,1,0:T(8,128)(2,1)}), bf16[8,144,512]{2,1,0:T(8,128)(2,1)}, u32[]{:S(2)}, u32[]{:S(2)}) %all-to-all-start.2) | async-done | bytes 1179680 | tf_op jit(solution)/shard_map/all_to_all | solution.py:43
  117.4 2.3 %convolution_convert_fusion = bf16[1024,512]{1,0:T(8,128)(2,1)} fusion(bf16[1024,512]{1,0:T(8,128)(2,1)S(1)} %copy-done.2, f32[512,512]{1,0:T(8,128)S(1)} %fusion.10, bf16[1,512,512]{2,1,0:T(8,128)(2,1)S(1)} %copy-done.10, bf16[1,512,512]{2,1,0:T(8,128)(2,1)S(1)} %copy-done, bf16[1,512,512]{2,1,0:T(8,128)(2,1)S(1)} %copy-done.12), kind=kOutput, calls=%fused_computation.2 | convolution fusion | flops 542113792 | bytes 4718592 | tf_op jit(solution)/shard_map/dot_general | solution.py:264
  119.7 3.6 %all-to-all-start.3 = ((bf16[8,128,512]{2,1,0:T(8,128)(2,1)}), bf16[8,128,512]{2,1,0:T(8,128)(2,1)S(1)}, u32[]{:S(2)}, u32[]{:S(2)}) async-start(bf16[8,128,512]{2,1,0:T(8,128)(2,1)} %bitcast.70), calls=%async_computation.3 | async-start | bytes 2097152 | tf_op jit(solution)/shard_map/all_to_all | solution.py:43
  123.3 3.3 %collective-permute-start.6 = (f32[128,128]{1,0:T(8,128)S(1)}, f32[128,128]{1,0:T(8,128)S(1)}, u32[]{:S(2)}, u32[]{:S(2)}) collective-permute-start(f32[128,128]{1,0:T(8,128)S(1)} %add.81), channel_id=1, source_target_pairs={{0,32},{32,0},{64,96},{96,64},{128,160},{160,128},{192,224},{224,1... | collective-permute-start | bytes 196616 | tf_op jit(solution)/shard_map/ppermute | solution.py:48
  126.6 2.9 %collective-permute-done.6 = f32[128,128]{1,0:T(8,128)S(1)} collective-permute-done((f32[128,128]{1,0:T(8,128)S(1)}, f32[128,128]{1,0:T(8,128)S(1)}, u32[]{:S(2)}, u32[]{:S(2)}) %collective-permute-start.6) | collective-permute-done | bytes 65568 | tf_op jit(solution)/shard_map/ppermute | solution.py:48
  129.5 5.8 %all-to-all-done.3 = bf16[8,128,512]{2,1,0:T(8,128)(2,1)S(1)} async-done(((bf16[8,128,512]{2,1,0:T(8,128)(2,1)}), bf16[8,128,512]{2,1,0:T(8,128)(2,1)S(1)}, u32[]{:S(2)}, u32[]{:S(2)}) %all-to-all-start.3) | async-done | bytes 1048608 | tf_op jit(solution)/shard_map/all_to_all | solution.py:43
  137.5 6.9 %collective-permute-done.7.got_ref = bf16[128,512]{1,0:T(8,128)(2,1)S(1)} collective-permute-done((bf16[128,512]{1,0:T(8,128)(2,1)S(1)}, bf16[128,512]{1,0:T(8,128)(2,1)S(1)}, u32[]{:S(2)}, u32[]{:S(2)}) %collective-permute-start.7) | collective-permute-done | bytes 131104 | tf_op jit(solution)/shard_map/ppermute | solution.py:48
  145.6 3.7 %all-to-all-start.4 = ((bf16[8,144,512]{2,1,0:T(8,128)(2,1)}), bf16[8,144,512]{2,1,0:T(8,128)(2,1)S(1)}, u32[]{:S(2)}, u32[]{:S(2)}) async-start(bf16[8,144,512]{2,1,0:T(8,128)(2,1)} %errors.3), calls=%async_computation.4 | async-start | bytes 2359296 | tf_op jit(solution)/shard_map/all_to_all | solution.py:43
  152.7 8.8 %all-to-all-done.4 = bf16[8,144,512]{2,1,0:T(8,128)(2,1)S(1)} async-done(((bf16[8,144,512]{2,1,0:T(8,128)(2,1)}), bf16[8,144,512]{2,1,0:T(8,128)(2,1)S(1)}, u32[]{:S(2)}, u32[]{:S(2)}) %all-to-all-start.4) | async-done | bytes 1179680 | tf_op jit(solution)/shard_map/all_to_all | solution.py:43
  (74 shorter events, 22.3 us)
Async XLA Ops:
  3.6 10.7 %copy-start = (bf16[1,512,512]{2,1,0:T(8,128)(2,1)S(1)}, bf16[1,512,512]{2,1,0:T(8,128)(2,1)}, u32[]{:S(2)}) copy-start(bf16[1,512,512]{2,1,0:T(8,128)(2,1)} %weights_ref) | copy-start | bytes 1572868
  3.6 12.7 %copy-start.9 = (s32[1,2,64]{2,1,0:T(2,128)S(1)}, s32[1,2,64]{2,1,0:T(2,128)}, u32[]{:S(2)}) copy-start(s32[1,2,64]{2,1,0:T(2,128)} %param.11) | copy-start | bytes 1540
  3.6 12.7 %copy-start.6 = (bf16[1,2,64,512]{3,2,1,0:T(8,128)(2,1)S(1)}, bf16[1,2,64,512]{3,2,1,0:T(8,128)(2,1)}, u32[]{:S(2)}) copy-start(bf16[1,2,64,512]{3,2,1,0:T(8,128)(2,1)} %param.10) | copy-start | bytes 393220
  3.6 60.9 %all-to-all-start = ((bf16[16,2,64,512]{3,2,1,0:T(8,128)(2,1)}), bf16[16,2,64,512]{3,2,1,0:T(8,128)(2,1)S(1)}, u32[]{:S(2)}, u32[]{:S(2)}) async-start(bf16[16,2,64,512]{3,2,1,0:T(8,128)(2,1)} %normalize.1), calls=%async_computation | async-start | bytes 4194304 | tf_op jit(solution)/shard_map/all_to_all | solution.py:43
  14.3 3.3 %collective-permute-start = (bf16[256,128]{1,0:T(8,128)(2,1)S(1)}, bf16[256,128]{1,0:T(8,128)(2,1)}, u32[]{:S(2)}, u32[]{:S(2)}) collective-permute-start(bf16[256,128]{1,0:T(8,128)(2,1)S(1)} %dynamic-slice_bitcast_fusion.1), channel_id=1, source_target_pairs={{0,16},{16,0},{1,17},{17,1},{2,18},{18,2},{3,19},{19,3},{4,20},{20... | collective-permute-start | bytes 196616 | tf_op jit(solution)/shard_map/ppermute | solution.py:48
  18.5 6.2 %collective-permute-start.1 = (f32[128,128]{1,0:T(8,128)S(1)}, f32[128,128]{1,0:T(8,128)S(1)}, u32[]{:S(2)}, u32[]{:S(2)}) collective-permute-start(f32[128,128]{1,0:T(8,128)S(1)} %dynamic-slice_bitcast_fusion), channel_id=1, source_target_pairs={{0,32},{32,0},{64,96},{96,64},{128,160},{160,128},{192,224},{224,1... | collective-permute-start | bytes 196616 | tf_op jit(solution)/shard_map/ppermute | solution.py:48
  24.6 7.1 %collective-permute-start.2 = (f32[128,128]{1,0:T(8,128)S(1)}, f32[128,128]{1,0:T(8,128)S(1)}, u32[]{:S(2)}, u32[]{:S(2)}) collective-permute-start(f32[128,128]{1,0:T(8,128)S(1)} %bitcast_add_fusion.2), channel_id=1, source_target_pairs={{0,64},{32,96},{64,0},{96,32},{128,192},{160,224},{192,128},{224,1... | collective-permute-start | bytes 196616 | tf_op jit(solution)/shard_map/ppermute | solution.py:48
  31.7 25.4 %collective-permute-start.3 = (f32[128,128]{1,0:T(8,128)S(1)}, f32[128,128]{1,0:T(8,128)S(1)}, u32[]{:S(2)}, u32[]{:S(2)}) collective-permute-start(f32[128,128]{1,0:T(8,128)S(1)} %add.79), channel_id=1, source_target_pairs={{0,256},{256,0},{1,257},{257,1},{2,258},{258,2},{3,259},{259,3},{4... | collective-permute-start | bytes 196616 | tf_op jit(solution)/shard_map/ppermute | solution.py:48
  66.0 19.8 %copy-start.1 = (bf16[1024,512]{1,0:T(8,128)(2,1)}, bf16[1024,512]{1,0:T(8,128)(2,1)S(1)}, u32[]{:S(2)}) copy-start(bf16[1024,512]{1,0:T(8,128)(2,1)S(1)} %get-tuple-element.42) | copy-start | bytes 3145732
  66.0 19.8 %copy-start.3 = (bf16[1024,512]{1,0:T(8,128)(2,1)}, bf16[1024,512]{1,0:T(8,128)(2,1)S(1)}, u32[]{:S(2)}) copy-start(bf16[1024,512]{1,0:T(8,128)(2,1)S(1)} %get-tuple-element.34) | copy-start | bytes 3145732
  86.1 9.5 %collective-permute-start.4 = (bf16[144,512]{1,0:T(8,128)(2,1)S(1)}, bf16[144,512]{1,0:T(8,128)(2,1)S(1)}, u32[]{:S(2)}, u32[]{:S(2)}) collective-permute-start(bf16[144,512]{1,0:T(8,128)(2,1)S(1)} %get-tuple-element.56), channel_id=1, source_target_pairs={{0,2},{2,0},{1,3},{3,1},{4,6},{6,4},{5,7},{7,5},{8,10},{10,8},{9,1... | collective-permute-start | bytes 442376 | tf_op jit(solution)/shard_map/ppermute | solution.py:48
  96.8 17.7 %all-to-all-start.2 = ((bf16[8,144,512]{2,1,0:T(8,128)(2,1)}), bf16[8,144,512]{2,1,0:T(8,128)(2,1)}, u32[]{:S(2)}, u32[]{:S(2)}) async-start(bf16[8,144,512]{2,1,0:T(8,128)(2,1)} %get-tuple-element.39), calls=%async_computation.2 | async-start | bytes 2359296 | tf_op jit(solution)/shard_map/all_to_all | solution.py:43
  101.1 14.8 %copy-start.4 = (bf16[1024,512]{1,0:T(8,128)(2,1)S(1)}, bf16[1024,512]{1,0:T(8,128)(2,1)}, u32[]{:S(2)}) copy-start(bf16[1024,512]{1,0:T(8,128)(2,1)} %copy-done.3) | copy-start | bytes 3145732
  101.1 10.9 %collective-permute-start.5 = (f32[128,128]{1,0:T(8,128)S(1)}, f32[128,128]{1,0:T(8,128)S(1)}, u32[]{:S(2)}, u32[]{:S(2)}) collective-permute-start(f32[128,128]{1,0:T(8,128)S(1)} %add.80), channel_id=1, source_target_pairs={{0,128},{32,160},{64,192},{96,224},{128,0},{160,32},{192,64},{224,... | collective-permute-start | bytes 196616 | tf_op jit(solution)/shard_map/ppermute | solution.py:48
  115.9 1.5 copy-start.12
  116.7 3.1 %copy-start.14 = (f32[512,512]{1,0:T(8,128)}, f32[512,512]{1,0:T(8,128)S(1)}, u32[]{:S(2)}) copy-start(f32[512,512]{1,0:T(8,128)S(1)} %fusion.10) | copy-start | bytes 3145732
  119.7 15.5 %all-to-all-start.3 = ((bf16[8,128,512]{2,1,0:T(8,128)(2,1)}), bf16[8,128,512]{2,1,0:T(8,128)(2,1)S(1)}, u32[]{:S(2)}, u32[]{:S(2)}) async-start(bf16[8,128,512]{2,1,0:T(8,128)(2,1)} %bitcast.70), calls=%async_computation.3 | async-start | bytes 2097152 | tf_op jit(solution)/shard_map/all_to_all | solution.py:43
  123.3 6.2 %collective-permute-start.6 = (f32[128,128]{1,0:T(8,128)S(1)}, f32[128,128]{1,0:T(8,128)S(1)}, u32[]{:S(2)}, u32[]{:S(2)}) collective-permute-start(f32[128,128]{1,0:T(8,128)S(1)} %add.81), channel_id=1, source_target_pairs={{0,32},{32,0},{64,96},{96,64},{128,160},{160,128},{192,224},{224,1... | collective-permute-start | bytes 196616 | tf_op jit(solution)/shard_map/ppermute | solution.py:48
  135.5 8.9 %collective-permute-start.7 = (bf16[128,512]{1,0:T(8,128)(2,1)S(1)}, bf16[128,512]{1,0:T(8,128)(2,1)S(1)}, u32[]{:S(2)}, u32[]{:S(2)}) collective-permute-start(bf16[128,512]{1,0:T(8,128)(2,1)S(1)} %get-tuple-element.54), channel_id=1, source_target_pairs={{0,2},{2,0},{1,3},{3,1},{4,6},{6,4},{5,7},{7,5},{8,10},{10,8},{9,1... | collective-permute-start | bytes 393224 | tf_op jit(solution)/shard_map/ppermute | solution.py:48
  145.6 7.0 %copy-start.7 = (bf16[512,128]{1,0:T(8,128)(2,1)S(1)}, bf16[512,128]{1,0:T(8,128)(2,1)}, u32[]{:S(2)}) copy-start(bf16[512,128]{1,0:T(8,128)(2,1)} %param.15) | copy-start | bytes 393220
  145.6 7.0 %copy-start.8 = (bf16[512,128]{1,0:T(8,128)(2,1)S(1)}, bf16[512,128]{1,0:T(8,128)(2,1)}, u32[]{:S(2)}) copy-start(bf16[512,128]{1,0:T(8,128)(2,1)} %param.16) | copy-start | bytes 393220
  145.6 15.9 %all-to-all-start.4 = ((bf16[8,144,512]{2,1,0:T(8,128)(2,1)}), bf16[8,144,512]{2,1,0:T(8,128)(2,1)S(1)}, u32[]{:S(2)}, u32[]{:S(2)}) async-start(bf16[8,144,512]{2,1,0:T(8,128)(2,1)} %errors.3), calls=%async_computation.4 | async-start | bytes 2359296 | tf_op jit(solution)/shard_map/all_to_all | solution.py:43
  149.3 3.2 %collective-permute-start.8 = (f32[256,128]{1,0:T(8,128)S(1)}, f32[256,128]{1,0:T(8,128)S(1)}, u32[]{:S(2)}, u32[]{:S(2)}) collective-permute-start(f32[256,128]{1,0:T(8,128)S(1)} %pad_maximum_fusion.2), channel_id=1, source_target_pairs={{0,16},{16,0},{1,17},{17,1},{2,18},{18,2},{3,19},{19,3},{4,20},{20... | collective-permute-start | bytes 393224 | tf_op jit(solution)/shard_map/ppermute | solution.py:48
  161.5 1.5 copy-start.15
  (5 other events, 5.8 us)

commit v12 on v11

--- a/solution.py
+++ b/solution.py
@@ -162,7 +162,7 @@
     )(own, got, *(() if counted else (weight,)))
 
 
-def project_kernel(columns_ref, weights_ref, counts_ref, out_ref, first_ref, later_ref, made, sent):
+def project_kernel(columns_ref, weights_ref, counts_ref, out_ref, first_ref, made, sent):
     shards, _, rows, _ = columns_ref.shape
     groups, tokens, _ = made.shape
     tokens = tokens - EXTRA
@@ -181,8 +181,6 @@
             made[at + group, :tokens] = product[group * tokens : (group + 1) * tokens]
             made[at + group, tokens:] = counts_ref[...]
         give(at).start()
-    for shard in range(shards):
-        later_ref[shard * rows : (shard + 1) * rows] = columns_ref[shard, 1]
     for at in range(0, groups, 2):
         give(at).wait()
 
@@ -191,14 +189,17 @@
     shards, _, rows, features = columns.shape
     tokens, wide = shards * rows, weights.shape[2]
     block = jax.ShapeDtypeStruct((groups, tokens // groups + EXTRA, wide), bf16)
-    plain = jax.ShapeDtypeStruct((tokens, features), bf16)
     vmem = pl.BlockSpec(memory_space=pltpu.MemorySpace.VMEM)
     return pl.pallas_call(
         project_kernel,
         in_specs=[vmem, vmem, vmem],
-        out_specs=(pl.BlockSpec(memory_space=pl.ANY), vmem, vmem),
-        out_shape=(block, plain, plain),
-        scratch_shapes=[pltpu.VMEM(block.shape, bf16), pltpu.SemaphoreType.DMA((groups // 2,))],
+        out_specs=pl.BlockSpec(memory_space=pl.ANY),
+        out_shape=block,
+        scratch_shapes=[
+            pltpu.VMEM((tokens, features), bf16),
+            pltpu.VMEM(block.shape, bf16),
+            pltpu.SemaphoreType.DMA((groups // 2,)),
+        ],
         compiler_params=pltpu.CompilerParams(vmem_limit_bytes=VMEM),
         name="project",
     )(columns, weights, count_rows)
@@ -251,7 +252,7 @@
         return jnp.concatenate([jnp.where(at == 0, mine, other), jnp.where(at == 0, other, mine)])
 
     columns, goal, count_rows, summed = tie(columns, goal, count_rows, summed)
-    partial, *step_rows = project(columns, weights, count_rows, groups)
+    partial = project(columns, weights, count_rows, groups)
 
     master = weights[0].astype(f32)
     first = adam_m[0].astype(f32)
@@ -259,8 +260,8 @@
     anchor_rows = anchor.astype(f32)
     loss_rows, weight = [], None
     for step in range(steps_total):
-        rows_now = step_rows[step]
         if step == 1:
+            rows_now = step_rows[1]
             partial = jnp.dot(rows_now, master.astype(bf16), preferred_element_type=f32)
             partial = partial.astype(bf16).reshape(groups, tokens, value_width)
             partial, summed = tie(partial, summed)
@@ -273,11 +274,17 @@
         sent = errors(own, got, weight, tokens, groups, scale)
         if step == 0:
             sent, weight = sent
+            sent, columns = tie(sent, columns)
         sent, summed = tie(sent, summed)
         got = exchange(sent, GROUP)
         if step == 0:
             summed = summed + swap(summed, "y", 4)
-            got, summed = tie(got, summed)
+            step_rows = [columns[:, at].reshape(shards * rows, -1) for at in range(steps_total)]
+            spaced = step_rows[0].reshape(groups, tokens, -1)
+            spaced = jnp.pad(spaced, ((0, 0), (0, EXTRA), (0, 0)))
+            step_rows[0] = spaced.reshape(groups * (tokens + EXTRA), -1)
+            got, summed, step_rows = tie(got, summed, step_rows)
+            rows_now = step_rows[0]
         else:
             summed = whole(summed, swap(summed, "c"), c_at)
             mean_delta = anchor_rows - summed / replicas
@@ -285,7 +292,7 @@
             global_fragment = anchor_rows - OUTER_RATE * (mean_delta + NESTEROV * new_moment)
             got, global_fragment = tie(got, global_fragment)
         loss_rows.append(got[:, tokens, :128])
-        everyone = got[:, :tokens].reshape(shards * rows, value_width)
+        everyone = got.reshape(-1, value_width) if step == 0 else got[:, :tokens].reshape(-1, value_width)
         gradient = (
             lax.dot_general(
                 rows_now, everyone, (((0,), (0,)), ((), ())), preferred_element_type=f32

time: 168 us -> 168 us (level)
  matrix products: 5.19 us -> 7.94 us
    dot_general x2, matrix products: 2.86 us -> 5.64 us  [body(): lax.dot_general(rows_now, everyone, (((0,), (0,)), ((), ())), preferred_e...]
  transfers between devices with their start and end apart: 13 -> 13, of which waited for: 13 -> 13; matrix products, arithmetic and copies ran while one was open for 1% -> 2% of each run, Pallas kernels for 0% -> 0%
where the time goes in v12:
time: 168 us; the launch traced here: 167 us
  waiting for transfers between devices  70.6 us (42%)
  starting transfers between devices  53.4 us (32%)
  blocking collectives  19.8 us (12%)
  matrix products  7.94 us (5%)
  Pallas kernels  6.96 us (4%)
  local copies, waits for them, and re-layouts  4.24 us (3%)
  other arithmetic  2.36 us (1%)
  between operations  1.74 us (1%)
    ppermute x9, waiting for transfers between devices, swap(): return lax.ppermute(block, axis, [(i, i ^ bit) for i in range(size)])  46.1 us
    ppermute x9, starting transfers between devices, swap(): return lax.ppermute(block, axis, [(i, i ^ bit) for i in range(size)])  31.9 us
    all_to_all x4, waiting for transfers between devices, exchange(): lax.all_to_all(blocks, axes, split_axis=0, concat_axis=0, tiled=False)  24.6 us
    all_to_all x4, starting transfers between devices, exchange(): lax.all_to_all(blocks, axes, split_axis=0, concat_axis=0, tiled=False)  21.5 us
    all_to_all x1, blocking collectives, exchange(): lax.all_to_all(blocks, axes, split_axis=0, concat_axis=0, tiled=False)  19.8 us
    dot_general x2, matrix products, body(): lax.dot_general(rows_now, everyone, (((0,), (0,)), ((), ())), preferred_e...  5.64 us
  transfers between devices with their start and end apart: 13, of which 13 were waited for; matrix products, arithmetic and copies ran while one was open for 2% of the time, Pallas kernels for 0%

profile of v12, /device:TPU:56, one launch (start us, length us, event | category | flops | bytes accessed | tf_op | source)
XLA Modules:
  0.0 167.0 jit_solution(4331493087940330015)
XLA Ops:
  0.6 3.0 %normalize.1 = bf16[16,2,64,512]{3,2,1,0:T(8,128)(2,1)} custom-call(bf16[1,2,64,8192]{3,2,1,0:T(8,128)(2,1)} %hidden_ref.1), custom_call_target="tpu_custom_call" | custom-call | tf_op jit(solution)/shard_map/normalize/pallas_call | solution.py:97
  3.6 10.0 %all-to-all-start = ((bf16[16,2,64,512]{3,2,1,0:T(8,128)(2,1)}), bf16[16,2,64,512]{3,2,1,0:T(8,128)(2,1)S(1)}, u32[]{:S(2)}, u32[]{:S(2)}) async-start(bf16[16,2,64,512]{3,2,1,0:T(8,128)(2,1)} %normalize.1), calls=%async_computation | async-start | bytes 4194304 | tf_op jit(solution)/shard_map/all_to_all | solution.py:43
  18.5 3.3 %collective-permute-start.1 = (f32[128,128]{1,0:T(8,128)S(1)}, f32[128,128]{1,0:T(8,128)S(1)}, u32[]{:S(2)}, u32[]{:S(2)}) collective-permute-start(f32[128,128]{1,0:T(8,128)S(1)} %dynamic-slice_bitcast_fusion), channel_id=1, source_target_pairs={{0,32},{32,0},{64,96},{96,64},{128,160},{160,128},{192,224},{224,1... | collective-permute-start | bytes 196616 | tf_op jit(solution)/shard_map/ppermute | solution.py:48
  21.8 2.9 %collective-permute-done.1 = f32[128,128]{1,0:T(8,128)S(1)} collective-permute-done((f32[128,128]{1,0:T(8,128)S(1)}, f32[128,128]{1,0:T(8,128)S(1)}, u32[]{:S(2)}, u32[]{:S(2)}) %collective-permute-start.1) | collective-permute-done | bytes 65568 | tf_op jit(solution)/shard_map/ppermute | solution.py:48
  24.7 4.0 %collective-permute-start.2 = (f32[128,128]{1,0:T(8,128)S(1)}, f32[128,128]{1,0:T(8,128)S(1)}, u32[]{:S(2)}, u32[]{:S(2)}) collective-permute-start(f32[128,128]{1,0:T(8,128)S(1)} %bitcast_add_fusion.2), channel_id=1, source_target_pairs={{0,64},{32,96},{64,0},{96,32},{128,192},{160,224},{192,128},{224,1... | collective-permute-start | bytes 196616 | tf_op jit(solution)/shard_map/ppermute | solution.py:48
  28.8 2.9 %collective-permute-done.2 = f32[128,128]{1,0:T(8,128)S(1)} collective-permute-done((f32[128,128]{1,0:T(8,128)S(1)}, f32[128,128]{1,0:T(8,128)S(1)}, u32[]{:S(2)}, u32[]{:S(2)}) %collective-permute-start.2) | collective-permute-done | bytes 65568 | tf_op jit(solution)/shard_map/ppermute | solution.py:48
  31.8 8.2 %collective-permute-start.3 = (f32[128,128]{1,0:T(8,128)S(1)}, f32[128,128]{1,0:T(8,128)S(1)}, u32[]{:S(2)}, u32[]{:S(2)}) collective-permute-start(f32[128,128]{1,0:T(8,128)S(1)} %add.81), channel_id=1, source_target_pairs={{0,256},{256,0},{1,257},{257,1},{2,258},{258,2},{3,259},{259,3},{4... | collective-permute-start | bytes 196616 | tf_op jit(solution)/shard_map/ppermute | solution.py:48
  40.0 17.1 %collective-permute-done.3 = f32[128,128]{1,0:T(8,128)S(1)} collective-permute-done((f32[128,128]{1,0:T(8,128)S(1)}, f32[128,128]{1,0:T(8,128)S(1)}, u32[]{:S(2)}, u32[]{:S(2)}) %collective-permute-start.3) | collective-permute-done | bytes 65568 | tf_op jit(solution)/shard_map/ppermute | solution.py:48
  57.2 7.4 %all-to-all-done.columns_ref = bf16[16,2,64,512]{3,2,1,0:T(8,128)(2,1)S(1)} async-done(((bf16[16,2,64,512]{3,2,1,0:T(8,128)(2,1)}), bf16[16,2,64,512]{3,2,1,0:T(8,128)(2,1)S(1)}, u32[]{:S(2)}, u32[]{:S(2)}) %all-to-all-start) | async-done | bytes 2097184 | tf_op jit(solution)/shard_map/all_to_all | solution.py:43
  66.0 19.8 %all_to_all.25 = bf16[8,144,512]{2,1,0:T(8,128)(2,1)S(1)} all-to-all(bf16[8,144,512]{2,1,0:T(8,128)(2,1)S(1)} %project.1), channel_id=1, replica_groups=mesh['zh'=2,'y'=8,'c'=2,'x'=4,'zf'=2,'zn'=2] {'x','zn'}, dimensions={0} | all-to-all | bytes 2359296 | tf_op jit(solution)/shard_map/all_to_all | solution.py:43
  86.0 2.6 %collective-permute-start.4 = (bf16[144,512]{1,0:T(8,128)(2,1)S(1)}, bf16[144,512]{1,0:T(8,128)(2,1)S(1)}, u32[]{:S(2)}, u32[]{:S(2)}) collective-permute-start(bf16[144,512]{1,0:T(8,128)(2,1)S(1)} %get-tuple-element.58), channel_id=1, source_target_pairs={{0,2},{2,0},{1,3},{3,1},{4,6},{6,4},{5,7},{7,5},{8,10},{10,8},{9,1... | collective-permute-start | bytes 442376 | tf_op jit(solution)/shard_map/ppermute | solution.py:48
  88.6 6.9 %collective-permute-done.4.got_ref = bf16[144,512]{1,0:T(8,128)(2,1)S(1)} collective-permute-done((bf16[144,512]{1,0:T(8,128)(2,1)S(1)}, bf16[144,512]{1,0:T(8,128)(2,1)S(1)}, u32[]{:S(2)}, u32[]{:S(2)}) %collective-permute-start.4) | collective-permute-done | bytes 147488 | tf_op jit(solution)/shard_map/ppermute | solution.py:48
  96.8 4.3 %all-to-all-start.2 = ((bf16[8,144,512]{2,1,0:T(8,128)(2,1)}), bf16[8,144,512]{2,1,0:T(8,128)(2,1)}, u32[]{:S(2)}, u32[]{:S(2)}) async-start(bf16[8,144,512]{2,1,0:T(8,128)(2,1)} %get-tuple-element.39), calls=%async_computation.2 | async-start | bytes 2359296 | tf_op jit(solution)/shard_map/all_to_all | solution.py:43
  101.0 4.7 %collective-permute-start.5 = (f32[128,128]{1,0:T(8,128)S(1)}, f32[128,128]{1,0:T(8,128)S(1)}, u32[]{:S(2)}, u32[]{:S(2)}) collective-permute-start(f32[128,128]{1,0:T(8,128)S(1)} %add.82), channel_id=1, source_target_pairs={{0,128},{32,160},{64,192},{96,224},{128,0},{160,32},{192,64},{224,... | collective-permute-start | bytes 196616 | tf_op jit(solution)/shard_map/ppermute | solution.py:48
  107.0 4.8 %collective-permute-done.5 = f32[128,128]{1,0:T(8,128)S(1)} collective-permute-done((f32[128,128]{1,0:T(8,128)S(1)}, f32[128,128]{1,0:T(8,128)S(1)}, u32[]{:S(2)}, u32[]{:S(2)}) %collective-permute-start.5) | collective-permute-done | bytes 65568 | tf_op jit(solution)/shard_map/ppermute | solution.py:48
  111.8 2.6 %all-to-all-done.2 = bf16[8,144,512]{2,1,0:T(8,128)(2,1)} async-done(((bf16[8,144,512]{2,1,0:T(8,128)(2,1)}), bf16[8,144,512]{2,1,0:T(8,128)(2,1)}, u32[]{:S(2)}, u32[]{:S(2)}) %all-to-all-start.2) | async-done | bytes 1179680 | tf_op jit(solution)/shard_map/all_to_all | solution.py:43
  119.1 3.6 %all-to-all-start.3 = ((bf16[8,128,512]{2,1,0:T(8,128)(2,1)}), bf16[8,128,512]{2,1,0:T(8,128)(2,1)S(1)}, u32[]{:S(2)}, u32[]{:S(2)}) async-start(bf16[8,128,512]{2,1,0:T(8,128)(2,1)} %bitcast.20), calls=%async_computation.3 | async-start | bytes 2097152 | tf_op jit(solution)/shard_map/all_to_all | solution.py:43
  122.7 3.3 %collective-permute-start.6 = (f32[128,128]{1,0:T(8,128)S(1)}, f32[128,128]{1,0:T(8,128)S(1)}, u32[]{:S(2)}, u32[]{:S(2)}) collective-permute-start(f32[128,128]{1,0:T(8,128)S(1)} %add.83), channel_id=1, source_target_pairs={{0,32},{32,0},{64,96},{96,64},{128,160},{160,128},{192,224},{224,1... | collective-permute-start | bytes 196616 | tf_op jit(solution)/shard_map/ppermute | solution.py:48
  125.9 2.9 %collective-permute-done.6 = f32[128,128]{1,0:T(8,128)S(1)} collective-permute-done((f32[128,128]{1,0:T(8,128)S(1)}, f32[128,128]{1,0:T(8,128)S(1)}, u32[]{:S(2)}, u32[]{:S(2)}) %collective-permute-start.6) | collective-permute-done | bytes 65568 | tf_op jit(solution)/shard_map/ppermute | solution.py:48
  128.9 5.8 %all-to-all-done.3 = bf16[8,128,512]{2,1,0:T(8,128)(2,1)S(1)} async-done(((bf16[8,128,512]{2,1,0:T(8,128)(2,1)}), bf16[8,128,512]{2,1,0:T(8,128)(2,1)S(1)}, u32[]{:S(2)}, u32[]{:S(2)}) %all-to-all-start.3) | async-done | bytes 1048608 | tf_op jit(solution)/shard_map/all_to_all | solution.py:43
  136.8 6.9 %collective-permute-done.7.got_ref = bf16[128,512]{1,0:T(8,128)(2,1)S(1)} collective-permute-done((bf16[128,512]{1,0:T(8,128)(2,1)S(1)}, bf16[128,512]{1,0:T(8,128)(2,1)S(1)}, u32[]{:S(2)}, u32[]{:S(2)}) %collective-permute-start.7) | collective-permute-done | bytes 131104 | tf_op jit(solution)/shard_map/ppermute | solution.py:48
  145.0 3.7 %all-to-all-start.4 = ((bf16[8,144,512]{2,1,0:T(8,128)(2,1)}), bf16[8,144,512]{2,1,0:T(8,128)(2,1)S(1)}, u32[]{:S(2)}, u32[]{:S(2)}) async-start(bf16[8,144,512]{2,1,0:T(8,128)(2,1)} %errors.3), calls=%async_computation.4 | async-start | bytes 2359296 | tf_op jit(solution)/shard_map/all_to_all | solution.py:43
  152.1 8.8 %all-to-all-done.4 = bf16[8,144,512]{2,1,0:T(8,128)(2,1)S(1)} async-done(((bf16[8,144,512]{2,1,0:T(8,128)(2,1)}), bf16[8,144,512]{2,1,0:T(8,128)(2,1)S(1)}, u32[]{:S(2)}, u32[]{:S(2)}) %all-to-all-start.4) | async-done | bytes 1179680 | tf_op jit(solution)/shard_map/all_to_all | solution.py:43
  161.9 3.4 %multiply_subtract_fusion = f32[512,512]{1,0:T(8,128)S(1)} fusion(f32[512,512]{1,0:T(8,128)} %copy-done.12, bf16[1,512,512]{2,1,0:T(8,128)(2,1)S(1)} %copy-done.9, bf16[1,512,512]{2,1,0:T(8,128)(2,1)S(1)} %copy-done.11, bf16[1,512,512]{2,1,0:T(8,128)(2,1)S(1)} %copy-done, bf16[1024,512]{1,0:T(8,128)(2,1)S(1)} %bitcast.77, bf16[1024,512]{1,0:T(8,128)(2,1)S(1)} %bitcast.75), kind=kOutput, calls=%fused_computation.9 | convolution fusion | flops 544997376 | bytes 5767168 | tf_op jit(solution)/shard_map/dot_general | solution.py:297
  (69 shorter events, 22.7 us)
Async XLA Ops:
  3.6 10.7 %copy-start = (bf16[1,512,512]{2,1,0:T(8,128)(2,1)S(1)}, bf16[1,512,512]{2,1,0:T(8,128)(2,1)}, u32[]{:S(2)}) copy-start(bf16[1,512,512]{2,1,0:T(8,128)(2,1)} %weights_ref) | copy-start | bytes 1572868
  3.6 12.7 %copy-start.7 = (s32[1,2,64]{2,1,0:T(2,128)S(1)}, s32[1,2,64]{2,1,0:T(2,128)}, u32[]{:S(2)}) copy-start(s32[1,2,64]{2,1,0:T(2,128)} %param.11) | copy-start | bytes 1540
  3.6 12.7 %copy-start.4 = (bf16[1,2,64,512]{3,2,1,0:T(8,128)(2,1)S(1)}, bf16[1,2,64,512]{3,2,1,0:T(8,128)(2,1)}, u32[]{:S(2)}) copy-start(bf16[1,2,64,512]{3,2,1,0:T(8,128)(2,1)} %param.10) | copy-start | bytes 393220
  3.6 60.9 %all-to-all-start = ((bf16[16,2,64,512]{3,2,1,0:T(8,128)(2,1)}), bf16[16,2,64,512]{3,2,1,0:T(8,128)(2,1)S(1)}, u32[]{:S(2)}, u32[]{:S(2)}) async-start(bf16[16,2,64,512]{3,2,1,0:T(8,128)(2,1)} %normalize.1), calls=%async_computation | async-start | bytes 4194304 | tf_op jit(solution)/shard_map/all_to_all | solution.py:43
  14.3 3.3 %collective-permute-start = (bf16[256,128]{1,0:T(8,128)(2,1)S(1)}, bf16[256,128]{1,0:T(8,128)(2,1)}, u32[]{:S(2)}, u32[]{:S(2)}) collective-permute-start(bf16[256,128]{1,0:T(8,128)(2,1)S(1)} %dynamic-slice_bitcast_fusion.1), channel_id=1, source_target_pairs={{0,16},{16,0},{1,17},{17,1},{2,18},{18,2},{3,19},{19,3},{4,20},{20... | collective-permute-start | bytes 196616 | tf_op jit(solution)/shard_map/ppermute | solution.py:48
  18.5 6.2 %collective-permute-start.1 = (f32[128,128]{1,0:T(8,128)S(1)}, f32[128,128]{1,0:T(8,128)S(1)}, u32[]{:S(2)}, u32[]{:S(2)}) collective-permute-start(f32[128,128]{1,0:T(8,128)S(1)} %dynamic-slice_bitcast_fusion), channel_id=1, source_target_pairs={{0,32},{32,0},{64,96},{96,64},{128,160},{160,128},{192,224},{224,1... | collective-permute-start | bytes 196616 | tf_op jit(solution)/shard_map/ppermute | solution.py:48
  24.7 7.1 %collective-permute-start.2 = (f32[128,128]{1,0:T(8,128)S(1)}, f32[128,128]{1,0:T(8,128)S(1)}, u32[]{:S(2)}, u32[]{:S(2)}) collective-permute-start(f32[128,128]{1,0:T(8,128)S(1)} %bitcast_add_fusion.2), channel_id=1, source_target_pairs={{0,64},{32,96},{64,0},{96,32},{128,192},{160,224},{192,128},{224,1... | collective-permute-start | bytes 196616 | tf_op jit(solution)/shard_map/ppermute | solution.py:48
  31.8 25.4 %collective-permute-start.3 = (f32[128,128]{1,0:T(8,128)S(1)}, f32[128,128]{1,0:T(8,128)S(1)}, u32[]{:S(2)}, u32[]{:S(2)}) collective-permute-start(f32[128,128]{1,0:T(8,128)S(1)} %add.81), channel_id=1, source_target_pairs={{0,256},{256,0},{1,257},{257,1},{2,258},{258,2},{3,259},{259,3},{4... | collective-permute-start | bytes 196616 | tf_op jit(solution)/shard_map/ppermute | solution.py:48
  86.0 9.5 %collective-permute-start.4 = (bf16[144,512]{1,0:T(8,128)(2,1)S(1)}, bf16[144,512]{1,0:T(8,128)(2,1)S(1)}, u32[]{:S(2)}, u32[]{:S(2)}) collective-permute-start(bf16[144,512]{1,0:T(8,128)(2,1)S(1)} %get-tuple-element.58), channel_id=1, source_target_pairs={{0,2},{2,0},{1,3},{3,1},{4,6},{6,4},{5,7},{7,5},{8,10},{10,8},{9,1... | collective-permute-start | bytes 442376 | tf_op jit(solution)/shard_map/ppermute | solution.py:48
  96.8 17.7 %all-to-all-start.2 = ((bf16[8,144,512]{2,1,0:T(8,128)(2,1)}), bf16[8,144,512]{2,1,0:T(8,128)(2,1)}, u32[]{:S(2)}, u32[]{:S(2)}) async-start(bf16[8,144,512]{2,1,0:T(8,128)(2,1)} %get-tuple-element.39), calls=%async_computation.2 | async-start | bytes 2359296 | tf_op jit(solution)/shard_map/all_to_all | solution.py:43
  101.0 10.8 %collective-permute-start.5 = (f32[128,128]{1,0:T(8,128)S(1)}, f32[128,128]{1,0:T(8,128)S(1)}, u32[]{:S(2)}, u32[]{:S(2)}) collective-permute-start(f32[128,128]{1,0:T(8,128)S(1)} %add.82), channel_id=1, source_target_pairs={{0,128},{32,160},{64,192},{96,224},{128,0},{160,32},{192,64},{224,... | collective-permute-start | bytes 196616 | tf_op jit(solution)/shard_map/ppermute | solution.py:48
  114.5 2.3 %copy-start.2 = (bf16[16,1,64,512]{3,2,1,0:T(8,128)(2,1)S(1)}, bf16[16,1,64,512]{3,2,1,0:T(8,128)(2,1)}, u32[]{:S(2)}) copy-start(bf16[16,1,64,512]{3,2,1,0:T(8,128)(2,1)} %get-tuple-element.60) | copy-start | bytes 3145732
  114.5 2.3 %copy-start.8 = (bf16[1,512,512]{2,1,0:T(8,128)(2,1)S(1)}, bf16[1,512,512]{2,1,0:T(8,128)(2,1)}, u32[]{:S(2)}) copy-start(bf16[1,512,512]{2,1,0:T(8,128)(2,1)} %param.13) | copy-start | bytes 1572868
  114.5 2.3 %copy-start.10 = (bf16[1,512,512]{2,1,0:T(8,128)(2,1)S(1)}, bf16[1,512,512]{2,1,0:T(8,128)(2,1)}, u32[]{:S(2)}) copy-start(bf16[1,512,512]{2,1,0:T(8,128)(2,1)} %param.14) | copy-start | bytes 1572868
  116.8 2.3 %copy-start.12 = (f32[512,512]{1,0:T(8,128)}, f32[512,512]{1,0:T(8,128)S(1)}, u32[]{:S(2)}) copy-start(f32[512,512]{1,0:T(8,128)S(1)} %fusion.11) | copy-start | bytes 3145732
  119.1 15.5 %all-to-all-start.3 = ((bf16[8,128,512]{2,1,0:T(8,128)(2,1)}), bf16[8,128,512]{2,1,0:T(8,128)(2,1)S(1)}, u32[]{:S(2)}, u32[]{:S(2)}) async-start(bf16[8,128,512]{2,1,0:T(8,128)(2,1)} %bitcast.20), calls=%async_computation.3 | async-start | bytes 2097152 | tf_op jit(solution)/shard_map/all_to_all | solution.py:43
  122.7 6.2 %collective-permute-start.6 = (f32[128,128]{1,0:T(8,128)S(1)}, f32[128,128]{1,0:T(8,128)S(1)}, u32[]{:S(2)}, u32[]{:S(2)}) collective-permute-start(f32[128,128]{1,0:T(8,128)S(1)} %add.83), channel_id=1, source_target_pairs={{0,32},{32,0},{64,96},{96,64},{128,160},{160,128},{192,224},{224,1... | collective-permute-start | bytes 196616 | tf_op jit(solution)/shard_map/ppermute | solution.py:48
  134.8 8.9 %collective-permute-start.7 = (bf16[128,512]{1,0:T(8,128)(2,1)S(1)}, bf16[128,512]{1,0:T(8,128)(2,1)S(1)}, u32[]{:S(2)}, u32[]{:S(2)}) collective-permute-start(bf16[128,512]{1,0:T(8,128)(2,1)S(1)} %get-tuple-element.56), channel_id=1, source_target_pairs={{0,2},{2,0},{1,3},{3,1},{4,6},{6,4},{5,7},{7,5},{8,10},{10,8},{9,1... | collective-permute-start | bytes 393224 | tf_op jit(solution)/shard_map/ppermute | solution.py:48
  145.0 7.0 %copy-start.5 = (bf16[512,128]{1,0:T(8,128)(2,1)S(1)}, bf16[512,128]{1,0:T(8,128)(2,1)}, u32[]{:S(2)}) copy-start(bf16[512,128]{1,0:T(8,128)(2,1)} %param.15) | copy-start | bytes 393220
  145.0 7.0 %copy-start.6 = (bf16[512,128]{1,0:T(8,128)(2,1)S(1)}, bf16[512,128]{1,0:T(8,128)(2,1)}, u32[]{:S(2)}) copy-start(bf16[512,128]{1,0:T(8,128)(2,1)} %param.16) | copy-start | bytes 393220
  145.0 15.9 %all-to-all-start.4 = ((bf16[8,144,512]{2,1,0:T(8,128)(2,1)}), bf16[8,144,512]{2,1,0:T(8,128)(2,1)S(1)}, u32[]{:S(2)}, u32[]{:S(2)}) async-start(bf16[8,144,512]{2,1,0:T(8,128)(2,1)} %errors.3), calls=%async_computation.4 | async-start | bytes 2359296 | tf_op jit(solution)/shard_map/all_to_all | solution.py:43
  148.7 3.2 %collective-permute-start.8 = (f32[256,128]{1,0:T(8,128)S(1)}, f32[256,128]{1,0:T(8,128)S(1)}, u32[]{:S(2)}, u32[]{:S(2)}) collective-permute-start(f32[256,128]{1,0:T(8,128)S(1)} %pad_maximum_fusion.2), channel_id=1, source_target_pairs={{0,16},{16,0},{1,17},{17,1},{2,18},{18,2},{3,19},{19,3},{4,20},{20... | collective-permute-start | bytes 393224 | tf_op jit(solution)/shard_map/ppermute | solution.py:48
  152.1 8.9 %copy-start.3 = (bf16[16,1,64,512]{3,2,1,0:T(8,128)(2,1)S(1)}, bf16[16,1,64,512]{3,2,1,0:T(8,128)(2,1)}, u32[]{:S(2)}) copy-start(bf16[16,1,64,512]{3,2,1,0:T(8,128)(2,1)} %get-tuple-element.60) | copy-start | bytes 3145732
  152.1 8.9 %copy-start.9 = (bf16[1,512,512]{2,1,0:T(8,128)(2,1)S(1)}, bf16[1,512,512]{2,1,0:T(8,128)(2,1)}, u32[]{:S(2)}) copy-start(bf16[1,512,512]{2,1,0:T(8,128)(2,1)} %param.13) | copy-start | bytes 1572868
  (2 other events, 2.0 us)

commit v13 on v11

--- a/solution.py
+++ b/solution.py
@@ -164,8 +164,8 @@
 
 def project_kernel(columns_ref, weights_ref, counts_ref, out_ref, first_ref, later_ref, made, sent):
     shards, _, rows, _ = columns_ref.shape
-    groups, tokens, _ = made.shape
-    tokens = tokens - EXTRA
+    groups, block, _ = made.shape
+    tokens = block - EXTRA
     share = tokens // rows
 
     def give(at):
@@ -173,12 +173,16 @@
 
     for at in range(0, groups, 2):
         for shard in range(at * share, (at + 2) * share):
-            first_ref[shard * rows : (shard + 1) * rows] = columns_ref[shard, 0]
+            row = shard * rows + shard // share * EXTRA
+            first_ref[row : row + rows] = columns_ref[shard, 0]
+        for group in (at, at + 1):
+            row = group * block + tokens
+            first_ref[row : row + EXTRA] = jnp.zeros((EXTRA, first_ref.shape[1]), bf16)
         product = jnp.dot(
-            first_ref[at * tokens : (at + 2) * tokens], weights_ref[0], preferred_element_type=f32
+            first_ref[at * block : (at + 2) * block], weights_ref[0], preferred_element_type=f32
         ).astype(bf16)
         for group in range(2):
-            made[at + group, :tokens] = product[group * tokens : (group + 1) * tokens]
+            made[at + group, :tokens] = product[group * block : group * block + tokens]
             made[at + group, tokens:] = counts_ref[...]
         give(at).start()
     for shard in range(shards):
@@ -192,12 +196,13 @@
     tokens, wide = shards * rows, weights.shape[2]
     block = jax.ShapeDtypeStruct((groups, tokens // groups + EXTRA, wide), bf16)
     plain = jax.ShapeDtypeStruct((tokens, features), bf16)
+    spaced = jax.ShapeDtypeStruct((tokens + groups * EXTRA, features), bf16)
     vmem = pl.BlockSpec(memory_space=pltpu.MemorySpace.VMEM)
     return pl.pallas_call(
         project_kernel,
         in_specs=[vmem, vmem, vmem],
         out_specs=(pl.BlockSpec(memory_space=pl.ANY), vmem, vmem),
-        out_shape=(block, plain, plain),
+        out_shape=(block, spaced, plain),
         scratch_shapes=[pltpu.VMEM(block.shape, bf16), pltpu.SemaphoreType.DMA((groups // 2,))],
         compiler_params=pltpu.CompilerParams(vmem_limit_bytes=VMEM),
         name="project",
@@ -285,7 +290,7 @@
             global_fragment = anchor_rows - OUTER_RATE * (mean_delta + NESTEROV * new_moment)
             got, global_fragment = tie(got, global_fragment)
         loss_rows.append(got[:, tokens, :128])
-        everyone = got[:, :tokens].reshape(shards * rows, value_width)
+        everyone = (got if step == 0 else got[:, :tokens]).reshape(-1, value_width)
         gradient = (
             lax.dot_general(
                 rows_now, everyone, (((0,), (0,)), ((), ())), preferred_element_type=f32

time: 168 us -> 167 us (level)
  local copies, waits for them, and re-layouts: 5.57 us -> 3.04 us
where the time goes in v13:
time: 167 us; the launch traced here: 166 us
  waiting for transfers between devices  71.7 us (43%)
  starting transfers between devices  52.7 us (32%)
  blocking collectives  19.8 us (12%)
  Pallas kernels  7.04 us (4%)
  matrix products  6.56 us (4%)
  other arithmetic  3.28 us (2%)
  local copies, waits for them, and re-layouts  3.04 us (2%)
  between operations  1.72 us (1%)
    ppermute x9, waiting for transfers between devices, swap(): return lax.ppermute(block, axis, [(i, i ^ bit) for i in range(size)])  48.1 us
    ppermute x9, starting transfers between devices, swap(): return lax.ppermute(block, axis, [(i, i ^ bit) for i in range(size)])  31.8 us
    all_to_all x4, waiting for transfers between devices, exchange(): lax.all_to_all(blocks, axes, split_axis=0, concat_axis=0, tiled=False)  23.6 us
    all_to_all x4, starting transfers between devices, exchange(): lax.all_to_all(blocks, axes, split_axis=0, concat_axis=0, tiled=False)  20.9 us
    all_to_all x1, blocking collectives, exchange(): lax.all_to_all(blocks, axes, split_axis=0, concat_axis=0, tiled=False)  19.8 us
    dot_general x2, matrix products, body(): lax.dot_general(rows_now, everyone, (((0,), (0,)), ((), ())), preferred_e...  4.22 us
  transfers between devices with their start and end apart: 13, of which 13 were waited for; matrix products, arithmetic and copies ran while one was open for 1% of the time, Pallas kernels for 0%

profile of v13, /device:TPU:56, one launch (start us, length us, event | category | flops | bytes accessed | tf_op | source)
XLA Modules:
  0.0 165.9 jit_solution(15359866856997109708)
XLA Ops:
  0.6 2.9 %normalize.1 = bf16[16,2,64,512]{3,2,1,0:T(8,128)(2,1)} custom-call(bf16[1,2,64,8192]{3,2,1,0:T(8,128)(2,1)} %hidden_ref.1), custom_call_target="tpu_custom_call" | custom-call | tf_op jit(solution)/shard_map/normalize/pallas_call | solution.py:97
  3.6 10.0 %all-to-all-start = ((bf16[16,2,64,512]{3,2,1,0:T(8,128)(2,1)}), bf16[16,2,64,512]{3,2,1,0:T(8,128)(2,1)S(1)}, u32[]{:S(2)}, u32[]{:S(2)}) async-start(bf16[16,2,64,512]{3,2,1,0:T(8,128)(2,1)} %normalize.1), calls=%async_computation | async-start | bytes 4194304 | tf_op jit(solution)/shard_map/all_to_all | solution.py:43
  18.5 3.3 %collective-permute-start.1 = (f32[128,128]{1,0:T(8,128)S(1)}, f32[128,128]{1,0:T(8,128)S(1)}, u32[]{:S(2)}, u32[]{:S(2)}) collective-permute-start(f32[128,128]{1,0:T(8,128)S(1)} %dynamic-slice_bitcast_fusion), channel_id=1, source_target_pairs={{0,32},{32,0},{64,96},{96,64},{128,160},{160,128},{192,224},{224,1... | collective-permute-start | bytes 196616 | tf_op jit(solution)/shard_map/ppermute | solution.py:48
  21.8 2.9 %collective-permute-done.1 = f32[128,128]{1,0:T(8,128)S(1)} collective-permute-done((f32[128,128]{1,0:T(8,128)S(1)}, f32[128,128]{1,0:T(8,128)S(1)}, u32[]{:S(2)}, u32[]{:S(2)}) %collective-permute-start.1) | collective-permute-done | bytes 65568 | tf_op jit(solution)/shard_map/ppermute | solution.py:48
  24.6 4.0 %collective-permute-start.2 = (f32[128,128]{1,0:T(8,128)S(1)}, f32[128,128]{1,0:T(8,128)S(1)}, u32[]{:S(2)}, u32[]{:S(2)}) collective-permute-start(f32[128,128]{1,0:T(8,128)S(1)} %bitcast_add_fusion.2), channel_id=1, source_target_pairs={{0,64},{32,96},{64,0},{96,32},{128,192},{160,224},{192,128},{224,1... | collective-permute-start | bytes 196616 | tf_op jit(solution)/shard_map/ppermute | solution.py:48
  28.8 2.9 %collective-permute-done.2 = f32[128,128]{1,0:T(8,128)S(1)} collective-permute-done((f32[128,128]{1,0:T(8,128)S(1)}, f32[128,128]{1,0:T(8,128)S(1)}, u32[]{:S(2)}, u32[]{:S(2)}) %collective-permute-start.2) | collective-permute-done | bytes 65568 | tf_op jit(solution)/shard_map/ppermute | solution.py:48
  31.7 8.2 %collective-permute-start.3 = (f32[128,128]{1,0:T(8,128)S(1)}, f32[128,128]{1,0:T(8,128)S(1)}, u32[]{:S(2)}, u32[]{:S(2)}) collective-permute-start(f32[128,128]{1,0:T(8,128)S(1)} %add.79), channel_id=1, source_target_pairs={{0,256},{256,0},{1,257},{257,1},{2,258},{258,2},{3,259},{259,3},{4... | collective-permute-start | bytes 196616 | tf_op jit(solution)/shard_map/ppermute | solution.py:48
  40.0 17.1 %collective-permute-done.3 = f32[128,128]{1,0:T(8,128)S(1)} collective-permute-done((f32[128,128]{1,0:T(8,128)S(1)}, f32[128,128]{1,0:T(8,128)S(1)}, u32[]{:S(2)}, u32[]{:S(2)}) %collective-permute-start.3) | collective-permute-done | bytes 65568 | tf_op jit(solution)/shard_map/ppermute | solution.py:48
  57.1 7.4 %all-to-all-done.columns_ref = bf16[16,2,64,512]{3,2,1,0:T(8,128)(2,1)S(1)} async-done(((bf16[16,2,64,512]{3,2,1,0:T(8,128)(2,1)}), bf16[16,2,64,512]{3,2,1,0:T(8,128)(2,1)S(1)}, u32[]{:S(2)}, u32[]{:S(2)}) %all-to-all-start) | async-done | bytes 2097184 | tf_op jit(solution)/shard_map/all_to_all | solution.py:43
  66.1 19.8 %all_to_all.25 = bf16[8,144,512]{2,1,0:T(8,128)(2,1)S(1)} all-to-all(bf16[8,144,512]{2,1,0:T(8,128)(2,1)S(1)} %get-tuple-element.35), channel_id=1, replica_groups=mesh['zh'=2,'y'=8,'c'=2,'x'=4,'zf'=2,'zn'=2] {'x','zn'}, dimensions={0} | all-to-all | bytes 2359296 | tf_op jit(solution)/shard_map/all_to_all | solution.py:43
  86.1 2.6 %collective-permute-start.4 = (bf16[144,512]{1,0:T(8,128)(2,1)S(1)}, bf16[144,512]{1,0:T(8,128)(2,1)S(1)}, u32[]{:S(2)}, u32[]{:S(2)}) collective-permute-start(bf16[144,512]{1,0:T(8,128)(2,1)S(1)} %get-tuple-element.56), channel_id=1, source_target_pairs={{0,2},{2,0},{1,3},{3,1},{4,6},{6,4},{5,7},{7,5},{8,10},{10,8},{9,1... | collective-permute-start | bytes 442376 | tf_op jit(solution)/shard_map/ppermute | solution.py:48
  88.7 6.9 %collective-permute-done.4.got_ref = bf16[144,512]{1,0:T(8,128)(2,1)S(1)} collective-permute-done((bf16[144,512]{1,0:T(8,128)(2,1)S(1)}, bf16[144,512]{1,0:T(8,128)(2,1)S(1)}, u32[]{:S(2)}, u32[]{:S(2)}) %collective-permute-start.4) | collective-permute-done | bytes 147488 | tf_op jit(solution)/shard_map/ppermute | solution.py:48
  96.9 3.7 %all-to-all-start.2 = ((bf16[8,144,512]{2,1,0:T(8,128)(2,1)}), bf16[8,144,512]{2,1,0:T(8,128)(2,1)S(1)}, u32[]{:S(2)}, u32[]{:S(2)}) async-start(bf16[8,144,512]{2,1,0:T(8,128)(2,1)} %get-tuple-element.39), calls=%async_computation.2 | async-start | bytes 2359296 | tf_op jit(solution)/shard_map/all_to_all | solution.py:43
  100.6 4.7 %collective-permute-start.5 = (f32[128,128]{1,0:T(8,128)S(1)}, f32[128,128]{1,0:T(8,128)S(1)}, u32[]{:S(2)}, u32[]{:S(2)}) collective-permute-start(f32[128,128]{1,0:T(8,128)S(1)} %add.80), channel_id=1, source_target_pairs={{0,128},{32,160},{64,192},{96,224},{128,0},{160,32},{192,64},{224,... | collective-permute-start | bytes 196616 | tf_op jit(solution)/shard_map/ppermute | solution.py:48
  105.3 6.0 %collective-permute-done.5 = f32[128,128]{1,0:T(8,128)S(1)} collective-permute-done((f32[128,128]{1,0:T(8,128)S(1)}, f32[128,128]{1,0:T(8,128)S(1)}, u32[]{:S(2)}, u32[]{:S(2)}) %collective-permute-start.5) | collective-permute-done | bytes 65568 | tf_op jit(solution)/shard_map/ppermute | solution.py:48
  111.4 2.6 %all-to-all-done.2 = bf16[8,144,512]{2,1,0:T(8,128)(2,1)S(1)} async-done(((bf16[8,144,512]{2,1,0:T(8,128)(2,1)}), bf16[8,144,512]{2,1,0:T(8,128)(2,1)S(1)}, u32[]{:S(2)}, u32[]{:S(2)}) %all-to-all-start.2) | async-done | bytes 1179680 | tf_op jit(solution)/shard_map/all_to_all | solution.py:43
  117.8 3.6 %all-to-all-start.3 = ((bf16[8,128,512]{2,1,0:T(8,128)(2,1)}), bf16[8,128,512]{2,1,0:T(8,128)(2,1)S(1)}, u32[]{:S(2)}, u32[]{:S(2)}) async-start(bf16[8,128,512]{2,1,0:T(8,128)(2,1)} %bitcast.71), calls=%async_computation.3 | async-start | bytes 2097152 | tf_op jit(solution)/shard_map/all_to_all | solution.py:43
  121.4 3.3 %collective-permute-start.6 = (f32[128,128]{1,0:T(8,128)S(1)}, f32[128,128]{1,0:T(8,128)S(1)}, u32[]{:S(2)}, u32[]{:S(2)}) collective-permute-start(f32[128,128]{1,0:T(8,128)S(1)} %add.81), channel_id=1, source_target_pairs={{0,32},{32,0},{64,96},{96,64},{128,160},{160,128},{192,224},{224,1... | collective-permute-start | bytes 196616 | tf_op jit(solution)/shard_map/ppermute | solution.py:48
  124.6 2.9 %collective-permute-done.6 = f32[128,128]{1,0:T(8,128)S(1)} collective-permute-done((f32[128,128]{1,0:T(8,128)S(1)}, f32[128,128]{1,0:T(8,128)S(1)}, u32[]{:S(2)}, u32[]{:S(2)}) %collective-permute-start.6) | collective-permute-done | bytes 65568 | tf_op jit(solution)/shard_map/ppermute | solution.py:48
  127.5 5.8 %all-to-all-done.3 = bf16[8,128,512]{2,1,0:T(8,128)(2,1)S(1)} async-done(((bf16[8,128,512]{2,1,0:T(8,128)(2,1)}), bf16[8,128,512]{2,1,0:T(8,128)(2,1)S(1)}, u32[]{:S(2)}, u32[]{:S(2)}) %all-to-all-start.3) | async-done | bytes 1048608 | tf_op jit(solution)/shard_map/all_to_all | solution.py:43
  135.5 7.0 %collective-permute-done.7.got_ref = bf16[128,512]{1,0:T(8,128)(2,1)S(1)} collective-permute-done((bf16[128,512]{1,0:T(8,128)(2,1)S(1)}, bf16[128,512]{1,0:T(8,128)(2,1)S(1)}, u32[]{:S(2)}, u32[]{:S(2)}) %collective-permute-start.7) | collective-permute-done | bytes 131104 | tf_op jit(solution)/shard_map/ppermute | solution.py:48
  143.7 3.7 %all-to-all-start.4 = ((bf16[8,144,512]{2,1,0:T(8,128)(2,1)}), bf16[8,144,512]{2,1,0:T(8,128)(2,1)S(1)}, u32[]{:S(2)}, u32[]{:S(2)}) async-start(bf16[8,144,512]{2,1,0:T(8,128)(2,1)} %errors.3), calls=%async_computation.4 | async-start | bytes 2359296 | tf_op jit(solution)/shard_map/all_to_all | solution.py:43
  151.7 7.9 %all-to-all-done.4 = bf16[8,144,512]{2,1,0:T(8,128)(2,1)S(1)} async-done(((bf16[8,144,512]{2,1,0:T(8,128)(2,1)}), bf16[8,144,512]{2,1,0:T(8,128)(2,1)S(1)}, u32[]{:S(2)}, u32[]{:S(2)}) %all-to-all-start.4) | async-done | bytes 1179680 | tf_op jit(solution)/shard_map/all_to_all | solution.py:43
  160.8 3.4 %multiply_subtract_fusion = f32[512,512]{1,0:T(8,128)S(1)} fusion(f32[512,512]{1,0:T(8,128)} %copy-done.14, bf16[1,512,512]{2,1,0:T(8,128)(2,1)S(1)} %copy-done.11, bf16[1,512,512]{2,1,0:T(8,128)(2,1)S(1)} %copy-done.13, bf16[1,512,512]{2,1,0:T(8,128)(2,1)S(1)} %copy-done, bf16[1024,512]{1,0:T(8,128)(2,1)S(1)} %copy-done.5, bf16[1024,512]{1,0:T(8,128)(2,1)S(1)} %bitcast.72), kind=kOutput, calls=%fused_computation.9 | convolution fusion | flops 544997376 | bytes 5767168 | tf_op jit(solution)/shard_map/dot_general | solution.py:295
  (71 shorter events, 21.8 us)
Async XLA Ops:
  3.6 10.7 %copy-start = (bf16[1,512,512]{2,1,0:T(8,128)(2,1)S(1)}, bf16[1,512,512]{2,1,0:T(8,128)(2,1)}, u32[]{:S(2)}) copy-start(bf16[1,512,512]{2,1,0:T(8,128)(2,1)} %weights_ref) | copy-start | bytes 1572868
  3.6 12.7 %copy-start.9 = (s32[1,2,64]{2,1,0:T(2,128)S(1)}, s32[1,2,64]{2,1,0:T(2,128)}, u32[]{:S(2)}) copy-start(s32[1,2,64]{2,1,0:T(2,128)} %param.11) | copy-start | bytes 1540
  3.6 12.7 %copy-start.7 = (bf16[1,2,64,512]{3,2,1,0:T(8,128)(2,1)S(1)}, bf16[1,2,64,512]{3,2,1,0:T(8,128)(2,1)}, u32[]{:S(2)}) copy-start(bf16[1,2,64,512]{3,2,1,0:T(8,128)(2,1)} %param.10) | copy-start | bytes 393220
  3.6 60.9 %all-to-all-start = ((bf16[16,2,64,512]{3,2,1,0:T(8,128)(2,1)}), bf16[16,2,64,512]{3,2,1,0:T(8,128)(2,1)S(1)}, u32[]{:S(2)}, u32[]{:S(2)}) async-start(bf16[16,2,64,512]{3,2,1,0:T(8,128)(2,1)} %normalize.1), calls=%async_computation | async-start | bytes 4194304 | tf_op jit(solution)/shard_map/all_to_all | solution.py:43
  14.3 3.3 %collective-permute-start = (bf16[256,128]{1,0:T(8,128)(2,1)S(1)}, bf16[256,128]{1,0:T(8,128)(2,1)}, u32[]{:S(2)}, u32[]{:S(2)}) collective-permute-start(bf16[256,128]{1,0:T(8,128)(2,1)S(1)} %dynamic-slice_bitcast_fusion.1), channel_id=1, source_target_pairs={{0,16},{16,0},{1,17},{17,1},{2,18},{18,2},{3,19},{19,3},{4,20},{20... | collective-permute-start | bytes 196616 | tf_op jit(solution)/shard_map/ppermute | solution.py:48
  18.5 6.2 %collective-permute-start.1 = (f32[128,128]{1,0:T(8,128)S(1)}, f32[128,128]{1,0:T(8,128)S(1)}, u32[]{:S(2)}, u32[]{:S(2)}) collective-permute-start(f32[128,128]{1,0:T(8,128)S(1)} %dynamic-slice_bitcast_fusion), channel_id=1, source_target_pairs={{0,32},{32,0},{64,96},{96,64},{128,160},{160,128},{192,224},{224,1... | collective-permute-start | bytes 196616 | tf_op jit(solution)/shard_map/ppermute | solution.py:48
  24.6 7.1 %collective-permute-start.2 = (f32[128,128]{1,0:T(8,128)S(1)}, f32[128,128]{1,0:T(8,128)S(1)}, u32[]{:S(2)}, u32[]{:S(2)}) collective-permute-start(f32[128,128]{1,0:T(8,128)S(1)} %bitcast_add_fusion.2), channel_id=1, source_target_pairs={{0,64},{32,96},{64,0},{96,32},{128,192},{160,224},{192,128},{224,1... | collective-permute-start | bytes 196616 | tf_op jit(solution)/shard_map/ppermute | solution.py:48
  31.7 25.4 %collective-permute-start.3 = (f32[128,128]{1,0:T(8,128)S(1)}, f32[128,128]{1,0:T(8,128)S(1)}, u32[]{:S(2)}, u32[]{:S(2)}) collective-permute-start(f32[128,128]{1,0:T(8,128)S(1)} %add.79), channel_id=1, source_target_pairs={{0,256},{256,0},{1,257},{257,1},{2,258},{258,2},{3,259},{259,3},{4... | collective-permute-start | bytes 196616 | tf_op jit(solution)/shard_map/ppermute | solution.py:48
  66.1 19.8 %copy-start.1 = (bf16[1152,512]{1,0:T(8,128)(2,1)}, bf16[1152,512]{1,0:T(8,128)(2,1)S(1)}, u32[]{:S(2)}) copy-start(bf16[1152,512]{1,0:T(8,128)(2,1)S(1)} %get-tuple-element.34) | copy-start | bytes 3538948
  66.1 19.8 %copy-start.3 = (bf16[1024,512]{1,0:T(8,128)(2,1)}, bf16[1024,512]{1,0:T(8,128)(2,1)S(1)}, u32[]{:S(2)}) copy-start(bf16[1024,512]{1,0:T(8,128)(2,1)S(1)} %get-tuple-element.42) | copy-start | bytes 3145732
  86.1 9.5 %collective-permute-start.4 = (bf16[144,512]{1,0:T(8,128)(2,1)S(1)}, bf16[144,512]{1,0:T(8,128)(2,1)S(1)}, u32[]{:S(2)}, u32[]{:S(2)}) collective-permute-start(bf16[144,512]{1,0:T(8,128)(2,1)S(1)} %get-tuple-element.56), channel_id=1, source_target_pairs={{0,2},{2,0},{1,3},{3,1},{4,6},{6,4},{5,7},{7,5},{8,10},{10,8},{9,1... | collective-permute-start | bytes 442376 | tf_op jit(solution)/shard_map/ppermute | solution.py:48
  96.9 17.0 %copy-start.2 = (bf16[1152,512]{1,0:T(8,128)(2,1)S(1)}, bf16[1152,512]{1,0:T(8,128)(2,1)}, u32[]{:S(2)}) copy-start(bf16[1152,512]{1,0:T(8,128)(2,1)} %copy-done.1) | copy-start | bytes 3538948
  96.9 17.0 %all-to-all-start.2 = ((bf16[8,144,512]{2,1,0:T(8,128)(2,1)}), bf16[8,144,512]{2,1,0:T(8,128)(2,1)S(1)}, u32[]{:S(2)}, u32[]{:S(2)}) async-start(bf16[8,144,512]{2,1,0:T(8,128)(2,1)} %get-tuple-element.39), calls=%async_computation.2 | async-start | bytes 2359296 | tf_op jit(solution)/shard_map/all_to_all | solution.py:43
  100.6 10.8 %collective-permute-start.5 = (f32[128,128]{1,0:T(8,128)S(1)}, f32[128,128]{1,0:T(8,128)S(1)}, u32[]{:S(2)}, u32[]{:S(2)}) collective-permute-start(f32[128,128]{1,0:T(8,128)S(1)} %add.80), channel_id=1, source_target_pairs={{0,128},{32,160},{64,192},{96,224},{128,0},{160,32},{192,64},{224,... | collective-permute-start | bytes 196616 | tf_op jit(solution)/shard_map/ppermute | solution.py:48
  113.9 1.4 copy-start.10
  113.9 1.5 copy-start.12
  114.8 3.0 %copy-start.14 = (f32[512,512]{1,0:T(8,128)}, f32[512,512]{1,0:T(8,128)S(1)}, u32[]{:S(2)}) copy-start(f32[512,512]{1,0:T(8,128)S(1)} %fusion.10) | copy-start | bytes 3145732
  117.8 15.5 %all-to-all-start.3 = ((bf16[8,128,512]{2,1,0:T(8,128)(2,1)}), bf16[8,128,512]{2,1,0:T(8,128)(2,1)S(1)}, u32[]{:S(2)}, u32[]{:S(2)}) async-start(bf16[8,128,512]{2,1,0:T(8,128)(2,1)} %bitcast.71), calls=%async_computation.3 | async-start | bytes 2097152 | tf_op jit(solution)/shard_map/all_to_all | solution.py:43
  121.4 6.2 %collective-permute-start.6 = (f32[128,128]{1,0:T(8,128)S(1)}, f32[128,128]{1,0:T(8,128)S(1)}, u32[]{:S(2)}, u32[]{:S(2)}) collective-permute-start(f32[128,128]{1,0:T(8,128)S(1)} %add.81), channel_id=1, source_target_pairs={{0,32},{32,0},{64,96},{96,64},{128,160},{160,128},{192,224},{224,1... | collective-permute-start | bytes 196616 | tf_op jit(solution)/shard_map/ppermute | solution.py:48
  133.5 8.9 %collective-permute-start.7 = (bf16[128,512]{1,0:T(8,128)(2,1)S(1)}, bf16[128,512]{1,0:T(8,128)(2,1)S(1)}, u32[]{:S(2)}, u32[]{:S(2)}) collective-permute-start(bf16[128,512]{1,0:T(8,128)(2,1)S(1)} %get-tuple-element.54), channel_id=1, source_target_pairs={{0,2},{2,0},{1,3},{3,1},{4,6},{6,4},{5,7},{7,5},{8,10},{10,8},{9,1... | collective-permute-start | bytes 393224 | tf_op jit(solution)/shard_map/ppermute | solution.py:48
  143.7 7.0 %copy-start.8 = (bf16[512,128]{1,0:T(8,128)(2,1)S(1)}, bf16[512,128]{1,0:T(8,128)(2,1)}, u32[]{:S(2)}) copy-start(bf16[512,128]{1,0:T(8,128)(2,1)} %param.15) | copy-start | bytes 393220
  143.7 15.9 %all-to-all-start.4 = ((bf16[8,144,512]{2,1,0:T(8,128)(2,1)}), bf16[8,144,512]{2,1,0:T(8,128)(2,1)S(1)}, u32[]{:S(2)}, u32[]{:S(2)}) async-start(bf16[8,144,512]{2,1,0:T(8,128)(2,1)} %errors.3), calls=%async_computation.4 | async-start | bytes 2359296 | tf_op jit(solution)/shard_map/all_to_all | solution.py:43
  147.4 3.2 %collective-permute-start.8 = (f32[256,128]{1,0:T(8,128)S(1)}, f32[256,128]{1,0:T(8,128)S(1)}, u32[]{:S(2)}, u32[]{:S(2)}) collective-permute-start(f32[256,128]{1,0:T(8,128)S(1)} %pad_maximum_fusion.2), channel_id=1, source_target_pairs={{0,16},{16,0},{1,17},{17,1},{2,18},{18,2},{3,19},{19,3},{4,20},{20... | collective-permute-start | bytes 393224 | tf_op jit(solution)/shard_map/ppermute | solution.py:48
  151.7 8.0 %copy-start.5 = (bf16[1024,512]{1,0:T(8,128)(2,1)S(1)}, bf16[1024,512]{1,0:T(8,128)(2,1)}, u32[]{:S(2)}) copy-start(bf16[1024,512]{1,0:T(8,128)(2,1)} %copy-done.3) | copy-start | bytes 3145732
  (4 other events, 4.4 us)

commit v14 on v13

--- a/solution.py
+++ b/solution.py
@@ -249,7 +249,7 @@
     y_at = lax.rem(lax.axis_index("y"), 2)
     summed = summed.reshape(2, half // 2, frag_width)
     summed = pick(summed, y_at, 0) + swap(pick(summed, y_at ^ 1, 0), "y")
-    for axis, bit in (("y", 2), ("zh", 1)):
+    for axis, bit in (("y", 2), ("y", 4), ("zh", 1)):
         summed = summed + swap(summed, axis, bit)
 
     def whole(mine, other, at):
@@ -281,7 +281,6 @@
         sent, summed = tie(sent, summed)
         got = exchange(sent, GROUP)
         if step == 0:
-            summed = summed + swap(summed, "y", 4)
             got, summed = tie(got, summed)
         else:
             summed = whole(summed, swap(summed, "c"), c_at)

time: 167 us -> 164 us (0.982)
  blocking collectives: 19.8 us -> 35.6 us
  waiting for transfers between devices: 71.7 us -> 56.7 us
  starting transfers between devices: 52.7 us -> 50.4 us
    all_to_all x1 -> x2, blocking collectives: 19.8 us -> 35.6 us  [exchange(): lax.all_to_all(blocks, axes, split_axis=0, concat_axis=0, tiled=False)]
    ppermute x9, waiting for transfers between devices: 48.1 us -> 35.4 us  [swap(): return lax.ppermute(block, axis, [(i, i ^ bit) for i in range(size)])]
    all_to_all x4 -> x3, starting transfers between devices: 20.9 us -> 17.2 us  [exchange(): lax.all_to_all(blocks, axes, split_axis=0, concat_axis=0, tiled=False)]
    all_to_all x4 -> x3, waiting for transfers between devices: 23.6 us -> 21.3 us  [exchange(): lax.all_to_all(blocks, axes, split_axis=0, concat_axis=0, tiled=False)]
  transfers between devices with their start and end apart: 13 -> 12, of which waited for: 13 -> 12; matrix products, arithmetic and copies ran while one was open for 1% -> 1% of each run, Pallas kernels for 0% -> 0%
where the time goes in v14:
time: 164 us; the launch traced here: 163 us
  waiting for transfers between devices  56.7 us (35%)
  starting transfers between devices  50.4 us (31%)
  blocking collectives  35.6 us (22%)
  matrix products  6.57 us (4%)
  Pallas kernels  6.01 us (4%)
  other arithmetic  3.27 us (2%)
  local copies, waits for them, and re-layouts  2.72 us (2%)
  between operations  1.71 us (1%)
    all_to_all x2, blocking collectives, exchange(): lax.all_to_all(blocks, axes, split_axis=0, concat_axis=0, tiled=False)  35.6 us
    ppermute x9, waiting for transfers between devices, swap(): return lax.ppermute(block, axis, [(i, i ^ bit) for i in range(size)])  35.4 us
    ppermute x9, starting transfers between devices, swap(): return lax.ppermute(block, axis, [(i, i ^ bit) for i in range(size)])  33.2 us
    all_to_all x3, waiting for transfers between devices, exchange(): lax.all_to_all(blocks, axes, split_axis=0, concat_axis=0, tiled=False)  21.3 us
    all_to_all x3, starting transfers between devices, exchange(): lax.all_to_all(blocks, axes, split_axis=0, concat_axis=0, tiled=False)  17.2 us
    dot_general x2, matrix products, body(): lax.dot_general(rows_now, everyone, (((0,), (0,)), ((), ())), preferred_e...  4.21 us
  transfers between devices with their start and end apart: 12, of which 12 were waited for; matrix products, arithmetic and copies ran while one was open for 1% of the time, Pallas kernels for 0%

profile of v14, /device:TPU:56, one launch (start us, length us, event | category | flops | bytes accessed | tf_op | source)
XLA Modules:
  0.0 163.1 jit_solution(6246705981723578433)
XLA Ops:
  0.6 2.9 %normalize.1 = bf16[16,2,64,512]{3,2,1,0:T(8,128)(2,1)} custom-call(bf16[1,2,64,8192]{3,2,1,0:T(8,128)(2,1)} %hidden_ref.1), custom_call_target="tpu_custom_call" | custom-call | tf_op jit(solution)/shard_map/normalize/pallas_call | solution.py:97
  3.6 10.0 %all-to-all-start = ((bf16[16,2,64,512]{3,2,1,0:T(8,128)(2,1)}), bf16[16,2,64,512]{3,2,1,0:T(8,128)(2,1)S(1)}, u32[]{:S(2)}, u32[]{:S(2)}) async-start(bf16[16,2,64,512]{3,2,1,0:T(8,128)(2,1)} %normalize.1), calls=%async_computation | async-start | bytes 4194304 | tf_op jit(solution)/shard_map/all_to_all | solution.py:43
  18.4 3.3 %collective-permute-start.1 = (f32[128,128]{1,0:T(8,128)S(1)}, f32[128,128]{1,0:T(8,128)S(1)}, u32[]{:S(2)}, u32[]{:S(2)}) collective-permute-start(f32[128,128]{1,0:T(8,128)S(1)} %dynamic-slice_bitcast_fusion), channel_id=1, source_target_pairs={{0,32},{32,0},{64,96},{96,64},{128,160},{160,128},{192,224},{224,1... | collective-permute-start | bytes 196616 | tf_op jit(solution)/shard_map/ppermute | solution.py:48
  21.9 2.7 %collective-permute-done.1 = f32[128,128]{1,0:T(8,128)S(1)} collective-permute-done((f32[128,128]{1,0:T(8,128)S(1)}, f32[128,128]{1,0:T(8,128)S(1)}, u32[]{:S(2)}, u32[]{:S(2)}) %collective-permute-start.1) | collective-permute-done | bytes 65568 | tf_op jit(solution)/shard_map/ppermute | solution.py:48
  24.6 4.0 %collective-permute-start.2 = (f32[128,128]{1,0:T(8,128)S(1)}, f32[128,128]{1,0:T(8,128)S(1)}, u32[]{:S(2)}, u32[]{:S(2)}) collective-permute-start(f32[128,128]{1,0:T(8,128)S(1)} %bitcast_add_fusion.2), channel_id=1, source_target_pairs={{0,64},{32,96},{64,0},{96,32},{128,192},{160,224},{192,128},{224,1... | collective-permute-start | bytes 196616 | tf_op jit(solution)/shard_map/ppermute | solution.py:48
  28.7 3.0 %collective-permute-done.2 = f32[128,128]{1,0:T(8,128)S(1)} collective-permute-done((f32[128,128]{1,0:T(8,128)S(1)}, f32[128,128]{1,0:T(8,128)S(1)}, u32[]{:S(2)}, u32[]{:S(2)}) %collective-permute-start.2) | collective-permute-done | bytes 65568 | tf_op jit(solution)/shard_map/ppermute | solution.py:48
  31.7 5.3 %collective-permute-start.3 = (f32[128,128]{1,0:T(8,128)S(1)}, f32[128,128]{1,0:T(8,128)S(1)}, u32[]{:S(2)}, u32[]{:S(2)}) collective-permute-start(f32[128,128]{1,0:T(8,128)S(1)} %add.79), channel_id=1, source_target_pairs={{0,128},{32,160},{64,192},{96,224},{128,0},{160,32},{192,64},{224,... | collective-permute-start | bytes 196616 | tf_op jit(solution)/shard_map/ppermute | solution.py:48
  37.1 4.9 %collective-permute-done.3 = f32[128,128]{1,0:T(8,128)S(1)} collective-permute-done((f32[128,128]{1,0:T(8,128)S(1)}, f32[128,128]{1,0:T(8,128)S(1)}, u32[]{:S(2)}, u32[]{:S(2)}) %collective-permute-start.3) | collective-permute-done | bytes 65568 | tf_op jit(solution)/shard_map/ppermute | solution.py:48
  41.9 8.2 %collective-permute-start.4 = (f32[128,128]{1,0:T(8,128)S(1)}, f32[128,128]{1,0:T(8,128)S(1)}, u32[]{:S(2)}, u32[]{:S(2)}) collective-permute-start(f32[128,128]{1,0:T(8,128)S(1)} %add.80), channel_id=1, source_target_pairs={{0,256},{256,0},{1,257},{257,1},{2,258},{258,2},{3,259},{259,3},{4... | collective-permute-start | bytes 196616 | tf_op jit(solution)/shard_map/ppermute | solution.py:48
  50.2 6.1 %collective-permute-done.4 = f32[128,128]{1,0:T(8,128)S(1)} collective-permute-done((f32[128,128]{1,0:T(8,128)S(1)}, f32[128,128]{1,0:T(8,128)S(1)}, u32[]{:S(2)}, u32[]{:S(2)}) %collective-permute-start.4) | collective-permute-done | bytes 65568 | tf_op jit(solution)/shard_map/ppermute | solution.py:48
  56.3 8.2 %all-to-all-done.columns_ref = bf16[16,2,64,512]{3,2,1,0:T(8,128)(2,1)S(1)} async-done(((bf16[16,2,64,512]{3,2,1,0:T(8,128)(2,1)}), bf16[16,2,64,512]{3,2,1,0:T(8,128)(2,1)S(1)}, u32[]{:S(2)}, u32[]{:S(2)}) %all-to-all-start) | async-done | bytes 2097184 | tf_op jit(solution)/shard_map/all_to_all | solution.py:43
  66.1 19.8 %all_to_all.25 = bf16[8,144,512]{2,1,0:T(8,128)(2,1)S(1)} all-to-all(bf16[8,144,512]{2,1,0:T(8,128)(2,1)S(1)} %get-tuple-element.35), channel_id=1, replica_groups=mesh['zh'=2,'y'=8,'c'=2,'x'=4,'zf'=2,'zn'=2] {'x','zn'}, dimensions={0} | all-to-all | bytes 2359296 | tf_op jit(solution)/shard_map/all_to_all | solution.py:43
  86.1 2.6 %collective-permute-start.5 = (bf16[144,512]{1,0:T(8,128)(2,1)S(1)}, bf16[144,512]{1,0:T(8,128)(2,1)S(1)}, u32[]{:S(2)}, u32[]{:S(2)}) collective-permute-start(bf16[144,512]{1,0:T(8,128)(2,1)S(1)} %get-tuple-element.56), channel_id=1, source_target_pairs={{0,2},{2,0},{1,3},{3,1},{4,6},{6,4},{5,7},{7,5},{8,10},{10,8},{9,1... | collective-permute-start | bytes 442376 | tf_op jit(solution)/shard_map/ppermute | solution.py:48
  88.6 6.9 %collective-permute-done.5.got_ref = bf16[144,512]{1,0:T(8,128)(2,1)S(1)} collective-permute-done((bf16[144,512]{1,0:T(8,128)(2,1)S(1)}, bf16[144,512]{1,0:T(8,128)(2,1)S(1)}, u32[]{:S(2)}, u32[]{:S(2)}) %collective-permute-start.5) | collective-permute-done | bytes 147488 | tf_op jit(solution)/shard_map/ppermute | solution.py:48
  95.8 15.8 %all_to_all.26 = bf16[8,144,512]{2,1,0:T(8,128)(2,1)S(1)} all-to-all(bf16[8,144,512]{2,1,0:T(8,128)(2,1)S(1)} %get-tuple-element.39), channel_id=1, replica_groups=mesh['zh'=2,'y'=8,'c'=2,'x'=4,'zf'=2,'zn'=2] {'x','zn'}, dimensions={0} | all-to-all | bytes 2359296 | tf_op jit(solution)/shard_map/all_to_all | solution.py:43
  115.2 3.6 %all-to-all-start.3 = ((bf16[8,128,512]{2,1,0:T(8,128)(2,1)}), bf16[8,128,512]{2,1,0:T(8,128)(2,1)S(1)}, u32[]{:S(2)}, u32[]{:S(2)}) async-start(bf16[8,128,512]{2,1,0:T(8,128)(2,1)} %bitcast.71), calls=%async_computation.3 | async-start | bytes 2097152 | tf_op jit(solution)/shard_map/all_to_all | solution.py:43
  118.8 3.3 %collective-permute-start.6 = (f32[128,128]{1,0:T(8,128)S(1)}, f32[128,128]{1,0:T(8,128)S(1)}, u32[]{:S(2)}, u32[]{:S(2)}) collective-permute-start(f32[128,128]{1,0:T(8,128)S(1)} %add.81), channel_id=1, source_target_pairs={{0,32},{32,0},{64,96},{96,64},{128,160},{160,128},{192,224},{224,1... | collective-permute-start | bytes 196616 | tf_op jit(solution)/shard_map/ppermute | solution.py:48
  122.1 2.9 %collective-permute-done.6 = f32[128,128]{1,0:T(8,128)S(1)} collective-permute-done((f32[128,128]{1,0:T(8,128)S(1)}, f32[128,128]{1,0:T(8,128)S(1)}, u32[]{:S(2)}, u32[]{:S(2)}) %collective-permute-start.6) | collective-permute-done | bytes 65568 | tf_op jit(solution)/shard_map/ppermute | solution.py:48
  125.0 5.3 %all-to-all-done.3 = bf16[8,128,512]{2,1,0:T(8,128)(2,1)S(1)} async-done(((bf16[8,128,512]{2,1,0:T(8,128)(2,1)}), bf16[8,128,512]{2,1,0:T(8,128)(2,1)S(1)}, u32[]{:S(2)}, u32[]{:S(2)}) %all-to-all-start.3) | async-done | bytes 1048608 | tf_op jit(solution)/shard_map/all_to_all | solution.py:43
  130.5 2.7 %collective-permute-start.7 = (bf16[128,512]{1,0:T(8,128)(2,1)S(1)}, bf16[128,512]{1,0:T(8,128)(2,1)S(1)}, u32[]{:S(2)}, u32[]{:S(2)}) collective-permute-start(bf16[128,512]{1,0:T(8,128)(2,1)S(1)} %get-tuple-element.54), channel_id=1, source_target_pairs={{0,2},{2,0},{1,3},{3,1},{4,6},{6,4},{5,7},{7,5},{8,10},{10,8},{9,1... | collective-permute-start | bytes 393224 | tf_op jit(solution)/shard_map/ppermute | solution.py:48
  133.2 6.4 %collective-permute-done.7.got_ref = bf16[128,512]{1,0:T(8,128)(2,1)S(1)} collective-permute-done((bf16[128,512]{1,0:T(8,128)(2,1)S(1)}, bf16[128,512]{1,0:T(8,128)(2,1)S(1)}, u32[]{:S(2)}, u32[]{:S(2)}) %collective-permute-start.7) | collective-permute-done | bytes 131104 | tf_op jit(solution)/shard_map/ppermute | solution.py:48
  140.9 3.7 %all-to-all-start.4 = ((bf16[8,144,512]{2,1,0:T(8,128)(2,1)}), bf16[8,144,512]{2,1,0:T(8,128)(2,1)S(1)}, u32[]{:S(2)}, u32[]{:S(2)}) async-start(bf16[8,144,512]{2,1,0:T(8,128)(2,1)} %errors.3), calls=%async_computation.4 | async-start | bytes 2359296 | tf_op jit(solution)/shard_map/all_to_all | solution.py:43
  148.9 7.9 %all-to-all-done.4 = bf16[8,144,512]{2,1,0:T(8,128)(2,1)S(1)} async-done(((bf16[8,144,512]{2,1,0:T(8,128)(2,1)}), bf16[8,144,512]{2,1,0:T(8,128)(2,1)S(1)}, u32[]{:S(2)}, u32[]{:S(2)}) %all-to-all-start.4) | async-done | bytes 1179680 | tf_op jit(solution)/shard_map/all_to_all | solution.py:43
  158.0 3.4 %multiply_subtract_fusion = f32[512,512]{1,0:T(8,128)S(1)} fusion(f32[512,512]{1,0:T(8,128)} %copy-done.11, bf16[1,512,512]{2,1,0:T(8,128)(2,1)S(1)} %copy-done.8, bf16[1,512,512]{2,1,0:T(8,128)(2,1)S(1)} %copy-done.10, bf16[1,512,512]{2,1,0:T(8,128)(2,1)S(1)} %copy-done, bf16[1024,512]{1,0:T(8,128)(2,1)S(1)} %copy-done.2, bf16[1024,512]{1,0:T(8,128)(2,1)S(1)} %bitcast.72), kind=kOutput, calls=%fused_computation.9 | convolution fusion | flops 544997376 | bytes 5767168 | tf_op jit(solution)/shard_map/dot_general | solution.py:294
  (64 shorter events, 18.7 us)
Async XLA Ops:
  3.5 10.7 %copy-start = (bf16[1,512,512]{2,1,0:T(8,128)(2,1)S(1)}, bf16[1,512,512]{2,1,0:T(8,128)(2,1)}, u32[]{:S(2)}) copy-start(bf16[1,512,512]{2,1,0:T(8,128)(2,1)} %weights_ref) | copy-start | bytes 1572868
  3.5 12.7 %copy-start.4 = (bf16[1,2,64,512]{3,2,1,0:T(8,128)(2,1)S(1)}, bf16[1,2,64,512]{3,2,1,0:T(8,128)(2,1)}, u32[]{:S(2)}) copy-start(bf16[1,2,64,512]{3,2,1,0:T(8,128)(2,1)} %param.10) | copy-start | bytes 393220
  3.5 12.7 %copy-start.6 = (s32[1,2,64]{2,1,0:T(2,128)S(1)}, s32[1,2,64]{2,1,0:T(2,128)}, u32[]{:S(2)}) copy-start(s32[1,2,64]{2,1,0:T(2,128)} %param.11) | copy-start | bytes 1540
  3.6 60.9 %all-to-all-start = ((bf16[16,2,64,512]{3,2,1,0:T(8,128)(2,1)}), bf16[16,2,64,512]{3,2,1,0:T(8,128)(2,1)S(1)}, u32[]{:S(2)}, u32[]{:S(2)}) async-start(bf16[16,2,64,512]{3,2,1,0:T(8,128)(2,1)} %normalize.1), calls=%async_computation | async-start | bytes 4194304 | tf_op jit(solution)/shard_map/all_to_all | solution.py:43
  14.3 3.3 %collective-permute-start = (bf16[256,128]{1,0:T(8,128)(2,1)S(1)}, bf16[256,128]{1,0:T(8,128)(2,1)}, u32[]{:S(2)}, u32[]{:S(2)}) collective-permute-start(bf16[256,128]{1,0:T(8,128)(2,1)S(1)} %dynamic-slice_bitcast_fusion.1), channel_id=1, source_target_pairs={{0,16},{16,0},{1,17},{17,1},{2,18},{18,2},{3,19},{19,3},{4,20},{20... | collective-permute-start | bytes 196616 | tf_op jit(solution)/shard_map/ppermute | solution.py:48
  18.4 6.2 %collective-permute-start.1 = (f32[128,128]{1,0:T(8,128)S(1)}, f32[128,128]{1,0:T(8,128)S(1)}, u32[]{:S(2)}, u32[]{:S(2)}) collective-permute-start(f32[128,128]{1,0:T(8,128)S(1)} %dynamic-slice_bitcast_fusion), channel_id=1, source_target_pairs={{0,32},{32,0},{64,96},{96,64},{128,160},{160,128},{192,224},{224,1... | collective-permute-start | bytes 196616 | tf_op jit(solution)/shard_map/ppermute | solution.py:48
  24.6 7.1 %collective-permute-start.2 = (f32[128,128]{1,0:T(8,128)S(1)}, f32[128,128]{1,0:T(8,128)S(1)}, u32[]{:S(2)}, u32[]{:S(2)}) collective-permute-start(f32[128,128]{1,0:T(8,128)S(1)} %bitcast_add_fusion.2), channel_id=1, source_target_pairs={{0,64},{32,96},{64,0},{96,32},{128,192},{160,224},{192,128},{224,1... | collective-permute-start | bytes 196616 | tf_op jit(solution)/shard_map/ppermute | solution.py:48
  31.7 10.3 %collective-permute-start.3 = (f32[128,128]{1,0:T(8,128)S(1)}, f32[128,128]{1,0:T(8,128)S(1)}, u32[]{:S(2)}, u32[]{:S(2)}) collective-permute-start(f32[128,128]{1,0:T(8,128)S(1)} %add.79), channel_id=1, source_target_pairs={{0,128},{32,160},{64,192},{96,224},{128,0},{160,32},{192,64},{224,... | collective-permute-start | bytes 196616 | tf_op jit(solution)/shard_map/ppermute | solution.py:48
  41.9 14.3 %collective-permute-start.4 = (f32[128,128]{1,0:T(8,128)S(1)}, f32[128,128]{1,0:T(8,128)S(1)}, u32[]{:S(2)}, u32[]{:S(2)}) collective-permute-start(f32[128,128]{1,0:T(8,128)S(1)} %add.80), channel_id=1, source_target_pairs={{0,256},{256,0},{1,257},{257,1},{2,258},{258,2},{3,259},{259,3},{4... | collective-permute-start | bytes 196616 | tf_op jit(solution)/shard_map/ppermute | solution.py:48
  66.1 46.5 %copy-start.1 = (bf16[1024,512]{1,0:T(8,128)(2,1)}, bf16[1024,512]{1,0:T(8,128)(2,1)S(1)}, u32[]{:S(2)}) copy-start(bf16[1024,512]{1,0:T(8,128)(2,1)S(1)} %get-tuple-element.42) | copy-start | bytes 3145732
  86.1 9.5 %collective-permute-start.5 = (bf16[144,512]{1,0:T(8,128)(2,1)S(1)}, bf16[144,512]{1,0:T(8,128)(2,1)S(1)}, u32[]{:S(2)}, u32[]{:S(2)}) collective-permute-start(bf16[144,512]{1,0:T(8,128)(2,1)S(1)} %get-tuple-element.56), channel_id=1, source_target_pairs={{0,2},{2,0},{1,3},{3,1},{4,6},{6,4},{5,7},{7,5},{8,10},{10,8},{9,1... | collective-permute-start | bytes 442376 | tf_op jit(solution)/shard_map/ppermute | solution.py:48
  111.7 1.0 copy-start.7
  111.7 1.2 copy-start.9
  112.5 2.7 %copy-start.11 = (f32[512,512]{1,0:T(8,128)}, f32[512,512]{1,0:T(8,128)S(1)}, u32[]{:S(2)}) copy-start(f32[512,512]{1,0:T(8,128)S(1)} %fusion.10) | copy-start | bytes 3145732
  115.2 15.0 %all-to-all-start.3 = ((bf16[8,128,512]{2,1,0:T(8,128)(2,1)}), bf16[8,128,512]{2,1,0:T(8,128)(2,1)S(1)}, u32[]{:S(2)}, u32[]{:S(2)}) async-start(bf16[8,128,512]{2,1,0:T(8,128)(2,1)} %bitcast.71), calls=%async_computation.3 | async-start | bytes 2097152 | tf_op jit(solution)/shard_map/all_to_all | solution.py:43
  118.8 6.2 %collective-permute-start.6 = (f32[128,128]{1,0:T(8,128)S(1)}, f32[128,128]{1,0:T(8,128)S(1)}, u32[]{:S(2)}, u32[]{:S(2)}) collective-permute-start(f32[128,128]{1,0:T(8,128)S(1)} %add.81), channel_id=1, source_target_pairs={{0,32},{32,0},{64,96},{96,64},{128,160},{160,128},{192,224},{224,1... | collective-permute-start | bytes 196616 | tf_op jit(solution)/shard_map/ppermute | solution.py:48
  130.5 9.2 %collective-permute-start.7 = (bf16[128,512]{1,0:T(8,128)(2,1)S(1)}, bf16[128,512]{1,0:T(8,128)(2,1)S(1)}, u32[]{:S(2)}, u32[]{:S(2)}) collective-permute-start(bf16[128,512]{1,0:T(8,128)(2,1)S(1)} %get-tuple-element.54), channel_id=1, source_target_pairs={{0,2},{2,0},{1,3},{3,1},{4,6},{6,4},{5,7},{7,5},{8,10},{10,8},{9,1... | collective-permute-start | bytes 393224 | tf_op jit(solution)/shard_map/ppermute | solution.py:48
  140.9 7.0 %copy-start.5 = (bf16[512,128]{1,0:T(8,128)(2,1)S(1)}, bf16[512,128]{1,0:T(8,128)(2,1)}, u32[]{:S(2)}) copy-start(bf16[512,128]{1,0:T(8,128)(2,1)} %param.15) | copy-start | bytes 393220
  140.9 15.9 %all-to-all-start.4 = ((bf16[8,144,512]{2,1,0:T(8,128)(2,1)}), bf16[8,144,512]{2,1,0:T(8,128)(2,1)S(1)}, u32[]{:S(2)}, u32[]{:S(2)}) async-start(bf16[8,144,512]{2,1,0:T(8,128)(2,1)} %errors.3), calls=%async_computation.4 | async-start | bytes 2359296 | tf_op jit(solution)/shard_map/all_to_all | solution.py:43
  144.6 3.2 %collective-permute-start.8 = (f32[256,128]{1,0:T(8,128)S(1)}, f32[256,128]{1,0:T(8,128)S(1)}, u32[]{:S(2)}, u32[]{:S(2)}) collective-permute-start(f32[256,128]{1,0:T(8,128)S(1)} %pad_maximum_fusion.2), channel_id=1, source_target_pairs={{0,16},{16,0},{1,17},{17,1},{2,18},{18,2},{3,19},{19,3},{4,20},{20... | collective-permute-start | bytes 393224 | tf_op jit(solution)/shard_map/ppermute | solution.py:48
  148.9 8.0 %copy-start.2 = (bf16[1024,512]{1,0:T(8,128)(2,1)S(1)}, bf16[1024,512]{1,0:T(8,128)(2,1)}, u32[]{:S(2)}) copy-start(bf16[1024,512]{1,0:T(8,128)(2,1)} %copy-done.1) | copy-start | bytes 3145732
  156.8 1.0 copy-start.8
  156.8 1.2 copy-start.10
  162.1 1.0 copy-start.3
